TPU v7x, 32 devices: a whole 2x2x4 slice. The times are simulated.
32 devices in a mesh: parts: 2 (over y), wide: 4 (over z), narrow: 2 (over x), pair: 2 (over core).
Axes of the slice: x: 2, y: 2, z: 4, core: 2. Of those that a mesh axis runs over, the one named last changes fastest.
Arguments:
- low_sino: bfloat16 [8, 24, 32, 512], P(('parts', 'wide'), None, None, ('narrow', 'pair')), parts along dimension 0, may hold values from -6 to 6
- angle_weight: bfloat16 [4, 24, 24], replicated, may hold values from -1.25 to 1.25
- angle_bias: float32 [24], replicated, may hold values from -3 to 3
- column_weight: bfloat16 [4, 24, 24], replicated, may hold values from -0.875 to 0.875
- column_bias: float32 [24], replicated, may hold values from -3 to 3
- head_weight: float32 [24], replicated, may hold values from -1.25 to 1.25
- sparse_views: int32 [4, 16], P(('parts', 'narrow')), parts along dimension 0, may hold values from 0 to 7
- measured: float32 [32, 16, 512], P('parts', 'wide', ('narrow', 'pair')), parts along dimension 0, may hold values from -6 to 6
- row_weights: float32 [512, 512], P(('narrow', 'pair')), may hold values from -0.25 to 0.25
Outputs:
- predicted: float32 [16, 16, 512], P('parts', 'wide', ('narrow', 'pair')), parts along dimension 0
- adjoint: float32 [32, 16, 512], P('parts', 'wide', ('narrow', 'pair')), parts along dimension 0
There are 2 independent parts, one for each index of `parts`. A program takes and returns all parts, laid end to end along the dimension named above; an argument that names none is the same for every part. Nothing has to cross between parts.
All inputs are finite; a program needn't handle non-finite values.
Results may differ from a plain program's by a relative error of at most 0.0034.
Values may be sent and summed in bfloat16 or wider, within the bound.
No kernel may reach another device: no remote copies, remote signals or barrier semaphores. Data moves between devices by JAX's collectives and lax.ppermute only.
A program may use at most 64 MiB of HBM per device.

v0:
```python
import jax
import jax.numpy as jnp
from jax import lax
from jax.sharding import PartitionSpec as P


def from_behind(block, axis, distance):
    devices = range(lax.axis_size(axis))
    route = [((i - distance) % len(devices), i) for i in devices]
    return lax.ppermute(block, axis, route)


def leaky_relu(values):
    return jnp.where(values > 0, values, 0.1 * values)


def channel_mix(inputs, weight):
    return jnp.einsum("vcwr,cd->vdwr", inputs, weight, preferred_element_type=jnp.float32)


def upsample(current, previous, weight, bias_values):
    even_views = channel_mix(current, weight[0]) + channel_mix(previous, weight[2])
    odd_views = channel_mix(current, weight[1]) + channel_mix(previous, weight[3])
    stacked = jnp.stack([even_views, odd_views], axis=1) + bias_values[None, None, :, None, None]
    return (
        leaky_relu(stacked)
        .reshape(2 * current.shape[0], current.shape[1], current.shape[2], current.shape[3])
        .astype(jnp.bfloat16)
    )


def detector_head(padded, col_count, column_weight, column_bias, head_weight):
    summed = channel_mix(padded[:, :, 0:col_count:2], column_weight[0])
    for tap_index in range(1, 4):
        summed = summed + channel_mix(
            padded[:, :, tap_index : tap_index + col_count : 2], column_weight[tap_index]
        )
    hidden = leaky_relu(summed + column_bias[None, :, None, None])
    return jnp.sum(hidden * head_weight[None, :, None, None], axis=1)


def local(
    low_sino,
    angle_weight,
    angle_bias,
    column_weight,
    column_bias,
    head_weight,
    sparse_views,
    measured,
    row_weights,
):
    last_view = from_behind(low_sino, "wide", 1)
    previous = jnp.concatenate([last_view, low_sino[:-1]], axis=0)
    upsampled = upsample(low_sino, previous, angle_weight, angle_bias)
    padded = jnp.pad(upsampled, ((0, 0), (0, 0), (1, 1), (0, 0)))
    own_views = detector_head(padded, upsampled.shape[2], column_weight, column_bias, head_weight)
    predicted = lax.all_to_all(own_views, "wide", split_axis=1, concat_axis=0, tiled=True)
    residual_slab = jnp.take(predicted, sparse_views[0], axis=0) - measured
    adjoint = jnp.einsum(
        "kjr,zr->kjz",
        lax.all_gather(residual_slab, ("narrow", "pair"), axis=2, tiled=True),
        row_weights,
        precision=lax.Precision.HIGHEST,
    )
    return (predicted, adjoint)


def solution(mesh):
    in_specs = (
        P(("parts", "wide"), None, None, ("narrow", "pair")),
        P(),
        P(),
        P(),
        P(),
        P(),
        P(("parts", "narrow"), None),
        P("parts", "wide", ("narrow", "pair")),
        P(("narrow", "pair"), None),
    )
    out_specs = (P("parts", "wide", ("narrow", "pair")), P("parts", "wide", ("narrow", "pair")))
    return jax.shard_map(local, mesh=mesh, in_specs=in_specs, out_specs=out_specs, check_vma=False)
```

profile of v0, /device:TPU:0, one launch (start us, length us, event | category | flops | bytes accessed | tf_op | source)
XLA Modules:
  0.0 31.6 jit_solution(15347137212192712056)
XLA Ops:
  0.6 0.0 copy-start
  0.7 1.1 %copy.58 = bf16[1,24,32,128]{3,1,2,0:T(8,128)(2,1)S(1)} copy(bf16[1,24,32,128]{3,2,1,0:T(8,128)(2,1)} %param.9) | data formatting | bytes 393216 | tf_op args[0]
  1.7 3.1 %collective-permute-start = (bf16[1,24,32,128]{3,1,2,0:T(8,128)(2,1)S(1)}, bf16[1,24,32,128]{3,1,2,0:T(8,128)(2,1)S(1)}, u32[]{:S(2)}, u32[]{:S(2)}) collective-permute-start(bf16[1,24,32,128]{3,1,2,0:T(8,128)(2,1)S(1)} %copy.58), channel_id=1, source_target_pairs={{12,0},{0,4},{4,8},{8,12},{13,1},{1,5},{5,9},{9,13},{14,2},{2,6},{... | collective-permute-start | bytes 589832 | tf_op jit(solution)/shard_map/ppermute | solution.py:10
  4.8 0.2 fusion.12
  5.1 0.0 copy-start.7
  5.1 0.2 fusion.14
  5.3 0.4 %copy-done.7 = s32[1,16]{1,0:T(1,128)S(1)} copy-done((s32[1,16]{1,0:T(1,128)S(1)}, s32[1,16]{1,0:T(1,128)}, u32[]{:S(2)}) %copy-start.7) | copy-done | bytes 88
  5.7 6.0 %collective-permute-done = bf16[1,24,32,128]{3,1,2,0:T(8,128)(2,1)S(1)} collective-permute-done((bf16[1,24,32,128]{3,1,2,0:T(8,128)(2,1)S(1)}, bf16[1,24,32,128]{3,1,2,0:T(8,128)(2,1)S(1)}, u32[]{:S(2)}, u32[]{:S(2)}) %collective-permute-start) | collective-permute-done | bytes 196640 | tf_op jit(solution)/shard_map/ppermute | solution.py:10
  11.7 0.2 fusion
  12.0 0.0 copy-start.6
  12.0 0.2 fusion.1
  12.2 0.4 %copy-done.6 = f32[24]{0:T(128)S(1)} copy-done((f32[24]{0:T(128)S(1)}, f32[24]{0:T(128)}, u32[]{:S(2)}) %copy-start.6) | copy-done | bytes 120
  12.6 0.2 fusion.4
  12.8 0.5 %copy-done.5 = bf16[4,24,24]{2,1,0:T(8,128)(2,1)S(1)} copy-done((bf16[4,24,24]{2,1,0:T(8,128)(2,1)S(1)}, bf16[4,24,24]{2,1,0:T(8,128)(2,1)}, u32[]{:S(2)}) %copy-start.5) | copy-done | bytes 4632
  13.4 0.2 fusion.9
  13.6 0.2 convolution_add_fusion.2
  13.9 0.0 copy-start.8
  13.9 0.0 copy-start.9
  13.9 0.3 convolution_add_fusion.1
  14.2 0.4 %copy-done.8 = f32[24]{0:T(128)S(1)} copy-done((f32[24]{0:T(128)S(1)}, f32[24]{0:T(128)}, u32[]{:S(2)}) %copy-start.8) | copy-done | bytes 120
  14.5 0.0 copy-done.9
  14.6 0.3 %fusion.6 = f32[2,16,128]{2,1,0:T(8,128)S(1)} fusion(f32[2,16,128,24]{2,3,1,0:T(8,128)S(1)} %convolution_add_fusion.1, bf16[2,24,32,128]{3,1,2,0:T(8,128)(2,1)S(1)} %fusion.4, f32[24]{0:T(128)S(1)} %copy-done.8, f32[24]{0:T(128)S(1)} %copy-done.9, bf16[4,24,24]{2,1,0:T(8,128)(2,1)S(1)} %copy-done.5), kind=kOutput, calls=%fused_computation.15 | convolution fusion | flops 5402624 | bytes 809984 | tf_op jit(solution)/shard_map/vcwr,cd->vdwr/dot_general | solution.py:18
  14.9 0.6 %copy.66 = f32[2,16,128]{2,0,1:T(2,128)} copy(f32[2,16,128]{2,1,0:T(8,128)S(1)} %fusion.6) | data formatting | bytes 32768 | tf_op jit(solution)/shard_map/reduce_sum | solution.py:39
  15.5 3.3 %all-to-all-start = ((f32[2,16,128]{2,0,1:T(2,128)}), f32[2,16,128]{2,0,1:T(2,128)S(1)}, u32[]{:S(2)}, u32[]{:S(2)}) async-start(f32[2,16,128]{2,0,1:T(2,128)} %copy.66), calls=%async_computation | async-start | bytes 32768 | tf_op jit(solution)/shard_map/all_to_all | solution.py:58
  18.8 5.6 %all-to-all-done = f32[2,16,128]{2,0,1:T(2,128)S(1)} async-done(((f32[2,16,128]{2,0,1:T(2,128)}), f32[2,16,128]{2,0,1:T(2,128)S(1)}, u32[]{:S(2)}, u32[]{:S(2)}) %all-to-all-start) | async-done | bytes 16416 | tf_op jit(solution)/shard_map/all_to_all | solution.py:58
  24.4 0.0 copy-start.3
  24.4 0.6 %gather_fusion = f32[16,4,128]{2,1,0:T(4,128)S(1)} fusion(f32[8,4,128]{2,1,0:T(4,128)S(1)} %bitcast.86, s32[1024]{0:T(1024)S(1)} %pad_clamp_fusion), kind=kCustom, calls=%fused_computation | custom fusion | bytes 65600 | tf_op jit(solution)/shard_map/jit(_take)/gather | solution.py:59
  25.0 0.2 copy-done.3
  25.1 0.1 copy_subtract_fusion
  25.2 5.4 %all_gather.3 = f32[16,4,512]{2,0,1:T(8,128)S(1)} all-gather(f32[16,4,128]{2,0,1:T(8,128)S(1)} %copy_subtract_fusion), channel_id=1, replica_groups=mesh['parts'=2,'wide'=4,'narrow'=2,'pair'=2] {'narrow','pair'}, dimensions={2}, use_global_device_ids=true | all-gather | bytes 163840 | tf_op jit(solution)/shard_map/all_gather | solution.py:62
  30.6 0.4 %fusion.7 = f32[16,4,128]{2,0,1:T(8,128)S(1)} fusion(f32[16,4,512]{2,0,1:T(8,128)S(1)} %all_gather.3, f32[128,512]{1,0:T(8,128)S(1)} %copy-done), kind=kOutput, calls=%fused_computation.20 | convolution fusion | flops 50331648 | bytes 425984 | tf_op jit(solution)/shard_map/kjr,zr->kjz/dot_general | solution.py:60
  31.0 0.6 %copy.71 = f32[16,4,128]{2,1,0:T(4,128)} copy(f32[16,4,128]{2,0,1:T(8,128)S(1)} %fusion.7) | data formatting | bytes 65536
  (13 shorter events, 0.0 us)
Async XLA Ops:
  0.6 30.0 %copy-start = (f32[128,512]{1,0:T(8,128)S(1)}, f32[128,512]{1,0:T(8,128)}, u32[]{:S(2)}) copy-start(f32[128,512]{1,0:T(8,128)} %param.17) | copy-start | bytes 786436
  0.6 4.2 %copy-start.1 = (bf16[1,24,32,128]{3,2,1,0:T(8,128)(2,1)S(1)}, bf16[1,24,32,128]{3,2,1,0:T(8,128)(2,1)}, u32[]{:S(2)}) copy-start(bf16[1,24,32,128]{3,2,1,0:T(8,128)(2,1)} %param.9) | copy-start | bytes 589828
  0.7 4.2 %copy-start.4 = (bf16[4,24,24]{2,1,0:T(8,128)(2,1)S(1)}, bf16[4,24,24]{2,1,0:T(8,128)(2,1)}, u32[]{:S(2)}) copy-start(bf16[4,24,24]{2,1,0:T(8,128)(2,1)} %param.10) | copy-start | bytes 13828
  1.7 10.0 %collective-permute-start = (bf16[1,24,32,128]{3,1,2,0:T(8,128)(2,1)S(1)}, bf16[1,24,32,128]{3,1,2,0:T(8,128)(2,1)S(1)}, u32[]{:S(2)}, u32[]{:S(2)}) collective-permute-start(bf16[1,24,32,128]{3,1,2,0:T(8,128)(2,1)S(1)} %copy.58), channel_id=1, source_target_pairs={{12,0},{0,4},{4,8},{8,12},{13,1},{1,5},{5,9},{9,13},{14,2},{2,6},{... | collective-permute-start | bytes 589832 | tf_op jit(solution)/shard_map/ppermute | solution.py:10
  5.1 0.7 %copy-start.7 = (s32[1,16]{1,0:T(1,128)S(1)}, s32[1,16]{1,0:T(1,128)}, u32[]{:S(2)}) copy-start(s32[1,16]{1,0:T(1,128)} %param.15) | copy-start | bytes 196
  12.0 0.7 %copy-start.6 = (f32[24]{0:T(128)S(1)}, f32[24]{0:T(128)}, u32[]{:S(2)}) copy-start(f32[24]{0:T(128)} %param.11) | copy-start | bytes 292
  12.6 0.7 %copy-start.5 = (bf16[4,24,24]{2,1,0:T(8,128)(2,1)S(1)}, bf16[4,24,24]{2,1,0:T(8,128)(2,1)}, u32[]{:S(2)}) copy-start(bf16[4,24,24]{2,1,0:T(8,128)(2,1)} %param.12) | copy-start | bytes 13828
  13.9 0.7 %copy-start.8 = (f32[24]{0:T(128)S(1)}, f32[24]{0:T(128)}, u32[]{:S(2)}) copy-start(f32[24]{0:T(128)} %param.14) | copy-start | bytes 292
  13.9 0.7 %copy-start.9 = (f32[24]{0:T(128)S(1)}, f32[24]{0:T(128)}, u32[]{:S(2)}) copy-start(f32[24]{0:T(128)} %param.13) | copy-start | bytes 292
  15.5 8.8 %all-to-all-start = ((f32[2,16,128]{2,0,1:T(2,128)}), f32[2,16,128]{2,0,1:T(2,128)S(1)}, u32[]{:S(2)}, u32[]{:S(2)}) async-start(f32[2,16,128]{2,0,1:T(2,128)} %copy.66), calls=%async_computation | async-start | bytes 32768 | tf_op jit(solution)/shard_map/all_to_all | solution.py:58
  24.3 0.6 %copy-start.2 = (f32[4,2,4,128]{3,2,1,0:T(4,128)}, f32[4,2,4,128]{3,2,1,0:T(4,128)S(1)}, u32[]{:S(2)}) copy-start(f32[4,2,4,128]{3,2,1,0:T(4,128)S(1)} %copy.68) | copy-start | bytes 49156
  24.4 0.8 %copy-start.3 = (f32[16,4,128]{2,1,0:T(4,128)S(1)}, f32[16,4,128]{2,1,0:T(4,128)}, u32[]{:S(2)}) copy-start(f32[16,4,128]{2,1,0:T(4,128)} %param.16) | copy-start | bytes 98308
where the time goes:
time: 32 us; the launch traced here: 31.6 us
  waiting for transfers between devices  11.6 us (36%)
  starting transfers between devices  6.33 us (20%)
  blocking collectives  5.41 us (17%)
  local copies, waits for them, and re-layouts  4.83 us (15%)
  matrix products  2.41 us (8%)
  between operations  0.8 us (2%)
    ppermute x1, waiting for transfers between devices, from_behind(): return lax.ppermute(block, axis, route)  6.01 us
    all_to_all x1, waiting for transfers between devices, local(): lax.all_to_all(own_views, 'wide', split_axis=1, concat_axis=0, tiled=True)  5.57 us
    all_gather x1, blocking collectives, local(): lax.all_gather(residual_slab, ('narrow', 'pair'), axis=2, tiled=True)  5.41 us
    unnamed x22, local copies, waits for them, and re-layouts  3.62 us
    all_to_all x1, starting transfers between devices, local(): lax.all_to_all(own_views, 'wide', split_axis=1, concat_axis=0, tiled=True)  3.25 us
    ppermute x1, starting transfers between devices, from_behind(): return lax.ppermute(block, axis, route)  3.08 us
    dot_general x8, matrix products, channel_mix(): jnp.einsum('vcwr,cd->vdwr', inputs, weight, preferred_element_type=jnp.fl...  2.02 us
  transfers between devices with their start and end apart: 2, of which 2 were waited for; matrix products, arithmetic and copies ran while one was open for 2% of the time, Pallas kernels for 0%

commit v1 on v0

v1 whole, which is shorter than its diff:
```python
import functools

import jax
import jax.numpy as jnp
from jax import lax
from jax.experimental import pallas as pl
from jax.experimental.pallas import tpu as pltpu
from jax.sharding import PartitionSpec as P

F32, BF16 = jnp.float32, jnp.bfloat16
VMEM = pl.BlockSpec(memory_space=pltpu.VMEM)
SMEM = pl.BlockSpec(memory_space=pltpu.SMEM)
TAPS = 4


def call(kernel, outs, in_specs, scratch=(), vmem=16, flops=10**6):
    nbytes = sum(o.size * o.dtype.itemsize for o in jax.tree.leaves(outs))
    return pl.pallas_call(
        kernel,
        out_shape=outs,
        in_specs=in_specs,
        out_specs=jax.tree.map(lambda _: VMEM, outs),
        scratch_shapes=list(scratch),
        compiler_params=pltpu.CompilerParams(vmem_limit_bytes=vmem << 20),
        cost_estimate=pl.CostEstimate(flops=flops, bytes_accessed=nbytes, transcendentals=0),
    )


def leaky_relu(values):
    return jnp.maximum(values, 0.1 * values)


def split(index, size):
    whole = ((index.astype(F32) + 0.5) * (1.0 / size)).astype(jnp.int32)
    return whole, index - whole * size


def iota(shape, axis):
    return lax.broadcasted_iota(jnp.int32, shape, axis)


def pack_kernel(wide, low_ref, *refs):
    windows, rows_ref = refs[:-1], refs[-1]
    _, channels, width, rows = low_ref.shape
    rows_ref[...] = low_ref[0].astype(F32).reshape(channels * width, rows)
    own = width // wide
    me = lax.axis_index("wide")
    for shift in range(wide):
        first = lax.rem(me + shift, wide) * own - 1
        columns = []
        for i in range(own + 2):
            column = jnp.clip(first + i, 0, width - 1)
            columns.append(rows_ref[pl.ds(column, channels, stride=width), :])
        windows[shift][...] = jnp.concatenate(columns, axis=0).astype(BF16)


def expand_kernel(wide, own_out, aw_ref, ab_ref, cw_ref, cb_ref, hw_ref, rw_ref, a1_ref, a2_ref, b1_ref, b2_ref, h_ref, hi_ref, lo_ref):
    channels = aw_ref.shape[1]
    span = 2 * own_out + 2
    size, outs = span * channels, own_out * channels
    rows, columns = split(iota((size, channels), 0), channels)
    pick = (columns == iota((size, channels), 1)).astype(F32)
    pick16 = pick.astype(BF16)
    out_channel, _ = split(iota((outs, channels), 0), own_out)
    pick_out = (out_channel == iota((outs, channels), 1)).astype(F32)
    pick_out16 = pick_out.astype(BF16)

    def spread(left, weight):
        half = lax.dot_general(left, weight, (((1,), (1,)), ((), ())), preferred_element_type=F32)
        return lax.dot_general(half.astype(BF16), pick16, (((1,), (1,)), ((), ())), preferred_element_type=F32)

    same = split(iota((size, size), 0), channels)[0] == split(iota((size, size), 1), channels)[0]
    for tap in range(4):
        full = jnp.where(same, spread(pick16, aw_ref[tap]), 0.0).astype(BF16)
        a1_ref[tap // 2, (tap % 2) * size : (tap % 2 + 1) * size, :] = full

    in_column = split(iota((outs, size), 1), channels)[0]
    out_column = split(iota((outs, size), 0), own_out)[1]
    me = lax.axis_index("wide")
    absolute = in_column + me * (2 * own_out) - 1
    inside = (absolute >= 0) & (absolute < 2 * own_out * wide)
    total = jnp.zeros((outs, size), F32)
    for tap in range(TAPS):
        here = (in_column == 2 * out_column + tap) & inside
        total = jnp.where(here, spread(pick_out16, cw_ref[tap]), total)
    a2_ref[...] = total.astype(BF16)

    def along(left, vector_ref, out_ref):
        out_ref[...] = jnp.broadcast_to(jnp.sum(left * vector_ref[...], axis=1, keepdims=True), out_ref.shape)

    along(pick, ab_ref, b1_ref)
    along(pick_out, cb_ref, b2_ref)
    along(pick_out, hw_ref, h_ref)

    turned = rw_ref[...].T
    high = turned.astype(BF16)
    hi_ref[...] = high
    lo_ref[...] = (turned - high.astype(F32)).astype(BF16)


def net_kernel(wide, own_out, *refs):
    views = refs[:wide]
    a1_ref, a2_ref, b1_ref, b2_ref, h_ref, sparse_ref, measured_ref, predicted_ref, residual_ref = refs[wide:]
    size, lanes = views[0].shape
    outs = a2_ref.shape[0]
    me = lax.axis_index("wide")
    group = 2 if wide % 2 == 0 else 1
    wider = lambda ref, times: jnp.concatenate([ref[...]] * times, axis=1)
    b1 = wider(b1_ref, group)
    b2, h = wider(b2_ref, 2 * group), wider(h_ref, 2 * group)
    fold = 8 // own_out
    for start in range(0, wide, group):
        current = jnp.concatenate([views[start + i][...] for i in range(group)], axis=1)
        previous = jnp.concatenate([views[(start + i + 1) % wide][...] for i in range(group)], axis=1)
        upsampled = []
        for e in range(2):
            rows = pl.ds(e * size, size)
            summed = jnp.dot(a1_ref[0, rows, :], current, preferred_element_type=F32)
            summed += jnp.dot(a1_ref[1, rows, :], previous, preferred_element_type=F32)
            upsampled.append(leaky_relu(summed + b1).astype(BF16))
        both = jnp.concatenate(upsampled, axis=1)
        hidden = leaky_relu(jnp.dot(a2_ref[...], both, preferred_element_type=F32) + b2) * h
        part = jnp.sum(hidden.reshape(outs // 8, 8, hidden.shape[1]), axis=0)
        value = part[:own_out]
        for i in range(1, fold):
            value += part[i * own_out : (i + 1) * own_out]
        for e in range(2):
            for i in range(group):
                view = lax.rem(me - (start + i) + wide, wide)
                at = (e * group + i) * lanes
                predicted_ref[2 * view + e] = value[:, at : at + lanes]
    for k in range(measured_ref.shape[0]):
        residual = predicted_ref[sparse_ref[0, k]] - measured_ref[k]
        residual_ref[k * own_out : (k + 1) * own_out, :] = residual


def adjoint_kernel(count, own_out, *refs):
    residuals = refs[:count]
    hi_ref, lo_ref, out_ref = refs[count:]
    lanes = residuals[0].shape[1]
    me = lax.axis_index(("narrow", "pair"))
    total = None
    for shift in range(count):
        block = lax.rem(me - shift + count, count)
        rows = pl.ds(pl.multiple_of(block * lanes, lanes), lanes)
        values = residuals[shift][...]
        high = values.astype(BF16)
        low = (values - high.astype(F32)).astype(BF16)
        term = jnp.dot(high, hi_ref[rows, :], preferred_element_type=F32)
        term += jnp.dot(low, hi_ref[rows, :], preferred_element_type=F32)
        term += jnp.dot(high, lo_ref[rows, :], preferred_element_type=F32)
        total = term if total is None else total + term
    for k in range(out_ref.shape[0]):
        out_ref[k] = total[k * own_out : (k + 1) * own_out]


def send(block, axis, distance):
    count = lax.axis_size(axis)
    return lax.ppermute(block, axis, [(i, (i + distance) % count) for i in range(count)])


def local(
    low_sino,
    angle_weight,
    angle_bias,
    column_weight,
    column_bias,
    head_weight,
    sparse_views,
    measured,
    row_weights,
):
    wide = lax.axis_size("wide")
    group = ("narrow", "pair")
    count = lax.axis_size(group)
    _, channels, width, lanes = low_sino.shape
    own_out = width // wide // 2
    span = 2 * own_out + 2
    size, outs = span * channels, own_out * channels
    shape = jax.ShapeDtypeStruct
    big = 16 if width <= 64 else 48

    windows = call(
        functools.partial(pack_kernel, wide),
        [shape((size, lanes), BF16)] * wide,
        [VMEM],
        [pltpu.VMEM((channels * width, lanes), F32)],
        vmem=big,
    )(low_sino)
    views = [windows[0]] + [send(windows[s], "wide", s) for s in range(1, wide)]

    rows = row_weights.shape[1]
    a1, a2, b1, b2, head, high, low = call(
        functools.partial(expand_kernel, wide, own_out),
        [
            shape((2, 2 * size, size), BF16),
            shape((outs, size), BF16),
            shape((size, lanes), F32),
            shape((outs, lanes), F32),
            shape((outs, lanes), F32),
            shape((rows, lanes), BF16),
            shape((rows, lanes), BF16),
        ],
        [VMEM] * 6,
        vmem=big,
    )(angle_weight, angle_bias[None], column_weight, column_bias[None], head_weight[None], row_weights)

    sparse_count = measured.shape[0]
    predicted, residual = call(
        functools.partial(net_kernel, wide, own_out),
        [shape((2 * wide, own_out, lanes), F32), shape((sparse_count * own_out, lanes), F32)],
        [VMEM] * (wide + 5) + [SMEM, VMEM],
        vmem=big,
    )(*views, a1, a2, b1, b2, head, sparse_views, measured)

    blocks = [residual] + [send(residual, group, s) for s in range(1, count)]
    adjoint = call(
        functools.partial(adjoint_kernel, count, own_out),
        shape((sparse_count, own_out, lanes), F32),
        [VMEM] * (count + 2),
        vmem=big,
    )(*blocks, high, low)
    return (predicted, adjoint)


def solution(mesh):
    in_specs = (
        P(("parts", "wide"), None, None, ("narrow", "pair")),
        P(),
        P(),
        P(),
        P(),
        P(),
        P(("parts", "narrow"), None),
        P("parts", "wide", ("narrow", "pair")),
        P(("narrow", "pair"), None),
    )
    out_specs = (P("parts", "wide", ("narrow", "pair")), P("parts", "wide", ("narrow", "pair")))
    return jax.shard_map(local, mesh=mesh, in_specs=in_specs, out_specs=out_specs, check_vma=False)
```

time: 32 us -> 20.8 us (0.65)
  waiting for transfers between devices: 11.6 us -> 3.88 us
  blocking collectives: 5.41 us -> 0 us
  Pallas kernels: 0 us -> 4.12 us
  matrix products: 2.41 us -> 0 us
  starting transfers between devices: 6.33 us -> 8.73 us
  local copies, waits for them, and re-layouts: 4.83 us -> 3.2 us
    ppermute x1 -> x6, starting transfers between devices: 3.08 us -> 8.73 us  [send(): lax.ppermute(block, axis, [(i, (i + distance) % count) for i in range(cou...]
    all_to_all x1 -> x0, waiting for transfers between devices: 5.57 us -> none  [local(): lax.all_to_all(own_views, 'wide', split_axis=1, concat_axis=0, tiled=True)]
    all_gather x1 -> x0, blocking collectives: 5.41 us -> none  [local(): lax.all_gather(residual_slab, ('narrow', 'pair'), axis=2, tiled=True)]
    pallas_call x0 -> x4, Pallas kernels: none -> 4.12 us  [the longest x1 1.9 us: local(): call(functools.partial(net_kernel, wide, own_out), [shape((2 * wide, own_...]
    all_to_all x1 -> x0, starting transfers between devices: 3.25 us -> none  [local(): lax.all_to_all(own_views, 'wide', split_axis=1, concat_axis=0, tiled=True)]
    dot_general x9 -> x0, matrix products: 2.41 us -> none  [the longest x8 2.02 us: channel_mix(): jnp.einsum('vcwr,cd->vdwr', inputs, weight, preferred_element_type=jnp.fl...]
    ppermute x1 -> x6, waiting for transfers between devices: 6.01 us -> 3.88 us  [send(): lax.ppermute(block, axis, [(i, (i + distance) % count) for i in range(cou...]
    reduce_sum x1 -> x0, local copies, waits for them, and re-layouts: 0.62 us -> none  [detector_head(): return jnp.sum(hidden * head_weight[None, :, None, None], axis=1)]
  transfers between devices with their start and end apart: 2 -> 6, of which waited for: 2 -> 4; matrix products, arithmetic and copies ran while one was open for 2% -> 0% of each run, Pallas kernels for 0% -> 4%
where the time goes in v1:
time: 20.8 us; the launch traced here: 20.6 us
  starting transfers between devices  8.73 us (42%)
  Pallas kernels  4.12 us (20%)
  waiting for transfers between devices  3.88 us (19%)
  local copies, waits for them, and re-layouts  3.2 us (15%)
  between operations  0.67 us (3%)
    ppermute x6, starting transfers between devices, send(): lax.ppermute(block, axis, [(i, (i + distance) % count) for i in range(cou...  8.73 us
    ppermute x6, waiting for transfers between devices, send(): lax.ppermute(block, axis, [(i, (i + distance) % count) for i in range(cou...  3.88 us
    unnamed x18, local copies, waits for them, and re-layouts  3.2 us
    pallas_call x1, Pallas kernels, local(): call(functools.partial(net_kernel, wide, own_out), [shape((2 * wide, own_...  1.9 us
    pallas_call x1, Pallas kernels, local(): call(functools.partial(adjoint_kernel, count, own_out), shape((sparse_cou...  0.86 us
    pallas_call x1, Pallas kernels, local(): call(functools.partial(expand_kernel, wide, own_out), [shape((2, 2 * size...  0.82 us
    pallas_call x1, Pallas kernels, local(): call(functools.partial(pack_kernel, wide), [shape((size, lanes), BF16)] *...  0.54 us
  transfers between devices with their start and end apart: 6, of which 4 were waited for; matrix products, arithmetic and copies ran while one was open for 0% of the time, Pallas kernels for 4%

profile of v1, /device:TPU:0, one launch (start us, length us, event | category | flops | bytes accessed | tf_op | source)
XLA Modules:
  0.0 20.6 jit_solution(16359360684186433103)
XLA Ops:
  0.6 0.0 copy-start.1
  0.6 0.9 %copy-done.1 = bf16[1,24,32,128]{3,2,1,0:T(8,128)(2,1)S(1)} copy-done((bf16[1,24,32,128]{3,2,1,0:T(8,128)(2,1)S(1)}, bf16[1,24,32,128]{3,2,1,0:T(8,128)(2,1)}, u32[]{:S(2)}) %copy-start.1) | copy-done | bytes 196632
  1.6 0.0 copy-start.3
  1.6 0.0 copy-start.4
  1.6 0.5 %shard_map.104 = (bf16[240,128]{1,0:T(8,128)(2,1)S(1)}, bf16[240,128]{1,0:T(8,128)(2,1)S(1)}, bf16[240,128]{1,0:T(8,128)(2,1)S(1)}, bf16[240,128]{1,0:T(8,128)(2,1)S(1)}) custom-call(bf16[1,24,32,128]{3,2,1,0:T(8,128)(2,1)S(1)} %copy-done.1), custom_call_target="tpu_custom_call" | custom-call | flops 1000000 | bytes 245760 | tf_op jit(solution)/shard_map/pallas_call | solution.py:183
  2.1 3.1 %collective-permute-start = (bf16[240,128]{1,0:T(8,128)(2,1)S(1)}, bf16[240,128]{1,0:T(8,128)(2,1)S(1)}, u32[]{:S(2)}, u32[]{:S(2)}) collective-permute-start(bf16[240,128]{1,0:T(8,128)(2,1)S(1)} %get-tuple-element.16), channel_id=1, source_target_pairs={{0,4},{4,8},{8,12},{12,0},{1,5},{5,9},{9,13},{13,1},{2,6},{6,10},{... | collective-permute-start | bytes 184328 | tf_op jit(solution)/shard_map/ppermute | solution.py:159
  5.2 2.6 %collective-permute-start.1 = (bf16[240,128]{1,0:T(8,128)(2,1)S(1)}, bf16[240,128]{1,0:T(8,128)(2,1)S(1)}, u32[]{:S(2)}, u32[]{:S(2)}) collective-permute-start(bf16[240,128]{1,0:T(8,128)(2,1)S(1)} %get-tuple-element.17), channel_id=1, source_target_pairs={{0,8},{4,12},{8,0},{12,4},{1,9},{5,13},{9,1},{13,5},{2,10},{6,14},... | collective-permute-start | bytes 184328 | tf_op jit(solution)/shard_map/ppermute | solution.py:159
  7.8 1.3 %collective-permute-start.2 = (bf16[240,128]{1,0:T(8,128)(2,1)S(1)}, bf16[240,128]{1,0:T(8,128)(2,1)S(1)}, u32[]{:S(2)}, u32[]{:S(2)}) collective-permute-start(bf16[240,128]{1,0:T(8,128)(2,1)S(1)} %get-tuple-element.18), channel_id=1, source_target_pairs={{0,12},{4,0},{8,4},{12,8},{1,13},{5,1},{9,5},{13,9},{2,14},{6,2},{... | collective-permute-start | bytes 184328 | tf_op jit(solution)/shard_map/ppermute | solution.py:159
  9.1 0.0 copy-start.5
  9.1 0.0 copy-start.6
  9.1 0.0 copy-start.7
  9.1 0.0 copy-done.3
  9.1 0.0 copy-done.4
  9.1 0.6 %copy-done.5 = f32[24]{0:T(128)S(1)} copy-done((f32[24]{0:T(128)S(1)}, f32[24]{0:T(128)}, u32[]{:S(2)}) %copy-start.5) | copy-done | bytes 120
  9.8 0.0 copy-done.6
  9.8 0.0 copy-done.7
  9.8 0.0 copy-start
  9.8 0.9 %copy-done = f32[128,512]{1,0:T(8,128)S(1)} copy-done((f32[128,512]{1,0:T(8,128)S(1)}, f32[128,512]{1,0:T(8,128)}, u32[]{:S(2)}) %copy-start) | copy-done | bytes 262168
  10.8 0.8 %shard_map.105 = (bf16[2,480,240]{2,1,0:T(8,128)(2,1)S(1)}, bf16[96,240]{1,0:T(8,128)(2,1)S(1)}, f32[240,128]{1,0:T(8,128)S(1)}, f32[96,128]{1,0:T(8,128)S(1)}, ...) custom-call(bf16[4,24,24]{2,1,0:T(8,128)(2,1)S(1)} %copy-done.3, ...), custom_call_target="tpu_custom_call" | custom-call | flops 1000000 | bytes 990208 | tf_op jit(solution)/shard_map/pallas_call | solution.py:193
  11.6 0.0 collective-permute-done.refs_1_
  11.6 0.4 %collective-permute-done.1.refs_2_ = bf16[240,128]{1,0:T(8,128)(2,1)S(1)} collective-permute-done((bf16[240,128]{1,0:T(8,128)(2,1)S(1)}, bf16[240,128]{1,0:T(8,128)(2,1)S(1)}, u32[]{:S(2)}, u32[]{:S(2)}) %collective-permute-start.1) | collective-permute-done | bytes 61472 | tf_op jit(solution)/shard_map/ppermute | solution.py:159
  12.0 0.3 %collective-permute-done.2.refs_3_ = bf16[240,128]{1,0:T(8,128)(2,1)S(1)} collective-permute-done((bf16[240,128]{1,0:T(8,128)(2,1)S(1)}, bf16[240,128]{1,0:T(8,128)(2,1)S(1)}, u32[]{:S(2)}, u32[]{:S(2)}) %collective-permute-start.2) | collective-permute-done | bytes 61472 | tf_op jit(solution)/shard_map/ppermute | solution.py:159
  12.4 0.0 copy-done.2
  12.4 0.7 %copy-done.8 = s32[1,16]{1,0:T(1,128)S(1)} copy-done((s32[1,16]{1,0:T(1,128)S(1)}, s32[1,16]{1,0:T(1,128)}, u32[]{:S(2)}) %copy-start.8) | copy-done | bytes 88
  13.0 1.9 %shard_map.106 = (f32[8,4,128]{2,1,0:T(4,128)}, f32[64,128]{1,0:T(8,128)S(1)}) custom-call(bf16[240,128]{1,0:T(8,128)(2,1)S(1)} %get-tuple-element.15.refs_0_, bf16[240,128]{1,0:T(8,128)(2,1)S(1)} %collective-permute-done.refs_1_, bf16[240,128]{1,0:T(8,128)(2,1)S(1)} %collective-permute-done.1.refs_2_, bf16[240,128]{1,0:T(8,128)(2,1)S(1)} %collective-permute-done.2.refs_3_, ...), custom_call_target="tpu_custom_call" | custom-call | flops 1000000 | bytes 49152 | tf_op jit(solution)/shard_map/pallas_call | solution.py:209
  14.9 0.0 collective-permute-start.5
  14.9 1.5 %collective-permute-start.4 = (f32[64,128]{1,0:T(8,128)S(1)}, f32[64,128]{1,0:T(8,128)S(1)}, u32[]{:S(2)}, u32[]{:S(2)}) collective-permute-start(f32[64,128]{1,0:T(8,128)S(1)} %get-tuple-element.25.refs_0_), channel_id=1, source_target_pairs={{0,2},{1,3},{2,0},{3,1},{4,6},{5,7},{6,4},{7,5},{8,10},{9,11},{10,... | collective-permute-start | bytes 98312 | tf_op jit(solution)/shard_map/ppermute | solution.py:159
  16.4 0.2 %collective-permute-start.3 = (f32[64,128]{1,0:T(8,128)S(1)}, f32[64,128]{1,0:T(8,128)S(1)}, u32[]{:S(2)}, u32[]{:S(2)}) collective-permute-start(f32[64,128]{1,0:T(8,128)S(1)} %get-tuple-element.25.refs_0_), channel_id=1, source_target_pairs={{0,1},{1,2},{2,3},{3,0},{4,5},{5,6},{6,7},{7,4},{8,9},{9,10},{10,1... | collective-permute-start | bytes 98312 | tf_op jit(solution)/shard_map/ppermute | solution.py:159
  16.6 0.0 collective-permute-done.5.refs_3_
  16.6 2.4 %collective-permute-done.4.refs_2_ = f32[64,128]{1,0:T(8,128)S(1)} collective-permute-done((f32[64,128]{1,0:T(8,128)S(1)}, f32[64,128]{1,0:T(8,128)S(1)}, u32[]{:S(2)}, u32[]{:S(2)}) %collective-permute-start.4) | collective-permute-done | bytes 32800 | tf_op jit(solution)/shard_map/ppermute | solution.py:159
  19.0 0.7 %collective-permute-done.3.refs_1_ = f32[64,128]{1,0:T(8,128)S(1)} collective-permute-done((f32[64,128]{1,0:T(8,128)S(1)}, f32[64,128]{1,0:T(8,128)S(1)}, u32[]{:S(2)}, u32[]{:S(2)}) %collective-permute-start.3) | collective-permute-done | bytes 32800 | tf_op jit(solution)/shard_map/ppermute | solution.py:159
  19.7 0.9 %shard_map.107 = f32[16,4,128]{2,1,0:T(4,128)} custom-call(f32[64,128]{1,0:T(8,128)S(1)} %get-tuple-element.25.refs_0_, f32[64,128]{1,0:T(8,128)S(1)} %collective-permute-done.3.refs_1_, f32[64,128]{1,0:T(8,128)S(1)} %collective-permute-done.4.refs_2_, f32[64,128]{1,0:T(8,128)S(1)} %collective-permute-done.5.refs_3_, ...), custom_call_target="tpu_custom_call" | custom-call | flops 1000000 | bytes 32768 | tf_op jit(solution)/shard_map/pallas_call | solution.py:217
  (2 shorter events, 0.0 us)
Async XLA Ops:
  0.6 0.9 %copy-start.1 = (bf16[1,24,32,128]{3,2,1,0:T(8,128)(2,1)S(1)}, bf16[1,24,32,128]{3,2,1,0:T(8,128)(2,1)}, u32[]{:S(2)}) copy-start(bf16[1,24,32,128]{3,2,1,0:T(8,128)(2,1)} %low_ref.1) | copy-start | bytes 589828
  1.6 7.6 %copy-start.3 = (bf16[4,24,24]{2,1,0:T(8,128)(2,1)S(1)}, bf16[4,24,24]{2,1,0:T(8,128)(2,1)}, u32[]{:S(2)}) copy-start(bf16[4,24,24]{2,1,0:T(8,128)(2,1)} %aw_ref.1) | copy-start | bytes 13828
  1.6 7.6 %copy-start.4 = (bf16[4,24,24]{2,1,0:T(8,128)(2,1)S(1)}, bf16[4,24,24]{2,1,0:T(8,128)(2,1)}, u32[]{:S(2)}) copy-start(bf16[4,24,24]{2,1,0:T(8,128)(2,1)} %cw_ref.1) | copy-start | bytes 13828
  2.1 9.5 %collective-permute-start = (bf16[240,128]{1,0:T(8,128)(2,1)S(1)}, bf16[240,128]{1,0:T(8,128)(2,1)S(1)}, u32[]{:S(2)}, u32[]{:S(2)}) collective-permute-start(bf16[240,128]{1,0:T(8,128)(2,1)S(1)} %get-tuple-element.16), channel_id=1, source_target_pairs={{0,4},{4,8},{8,12},{12,0},{1,5},{5,9},{9,13},{13,1},{2,6},{6,10},{... | collective-permute-start | bytes 184328 | tf_op jit(solution)/shard_map/ppermute | solution.py:159
  5.2 6.9 %collective-permute-start.1 = (bf16[240,128]{1,0:T(8,128)(2,1)S(1)}, bf16[240,128]{1,0:T(8,128)(2,1)S(1)}, u32[]{:S(2)}, u32[]{:S(2)}) collective-permute-start(bf16[240,128]{1,0:T(8,128)(2,1)S(1)} %get-tuple-element.17), channel_id=1, source_target_pairs={{0,8},{4,12},{8,0},{12,4},{1,9},{5,13},{9,1},{13,5},{2,10},{6,14},... | collective-permute-start | bytes 184328 | tf_op jit(solution)/shard_map/ppermute | solution.py:159
  7.8 4.6 %collective-permute-start.2 = (bf16[240,128]{1,0:T(8,128)(2,1)S(1)}, bf16[240,128]{1,0:T(8,128)(2,1)S(1)}, u32[]{:S(2)}, u32[]{:S(2)}) collective-permute-start(bf16[240,128]{1,0:T(8,128)(2,1)S(1)} %get-tuple-element.18), channel_id=1, source_target_pairs={{0,12},{4,0},{8,4},{12,8},{1,13},{5,1},{9,5},{13,9},{2,14},{6,2},{... | collective-permute-start | bytes 184328 | tf_op jit(solution)/shard_map/ppermute | solution.py:159
  9.1 0.7 %copy-start.5 = (f32[24]{0:T(128)S(1)}, f32[24]{0:T(128)}, u32[]{:S(2)}) copy-start(f32[24]{0:T(128)} %param.11) | copy-start | bytes 292
  9.1 0.7 %copy-start.6 = (f32[24]{0:T(128)S(1)}, f32[24]{0:T(128)}, u32[]{:S(2)}) copy-start(f32[24]{0:T(128)} %param.13) | copy-start | bytes 292
  9.1 0.7 %copy-start.7 = (f32[24]{0:T(128)S(1)}, f32[24]{0:T(128)}, u32[]{:S(2)}) copy-start(f32[24]{0:T(128)} %param.14) | copy-start | bytes 292
  9.8 0.9 %copy-start = (f32[128,512]{1,0:T(8,128)S(1)}, f32[128,512]{1,0:T(8,128)}, u32[]{:S(2)}) copy-start(f32[128,512]{1,0:T(8,128)} %rw_ref.1) | copy-start | bytes 786436
  10.8 1.6 %copy-start.2 = (f32[16,4,128]{2,1,0:T(4,128)S(1)}, f32[16,4,128]{2,1,0:T(4,128)}, u32[]{:S(2)}) copy-start(f32[16,4,128]{2,1,0:T(4,128)} %refs_10_.1) | copy-start | bytes 98308
  12.4 0.7 %copy-start.8 = (s32[1,16]{1,0:T(1,128)S(1)}, s32[1,16]{1,0:T(1,128)}, u32[]{:S(2)}) copy-start(s32[1,16]{1,0:T(1,128)} %refs_9_.1) | copy-start | bytes 196
  14.9 1.7 %collective-permute-start.5 = (f32[64,128]{1,0:T(8,128)S(1)}, f32[64,128]{1,0:T(8,128)S(1)}, u32[]{:S(2)}, u32[]{:S(2)}) collective-permute-start(f32[64,128]{1,0:T(8,128)S(1)} %get-tuple-element.25.refs_0_), channel_id=1, source_target_pairs={{0,3},{1,0},{2,1},{3,2},{4,7},{5,4},{6,5},{7,6},{8,11},{9,8},{10,9... | collective-permute-start | bytes 98312 | tf_op jit(solution)/shard_map/ppermute | solution.py:159
  14.9 4.1 %collective-permute-start.4 = (f32[64,128]{1,0:T(8,128)S(1)}, f32[64,128]{1,0:T(8,128)S(1)}, u32[]{:S(2)}, u32[]{:S(2)}) collective-permute-start(f32[64,128]{1,0:T(8,128)S(1)} %get-tuple-element.25.refs_0_), channel_id=1, source_target_pairs={{0,2},{1,3},{2,0},{3,1},{4,6},{5,7},{6,4},{7,5},{8,10},{9,11},{10,... | collective-permute-start | bytes 98312 | tf_op jit(solution)/shard_map/ppermute | solution.py:159
  16.4 3.3 %collective-permute-start.3 = (f32[64,128]{1,0:T(8,128)S(1)}, f32[64,128]{1,0:T(8,128)S(1)}, u32[]{:S(2)}, u32[]{:S(2)}) collective-permute-start(f32[64,128]{1,0:T(8,128)S(1)} %get-tuple-element.25.refs_0_), channel_id=1, source_target_pairs={{0,1},{1,2},{2,3},{3,0},{4,5},{5,6},{6,7},{7,4},{8,9},{9,10},{10,1... | collective-permute-start | bytes 98312 | tf_op jit(solution)/shard_map/ppermute | solution.py:159

commit v2 on v1

--- a/solution.py
+++ b/solution.py
@@ -54,7 +54,14 @@
         windows[shift][...] = jnp.concatenate(columns, axis=0).astype(BF16)
 
 
-def expand_kernel(wide, own_out, aw_ref, ab_ref, cw_ref, cb_ref, hw_ref, rw_ref, a1_ref, a2_ref, b1_ref, b2_ref, h_ref, hi_ref, lo_ref):
+def prepare_kernel(
+    wide, own_out, aw_ref, ab_ref, cw_ref, cb_ref, hw_ref, rw_ref, sparse_ref, measured_ref, *refs
+):
+    waiting, refs = refs[: wide - 1], refs[wide - 1 :]
+    onward, refs = refs[: wide - 1], refs[wide - 1 :]
+    a1_ref, a2_ref, b1_ref, b2_ref, h_ref, hi_ref, lo_ref, select_ref, target_ref = refs
+    for source, copy in zip(waiting, onward):
+        copy[...] = source[...]
     channels = aw_ref.shape[1]
     span = 2 * own_out + 2
     size, outs = span * channels, own_out * channels
@@ -97,21 +104,30 @@
     hi_ref[...] = high
     lo_ref[...] = (turned - high.astype(F32)).astype(BF16)
 
+    for k in range(measured_ref.shape[0]):
+        rows = slice(k * own_out, (k + 1) * own_out)
+        select_ref[rows, :] = jnp.full((own_out, select_ref.shape[1]), sparse_ref[0, k], jnp.int32)
+        target_ref[rows, :] = measured_ref[k]
+
 
 def net_kernel(wide, own_out, *refs):
-    views = refs[:wide]
-    a1_ref, a2_ref, b1_ref, b2_ref, h_ref, sparse_ref, measured_ref, predicted_ref, residual_ref = refs[wide:]
-    size, lanes = views[0].shape
+    near, wrapped, refs = refs[:wide], refs[wide : 2 * wide - 1], refs[2 * wide - 1 :]
+    a1_ref, a2_ref, b1_ref, b2_ref, h_ref, select_ref, target_ref, predicted_ref, residual_ref = refs
+    size, lanes = near[0].shape
     outs = a2_ref.shape[0]
     me = lax.axis_index("wide")
+    views = [near[0][...]]
+    for shift in range(1, wide):
+        views.append(jnp.where(me >= shift, near[shift][...], wrapped[shift - 1][...]))
     group = 2 if wide % 2 == 0 else 1
     wider = lambda ref, times: jnp.concatenate([ref[...]] * times, axis=1)
     b1 = wider(b1_ref, group)
     b2, h = wider(b2_ref, 2 * group), wider(h_ref, 2 * group)
-    fold = 8 // own_out
+    select = select_ref[...]
+    picked = jnp.zeros(select.shape, F32)
     for start in range(0, wide, group):
-        current = jnp.concatenate([views[start + i][...] for i in range(group)], axis=1)
-        previous = jnp.concatenate([views[(start + i + 1) % wide][...] for i in range(group)], axis=1)
+        current = jnp.concatenate([views[start + i] for i in range(group)], axis=1)
+        previous = jnp.concatenate([views[(start + i + 1) % wide] for i in range(group)], axis=1)
         upsampled = []
         for e in range(2):
             rows = pl.ds(e * size, size)
@@ -120,23 +136,26 @@
             upsampled.append(leaky_relu(summed + b1).astype(BF16))
         both = jnp.concatenate(upsampled, axis=1)
         hidden = leaky_relu(jnp.dot(a2_ref[...], both, preferred_element_type=F32) + b2) * h
-        part = jnp.sum(hidden.reshape(outs // 8, 8, hidden.shape[1]), axis=0)
-        value = part[:own_out]
-        for i in range(1, fold):
-            value += part[i * own_out : (i + 1) * own_out]
+        value = jnp.sum(hidden.reshape(outs // 8, 8, hidden.shape[1]), axis=0)
+        apart = own_out
+        while apart < 8:
+            value += pltpu.roll(value, apart, 0)
+            apart *= 2
         for e in range(2):
             for i in range(group):
-                view = lax.rem(me - (start + i) + wide, wide)
+                view = 2 * lax.rem(me - (start + i) + wide, wide) + e
                 at = (e * group + i) * lanes
-                predicted_ref[2 * view + e] = value[:, at : at + lanes]
-    for k in range(measured_ref.shape[0]):
-        residual = predicted_ref[sparse_ref[0, k]] - measured_ref[k]
-        residual_ref[k * own_out : (k + 1) * own_out, :] = residual
+                tile = value[:, at : at + lanes]
+                predicted_ref[view] = tile[:own_out]
+                repeated = jnp.concatenate([tile] * (select.shape[0] // 8), axis=0)
+                picked = jnp.where(select == view, repeated, picked)
+    residual_ref[...] = (picked - target_ref[...]).astype(BF16)
 
 
 def adjoint_kernel(count, own_out, *refs):
     residuals = refs[:count]
-    hi_ref, lo_ref, out_ref = refs[count:]
+    hi_ref, lo_ref, predicted_ref, out_ref, copied_ref = refs[count:]
+    copied_ref[...] = predicted_ref[...]
     lanes = residuals[0].shape[1]
     me = lax.axis_index(("narrow", "pair"))
     total = None
@@ -144,11 +163,8 @@
         block = lax.rem(me - shift + count, count)
         rows = pl.ds(pl.multiple_of(block * lanes, lanes), lanes)
         values = residuals[shift][...]
-        high = values.astype(BF16)
-        low = (values - high.astype(F32)).astype(BF16)
-        term = jnp.dot(high, hi_ref[rows, :], preferred_element_type=F32)
-        term += jnp.dot(low, hi_ref[rows, :], preferred_element_type=F32)
-        term += jnp.dot(high, lo_ref[rows, :], preferred_element_type=F32)
+        term = jnp.dot(values, hi_ref[rows, :], preferred_element_type=F32)
+        term += jnp.dot(values, lo_ref[rows, :], preferred_element_type=F32)
         total = term if total is None else total + term
     for k in range(out_ref.shape[0]):
         out_ref[k] = total[k * own_out : (k + 1) * own_out]
@@ -157,6 +173,11 @@
 def send(block, axis, distance):
     count = lax.axis_size(axis)
     return lax.ppermute(block, axis, [(i, (i + distance) % count) for i in range(count)])
+
+
+def send_onward(block, axis, distance):
+    count = lax.axis_size(axis)
+    return lax.ppermute(block, axis, [(i, i + distance) for i in range(count) if 0 <= i + distance < count])
 
 
 def local(
@@ -177,22 +198,26 @@
     own_out = width // wide // 2
     span = 2 * own_out + 2
     size, outs = span * channels, own_out * channels
+    sparse_count = measured.shape[0]
     shape = jax.ShapeDtypeStruct
     big = 16 if width <= 64 else 48
+    window = shape((size, lanes), BF16)
 
     windows = call(
         functools.partial(pack_kernel, wide),
-        [shape((size, lanes), BF16)] * wide,
+        [window] * wide,
         [VMEM],
         [pltpu.VMEM((channels * width, lanes), F32)],
         vmem=big,
     )(low_sino)
-    views = [windows[0]] + [send(windows[s], "wide", s) for s in range(1, wide)]
+    wrapped = [send_onward(windows[s], "wide", s - wide) for s in range(1, wide)]
 
     rows = row_weights.shape[1]
-    a1, a2, b1, b2, head, high, low = call(
-        functools.partial(expand_kernel, wide, own_out),
-        [
+    flat = (sparse_count * own_out, lanes)
+    prepared = call(
+        functools.partial(prepare_kernel, wide, own_out),
+        [window] * (wide - 1)
+        + [
             shape((2, 2 * size, size), BF16),
             shape((outs, size), BF16),
             shape((size, lanes), F32),
@@ -200,26 +225,39 @@
             shape((outs, lanes), F32),
             shape((rows, lanes), BF16),
             shape((rows, lanes), BF16),
+            shape(flat, jnp.int32),
+            shape(flat, F32),
         ],
-        [VMEM] * 6,
-        vmem=big,
-    )(angle_weight, angle_bias[None], column_weight, column_bias[None], head_weight[None], row_weights)
-
-    sparse_count = measured.shape[0]
+        [VMEM] * 6 + [SMEM] + [VMEM] * wide,
+        vmem=big,
+    )(
+        angle_weight,
+        angle_bias[None],
+        column_weight,
+        column_bias[None],
+        head_weight[None],
+        row_weights,
+        sparse_views,
+        measured,
+        *windows[1:],
+    )
+    onward, (a1, a2, b1, b2, head, high, low, select, target) = prepared[: wide - 1], prepared[wide - 1 :]
+    near = [windows[0]] + [send_onward(onward[s - 1], "wide", s) for s in range(1, wide)]
+
     predicted, residual = call(
         functools.partial(net_kernel, wide, own_out),
-        [shape((2 * wide, own_out, lanes), F32), shape((sparse_count * own_out, lanes), F32)],
-        [VMEM] * (wide + 5) + [SMEM, VMEM],
-        vmem=big,
-    )(*views, a1, a2, b1, b2, head, sparse_views, measured)
+        [shape((2 * wide, own_out, lanes), F32), shape(flat, BF16)],
+        [VMEM] * (2 * wide + 6),
+        vmem=big,
+    )(*near, *wrapped, a1, a2, b1, b2, head, select, target)
 
     blocks = [residual] + [send(residual, group, s) for s in range(1, count)]
-    adjoint = call(
+    adjoint, predicted = call(
         functools.partial(adjoint_kernel, count, own_out),
-        shape((sparse_count, own_out, lanes), F32),
-        [VMEM] * (count + 2),
-        vmem=big,
-    )(*blocks, high, low)
+        [shape((sparse_count, own_out, lanes), F32), shape(predicted.shape, F32)],
+        [VMEM] * (count + 3),
+        vmem=big,
+    )(*blocks, high, low, predicted)
     return (predicted, adjoint)
 
 

time: 20.8 us -> 33.5 us (1.61)
  starting transfers between devices: 8.73 us -> 19.5 us
  waiting for transfers between devices: 3.88 us -> 6.7 us
  local copies, waits for them, and re-layouts: 3.2 us -> 2.55 us
  Pallas kernels: 4.12 us -> 3.5 us
    ppermute x0 -> x6, starting transfers between devices: none -> 16.4 us  [send_onward(): lax.ppermute(block, axis, [(i, i + distance) for i in range(count) if 0 <...]
    ppermute x6 -> x3, starting transfers between devices: 8.73 us -> 3.01 us  [send(): lax.ppermute(block, axis, [(i, (i + distance) % count) for i in range(cou...]
    ppermute x0 -> x6, waiting for transfers between devices: none -> 5.26 us  [send_onward(): lax.ppermute(block, axis, [(i, i + distance) for i in range(count) if 0 <...]
    ppermute x6 -> x3, waiting for transfers between devices: 3.88 us -> 1.44 us  [send(): lax.ppermute(block, axis, [(i, (i + distance) % count) for i in range(cou...]
    pallas_call x1, Pallas kernels: 1.9 us -> 0.77 us  [local(): call(functools.partial(net_kernel, wide, own_out), [shape((2 * wide, own_...]
    unnamed x18, local copies, waits for them, and re-layouts: 3.2 us -> 2.55 us
    pallas_call x3, Pallas kernels: 2.22 us -> 2.73 us  [the longest x1 1.37 us: local(): call(functools.partial(prepare_kernel, wide, own_out), [window] * (wide -...]
  transfers between devices with their start and end apart: 6 -> 9, of which waited for: 4 -> 5; matrix products, arithmetic and copies ran while one was open for 0% -> 0% of each run, Pallas kernels for 4% -> 0%
where the time goes in v2:
time: 33.5 us; the launch traced here: 33 us
  starting transfers between devices  19.5 us (58%)
  waiting for transfers between devices  6.7 us (20%)
  Pallas kernels  3.5 us (10%)
  local copies, waits for them, and re-layouts  2.55 us (8%)
  between operations  0.78 us (2%)
    ppermute x6, starting transfers between devices, send_onward(): lax.ppermute(block, axis, [(i, i + distance) for i in range(count) if 0 <...  16.4 us
    ppermute x6, waiting for transfers between devices, send_onward(): lax.ppermute(block, axis, [(i, i + distance) for i in range(count) if 0 <...  5.26 us
    ppermute x3, starting transfers between devices, send(): lax.ppermute(block, axis, [(i, (i + distance) % count) for i in range(cou...  3.01 us
    unnamed x18, local copies, waits for them, and re-layouts  2.55 us
    ppermute x3, waiting for transfers between devices, send(): lax.ppermute(block, axis, [(i, (i + distance) % count) for i in range(cou...  1.44 us
    pallas_call x1, Pallas kernels, local(): call(functools.partial(prepare_kernel, wide, own_out), [window] * (wide -...  1.37 us
    pallas_call x1, Pallas kernels, local(): call(functools.partial(adjoint_kernel, count, own_out), [shape((sparse_co...  0.82 us
    pallas_call x1, Pallas kernels, local(): call(functools.partial(net_kernel, wide, own_out), [shape((2 * wide, own_...  0.77 us
  transfers between devices with their start and end apart: 9, of which 5 were waited for; matrix products, arithmetic and copies ran while one was open for 0% of the time, Pallas kernels for 0%

profile of v2, /device:TPU:0, one launch (start us, length us, event | category | flops | bytes accessed | tf_op | source)
XLA Modules:
  0.0 33.0 jit_solution(11801423746069176821)
XLA Ops:
  0.6 0.9 %copy-done.1 = bf16[1,24,32,128]{3,2,1,0:T(8,128)(2,1)S(1)} copy-done((bf16[1,24,32,128]{3,2,1,0:T(8,128)(2,1)S(1)}, bf16[1,24,32,128]{3,2,1,0:T(8,128)(2,1)}, u32[]{:S(2)}) %copy-start.1) | copy-done | bytes 196632
  1.6 0.5 %shard_map.104 = (bf16[240,128]{1,0:T(8,128)(2,1)S(1)}, bf16[240,128]{1,0:T(8,128)(2,1)S(1)}, bf16[240,128]{1,0:T(8,128)(2,1)S(1)}, bf16[240,128]{1,0:T(8,128)(2,1)S(1)}) custom-call(bf16[1,24,32,128]{3,2,1,0:T(8,128)(2,1)S(1)} %copy-done.1), custom_call_target="tpu_custom_call" | custom-call | flops 1000000 | bytes 245760 | tf_op jit(solution)/shard_map/pallas_call | solution.py:206
  2.1 0.0 copy-start.8
  2.1 0.0 copy-start.5
  2.1 0.0 copy-start.6
  2.1 0.0 copy-start.7
  2.2 0.2 copy-done.2
  2.3 0.0 copy-done.4
  2.3 0.4 %copy-done.8 = s32[1,16]{1,0:T(1,128)S(1)} copy-done((s32[1,16]{1,0:T(1,128)S(1)}, s32[1,16]{1,0:T(1,128)}, u32[]{:S(2)}) %copy-start.8) | copy-done | bytes 88
  2.8 0.0 copy-done.5
  2.8 0.0 copy-done.6
  2.8 0.0 copy-done.7
  2.8 0.9 %copy-done = f32[128,512]{1,0:T(8,128)S(1)} copy-done((f32[128,512]{1,0:T(8,128)S(1)}, f32[128,512]{1,0:T(8,128)}, u32[]{:S(2)}) %copy-start) | copy-done | bytes 262168
  3.8 1.4 %shard_map.105 = (bf16[240,128]{1,0:T(8,128)(2,1)S(1)}, bf16[240,128]{1,0:T(8,128)(2,1)S(1)}, bf16[240,128]{1,0:T(8,128)(2,1)S(1)}, bf16[2,480,240]{2,1,0:T(8,12...) custom-call(bf16[4,24,24]{2,1,0:T(8,128)(2,1)S(1)} %copy-done.3, ...), custom_call_target="tpu_custom_call" | custom-call | flops 1000000 | bytes 1240064 | tf_op jit(solution)/shard_map/pallas_call | solution.py:217
  5.1 4.9 %collective-permute-start = (bf16[240,128]{1,0:T(8,128)(2,1)S(1)}, bf16[240,128]{1,0:T(8,128)(2,1)S(1)}, u32[]{:S(2)}, u32[]{:S(2)}) collective-permute-start(bf16[240,128]{1,0:T(8,128)(2,1)S(1)} %get-tuple-element.26), channel_id=1, source_target_pairs={{0,4},{4,8},{8,12},{1,5},{5,9},{9,13},{2,6},{6,10},{10,14},{3,7},{... | collective-permute-start | bytes 184328 | tf_op jit(solution)/shard_map/ppermute | solution.py:180
  10.1 1.3 %collective-permute-start.3 = (bf16[240,128]{1,0:T(8,128)(2,1)S(1)}, bf16[240,128]{1,0:T(8,128)(2,1)S(1)}, u32[]{:S(2)}, u32[]{:S(2)}) collective-permute-start(bf16[240,128]{1,0:T(8,128)(2,1)S(1)} %get-tuple-element.23.refs_0_), channel_id=1, source_target_pairs={{12,0},{13,1},{14,2},{15,3},{28,16},{29,17},{30,18},{31,19}} | collective-permute-start | bytes 184328 | tf_op jit(solution)/shard_map/ppermute | solution.py:180
  11.4 3.9 %collective-permute-start.1 = (bf16[240,128]{1,0:T(8,128)(2,1)S(1)}, bf16[240,128]{1,0:T(8,128)(2,1)S(1)}, u32[]{:S(2)}, u32[]{:S(2)}) collective-permute-start(bf16[240,128]{1,0:T(8,128)(2,1)S(1)} %get-tuple-element.27), channel_id=1, source_target_pairs={{0,8},{4,12},{1,9},{5,13},{2,10},{6,14},{3,11},{7,15},{16,24},{20,... | collective-permute-start | bytes 184328 | tf_op jit(solution)/shard_map/ppermute | solution.py:180
  15.3 3.8 %collective-permute-start.2 = (bf16[240,128]{1,0:T(8,128)(2,1)S(1)}, bf16[240,128]{1,0:T(8,128)(2,1)S(1)}, u32[]{:S(2)}, u32[]{:S(2)}) collective-permute-start(bf16[240,128]{1,0:T(8,128)(2,1)S(1)} %get-tuple-element.28), channel_id=1, source_target_pairs={{0,12},{1,13},{2,14},{3,15},{16,28},{17,29},{18,30},{19,31}} | collective-permute-start | bytes 184328 | tf_op jit(solution)/shard_map/ppermute | solution.py:180
  19.0 1.3 %collective-permute-start.4 = (bf16[240,128]{1,0:T(8,128)(2,1)S(1)}, bf16[240,128]{1,0:T(8,128)(2,1)S(1)}, u32[]{:S(2)}, u32[]{:S(2)}) collective-permute-start(bf16[240,128]{1,0:T(8,128)(2,1)S(1)} %get-tuple-element.24.refs_1_), channel_id=1, source_target_pairs={{8,0},{12,4},{9,1},{13,5},{10,2},{14,6},{11,3},{15,7},{24,16},{28,... | collective-permute-start | bytes 184328 | tf_op jit(solution)/shard_map/ppermute | solution.py:180
  20.3 0.0 collective-permute-done.refs_1_
  20.3 1.3 %collective-permute-start.5 = (bf16[240,128]{1,0:T(8,128)(2,1)S(1)}, bf16[240,128]{1,0:T(8,128)(2,1)S(1)}, u32[]{:S(2)}, u32[]{:S(2)}) collective-permute-start(bf16[240,128]{1,0:T(8,128)(2,1)S(1)} %get-tuple-element.25.refs_2_), channel_id=1, source_target_pairs={{4,0},{8,4},{12,8},{5,1},{9,5},{13,9},{6,2},{10,6},{14,10},{7,3},{... | collective-permute-start | bytes 184328 | tf_op jit(solution)/shard_map/ppermute | solution.py:180
  21.7 0.0 collective-permute-done.2.refs_3_
  21.7 5.1 %collective-permute-done.4.refs_5_ = bf16[240,128]{1,0:T(8,128)(2,1)S(1)} collective-permute-done((bf16[240,128]{1,0:T(8,128)(2,1)S(1)}, bf16[240,128]{1,0:T(8,128)(2,1)S(1)}, u32[]{:S(2)}, u32[]{:S(2)}) %collective-permute-start.4) | collective-permute-done | bytes 61472 | tf_op jit(solution)/shard_map/ppermute | solution.py:180
  26.7 0.2 collective-permute-done.5.refs_6_
  26.9 0.8 %shard_map.106 = (f32[8,4,128]{2,1,0:T(4,128)S(1)}, bf16[64,128]{1,0:T(8,128)(2,1)S(1)}) custom-call(bf16[240,128]{1,0:T(8,128)(2,1)S(1)} %get-tuple-element.22.refs_0_, bf16[240,128]{1,0:T(8,128)(2,1)S(1)} %collective-permute-done.refs_1_, bf16[240,128]{1,0:T(8,128)(2,1)S(1)} %collective-permute-done.1.refs_2_, ...), custom_call_target="tpu_custom_call" | custom-call | flops 1000000 | bytes 32768 | tf_op jit(solution)/shard_map/pallas_call | solution.py:247
  27.7 0.1 collective-permute-start.6
  27.8 1.6 %collective-permute-start.7 = (bf16[64,128]{1,0:T(8,128)(2,1)S(1)}, bf16[64,128]{1,0:T(8,128)(2,1)S(1)}, u32[]{:S(2)}, u32[]{:S(2)}) collective-permute-start(bf16[64,128]{1,0:T(8,128)(2,1)S(1)} %get-tuple-element.36.refs_0_), channel_id=1, source_target_pairs={{0,2},{1,3},{2,0},{3,1},{4,6},{5,7},{6,4},{7,5},{8,10},{9,11},{10,... | collective-permute-start | bytes 49160 | tf_op jit(solution)/shard_map/ppermute | solution.py:175
  29.3 1.4 %collective-permute-start.8 = (bf16[64,128]{1,0:T(8,128)(2,1)S(1)}, bf16[64,128]{1,0:T(8,128)(2,1)S(1)}, u32[]{:S(2)}, u32[]{:S(2)}) collective-permute-start(bf16[64,128]{1,0:T(8,128)(2,1)S(1)} %get-tuple-element.36.refs_0_), channel_id=1, source_target_pairs={{0,3},{1,0},{2,1},{3,2},{4,7},{5,4},{6,5},{7,6},{8,11},{9,8},{10,9... | collective-permute-start | bytes 49160 | tf_op jit(solution)/shard_map/ppermute | solution.py:175
  30.7 0.2 collective-permute-done.6.refs_1_
  30.9 0.7 %collective-permute-done.7.refs_2_ = bf16[64,128]{1,0:T(8,128)(2,1)S(1)} collective-permute-done((bf16[64,128]{1,0:T(8,128)(2,1)S(1)}, bf16[64,128]{1,0:T(8,128)(2,1)S(1)}, u32[]{:S(2)}, u32[]{:S(2)}) %collective-permute-start.7) | collective-permute-done | bytes 16416 | tf_op jit(solution)/shard_map/ppermute | solution.py:175
  31.6 0.6 %collective-permute-done.8.refs_3_ = bf16[64,128]{1,0:T(8,128)(2,1)S(1)} collective-permute-done((bf16[64,128]{1,0:T(8,128)(2,1)S(1)}, bf16[64,128]{1,0:T(8,128)(2,1)S(1)}, u32[]{:S(2)}, u32[]{:S(2)}) %collective-permute-start.8) | collective-permute-done | bytes 16416 | tf_op jit(solution)/shard_map/ppermute | solution.py:175
  32.2 0.8 %shard_map.107 = (f32[16,4,128]{2,1,0:T(4,128)}, f32[8,4,128]{2,1,0:T(4,128)}) custom-call(bf16[64,128]{1,0:T(8,128)(2,1)S(1)} %get-tuple-element.36.refs_0_, bf16[64,128]{1,0:T(8,128)(2,1)S(1)} %collective-permute-done.6.refs_1_, bf16[64,128]{1,0:T(8,128)(2,1)S(1)} %collective-permute-done.7.refs_2_, bf16[64,128]{1,0:T(8,128)(2,1)S(1)} %collective-permute-done.8.refs_3_, ...), custom_call_target="tpu_custom_call" | custom-call | flops 1000000 | bytes 49152 | tf_op jit(solution)/shard_map/pallas_call | solution.py:255
  (8 shorter events, 0.0 us)
Async XLA Ops:
  0.6 0.9 %copy-start.1 = (bf16[1,24,32,128]{3,2,1,0:T(8,128)(2,1)S(1)}, bf16[1,24,32,128]{3,2,1,0:T(8,128)(2,1)}, u32[]{:S(2)}) copy-start(bf16[1,24,32,128]{3,2,1,0:T(8,128)(2,1)} %low_ref.1) | copy-start | bytes 589828
  1.6 0.8 %copy-start.2 = (f32[16,4,128]{2,1,0:T(4,128)S(1)}, f32[16,4,128]{2,1,0:T(4,128)}, u32[]{:S(2)}) copy-start(f32[16,4,128]{2,1,0:T(4,128)} %measured_ref.1) | copy-start | bytes 98308
  1.6 0.8 %copy-start.3 = (bf16[4,24,24]{2,1,0:T(8,128)(2,1)S(1)}, bf16[4,24,24]{2,1,0:T(8,128)(2,1)}, u32[]{:S(2)}) copy-start(bf16[4,24,24]{2,1,0:T(8,128)(2,1)} %aw_ref.1) | copy-start | bytes 13828
  1.6 0.8 %copy-start.4 = (bf16[4,24,24]{2,1,0:T(8,128)(2,1)S(1)}, bf16[4,24,24]{2,1,0:T(8,128)(2,1)}, u32[]{:S(2)}) copy-start(bf16[4,24,24]{2,1,0:T(8,128)(2,1)} %cw_ref.1) | copy-start | bytes 13828
  2.1 0.7 %copy-start.8 = (s32[1,16]{1,0:T(1,128)S(1)}, s32[1,16]{1,0:T(1,128)}, u32[]{:S(2)}) copy-start(s32[1,16]{1,0:T(1,128)} %sparse_ref.1) | copy-start | bytes 196
  2.1 0.7 %copy-start.5 = (f32[24]{0:T(128)S(1)}, f32[24]{0:T(128)}, u32[]{:S(2)}) copy-start(f32[24]{0:T(128)} %param.11) | copy-start | bytes 292
  2.1 0.7 %copy-start.6 = (f32[24]{0:T(128)S(1)}, f32[24]{0:T(128)}, u32[]{:S(2)}) copy-start(f32[24]{0:T(128)} %param.13) | copy-start | bytes 292
  2.1 0.7 %copy-start.7 = (f32[24]{0:T(128)S(1)}, f32[24]{0:T(128)}, u32[]{:S(2)}) copy-start(f32[24]{0:T(128)} %param.14) | copy-start | bytes 292
  2.8 0.9 %copy-start = (f32[128,512]{1,0:T(8,128)S(1)}, f32[128,512]{1,0:T(8,128)}, u32[]{:S(2)}) copy-start(f32[128,512]{1,0:T(8,128)} %rw_ref.1) | copy-start | bytes 786436
  5.1 15.2 %collective-permute-start = (bf16[240,128]{1,0:T(8,128)(2,1)S(1)}, bf16[240,128]{1,0:T(8,128)(2,1)S(1)}, u32[]{:S(2)}, u32[]{:S(2)}) collective-permute-start(bf16[240,128]{1,0:T(8,128)(2,1)S(1)} %get-tuple-element.26), channel_id=1, source_target_pairs={{0,4},{4,8},{8,12},{1,5},{5,9},{9,13},{2,6},{6,10},{10,14},{3,7},{... | collective-permute-start | bytes 184328 | tf_op jit(solution)/shard_map/ppermute | solution.py:180
  10.1 11.6 %collective-permute-start.3 = (bf16[240,128]{1,0:T(8,128)(2,1)S(1)}, bf16[240,128]{1,0:T(8,128)(2,1)S(1)}, u32[]{:S(2)}, u32[]{:S(2)}) collective-permute-start(bf16[240,128]{1,0:T(8,128)(2,1)S(1)} %get-tuple-element.23.refs_0_), channel_id=1, source_target_pairs={{12,0},{13,1},{14,2},{15,3},{28,16},{29,17},{30,18},{31,19}} | collective-permute-start | bytes 184328 | tf_op jit(solution)/shard_map/ppermute | solution.py:180
  11.4 10.3 %collective-permute-start.1 = (bf16[240,128]{1,0:T(8,128)(2,1)S(1)}, bf16[240,128]{1,0:T(8,128)(2,1)S(1)}, u32[]{:S(2)}, u32[]{:S(2)}) collective-permute-start(bf16[240,128]{1,0:T(8,128)(2,1)S(1)} %get-tuple-element.27), channel_id=1, source_target_pairs={{0,8},{4,12},{1,9},{5,13},{2,10},{6,14},{3,11},{7,15},{16,24},{20,... | collective-permute-start | bytes 184328 | tf_op jit(solution)/shard_map/ppermute | solution.py:180
  15.3 6.4 %collective-permute-start.2 = (bf16[240,128]{1,0:T(8,128)(2,1)S(1)}, bf16[240,128]{1,0:T(8,128)(2,1)S(1)}, u32[]{:S(2)}, u32[]{:S(2)}) collective-permute-start(bf16[240,128]{1,0:T(8,128)(2,1)S(1)} %get-tuple-element.28), channel_id=1, source_target_pairs={{0,12},{1,13},{2,14},{3,15},{16,28},{17,29},{18,30},{19,31}} | collective-permute-start | bytes 184328 | tf_op jit(solution)/shard_map/ppermute | solution.py:180
  19.0 7.7 %collective-permute-start.4 = (bf16[240,128]{1,0:T(8,128)(2,1)S(1)}, bf16[240,128]{1,0:T(8,128)(2,1)S(1)}, u32[]{:S(2)}, u32[]{:S(2)}) collective-permute-start(bf16[240,128]{1,0:T(8,128)(2,1)S(1)} %get-tuple-element.24.refs_1_), channel_id=1, source_target_pairs={{8,0},{12,4},{9,1},{13,5},{10,2},{14,6},{11,3},{15,7},{24,16},{28,... | collective-permute-start | bytes 184328 | tf_op jit(solution)/shard_map/ppermute | solution.py:180
  20.3 6.6 %collective-permute-start.5 = (bf16[240,128]{1,0:T(8,128)(2,1)S(1)}, bf16[240,128]{1,0:T(8,128)(2,1)S(1)}, u32[]{:S(2)}, u32[]{:S(2)}) collective-permute-start(bf16[240,128]{1,0:T(8,128)(2,1)S(1)} %get-tuple-element.25.refs_2_), channel_id=1, source_target_pairs={{4,0},{8,4},{12,8},{5,1},{9,5},{13,9},{6,2},{10,6},{14,10},{7,3},{... | collective-permute-start | bytes 184328 | tf_op jit(solution)/shard_map/ppermute | solution.py:180
  27.7 3.2 %collective-permute-start.6 = (bf16[64,128]{1,0:T(8,128)(2,1)S(1)}, bf16[64,128]{1,0:T(8,128)(2,1)S(1)}, u32[]{:S(2)}, u32[]{:S(2)}) collective-permute-start(bf16[64,128]{1,0:T(8,128)(2,1)S(1)} %get-tuple-element.36.refs_0_), channel_id=1, source_target_pairs={{0,1},{1,2},{2,3},{3,0},{4,5},{5,6},{6,7},{7,4},{8,9},{9,10},{10,1... | collective-permute-start | bytes 49160 | tf_op jit(solution)/shard_map/ppermute | solution.py:175
  27.8 3.8 %collective-permute-start.7 = (bf16[64,128]{1,0:T(8,128)(2,1)S(1)}, bf16[64,128]{1,0:T(8,128)(2,1)S(1)}, u32[]{:S(2)}, u32[]{:S(2)}) collective-permute-start(bf16[64,128]{1,0:T(8,128)(2,1)S(1)} %get-tuple-element.36.refs_0_), channel_id=1, source_target_pairs={{0,2},{1,3},{2,0},{3,1},{4,6},{5,7},{6,4},{7,5},{8,10},{9,11},{10,... | collective-permute-start | bytes 49160 | tf_op jit(solution)/shard_map/ppermute | solution.py:175
  29.3 2.8 %collective-permute-start.8 = (bf16[64,128]{1,0:T(8,128)(2,1)S(1)}, bf16[64,128]{1,0:T(8,128)(2,1)S(1)}, u32[]{:S(2)}, u32[]{:S(2)}) collective-permute-start(bf16[64,128]{1,0:T(8,128)(2,1)S(1)} %get-tuple-element.36.refs_0_), channel_id=1, source_target_pairs={{0,3},{1,0},{2,1},{3,2},{4,7},{5,4},{6,5},{7,6},{8,11},{9,8},{10,9... | collective-permute-start | bytes 49160 | tf_op jit(solution)/shard_map/ppermute | solution.py:175

commit v3 on v2

--- a/solution.py
+++ b/solution.py
@@ -9,7 +9,6 @@
 
 F32, BF16 = jnp.float32, jnp.bfloat16
 VMEM = pl.BlockSpec(memory_space=pltpu.VMEM)
-SMEM = pl.BlockSpec(memory_space=pltpu.SMEM)
 TAPS = 4
 
 
@@ -55,13 +54,26 @@
 
 
 def prepare_kernel(
-    wide, own_out, aw_ref, ab_ref, cw_ref, cb_ref, hw_ref, rw_ref, sparse_ref, measured_ref, *refs
+    wide,
+    own_out,
+    aw_ref,
+    ab_ref,
+    cw_ref,
+    cb_ref,
+    hw_ref,
+    rw_ref,
+    measured_ref,
+    sparse_ref,
+    a1_ref,
+    a2_ref,
+    b1_ref,
+    b2_ref,
+    h_ref,
+    hi_ref,
+    lo_ref,
+    select_ref,
+    target_ref,
 ):
-    waiting, refs = refs[: wide - 1], refs[wide - 1 :]
-    onward, refs = refs[: wide - 1], refs[wide - 1 :]
-    a1_ref, a2_ref, b1_ref, b2_ref, h_ref, hi_ref, lo_ref, select_ref, target_ref = refs
-    for source, copy in zip(waiting, onward):
-        copy[...] = source[...]
     channels = aw_ref.shape[1]
     span = 2 * own_out + 2
     size, outs = span * channels, own_out * channels
@@ -93,7 +105,7 @@
     a2_ref[...] = total.astype(BF16)
 
     def along(left, vector_ref, out_ref):
-        out_ref[...] = jnp.broadcast_to(jnp.sum(left * vector_ref[...], axis=1, keepdims=True), out_ref.shape)
+        out_ref[...] = jnp.broadcast_to(jnp.sum(left * vector_ref[...].astype(F32), axis=1, keepdims=True), out_ref.shape)
 
     along(pick, ab_ref, b1_ref)
     along(pick_out, cb_ref, b2_ref)
@@ -104,21 +116,20 @@
     hi_ref[...] = high
     lo_ref[...] = (turned - high.astype(F32)).astype(BF16)
 
-    for k in range(measured_ref.shape[0]):
-        rows = slice(k * own_out, (k + 1) * own_out)
-        select_ref[rows, :] = jnp.full((own_out, select_ref.shape[1]), sparse_ref[0, k], jnp.int32)
-        target_ref[rows, :] = measured_ref[k]
+    sparse_count = measured_ref.shape[0]
+    wanted = (select_ref.shape[0], sparse_count)
+    pick_view = (split(iota(wanted, 0), own_out)[0] == iota(wanted, 1)).astype(F32)
+    along(pick_view, sparse_ref, select_ref)
+    for k in range(sparse_count):
+        target_ref[k * own_out : (k + 1) * own_out, :] = measured_ref[k]
 
 
 def net_kernel(wide, own_out, *refs):
-    near, wrapped, refs = refs[:wide], refs[wide : 2 * wide - 1], refs[2 * wide - 1 :]
+    views, refs = [ref[...] for ref in refs[:wide]], refs[wide:]
     a1_ref, a2_ref, b1_ref, b2_ref, h_ref, select_ref, target_ref, predicted_ref, residual_ref = refs
-    size, lanes = near[0].shape
+    size, lanes = views[0].shape
     outs = a2_ref.shape[0]
     me = lax.axis_index("wide")
-    views = [near[0][...]]
-    for shift in range(1, wide):
-        views.append(jnp.where(me >= shift, near[shift][...], wrapped[shift - 1][...]))
     group = 2 if wide % 2 == 0 else 1
     wider = lambda ref, times: jnp.concatenate([ref[...]] * times, axis=1)
     b1 = wider(b1_ref, group)
@@ -148,21 +159,21 @@
                 tile = value[:, at : at + lanes]
                 predicted_ref[view] = tile[:own_out]
                 repeated = jnp.concatenate([tile] * (select.shape[0] // 8), axis=0)
-                picked = jnp.where(select == view, repeated, picked)
+                picked = jnp.where(select == view.astype(F32), repeated, picked)
     residual_ref[...] = (picked - target_ref[...]).astype(BF16)
 
 
-def adjoint_kernel(count, own_out, *refs):
-    residuals = refs[:count]
-    hi_ref, lo_ref, predicted_ref, out_ref, copied_ref = refs[count:]
+def adjoint_kernel(shifts, own_out, *refs):
+    residuals, refs = refs[: len(shifts)], refs[len(shifts) :]
+    hi_ref, lo_ref, predicted_ref, out_ref, copied_ref = refs
     copied_ref[...] = predicted_ref[...]
     lanes = residuals[0].shape[1]
-    me = lax.axis_index(("narrow", "pair"))
     total = None
-    for shift in range(count):
-        block = lax.rem(me - shift + count, count)
+    for residual_ref, (narrow_shift, pair_shift) in zip(residuals, shifts):
+        narrow, pair = came_from("narrow", narrow_shift), came_from("pair", pair_shift)
+        block = narrow * lax.axis_size("pair") + pair
         rows = pl.ds(pl.multiple_of(block * lanes, lanes), lanes)
-        values = residuals[shift][...]
+        values = residual_ref[...]
         term = jnp.dot(values, hi_ref[rows, :], preferred_element_type=F32)
         term += jnp.dot(values, lo_ref[rows, :], preferred_element_type=F32)
         total = term if total is None else total + term
@@ -170,14 +181,14 @@
         out_ref[k] = total[k * own_out : (k + 1) * own_out]
 
 
+def came_from(axis, distance):
+    count = lax.axis_size(axis)
+    return lax.rem(lax.axis_index(axis) - distance + count, count)
+
+
 def send(block, axis, distance):
     count = lax.axis_size(axis)
     return lax.ppermute(block, axis, [(i, (i + distance) % count) for i in range(count)])
-
-
-def send_onward(block, axis, distance):
-    count = lax.axis_size(axis)
-    return lax.ppermute(block, axis, [(i, i + distance) for i in range(count) if 0 <= i + distance < count])
 
 
 def local(
@@ -191,33 +202,39 @@
     measured,
     row_weights,
 ):
-    wide = lax.axis_size("wide")
-    group = ("narrow", "pair")
-    count = lax.axis_size(group)
+    wide, narrow, pair = (lax.axis_size(axis) for axis in ("wide", "narrow", "pair"))
     _, channels, width, lanes = low_sino.shape
     own_out = width // wide // 2
     span = 2 * own_out + 2
     size, outs = span * channels, own_out * channels
     sparse_count = measured.shape[0]
+    rows = row_weights.shape[1]
+    flat = (sparse_count * own_out, lanes)
     shape = jax.ShapeDtypeStruct
     big = 16 if width <= 64 else 48
-    window = shape((size, lanes), BF16)
-
+
+    small = (
+        angle_weight,
+        angle_bias[None],
+        column_weight,
+        column_bias[None],
+        head_weight[None],
+        row_weights,
+        measured,
+        sparse_views,
+    )
     windows = call(
         functools.partial(pack_kernel, wide),
-        [window] * wide,
+        [shape((size, lanes), BF16)] * wide,
         [VMEM],
         [pltpu.VMEM((channels * width, lanes), F32)],
         vmem=big,
     )(low_sino)
-    wrapped = [send_onward(windows[s], "wide", s - wide) for s in range(1, wide)]
-
-    rows = row_weights.shape[1]
-    flat = (sparse_count * own_out, lanes)
-    prepared = call(
+    views = [windows[0]] + [send(windows[s], "wide", s) for s in range(1, wide)]
+
+    a1, a2, b1, b2, head, high, low, select, target = call(
         functools.partial(prepare_kernel, wide, own_out),
-        [window] * (wide - 1)
-        + [
+        [
             shape((2, 2 * size, size), BF16),
             shape((outs, size), BF16),
             shape((size, lanes), F32),
@@ -225,37 +242,31 @@
             shape((outs, lanes), F32),
             shape((rows, lanes), BF16),
             shape((rows, lanes), BF16),
-            shape(flat, jnp.int32),
+            shape(flat, F32),
             shape(flat, F32),
         ],
-        [VMEM] * 6 + [SMEM] + [VMEM] * wide,
-        vmem=big,
-    )(
-        angle_weight,
-        angle_bias[None],
-        column_weight,
-        column_bias[None],
-        head_weight[None],
-        row_weights,
-        sparse_views,
-        measured,
-        *windows[1:],
-    )
-    onward, (a1, a2, b1, b2, head, high, low, select, target) = prepared[: wide - 1], prepared[wide - 1 :]
-    near = [windows[0]] + [send_onward(onward[s - 1], "wide", s) for s in range(1, wide)]
+        [VMEM] * 8,
+        vmem=big,
+    )(*small)
 
     predicted, residual = call(
         functools.partial(net_kernel, wide, own_out),
         [shape((2 * wide, own_out, lanes), F32), shape(flat, BF16)],
-        [VMEM] * (2 * wide + 6),
-        vmem=big,
-    )(*near, *wrapped, a1, a2, b1, b2, head, select, target)
-
-    blocks = [residual] + [send(residual, group, s) for s in range(1, count)]
+        [VMEM] * (wide + 7),
+        vmem=big,
+    )(*views, a1, a2, b1, b2, head, select, target)
+
+    shifts = [(0, 0)] + [(s, 0) for s in range(1, narrow)] + [(0, t) for t in range(1, pair)]
+    blocks = [residual] + [send(residual, "narrow", s) for s in range(1, narrow)]
+    blocks += [send(residual, "pair", t) for t in range(1, pair)]
+    for s in range(1, narrow):
+        for t in range(1, pair):
+            shifts.append((s, t))
+            blocks.append(send(blocks[s], "pair", t))
     adjoint, predicted = call(
-        functools.partial(adjoint_kernel, count, own_out),
+        functools.partial(adjoint_kernel, shifts, own_out),
         [shape((sparse_count, own_out, lanes), F32), shape(predicted.shape, F32)],
-        [VMEM] * (count + 3),
+        [VMEM] * (len(blocks) + 3),
         vmem=big,
     )(*blocks, high, low, predicted)
     return (predicted, adjoint)

time: 33.5 us -> 19.1 us (0.57); the launches traced: 33 us -> 18.9 us
  starting transfers between devices: 19.5 us -> 8.59 us
  waiting for transfers between devices: 6.7 us -> 4.17 us
  Pallas kernels: 3.5 us -> 2.94 us
    ppermute x6 -> x0, starting transfers between devices: 16.4 us -> none  [send_onward(): lax.ppermute(block, axis, [(i, i + distance) for i in range(count) if 0 <...]
    ppermute x3 -> x6, starting transfers between devices: 3.01 us -> 8.59 us  [send(): lax.ppermute(block, axis, [(i, (i + distance) % count) for i in range(cou...]
    ppermute x6 -> x0, waiting for transfers between devices: 5.26 us -> none  [send_onward(): lax.ppermute(block, axis, [(i, i + distance) for i in range(count) if 0 <...]
    ppermute x3 -> x6, waiting for transfers between devices: 1.44 us -> 4.17 us  [send(): lax.ppermute(block, axis, [(i, (i + distance) % count) for i in range(cou...]
    pallas_call x3, Pallas kernels: 2.73 us -> 2.18 us  [the longest x1 0.83 us: local(): call(functools.partial(adjoint_kernel, shifts, own_out), [shape((sparse_c...]
  transfers between devices with their start and end apart: 9 -> 6, of which waited for: 5 -> 4; matrix products, arithmetic and copies ran while one was open for 0% -> 0% of each run, Pallas kernels for 0% -> 4%
where the time goes in v3:
time: 19.1 us; the launch traced here: 18.9 us
  starting transfers between devices  8.59 us (45%)
  waiting for transfers between devices  4.17 us (22%)
  Pallas kernels  2.94 us (15%)
  local copies, waits for them, and re-layouts  2.55 us (13%)
  between operations  0.7 us (4%)
    ppermute x6, starting transfers between devices, send(): lax.ppermute(block, axis, [(i, (i + distance) % count) for i in range(cou...  8.59 us
    ppermute x6, waiting for transfers between devices, send(): lax.ppermute(block, axis, [(i, (i + distance) % count) for i in range(cou...  4.17 us
    unnamed x18, local copies, waits for them, and re-layouts  2.55 us
    pallas_call x1, Pallas kernels, local(): call(functools.partial(adjoint_kernel, shifts, own_out), [shape((sparse_c...  0.83 us
    pallas_call x1, Pallas kernels, local(): call(functools.partial(prepare_kernel, wide, own_out), [shape((2, 2 * siz...  0.82 us
    pallas_call x1, Pallas kernels, local(): call(functools.partial(net_kernel, wide, own_out), [shape((2 * wide, own_...  0.76 us
    pallas_call x1, Pallas kernels, local(): call(functools.partial(pack_kernel, wide), [shape((size, lanes), BF16)] *...  0.54 us
  transfers between devices with their start and end apart: 6, of which 4 were waited for; matrix products, arithmetic and copies ran while one was open for 0% of the time, Pallas kernels for 4%

profile of v3, /device:TPU:0, one launch (start us, length us, event | category | flops | bytes accessed | tf_op | source)
XLA Modules:
  0.0 18.9 jit_solution(16086908301991405120)
XLA Ops:
  0.6 0.0 copy-start.1
  0.6 0.9 %copy-done.1 = bf16[1,24,32,128]{3,2,1,0:T(8,128)(2,1)S(1)} copy-done((bf16[1,24,32,128]{3,2,1,0:T(8,128)(2,1)S(1)}, bf16[1,24,32,128]{3,2,1,0:T(8,128)(2,1)}, u32[]{:S(2)}) %copy-start.1) | copy-done | bytes 196632
  1.6 0.0 copy-start.2
  1.6 0.0 copy-start.3
  1.6 0.0 copy-start.4
  1.6 0.5 %shard_map.104 = (bf16[240,128]{1,0:T(8,128)(2,1)S(1)}, bf16[240,128]{1,0:T(8,128)(2,1)S(1)}, bf16[240,128]{1,0:T(8,128)(2,1)S(1)}, bf16[240,128]{1,0:T(8,128)(2,1)S(1)}) custom-call(bf16[1,24,32,128]{3,2,1,0:T(8,128)(2,1)S(1)} %copy-done.1), custom_call_target="tpu_custom_call" | custom-call | flops 1000000 | bytes 245760 | tf_op jit(solution)/shard_map/pallas_call | solution.py:226
  2.1 3.1 %collective-permute-start = (bf16[240,128]{1,0:T(8,128)(2,1)S(1)}, bf16[240,128]{1,0:T(8,128)(2,1)S(1)}, u32[]{:S(2)}, u32[]{:S(2)}) collective-permute-start(bf16[240,128]{1,0:T(8,128)(2,1)S(1)} %get-tuple-element.20), channel_id=1, source_target_pairs={{0,4},{4,8},{8,12},{12,0},{1,5},{5,9},{9,13},{13,1},{2,6},{6,10},{... | collective-permute-start | bytes 184328 | tf_op jit(solution)/shard_map/ppermute | solution.py:191
  5.2 2.6 %collective-permute-start.1 = (bf16[240,128]{1,0:T(8,128)(2,1)S(1)}, bf16[240,128]{1,0:T(8,128)(2,1)S(1)}, u32[]{:S(2)}, u32[]{:S(2)}) collective-permute-start(bf16[240,128]{1,0:T(8,128)(2,1)S(1)} %get-tuple-element.21), channel_id=1, source_target_pairs={{0,8},{4,12},{8,0},{12,4},{1,9},{5,13},{9,1},{13,5},{2,10},{6,14},... | collective-permute-start | bytes 184328 | tf_op jit(solution)/shard_map/ppermute | solution.py:191
  7.8 1.3 %collective-permute-start.2 = (bf16[240,128]{1,0:T(8,128)(2,1)S(1)}, bf16[240,128]{1,0:T(8,128)(2,1)S(1)}, u32[]{:S(2)}, u32[]{:S(2)}) collective-permute-start(bf16[240,128]{1,0:T(8,128)(2,1)S(1)} %get-tuple-element.22), channel_id=1, source_target_pairs={{0,12},{4,0},{8,4},{12,8},{1,13},{5,1},{9,5},{13,9},{2,14},{6,2},{... | collective-permute-start | bytes 184328 | tf_op jit(solution)/shard_map/ppermute | solution.py:191
  9.1 0.0 copy-start.8
  9.1 0.0 copy-start.5
  9.1 0.0 copy-start.6
  9.1 0.0 copy-done.2
  9.1 0.0 copy-done.3
  9.1 0.0 copy-done.4
  9.2 0.6 %copy-done.8 = s32[1,16]{1,0:T(1,128)S(1)} copy-done((s32[1,16]{1,0:T(1,128)S(1)}, s32[1,16]{1,0:T(1,128)}, u32[]{:S(2)}) %copy-start.8) | copy-done | bytes 88
  9.8 0.0 copy-done.5
  9.8 0.0 copy-done.6
  9.8 0.0 copy-done.7
  9.8 0.9 %copy-done = f32[128,512]{1,0:T(8,128)S(1)} copy-done((f32[128,512]{1,0:T(8,128)S(1)}, f32[128,512]{1,0:T(8,128)}, u32[]{:S(2)}) %copy-start) | copy-done | bytes 262168
  10.8 0.8 %shard_map.105 = (bf16[2,480,240]{2,1,0:T(8,128)(2,1)S(1)}, bf16[96,240]{1,0:T(8,128)(2,1)S(1)}, f32[240,128]{1,0:T(8,128)S(1)}, f32[96,128]{1,0:T(8,128)S(1)}, ...) custom-call(bf16[4,24,24]{2,1,0:T(8,128)(2,1)S(1)} %copy-done.3, ...), custom_call_target="tpu_custom_call" | custom-call | flops 1000000 | bytes 1055744 | tf_op jit(solution)/shard_map/pallas_call | solution.py:235
  11.6 0.0 collective-permute-done.refs_1_
  11.6 0.4 %collective-permute-done.1.refs_2_ = bf16[240,128]{1,0:T(8,128)(2,1)S(1)} collective-permute-done((bf16[240,128]{1,0:T(8,128)(2,1)S(1)}, bf16[240,128]{1,0:T(8,128)(2,1)S(1)}, u32[]{:S(2)}, u32[]{:S(2)}) %collective-permute-start.1) | collective-permute-done | bytes 61472 | tf_op jit(solution)/shard_map/ppermute | solution.py:191
  12.0 0.3 %collective-permute-done.2.refs_3_ = bf16[240,128]{1,0:T(8,128)(2,1)S(1)} collective-permute-done((bf16[240,128]{1,0:T(8,128)(2,1)S(1)}, bf16[240,128]{1,0:T(8,128)(2,1)S(1)}, u32[]{:S(2)}, u32[]{:S(2)}) %collective-permute-start.2) | collective-permute-done | bytes 61472 | tf_op jit(solution)/shard_map/ppermute | solution.py:191
  12.4 0.8 %shard_map.106 = (f32[8,4,128]{2,1,0:T(4,128)S(1)}, bf16[64,128]{1,0:T(8,128)(2,1)S(1)}) custom-call(bf16[240,128]{1,0:T(8,128)(2,1)S(1)} %get-tuple-element.19.refs_0_, bf16[240,128]{1,0:T(8,128)(2,1)S(1)} %collective-permute-done.refs_1_, bf16[240,128]{1,0:T(8,128)(2,1)S(1)} %collective-permute-done.1.refs_2_, ...), custom_call_target="tpu_custom_call" | custom-call | flops 1000000 | bytes 32768 | tf_op jit(solution)/shard_map/pallas_call | solution.py:252
  13.1 1.6 %collective-permute-start.3 = (bf16[64,128]{1,0:T(8,128)(2,1)S(1)}, bf16[64,128]{1,0:T(8,128)(2,1)S(1)}, u32[]{:S(2)}, u32[]{:S(2)}) collective-permute-start(bf16[64,128]{1,0:T(8,128)(2,1)S(1)} %get-tuple-element.30.refs_0_), channel_id=1, source_target_pairs={{0,2},{2,0},{1,3},{3,1},{4,6},{6,4},{5,7},{7,5},{8,10},{10,8},{9,1... | collective-permute-start | bytes 49160 | tf_op jit(solution)/shard_map/ppermute | solution.py:191
  14.7 0.0 collective-permute-start.4
  14.7 2.2 %collective-permute-done.3.refs_1_ = bf16[64,128]{1,0:T(8,128)(2,1)S(1)} collective-permute-done((bf16[64,128]{1,0:T(8,128)(2,1)S(1)}, bf16[64,128]{1,0:T(8,128)(2,1)S(1)}, u32[]{:S(2)}, u32[]{:S(2)}) %collective-permute-start.3) | collective-permute-done | bytes 16416 | tf_op jit(solution)/shard_map/ppermute | solution.py:191
  16.9 0.0 collective-permute-start.5
  16.9 0.0 collective-permute-done.4.refs_2_
  16.9 1.2 %collective-permute-done.5.refs_3_ = bf16[64,128]{1,0:T(8,128)(2,1)S(1)} collective-permute-done((bf16[64,128]{1,0:T(8,128)(2,1)S(1)}, bf16[64,128]{1,0:T(8,128)(2,1)S(1)}, u32[]{:S(2)}, u32[]{:S(2)}) %collective-permute-start.5) | collective-permute-done | bytes 16416 | tf_op jit(solution)/shard_map/ppermute | solution.py:191
  18.1 0.8 %shard_map.107 = (f32[16,4,128]{2,1,0:T(4,128)}, f32[8,4,128]{2,1,0:T(4,128)}) custom-call(bf16[64,128]{1,0:T(8,128)(2,1)S(1)} %get-tuple-element.30.refs_0_, bf16[64,128]{1,0:T(8,128)(2,1)S(1)} %collective-permute-done.3.refs_1_, bf16[64,128]{1,0:T(8,128)(2,1)S(1)} %collective-permute-done.4.refs_2_, bf16[64,128]{1,0:T(8,128)(2,1)S(1)} %collective-permute-done.5.refs_3_, ...), custom_call_target="tpu_custom_call" | custom-call | flops 1000000 | bytes 49152 | tf_op jit(solution)/shard_map/pallas_call | solution.py:266
  (2 shorter events, 0.0 us)
Async XLA Ops:
  0.6 0.9 %copy-start.1 = (bf16[1,24,32,128]{3,2,1,0:T(8,128)(2,1)S(1)}, bf16[1,24,32,128]{3,2,1,0:T(8,128)(2,1)}, u32[]{:S(2)}) copy-start(bf16[1,24,32,128]{3,2,1,0:T(8,128)(2,1)} %low_ref.1) | copy-start | bytes 589828
  1.6 7.6 %copy-start.2 = (f32[16,4,128]{2,1,0:T(4,128)S(1)}, f32[16,4,128]{2,1,0:T(4,128)}, u32[]{:S(2)}) copy-start(f32[16,4,128]{2,1,0:T(4,128)} %measured_ref.1) | copy-start | bytes 98308
  1.6 7.6 %copy-start.3 = (bf16[4,24,24]{2,1,0:T(8,128)(2,1)S(1)}, bf16[4,24,24]{2,1,0:T(8,128)(2,1)}, u32[]{:S(2)}) copy-start(bf16[4,24,24]{2,1,0:T(8,128)(2,1)} %aw_ref.1) | copy-start | bytes 13828
  1.6 7.6 %copy-start.4 = (bf16[4,24,24]{2,1,0:T(8,128)(2,1)S(1)}, bf16[4,24,24]{2,1,0:T(8,128)(2,1)}, u32[]{:S(2)}) copy-start(bf16[4,24,24]{2,1,0:T(8,128)(2,1)} %cw_ref.1) | copy-start | bytes 13828
  2.1 9.5 %collective-permute-start = (bf16[240,128]{1,0:T(8,128)(2,1)S(1)}, bf16[240,128]{1,0:T(8,128)(2,1)S(1)}, u32[]{:S(2)}, u32[]{:S(2)}) collective-permute-start(bf16[240,128]{1,0:T(8,128)(2,1)S(1)} %get-tuple-element.20), channel_id=1, source_target_pairs={{0,4},{4,8},{8,12},{12,0},{1,5},{5,9},{9,13},{13,1},{2,6},{6,10},{... | collective-permute-start | bytes 184328 | tf_op jit(solution)/shard_map/ppermute | solution.py:191
  5.2 6.9 %collective-permute-start.1 = (bf16[240,128]{1,0:T(8,128)(2,1)S(1)}, bf16[240,128]{1,0:T(8,128)(2,1)S(1)}, u32[]{:S(2)}, u32[]{:S(2)}) collective-permute-start(bf16[240,128]{1,0:T(8,128)(2,1)S(1)} %get-tuple-element.21), channel_id=1, source_target_pairs={{0,8},{4,12},{8,0},{12,4},{1,9},{5,13},{9,1},{13,5},{2,10},{6,14},... | collective-permute-start | bytes 184328 | tf_op jit(solution)/shard_map/ppermute | solution.py:191
  7.8 4.6 %collective-permute-start.2 = (bf16[240,128]{1,0:T(8,128)(2,1)S(1)}, bf16[240,128]{1,0:T(8,128)(2,1)S(1)}, u32[]{:S(2)}, u32[]{:S(2)}) collective-permute-start(bf16[240,128]{1,0:T(8,128)(2,1)S(1)} %get-tuple-element.22), channel_id=1, source_target_pairs={{0,12},{4,0},{8,4},{12,8},{1,13},{5,1},{9,5},{13,9},{2,14},{6,2},{... | collective-permute-start | bytes 184328 | tf_op jit(solution)/shard_map/ppermute | solution.py:191
  9.1 0.7 %copy-start.8 = (s32[1,16]{1,0:T(1,128)S(1)}, s32[1,16]{1,0:T(1,128)}, u32[]{:S(2)}) copy-start(s32[1,16]{1,0:T(1,128)} %sparse_ref.1) | copy-start | bytes 196
  9.1 0.7 %copy-start.5 = (f32[24]{0:T(128)S(1)}, f32[24]{0:T(128)}, u32[]{:S(2)}) copy-start(f32[24]{0:T(128)} %param.11) | copy-start | bytes 292
  9.1 0.7 %copy-start.6 = (f32[24]{0:T(128)S(1)}, f32[24]{0:T(128)}, u32[]{:S(2)}) copy-start(f32[24]{0:T(128)} %param.13) | copy-start | bytes 292
  9.1 0.7 %copy-start.7 = (f32[24]{0:T(128)S(1)}, f32[24]{0:T(128)}, u32[]{:S(2)}) copy-start(f32[24]{0:T(128)} %param.14) | copy-start | bytes 292
  9.8 0.9 %copy-start = (f32[128,512]{1,0:T(8,128)S(1)}, f32[128,512]{1,0:T(8,128)}, u32[]{:S(2)}) copy-start(f32[128,512]{1,0:T(8,128)} %rw_ref.1) | copy-start | bytes 786436
  13.1 3.8 %collective-permute-start.3 = (bf16[64,128]{1,0:T(8,128)(2,1)S(1)}, bf16[64,128]{1,0:T(8,128)(2,1)S(1)}, u32[]{:S(2)}, u32[]{:S(2)}) collective-permute-start(bf16[64,128]{1,0:T(8,128)(2,1)S(1)} %get-tuple-element.30.refs_0_), channel_id=1, source_target_pairs={{0,2},{2,0},{1,3},{3,1},{4,6},{6,4},{5,7},{7,5},{8,10},{10,8},{9,1... | collective-permute-start | bytes 49160 | tf_op jit(solution)/shard_map/ppermute | solution.py:191
  14.7 2.2 %collective-permute-start.4 = (bf16[64,128]{1,0:T(8,128)(2,1)S(1)}, bf16[64,128]{1,0:T(8,128)(2,1)S(1)}, u32[]{:S(2)}, u32[]{:S(2)}) collective-permute-start(bf16[64,128]{1,0:T(8,128)(2,1)S(1)} %get-tuple-element.30.refs_0_), channel_id=1, source_target_pairs={{0,1},{1,0},{2,3},{3,2},{4,5},{5,4},{6,7},{7,6},{8,9},{9,8},{10,11... | collective-permute-start | bytes 49160 | tf_op jit(solution)/shard_map/ppermute | solution.py:191
  16.9 1.2 %collective-permute-start.5 = (bf16[64,128]{1,0:T(8,128)(2,1)S(1)}, bf16[64,128]{1,0:T(8,128)(2,1)S(1)}, u32[]{:S(2)}, u32[]{:S(2)}) collective-permute-start(bf16[64,128]{1,0:T(8,128)(2,1)S(1)} %collective-permute-done.3.refs_1_), channel_id=1, source_target_pairs={{0,1},{1,0},{2,3},{3,2},{4,5},{5,4},{6,7},{7,6},{8,9},{9,8},{10,11... | collective-permute-start | bytes 49160 | tf_op jit(solution)/shard_map/ppermute | solution.py:191

commit v4 on v3

--- a/solution.py
+++ b/solution.py
@@ -163,27 +163,16 @@
     residual_ref[...] = (picked - target_ref[...]).astype(BF16)
 
 
-def adjoint_kernel(shifts, own_out, *refs):
-    residuals, refs = refs[: len(shifts)], refs[len(shifts) :]
-    hi_ref, lo_ref, predicted_ref, out_ref, copied_ref = refs
+def adjoint_kernel(own_out, residual_ref, hi_ref, lo_ref, predicted_ref, out_ref, copied_ref):
     copied_ref[...] = predicted_ref[...]
-    lanes = residuals[0].shape[1]
-    total = None
-    for residual_ref, (narrow_shift, pair_shift) in zip(residuals, shifts):
-        narrow, pair = came_from("narrow", narrow_shift), came_from("pair", pair_shift)
-        block = narrow * lax.axis_size("pair") + pair
-        rows = pl.ds(pl.multiple_of(block * lanes, lanes), lanes)
-        values = residual_ref[...]
-        term = jnp.dot(values, hi_ref[rows, :], preferred_element_type=F32)
-        term += jnp.dot(values, lo_ref[rows, :], preferred_element_type=F32)
-        total = term if total is None else total + term
+    count, size, lanes = residual_ref.shape
+    total = jnp.zeros((size, lanes), F32)
+    for block in range(count):
+        rows = slice(block * lanes, (block + 1) * lanes)
+        total += jnp.dot(residual_ref[block], hi_ref[rows, :], preferred_element_type=F32)
+        total += jnp.dot(residual_ref[block], lo_ref[rows, :], preferred_element_type=F32)
     for k in range(out_ref.shape[0]):
         out_ref[k] = total[k * own_out : (k + 1) * own_out]
-
-
-def came_from(axis, distance):
-    count = lax.axis_size(axis)
-    return lax.rem(lax.axis_index(axis) - distance + count, count)
 
 
 def send(block, axis, distance):
@@ -202,7 +191,7 @@
     measured,
     row_weights,
 ):
-    wide, narrow, pair = (lax.axis_size(axis) for axis in ("wide", "narrow", "pair"))
+    wide = lax.axis_size("wide")
     _, channels, width, lanes = low_sino.shape
     own_out = width // wide // 2
     span = 2 * own_out + 2
@@ -256,19 +245,13 @@
         vmem=big,
     )(*views, a1, a2, b1, b2, head, select, target)
 
-    shifts = [(0, 0)] + [(s, 0) for s in range(1, narrow)] + [(0, t) for t in range(1, pair)]
-    blocks = [residual] + [send(residual, "narrow", s) for s in range(1, narrow)]
-    blocks += [send(residual, "pair", t) for t in range(1, pair)]
-    for s in range(1, narrow):
-        for t in range(1, pair):
-            shifts.append((s, t))
-            blocks.append(send(blocks[s], "pair", t))
+    gathered = lax.all_gather(residual, ("narrow", "pair"), axis=0)
     adjoint, predicted = call(
-        functools.partial(adjoint_kernel, shifts, own_out),
+        functools.partial(adjoint_kernel, own_out),
         [shape((sparse_count, own_out, lanes), F32), shape(predicted.shape, F32)],
-        [VMEM] * (len(blocks) + 3),
-        vmem=big,
-    )(*blocks, high, low, predicted)
+        [VMEM] * 4,
+        vmem=big,
+    )(gathered, high, low, predicted)
     return (predicted, adjoint)
 
 

time: 19.1 us -> 19.4 us (1.016)
  blocking collectives: 0 us -> 5.25 us
  waiting for transfers between devices: 4.17 us -> 0.75 us
  starting transfers between devices: 8.59 us -> 7.01 us
    all_gather x0 -> x1, blocking collectives: none -> 5.25 us  [local(): gathered = lax.all_gather(residual, ('narrow', 'pair'), axis=0)]
    ppermute x6 -> x3, waiting for transfers between devices: 4.17 us -> 0.75 us  [send(): lax.ppermute(block, axis, [(i, (i + distance) % count) for i in range(cou...]
    ppermute x6 -> x3, starting transfers between devices: 8.59 us -> 7.01 us  [send(): lax.ppermute(block, axis, [(i, (i + distance) % count) for i in range(cou...]
  transfers between devices with their start and end apart: 6 -> 3, of which waited for: 4 -> 2; matrix products, arithmetic and copies ran while one was open for 0% -> 0% of each run, Pallas kernels for 4% -> 4%
where the time goes in v4:
time: 19.4 us; the launch traced here: 19.2 us
  starting transfers between devices  7.01 us (36%)
  blocking collectives  5.25 us (27%)
  Pallas kernels  2.94 us (15%)
  local copies, waits for them, and re-layouts  2.55 us (13%)
  waiting for transfers between devices  0.75 us (4%)
  between operations  0.7 us (4%)
    ppermute x3, starting transfers between devices, send(): lax.ppermute(block, axis, [(i, (i + distance) % count) for i in range(cou...  7.01 us
    all_gather x1, blocking collectives, local(): gathered = lax.all_gather(residual, ('narrow', 'pair'), axis=0)  5.25 us
    unnamed x18, local copies, waits for them, and re-layouts  2.55 us
    pallas_call x1, Pallas kernels, local(): call(functools.partial(adjoint_kernel, own_out), [shape((sparse_count, ow...  0.82 us
    pallas_call x1, Pallas kernels, local(): call(functools.partial(prepare_kernel, wide, own_out), [shape((2, 2 * siz...  0.82 us
    pallas_call x1, Pallas kernels, local(): call(functools.partial(net_kernel, wide, own_out), [shape((2 * wide, own_...  0.76 us
    ppermute x3, waiting for transfers between devices, send(): lax.ppermute(block, axis, [(i, (i + distance) % count) for i in range(cou...  0.75 us
    pallas_call x1, Pallas kernels, local(): call(functools.partial(pack_kernel, wide), [shape((size, lanes), BF16)] *...  0.54 us
  transfers between devices with their start and end apart: 3, of which 2 were waited for; matrix products, arithmetic and copies ran while one was open for 0% of the time, Pallas kernels for 4%

profile of v4, /device:TPU:0, one launch (start us, length us, event | category | flops | bytes accessed | tf_op | source)
XLA Modules:
  0.0 19.2 jit_solution(3292251692669445469)
XLA Ops:
  0.6 0.0 copy-start.1
  0.6 0.9 %copy-done.1 = bf16[1,24,32,128]{3,2,1,0:T(8,128)(2,1)S(1)} copy-done((bf16[1,24,32,128]{3,2,1,0:T(8,128)(2,1)S(1)}, bf16[1,24,32,128]{3,2,1,0:T(8,128)(2,1)}, u32[]{:S(2)}) %copy-start.1) | copy-done | bytes 196632
  1.6 0.0 copy-start.2
  1.6 0.0 copy-start.3
  1.6 0.0 copy-start.4
  1.6 0.5 %shard_map.104 = (bf16[240,128]{1,0:T(8,128)(2,1)S(1)}, bf16[240,128]{1,0:T(8,128)(2,1)S(1)}, bf16[240,128]{1,0:T(8,128)(2,1)S(1)}, bf16[240,128]{1,0:T(8,128)(2,1)S(1)}) custom-call(bf16[1,24,32,128]{3,2,1,0:T(8,128)(2,1)S(1)} %copy-done.1), custom_call_target="tpu_custom_call" | custom-call | flops 1000000 | bytes 245760 | tf_op jit(solution)/shard_map/pallas_call | solution.py:215
  2.1 3.1 %collective-permute-start = (bf16[240,128]{1,0:T(8,128)(2,1)S(1)}, bf16[240,128]{1,0:T(8,128)(2,1)S(1)}, u32[]{:S(2)}, u32[]{:S(2)}) collective-permute-start(bf16[240,128]{1,0:T(8,128)(2,1)S(1)} %get-tuple-element.20), channel_id=1, source_target_pairs={{0,4},{4,8},{8,12},{12,0},{1,5},{5,9},{9,13},{13,1},{2,6},{6,10},{... | collective-permute-start | bytes 184328 | tf_op jit(solution)/shard_map/ppermute | solution.py:180
  5.2 2.6 %collective-permute-start.1 = (bf16[240,128]{1,0:T(8,128)(2,1)S(1)}, bf16[240,128]{1,0:T(8,128)(2,1)S(1)}, u32[]{:S(2)}, u32[]{:S(2)}) collective-permute-start(bf16[240,128]{1,0:T(8,128)(2,1)S(1)} %get-tuple-element.21), channel_id=1, source_target_pairs={{0,8},{4,12},{8,0},{12,4},{1,9},{5,13},{9,1},{13,5},{2,10},{6,14},... | collective-permute-start | bytes 184328 | tf_op jit(solution)/shard_map/ppermute | solution.py:180
  7.8 1.3 %collective-permute-start.2 = (bf16[240,128]{1,0:T(8,128)(2,1)S(1)}, bf16[240,128]{1,0:T(8,128)(2,1)S(1)}, u32[]{:S(2)}, u32[]{:S(2)}) collective-permute-start(bf16[240,128]{1,0:T(8,128)(2,1)S(1)} %get-tuple-element.22), channel_id=1, source_target_pairs={{0,12},{4,0},{8,4},{12,8},{1,13},{5,1},{9,5},{13,9},{2,14},{6,2},{... | collective-permute-start | bytes 184328 | tf_op jit(solution)/shard_map/ppermute | solution.py:180
  9.1 0.0 copy-start.8
  9.1 0.0 copy-start.5
  9.1 0.0 copy-start.6
  9.1 0.0 copy-start.7
  9.1 0.0 copy-done.2
  9.1 0.0 copy-done.3
  9.1 0.0 copy-done.4
  9.2 0.6 %copy-done.8 = s32[1,16]{1,0:T(1,128)S(1)} copy-done((s32[1,16]{1,0:T(1,128)S(1)}, s32[1,16]{1,0:T(1,128)}, u32[]{:S(2)}) %copy-start.8) | copy-done | bytes 88
  9.8 0.0 copy-done.5
  9.8 0.0 copy-done.6
  9.8 0.0 copy-done.7
  9.8 0.0 copy-start
  9.8 0.9 %copy-done = f32[128,512]{1,0:T(8,128)S(1)} copy-done((f32[128,512]{1,0:T(8,128)S(1)}, f32[128,512]{1,0:T(8,128)}, u32[]{:S(2)}) %copy-start) | copy-done | bytes 262168
  10.8 0.8 %shard_map.105 = (bf16[2,480,240]{2,1,0:T(8,128)(2,1)S(1)}, bf16[96,240]{1,0:T(8,128)(2,1)S(1)}, f32[240,128]{1,0:T(8,128)S(1)}, f32[96,128]{1,0:T(8,128)S(1)}, ...) custom-call(bf16[4,24,24]{2,1,0:T(8,128)(2,1)S(1)} %copy-done.3, ...), custom_call_target="tpu_custom_call" | custom-call | flops 1000000 | bytes 1055744 | tf_op jit(solution)/shard_map/pallas_call | solution.py:224
  11.6 0.0 collective-permute-done.refs_1_
  11.6 0.4 %collective-permute-done.1.refs_2_ = bf16[240,128]{1,0:T(8,128)(2,1)S(1)} collective-permute-done((bf16[240,128]{1,0:T(8,128)(2,1)S(1)}, bf16[240,128]{1,0:T(8,128)(2,1)S(1)}, u32[]{:S(2)}, u32[]{:S(2)}) %collective-permute-start.1) | collective-permute-done | bytes 61472 | tf_op jit(solution)/shard_map/ppermute | solution.py:180
  12.0 0.3 %collective-permute-done.2.refs_3_ = bf16[240,128]{1,0:T(8,128)(2,1)S(1)} collective-permute-done((bf16[240,128]{1,0:T(8,128)(2,1)S(1)}, bf16[240,128]{1,0:T(8,128)(2,1)S(1)}, u32[]{:S(2)}, u32[]{:S(2)}) %collective-permute-start.2) | collective-permute-done | bytes 61472 | tf_op jit(solution)/shard_map/ppermute | solution.py:180
  12.4 0.8 %shard_map.106 = (f32[8,4,128]{2,1,0:T(4,128)S(1)}, bf16[64,128]{1,0:T(8,128)(2,1)S(1)}) custom-call(bf16[240,128]{1,0:T(8,128)(2,1)S(1)} %get-tuple-element.19.refs_0_, bf16[240,128]{1,0:T(8,128)(2,1)S(1)} %collective-permute-done.refs_1_, bf16[240,128]{1,0:T(8,128)(2,1)S(1)} %collective-permute-done.1.refs_2_, ...), custom_call_target="tpu_custom_call" | custom-call | flops 1000000 | bytes 32768 | tf_op jit(solution)/shard_map/pallas_call | solution.py:241
  13.1 5.2 %all-gather = bf16[256,128]{1,0:T(8,128)(2,1)S(1)} all-gather(bf16[64,128]{1,0:T(8,128)(2,1)S(1)} %get-tuple-element.30), channel_id=2, replica_groups=mesh['parts'=2,'wide'=4,'narrow'=2,'pair'=2] {'narrow','pair'}, dimensions={0}, use_global_device_ids=true | all-gather | bytes 81920 | tf_op jit(solution)/shard_map/all_gather | solution.py:248
  18.4 0.8 %shard_map.107 = (f32[16,4,128]{2,1,0:T(4,128)}, f32[8,4,128]{2,1,0:T(4,128)}) custom-call(bf16[4,64,128]{2,1,0:T(8,128)(2,1)S(1)} %bitcast.4, bf16[512,128]{1,0:T(8,128)(2,1)S(1)} %get-tuple-element.31.hi_ref, bf16[512,128]{1,0:T(8,128)(2,1)S(1)} %get-tuple-element.32.lo_ref, f32[8,4,128]{2,1,0:T(4,128)S(1)} %get-tuple-element.33.predicted_ref), custom_call_target="tpu_custom_call" | custom-call | flops 1000000 | bytes 49152 | tf_op jit(solution)/shard_map/pallas_call | solution.py:249
Async XLA Ops:
  0.6 0.9 %copy-start.1 = (bf16[1,24,32,128]{3,2,1,0:T(8,128)(2,1)S(1)}, bf16[1,24,32,128]{3,2,1,0:T(8,128)(2,1)}, u32[]{:S(2)}) copy-start(bf16[1,24,32,128]{3,2,1,0:T(8,128)(2,1)} %low_ref.1) | copy-start | bytes 589828
  1.6 7.6 %copy-start.2 = (f32[16,4,128]{2,1,0:T(4,128)S(1)}, f32[16,4,128]{2,1,0:T(4,128)}, u32[]{:S(2)}) copy-start(f32[16,4,128]{2,1,0:T(4,128)} %measured_ref.1) | copy-start | bytes 98308
  1.6 7.6 %copy-start.3 = (bf16[4,24,24]{2,1,0:T(8,128)(2,1)S(1)}, bf16[4,24,24]{2,1,0:T(8,128)(2,1)}, u32[]{:S(2)}) copy-start(bf16[4,24,24]{2,1,0:T(8,128)(2,1)} %aw_ref.1) | copy-start | bytes 13828
  1.6 7.6 %copy-start.4 = (bf16[4,24,24]{2,1,0:T(8,128)(2,1)S(1)}, bf16[4,24,24]{2,1,0:T(8,128)(2,1)}, u32[]{:S(2)}) copy-start(bf16[4,24,24]{2,1,0:T(8,128)(2,1)} %cw_ref.1) | copy-start | bytes 13828
  2.1 9.5 %collective-permute-start = (bf16[240,128]{1,0:T(8,128)(2,1)S(1)}, bf16[240,128]{1,0:T(8,128)(2,1)S(1)}, u32[]{:S(2)}, u32[]{:S(2)}) collective-permute-start(bf16[240,128]{1,0:T(8,128)(2,1)S(1)} %get-tuple-element.20), channel_id=1, source_target_pairs={{0,4},{4,8},{8,12},{12,0},{1,5},{5,9},{9,13},{13,1},{2,6},{6,10},{... | collective-permute-start | bytes 184328 | tf_op jit(solution)/shard_map/ppermute | solution.py:180
  5.2 6.9 %collective-permute-start.1 = (bf16[240,128]{1,0:T(8,128)(2,1)S(1)}, bf16[240,128]{1,0:T(8,128)(2,1)S(1)}, u32[]{:S(2)}, u32[]{:S(2)}) collective-permute-start(bf16[240,128]{1,0:T(8,128)(2,1)S(1)} %get-tuple-element.21), channel_id=1, source_target_pairs={{0,8},{4,12},{8,0},{12,4},{1,9},{5,13},{9,1},{13,5},{2,10},{6,14},... | collective-permute-start | bytes 184328 | tf_op jit(solution)/shard_map/ppermute | solution.py:180
  7.8 4.6 %collective-permute-start.2 = (bf16[240,128]{1,0:T(8,128)(2,1)S(1)}, bf16[240,128]{1,0:T(8,128)(2,1)S(1)}, u32[]{:S(2)}, u32[]{:S(2)}) collective-permute-start(bf16[240,128]{1,0:T(8,128)(2,1)S(1)} %get-tuple-element.22), channel_id=1, source_target_pairs={{0,12},{4,0},{8,4},{12,8},{1,13},{5,1},{9,5},{13,9},{2,14},{6,2},{... | collective-permute-start | bytes 184328 | tf_op jit(solution)/shard_map/ppermute | solution.py:180
  9.1 0.7 %copy-start.8 = (s32[1,16]{1,0:T(1,128)S(1)}, s32[1,16]{1,0:T(1,128)}, u32[]{:S(2)}) copy-start(s32[1,16]{1,0:T(1,128)} %sparse_ref.1) | copy-start | bytes 196
  9.1 0.7 %copy-start.5 = (f32[24]{0:T(128)S(1)}, f32[24]{0:T(128)}, u32[]{:S(2)}) copy-start(f32[24]{0:T(128)} %param.11) | copy-start | bytes 292
  9.1 0.7 %copy-start.6 = (f32[24]{0:T(128)S(1)}, f32[24]{0:T(128)}, u32[]{:S(2)}) copy-start(f32[24]{0:T(128)} %param.13) | copy-start | bytes 292
  9.1 0.7 %copy-start.7 = (f32[24]{0:T(128)S(1)}, f32[24]{0:T(128)}, u32[]{:S(2)}) copy-start(f32[24]{0:T(128)} %param.14) | copy-start | bytes 292
  9.8 0.9 %copy-start = (f32[128,512]{1,0:T(8,128)S(1)}, f32[128,512]{1,0:T(8,128)}, u32[]{:S(2)}) copy-start(f32[128,512]{1,0:T(8,128)} %rw_ref.1) | copy-start | bytes 786436

commit v5 on v3

--- a/solution.py
+++ b/solution.py
@@ -69,8 +69,7 @@
     b1_ref,
     b2_ref,
     h_ref,
-    hi_ref,
-    lo_ref,
+    turned_ref,
     select_ref,
     target_ref,
 ):
@@ -113,8 +112,8 @@
 
     turned = rw_ref[...].T
     high = turned.astype(BF16)
-    hi_ref[...] = high
-    lo_ref[...] = (turned - high.astype(F32)).astype(BF16)
+    turned_ref[:, : high.shape[1]] = high
+    turned_ref[:, high.shape[1] :] = (turned - high.astype(F32)).astype(BF16)
 
     sparse_count = measured_ref.shape[0]
     wanted = (select_ref.shape[0], sparse_count)
@@ -165,18 +164,17 @@
 
 def adjoint_kernel(shifts, own_out, *refs):
     residuals, refs = refs[: len(shifts)], refs[len(shifts) :]
-    hi_ref, lo_ref, predicted_ref, out_ref, copied_ref = refs
+    turned_ref, predicted_ref, out_ref, copied_ref = refs
     copied_ref[...] = predicted_ref[...]
     lanes = residuals[0].shape[1]
-    total = None
-    for residual_ref, (narrow_shift, pair_shift) in zip(residuals, shifts):
+    weights = []
+    for narrow_shift, pair_shift in shifts:
         narrow, pair = came_from("narrow", narrow_shift), came_from("pair", pair_shift)
         block = narrow * lax.axis_size("pair") + pair
-        rows = pl.ds(pl.multiple_of(block * lanes, lanes), lanes)
-        values = residual_ref[...]
-        term = jnp.dot(values, hi_ref[rows, :], preferred_element_type=F32)
-        term += jnp.dot(values, lo_ref[rows, :], preferred_element_type=F32)
-        total = term if total is None else total + term
+        weights.append(turned_ref[pl.ds(pl.multiple_of(block * lanes, lanes), lanes), :])
+    values = jnp.concatenate([ref[...] for ref in residuals], axis=1)
+    both = jnp.dot(values, jnp.concatenate(weights, axis=0), preferred_element_type=F32)
+    total = both[:, :lanes] + both[:, lanes:]
     for k in range(out_ref.shape[0]):
         out_ref[k] = total[k * own_out : (k + 1) * own_out]
 
@@ -189,6 +187,16 @@
 def send(block, axis, distance):
     count = lax.axis_size(axis)
     return lax.ppermute(block, axis, [(i, (i + distance) % count) for i in range(count)])
+
+
+def send_both(block, narrow_distance, pair_distance):
+    narrow, pair = lax.axis_size("narrow"), lax.axis_size("pair")
+    route = []
+    for i in range(narrow):
+        for j in range(pair):
+            target = (i + narrow_distance) % narrow * pair + (j + pair_distance) % pair
+            route.append((i * pair + j, target))
+    return lax.ppermute(block, ("narrow", "pair"), route)
 
 
 def local(
@@ -232,7 +240,7 @@
     )(low_sino)
     views = [windows[0]] + [send(windows[s], "wide", s) for s in range(1, wide)]
 
-    a1, a2, b1, b2, head, high, low, select, target = call(
+    a1, a2, b1, b2, head, turned, select, target = call(
         functools.partial(prepare_kernel, wide, own_out),
         [
             shape((2, 2 * size, size), BF16),
@@ -240,8 +248,7 @@
             shape((size, lanes), F32),
             shape((outs, lanes), F32),
             shape((outs, lanes), F32),
-            shape((rows, lanes), BF16),
-            shape((rows, lanes), BF16),
+            shape((rows, 2 * lanes), BF16),
             shape(flat, F32),
             shape(flat, F32),
         ],
@@ -256,19 +263,16 @@
         vmem=big,
     )(*views, a1, a2, b1, b2, head, select, target)
 
-    shifts = [(0, 0)] + [(s, 0) for s in range(1, narrow)] + [(0, t) for t in range(1, pair)]
-    blocks = [residual] + [send(residual, "narrow", s) for s in range(1, narrow)]
-    blocks += [send(residual, "pair", t) for t in range(1, pair)]
-    for s in range(1, narrow):
-        for t in range(1, pair):
-            shifts.append((s, t))
-            blocks.append(send(blocks[s], "pair", t))
+    shifts = [(s, t) for s in range(1, narrow) for t in range(1, pair)]
+    shifts += [(s, 0) for s in range(1, narrow)] + [(0, t) for t in range(1, pair)]
+    blocks = [residual] + [send_both(residual, s, t) for s, t in shifts]
+    shifts.insert(0, (0, 0))
     adjoint, predicted = call(
         functools.partial(adjoint_kernel, shifts, own_out),
         [shape((sparse_count, own_out, lanes), F32), shape(predicted.shape, F32)],
-        [VMEM] * (len(blocks) + 3),
-        vmem=big,
-    )(*blocks, high, low, predicted)
+        [VMEM] * (len(blocks) + 2),
+        vmem=big,
+    )(*blocks, turned, predicted)
     return (predicted, adjoint)
 
 

time: 19.1 us -> 18.9 us (0.990)
  waiting for transfers between devices: 4.17 us -> 3.62 us
  starting transfers between devices: 8.59 us -> 8.95 us
    ppermute x6 -> x3, waiting for transfers between devices: 4.17 us -> 0.75 us  [send(): lax.ppermute(block, axis, [(i, (i + distance) % count) for i in range(cou...]
    ppermute x0 -> x3, waiting for transfers between devices: none -> 2.87 us  [send_both(): return lax.ppermute(block, ('narrow', 'pair'), route)]
    ppermute x0 -> x3, starting transfers between devices: none -> 1.93 us  [send_both(): return lax.ppermute(block, ('narrow', 'pair'), route)]
    ppermute x6 -> x3, starting transfers between devices: 8.59 us -> 7.01 us  [send(): lax.ppermute(block, axis, [(i, (i + distance) % count) for i in range(cou...]
where the time goes in v5:
time: 18.9 us; the launch traced here: 18.7 us
  starting transfers between devices  8.95 us (47%)
  waiting for transfers between devices  3.62 us (19%)
  Pallas kernels  2.9 us (15%)
  local copies, waits for them, and re-layouts  2.55 us (13%)
  between operations  0.71 us (4%)
    ppermute x3, starting transfers between devices, send(): lax.ppermute(block, axis, [(i, (i + distance) % count) for i in range(cou...  7.01 us
    ppermute x3, waiting for transfers between devices, send_both(): return lax.ppermute(block, ('narrow', 'pair'), route)  2.87 us
    unnamed x18, local copies, waits for them, and re-layouts  2.55 us
    ppermute x3, starting transfers between devices, send_both(): return lax.ppermute(block, ('narrow', 'pair'), route)  1.93 us
    pallas_call x1, Pallas kernels, local(): call(functools.partial(prepare_kernel, wide, own_out), [shape((2, 2 * siz...  0.82 us
    pallas_call x1, Pallas kernels, local(): call(functools.partial(adjoint_kernel, shifts, own_out), [shape((sparse_c...  0.79 us
    pallas_call x1, Pallas kernels, local(): call(functools.partial(net_kernel, wide, own_out), [shape((2 * wide, own_...  0.76 us
    ppermute x3, waiting for transfers between devices, send(): lax.ppermute(block, axis, [(i, (i + distance) % count) for i in range(cou...  0.75 us
  transfers between devices with their start and end apart: 6, of which 4 were waited for; matrix products, arithmetic and copies ran while one was open for 0% of the time, Pallas kernels for 4%

profile of v5, /device:TPU:0, one launch (start us, length us, event | category | flops | bytes accessed | tf_op | source)
XLA Modules:
  0.0 18.7 jit_solution(1044141244293680268)
XLA Ops:
  0.6 0.0 copy-start.1
  0.6 0.9 %copy-done.1 = bf16[1,24,32,128]{3,2,1,0:T(8,128)(2,1)S(1)} copy-done((bf16[1,24,32,128]{3,2,1,0:T(8,128)(2,1)S(1)}, bf16[1,24,32,128]{3,2,1,0:T(8,128)(2,1)}, u32[]{:S(2)}) %copy-start.1) | copy-done | bytes 196632
  1.6 0.0 copy-start.2
  1.6 0.0 copy-start.3
  1.6 0.0 copy-start.4
  1.6 0.5 %shard_map.104 = (bf16[240,128]{1,0:T(8,128)(2,1)S(1)}, bf16[240,128]{1,0:T(8,128)(2,1)S(1)}, bf16[240,128]{1,0:T(8,128)(2,1)S(1)}, bf16[240,128]{1,0:T(8,128)(2,1)S(1)}) custom-call(bf16[1,24,32,128]{3,2,1,0:T(8,128)(2,1)S(1)} %copy-done.1), custom_call_target="tpu_custom_call" | custom-call | flops 1000000 | bytes 245760 | tf_op jit(solution)/shard_map/pallas_call | solution.py:234
  2.1 3.1 %collective-permute-start = (bf16[240,128]{1,0:T(8,128)(2,1)S(1)}, bf16[240,128]{1,0:T(8,128)(2,1)S(1)}, u32[]{:S(2)}, u32[]{:S(2)}) collective-permute-start(bf16[240,128]{1,0:T(8,128)(2,1)S(1)} %get-tuple-element.19), channel_id=1, source_target_pairs={{0,4},{4,8},{8,12},{12,0},{1,5},{5,9},{9,13},{13,1},{2,6},{6,10},{... | collective-permute-start | bytes 184328 | tf_op jit(solution)/shard_map/ppermute | solution.py:189
  5.2 2.6 %collective-permute-start.1 = (bf16[240,128]{1,0:T(8,128)(2,1)S(1)}, bf16[240,128]{1,0:T(8,128)(2,1)S(1)}, u32[]{:S(2)}, u32[]{:S(2)}) collective-permute-start(bf16[240,128]{1,0:T(8,128)(2,1)S(1)} %get-tuple-element.20), channel_id=1, source_target_pairs={{0,8},{4,12},{8,0},{12,4},{1,9},{5,13},{9,1},{13,5},{2,10},{6,14},... | collective-permute-start | bytes 184328 | tf_op jit(solution)/shard_map/ppermute | solution.py:189
  7.8 1.3 %collective-permute-start.2 = (bf16[240,128]{1,0:T(8,128)(2,1)S(1)}, bf16[240,128]{1,0:T(8,128)(2,1)S(1)}, u32[]{:S(2)}, u32[]{:S(2)}) collective-permute-start(bf16[240,128]{1,0:T(8,128)(2,1)S(1)} %get-tuple-element.21), channel_id=1, source_target_pairs={{0,12},{4,0},{8,4},{12,8},{1,13},{5,1},{9,5},{13,9},{2,14},{6,2},{... | collective-permute-start | bytes 184328 | tf_op jit(solution)/shard_map/ppermute | solution.py:189
  9.1 0.0 copy-start.8
  9.1 0.0 copy-start.5
  9.1 0.0 copy-start.6
  9.1 0.0 copy-done.2
  9.1 0.0 copy-done.3
  9.1 0.0 copy-done.4
  9.2 0.6 %copy-done.8 = s32[1,16]{1,0:T(1,128)S(1)} copy-done((s32[1,16]{1,0:T(1,128)S(1)}, s32[1,16]{1,0:T(1,128)}, u32[]{:S(2)}) %copy-start.8) | copy-done | bytes 88
  9.8 0.0 copy-done.5
  9.8 0.0 copy-done.6
  9.8 0.0 copy-done.7
  9.8 0.9 %copy-done = f32[128,512]{1,0:T(8,128)S(1)} copy-done((f32[128,512]{1,0:T(8,128)S(1)}, f32[128,512]{1,0:T(8,128)}, u32[]{:S(2)}) %copy-start) | copy-done | bytes 262168
  10.8 0.8 %shard_map.105 = (bf16[2,480,240]{2,1,0:T(8,128)(2,1)S(1)}, bf16[96,240]{1,0:T(8,128)(2,1)S(1)}, f32[240,128]{1,0:T(8,128)S(1)}, f32[96,128]{1,0:T(8,128)S(1)}, ...) custom-call(bf16[4,24,24]{2,1,0:T(8,128)(2,1)S(1)} %copy-done.3, ...), custom_call_target="tpu_custom_call" | custom-call | flops 1000000 | bytes 1055744 | tf_op jit(solution)/shard_map/pallas_call | solution.py:243
  11.6 0.0 collective-permute-done.refs_1_
  11.6 0.4 %collective-permute-done.1.refs_2_ = bf16[240,128]{1,0:T(8,128)(2,1)S(1)} collective-permute-done((bf16[240,128]{1,0:T(8,128)(2,1)S(1)}, bf16[240,128]{1,0:T(8,128)(2,1)S(1)}, u32[]{:S(2)}, u32[]{:S(2)}) %collective-permute-start.1) | collective-permute-done | bytes 61472 | tf_op jit(solution)/shard_map/ppermute | solution.py:189
  12.0 0.3 %collective-permute-done.2.refs_3_ = bf16[240,128]{1,0:T(8,128)(2,1)S(1)} collective-permute-done((bf16[240,128]{1,0:T(8,128)(2,1)S(1)}, bf16[240,128]{1,0:T(8,128)(2,1)S(1)}, u32[]{:S(2)}, u32[]{:S(2)}) %collective-permute-start.2) | collective-permute-done | bytes 61472 | tf_op jit(solution)/shard_map/ppermute | solution.py:189
  12.4 0.8 %shard_map.106 = (f32[8,4,128]{2,1,0:T(4,128)S(1)}, bf16[64,128]{1,0:T(8,128)(2,1)S(1)}) custom-call(bf16[240,128]{1,0:T(8,128)(2,1)S(1)} %get-tuple-element.18.refs_0_, bf16[240,128]{1,0:T(8,128)(2,1)S(1)} %collective-permute-done.refs_1_, bf16[240,128]{1,0:T(8,128)(2,1)S(1)} %collective-permute-done.1.refs_2_, ...), custom_call_target="tpu_custom_call" | custom-call | flops 1000000 | bytes 32768 | tf_op jit(solution)/shard_map/pallas_call | solution.py:259
  13.1 0.1 collective-permute-start.5
  13.2 1.6 %collective-permute-start.4 = (bf16[64,128]{1,0:T(8,128)(2,1)S(1)}, bf16[64,128]{1,0:T(8,128)(2,1)S(1)}, u32[]{:S(2)}, u32[]{:S(2)}) collective-permute-start(bf16[64,128]{1,0:T(8,128)(2,1)S(1)} %get-tuple-element.29.refs_0_), channel_id=1, source_target_pairs={{0,2},{1,3},{2,0},{3,1},{4,6},{5,7},{6,4},{7,5},{8,10},{9,11},{10,... | collective-permute-start | bytes 49160 | tf_op jit(solution)/shard_map/ppermute | solution.py:199
  14.8 0.3 %collective-permute-start.3 = (bf16[64,128]{1,0:T(8,128)(2,1)S(1)}, bf16[64,128]{1,0:T(8,128)(2,1)S(1)}, u32[]{:S(2)}, u32[]{:S(2)}) collective-permute-start(bf16[64,128]{1,0:T(8,128)(2,1)S(1)} %get-tuple-element.29.refs_0_), channel_id=1, source_target_pairs={{0,3},{1,2},{2,1},{3,0},{4,7},{5,6},{6,5},{7,4},{8,11},{9,10},{10,... | collective-permute-start | bytes 49160 | tf_op jit(solution)/shard_map/ppermute | solution.py:199
  15.1 0.0 collective-permute-done.5.refs_3_
  15.1 1.9 %collective-permute-done.4.refs_2_ = bf16[64,128]{1,0:T(8,128)(2,1)S(1)} collective-permute-done((bf16[64,128]{1,0:T(8,128)(2,1)S(1)}, bf16[64,128]{1,0:T(8,128)(2,1)S(1)}, u32[]{:S(2)}, u32[]{:S(2)}) %collective-permute-start.4) | collective-permute-done | bytes 16416 | tf_op jit(solution)/shard_map/ppermute | solution.py:199
  17.0 0.9 %collective-permute-done.3.refs_1_ = bf16[64,128]{1,0:T(8,128)(2,1)S(1)} collective-permute-done((bf16[64,128]{1,0:T(8,128)(2,1)S(1)}, bf16[64,128]{1,0:T(8,128)(2,1)S(1)}, u32[]{:S(2)}, u32[]{:S(2)}) %collective-permute-start.3) | collective-permute-done | bytes 16416 | tf_op jit(solution)/shard_map/ppermute | solution.py:199
  17.9 0.8 %shard_map.107 = (f32[16,4,128]{2,1,0:T(4,128)}, f32[8,4,128]{2,1,0:T(4,128)}) custom-call(bf16[64,128]{1,0:T(8,128)(2,1)S(1)} %get-tuple-element.29.refs_0_, bf16[64,128]{1,0:T(8,128)(2,1)S(1)} %collective-permute-done.3.refs_1_, bf16[64,128]{1,0:T(8,128)(2,1)S(1)} %collective-permute-done.4.refs_2_, bf16[64,128]{1,0:T(8,128)(2,1)S(1)} %collective-permute-done.5.refs_3_, ...), custom_call_target="tpu_custom_call" | custom-call | flops 1000000 | bytes 49152 | tf_op jit(solution)/shard_map/pallas_call | solution.py:270
  (2 shorter events, 0.0 us)
Async XLA Ops:
  0.6 0.9 %copy-start.1 = (bf16[1,24,32,128]{3,2,1,0:T(8,128)(2,1)S(1)}, bf16[1,24,32,128]{3,2,1,0:T(8,128)(2,1)}, u32[]{:S(2)}) copy-start(bf16[1,24,32,128]{3,2,1,0:T(8,128)(2,1)} %low_ref.1) | copy-start | bytes 589828
  1.6 7.6 %copy-start.2 = (f32[16,4,128]{2,1,0:T(4,128)S(1)}, f32[16,4,128]{2,1,0:T(4,128)}, u32[]{:S(2)}) copy-start(f32[16,4,128]{2,1,0:T(4,128)} %measured_ref.1) | copy-start | bytes 98308
  1.6 7.6 %copy-start.3 = (bf16[4,24,24]{2,1,0:T(8,128)(2,1)S(1)}, bf16[4,24,24]{2,1,0:T(8,128)(2,1)}, u32[]{:S(2)}) copy-start(bf16[4,24,24]{2,1,0:T(8,128)(2,1)} %aw_ref.1) | copy-start | bytes 13828
  1.6 7.6 %copy-start.4 = (bf16[4,24,24]{2,1,0:T(8,128)(2,1)S(1)}, bf16[4,24,24]{2,1,0:T(8,128)(2,1)}, u32[]{:S(2)}) copy-start(bf16[4,24,24]{2,1,0:T(8,128)(2,1)} %cw_ref.1) | copy-start | bytes 13828
  2.1 9.5 %collective-permute-start = (bf16[240,128]{1,0:T(8,128)(2,1)S(1)}, bf16[240,128]{1,0:T(8,128)(2,1)S(1)}, u32[]{:S(2)}, u32[]{:S(2)}) collective-permute-start(bf16[240,128]{1,0:T(8,128)(2,1)S(1)} %get-tuple-element.19), channel_id=1, source_target_pairs={{0,4},{4,8},{8,12},{12,0},{1,5},{5,9},{9,13},{13,1},{2,6},{6,10},{... | collective-permute-start | bytes 184328 | tf_op jit(solution)/shard_map/ppermute | solution.py:189
  5.2 6.9 %collective-permute-start.1 = (bf16[240,128]{1,0:T(8,128)(2,1)S(1)}, bf16[240,128]{1,0:T(8,128)(2,1)S(1)}, u32[]{:S(2)}, u32[]{:S(2)}) collective-permute-start(bf16[240,128]{1,0:T(8,128)(2,1)S(1)} %get-tuple-element.20), channel_id=1, source_target_pairs={{0,8},{4,12},{8,0},{12,4},{1,9},{5,13},{9,1},{13,5},{2,10},{6,14},... | collective-permute-start | bytes 184328 | tf_op jit(solution)/shard_map/ppermute | solution.py:189
  7.8 4.6 %collective-permute-start.2 = (bf16[240,128]{1,0:T(8,128)(2,1)S(1)}, bf16[240,128]{1,0:T(8,128)(2,1)S(1)}, u32[]{:S(2)}, u32[]{:S(2)}) collective-permute-start(bf16[240,128]{1,0:T(8,128)(2,1)S(1)} %get-tuple-element.21), channel_id=1, source_target_pairs={{0,12},{4,0},{8,4},{12,8},{1,13},{5,1},{9,5},{13,9},{2,14},{6,2},{... | collective-permute-start | bytes 184328 | tf_op jit(solution)/shard_map/ppermute | solution.py:189
  9.1 0.7 %copy-start.8 = (s32[1,16]{1,0:T(1,128)S(1)}, s32[1,16]{1,0:T(1,128)}, u32[]{:S(2)}) copy-start(s32[1,16]{1,0:T(1,128)} %sparse_ref.1) | copy-start | bytes 196
  9.1 0.7 %copy-start.5 = (f32[24]{0:T(128)S(1)}, f32[24]{0:T(128)}, u32[]{:S(2)}) copy-start(f32[24]{0:T(128)} %param.11) | copy-start | bytes 292
  9.1 0.7 %copy-start.6 = (f32[24]{0:T(128)S(1)}, f32[24]{0:T(128)}, u32[]{:S(2)}) copy-start(f32[24]{0:T(128)} %param.13) | copy-start | bytes 292
  9.1 0.7 %copy-start.7 = (f32[24]{0:T(128)S(1)}, f32[24]{0:T(128)}, u32[]{:S(2)}) copy-start(f32[24]{0:T(128)} %param.14) | copy-start | bytes 292
  9.8 0.9 %copy-start = (f32[128,512]{1,0:T(8,128)S(1)}, f32[128,512]{1,0:T(8,128)}, u32[]{:S(2)}) copy-start(f32[128,512]{1,0:T(8,128)} %rw_ref.1) | copy-start | bytes 786436
  13.1 1.9 %collective-permute-start.5 = (bf16[64,128]{1,0:T(8,128)(2,1)S(1)}, bf16[64,128]{1,0:T(8,128)(2,1)S(1)}, u32[]{:S(2)}, u32[]{:S(2)}) collective-permute-start(bf16[64,128]{1,0:T(8,128)(2,1)S(1)} %get-tuple-element.29.refs_0_), channel_id=1, source_target_pairs={{0,1},{1,0},{2,3},{3,2},{4,5},{5,4},{6,7},{7,6},{8,9},{9,8},{10,11... | collective-permute-start | bytes 49160 | tf_op jit(solution)/shard_map/ppermute | solution.py:199
  13.2 3.8 %collective-permute-start.4 = (bf16[64,128]{1,0:T(8,128)(2,1)S(1)}, bf16[64,128]{1,0:T(8,128)(2,1)S(1)}, u32[]{:S(2)}, u32[]{:S(2)}) collective-permute-start(bf16[64,128]{1,0:T(8,128)(2,1)S(1)} %get-tuple-element.29.refs_0_), channel_id=1, source_target_pairs={{0,2},{1,3},{2,0},{3,1},{4,6},{5,7},{6,4},{7,5},{8,10},{9,11},{10,... | collective-permute-start | bytes 49160 | tf_op jit(solution)/shard_map/ppermute | solution.py:199
  14.8 3.2 %collective-permute-start.3 = (bf16[64,128]{1,0:T(8,128)(2,1)S(1)}, bf16[64,128]{1,0:T(8,128)(2,1)S(1)}, u32[]{:S(2)}, u32[]{:S(2)}) collective-permute-start(bf16[64,128]{1,0:T(8,128)(2,1)S(1)} %get-tuple-element.29.refs_0_), channel_id=1, source_target_pairs={{0,3},{1,2},{2,1},{3,0},{4,7},{5,6},{6,5},{7,4},{8,11},{9,10},{10,... | collective-permute-start | bytes 49160 | tf_op jit(solution)/shard_map/ppermute | solution.py:199

commit v6 on v5

--- a/solution.py
+++ b/solution.py
@@ -20,7 +20,7 @@
         in_specs=in_specs,
         out_specs=jax.tree.map(lambda _: VMEM, outs),
         scratch_shapes=list(scratch),
-        compiler_params=pltpu.CompilerParams(vmem_limit_bytes=vmem << 20),
+        compiler_params=pltpu.CompilerParams(vmem_limit_bytes=int(vmem * 2**20)),
         cost_estimate=pl.CostEstimate(flops=flops, bytes_accessed=nbytes, transcendentals=0),
     )
 
@@ -39,9 +39,19 @@
 
 
 def pack_kernel(wide, low_ref, *refs):
-    windows, rows_ref = refs[:-1], refs[-1]
+    windows, (block_ref, rows_ref, sems) = refs[:wide], refs[wide:]
     _, channels, width, rows = low_ref.shape
-    rows_ref[...] = low_ref[0].astype(F32).reshape(channels * width, rows)
+    parts = sems.shape[0]
+    each = channels // parts
+    pieces = []
+    for i in range(parts):
+        piece = pl.ds(i * each, each)
+        pieces.append(pltpu.make_async_copy(low_ref.at[0, piece], block_ref.at[piece], sems.at[i]))
+        pieces[-1].start()
+    for i in range(parts):
+        pieces[i].wait()
+        values = block_ref[i * each : (i + 1) * each].astype(F32).reshape(each * width, rows)
+        rows_ref[i * each * width : (i + 1) * each * width, :] = values
     own = width // wide
     me = lax.axis_index("wide")
     for shift in range(wide):
@@ -234,9 +244,13 @@
     windows = call(
         functools.partial(pack_kernel, wide),
         [shape((size, lanes), BF16)] * wide,
-        [VMEM],
-        [pltpu.VMEM((channels * width, lanes), F32)],
-        vmem=big,
+        [pl.BlockSpec(memory_space=pltpu.HBM)],
+        [
+            pltpu.VMEM((channels, width, lanes), BF16),
+            pltpu.VMEM((channels * width, lanes), F32),
+            pltpu.SemaphoreType.DMA((4,)),
+        ],
+        vmem=53.6 if width <= 64 else 48,
     )(low_sino)
     views = [windows[0]] + [send(windows[s], "wide", s) for s in range(1, wide)]
 
@@ -263,8 +277,8 @@
         vmem=big,
     )(*views, a1, a2, b1, b2, head, select, target)
 
-    shifts = [(s, t) for s in range(1, narrow) for t in range(1, pair)]
-    shifts += [(s, 0) for s in range(1, narrow)] + [(0, t) for t in range(1, pair)]
+    shifts = [(0, t) for t in range(1, pair)] + [(s, 0) for s in range(1, narrow)]
+    shifts += [(s, t) for s in range(1, narrow) for t in range(1, pair)]
     blocks = [residual] + [send_both(residual, s, t) for s, t in shifts]
     shifts.insert(0, (0, 0))
     adjoint, predicted = call(

time: 18.9 us -> 18 us (0.952)
  local copies, waits for them, and re-layouts: 2.55 us -> 1.63 us
  waiting for transfers between devices: 3.62 us -> 2.71 us
  Pallas kernels: 2.9 us -> 3.8 us
    unnamed x18 -> x16, local copies, waits for them, and re-layouts: 2.55 us -> 1.63 us
    ppermute x3, waiting for transfers between devices: 2.87 us -> 1.96 us  [send_both(): return lax.ppermute(block, ('narrow', 'pair'), route)]
    pallas_call x1, Pallas kernels: 0.54 us -> 1.44 us  [local(): call(functools.partial(pack_kernel, wide), [shape((size, lanes), BF16)] *...]
  transfers between devices with their start and end apart: 6 -> 6, of which waited for: 4 -> 4; matrix products, arithmetic and copies ran while one was open for 0% -> 0% of each run, Pallas kernels for 4% -> 5%
where the time goes in v6:
time: 18 us; the launch traced here: 17.8 us
  starting transfers between devices  8.93 us (50%)
  Pallas kernels  3.8 us (21%)
  waiting for transfers between devices  2.71 us (15%)
  local copies, waits for them, and re-layouts  1.63 us (9%)
  between operations  0.73 us (4%)
    ppermute x3, starting transfers between devices, send(): lax.ppermute(block, axis, [(i, (i + distance) % count) for i in range(cou...  7.01 us
    ppermute x3, waiting for transfers between devices, send_both(): return lax.ppermute(block, ('narrow', 'pair'), route)  1.96 us
    ppermute x3, starting transfers between devices, send_both(): return lax.ppermute(block, ('narrow', 'pair'), route)  1.92 us
    unnamed x16, local copies, waits for them, and re-layouts  1.63 us
    pallas_call x1, Pallas kernels, local(): call(functools.partial(pack_kernel, wide), [shape((size, lanes), BF16)] *...  1.44 us
    pallas_call x1, Pallas kernels, local(): call(functools.partial(prepare_kernel, wide, own_out), [shape((2, 2 * siz...  0.82 us
    pallas_call x1, Pallas kernels, local(): call(functools.partial(adjoint_kernel, shifts, own_out), [shape((sparse_c...  0.79 us
    pallas_call x1, Pallas kernels, local(): call(functools.partial(net_kernel, wide, own_out), [shape((2 * wide, own_...  0.76 us
  transfers between devices with their start and end apart: 6, of which 4 were waited for; matrix products, arithmetic and copies ran while one was open for 0% of the time, Pallas kernels for 5%

profile of v6, /device:TPU:0, one launch (start us, length us, event | category | flops | bytes accessed | tf_op | source)
XLA Modules:
  0.0 17.8 jit_solution(3939105182191145024)
XLA Ops:
  0.6 0.0 copy-start.1
  0.6 0.0 copy-start.2
  0.7 0.0 copy-start.3
  0.7 1.4 %shard_map.104 = (bf16[240,128]{1,0:T(8,128)(2,1)S(1)}, bf16[240,128]{1,0:T(8,128)(2,1)S(1)}, bf16[240,128]{1,0:T(8,128)(2,1)S(1)}, bf16[240,128]{1,0:T(8,128)(2,1)S(1)}) custom-call(bf16[1,24,32,128]{3,2,1,0:T(8,128)(2,1)} %low_ref.1), custom_call_target="tpu_custom_call" | custom-call | flops 1000000 | bytes 245760 | tf_op jit(solution)/shard_map/pallas_call | solution.py:244
  2.1 3.1 %collective-permute-start = (bf16[240,128]{1,0:T(8,128)(2,1)S(1)}, bf16[240,128]{1,0:T(8,128)(2,1)S(1)}, u32[]{:S(2)}, u32[]{:S(2)}) collective-permute-start(bf16[240,128]{1,0:T(8,128)(2,1)S(1)} %get-tuple-element.19), channel_id=1, source_target_pairs={{0,4},{4,8},{8,12},{12,0},{1,5},{5,9},{9,13},{13,1},{2,6},{6,10},{... | collective-permute-start | bytes 184328 | tf_op jit(solution)/shard_map/ppermute | solution.py:199
  5.2 2.6 %collective-permute-start.1 = (bf16[240,128]{1,0:T(8,128)(2,1)S(1)}, bf16[240,128]{1,0:T(8,128)(2,1)S(1)}, u32[]{:S(2)}, u32[]{:S(2)}) collective-permute-start(bf16[240,128]{1,0:T(8,128)(2,1)S(1)} %get-tuple-element.20), channel_id=1, source_target_pairs={{0,8},{4,12},{8,0},{12,4},{1,9},{5,13},{9,1},{13,5},{2,10},{6,14},... | collective-permute-start | bytes 184328 | tf_op jit(solution)/shard_map/ppermute | solution.py:199
  7.8 1.3 %collective-permute-start.2 = (bf16[240,128]{1,0:T(8,128)(2,1)S(1)}, bf16[240,128]{1,0:T(8,128)(2,1)S(1)}, u32[]{:S(2)}, u32[]{:S(2)}) collective-permute-start(bf16[240,128]{1,0:T(8,128)(2,1)S(1)} %get-tuple-element.21), channel_id=1, source_target_pairs={{0,12},{4,0},{8,4},{12,8},{1,13},{5,1},{9,5},{13,9},{2,14},{6,2},{... | collective-permute-start | bytes 184328 | tf_op jit(solution)/shard_map/ppermute | solution.py:199
  9.1 0.0 copy-start.7
  9.1 0.0 copy-start.4
  9.1 0.0 copy-start.5
  9.1 0.0 copy-start.6
  9.1 0.0 copy-done.1
  9.1 0.0 copy-done.2
  9.2 0.0 copy-done.3
  9.2 0.6 %copy-done.7 = s32[1,16]{1,0:T(1,128)S(1)} copy-done((s32[1,16]{1,0:T(1,128)S(1)}, s32[1,16]{1,0:T(1,128)}, u32[]{:S(2)}) %copy-start.7) | copy-done | bytes 88
  9.8 0.0 copy-done.4
  9.8 0.0 copy-done.5
  9.8 0.0 copy-done.6
  9.8 0.0 copy-start
  9.8 0.9 %copy-done = f32[128,512]{1,0:T(8,128)S(1)} copy-done((f32[128,512]{1,0:T(8,128)S(1)}, f32[128,512]{1,0:T(8,128)}, u32[]{:S(2)}) %copy-start) | copy-done | bytes 262168
  10.8 0.8 %shard_map.105 = (bf16[2,480,240]{2,1,0:T(8,128)(2,1)S(1)}, bf16[96,240]{1,0:T(8,128)(2,1)S(1)}, f32[240,128]{1,0:T(8,128)S(1)}, f32[96,128]{1,0:T(8,128)S(1)}, ...) custom-call(bf16[4,24,24]{2,1,0:T(8,128)(2,1)S(1)} %copy-done.2, ...), custom_call_target="tpu_custom_call" | custom-call | flops 1000000 | bytes 1055744 | tf_op jit(solution)/shard_map/pallas_call | solution.py:257
  11.6 0.0 collective-permute-done.refs_1_
  11.6 0.4 %collective-permute-done.1.refs_2_ = bf16[240,128]{1,0:T(8,128)(2,1)S(1)} collective-permute-done((bf16[240,128]{1,0:T(8,128)(2,1)S(1)}, bf16[240,128]{1,0:T(8,128)(2,1)S(1)}, u32[]{:S(2)}, u32[]{:S(2)}) %collective-permute-start.1) | collective-permute-done | bytes 61472 | tf_op jit(solution)/shard_map/ppermute | solution.py:199
  12.0 0.3 %collective-permute-done.2.refs_3_ = bf16[240,128]{1,0:T(8,128)(2,1)S(1)} collective-permute-done((bf16[240,128]{1,0:T(8,128)(2,1)S(1)}, bf16[240,128]{1,0:T(8,128)(2,1)S(1)}, u32[]{:S(2)}, u32[]{:S(2)}) %collective-permute-start.2) | collective-permute-done | bytes 61472 | tf_op jit(solution)/shard_map/ppermute | solution.py:199
  12.4 0.8 %shard_map.106 = (f32[8,4,128]{2,1,0:T(4,128)S(1)}, bf16[64,128]{1,0:T(8,128)(2,1)S(1)}) custom-call(bf16[240,128]{1,0:T(8,128)(2,1)S(1)} %get-tuple-element.18.refs_0_, bf16[240,128]{1,0:T(8,128)(2,1)S(1)} %collective-permute-done.refs_1_, bf16[240,128]{1,0:T(8,128)(2,1)S(1)} %collective-permute-done.1.refs_2_, ...), custom_call_target="tpu_custom_call" | custom-call | flops 1000000 | bytes 32768 | tf_op jit(solution)/shard_map/pallas_call | solution.py:273
  13.1 0.1 collective-permute-start.5
  13.2 1.6 %collective-permute-start.4 = (bf16[64,128]{1,0:T(8,128)(2,1)S(1)}, bf16[64,128]{1,0:T(8,128)(2,1)S(1)}, u32[]{:S(2)}, u32[]{:S(2)}) collective-permute-start(bf16[64,128]{1,0:T(8,128)(2,1)S(1)} %get-tuple-element.29.refs_0_), channel_id=1, source_target_pairs={{0,2},{1,3},{2,0},{3,1},{4,6},{5,7},{6,4},{7,5},{8,10},{9,11},{10,... | collective-permute-start | bytes 49160 | tf_op jit(solution)/shard_map/ppermute | solution.py:209
  14.8 0.3 %collective-permute-start.3 = (bf16[64,128]{1,0:T(8,128)(2,1)S(1)}, bf16[64,128]{1,0:T(8,128)(2,1)S(1)}, u32[]{:S(2)}, u32[]{:S(2)}) collective-permute-start(bf16[64,128]{1,0:T(8,128)(2,1)S(1)} %get-tuple-element.29.refs_0_), channel_id=1, source_target_pairs={{0,1},{1,0},{2,3},{3,2},{4,5},{5,4},{6,7},{7,6},{8,9},{9,8},{10,11... | collective-permute-start | bytes 49160 | tf_op jit(solution)/shard_map/ppermute | solution.py:209
  15.0 1.4 %collective-permute-done.5.refs_3_ = bf16[64,128]{1,0:T(8,128)(2,1)S(1)} collective-permute-done((bf16[64,128]{1,0:T(8,128)(2,1)S(1)}, bf16[64,128]{1,0:T(8,128)(2,1)S(1)}, u32[]{:S(2)}, u32[]{:S(2)}) %collective-permute-start.5) | collective-permute-done | bytes 16416 | tf_op jit(solution)/shard_map/ppermute | solution.py:209
  16.5 0.5 %collective-permute-done.4.refs_2_ = bf16[64,128]{1,0:T(8,128)(2,1)S(1)} collective-permute-done((bf16[64,128]{1,0:T(8,128)(2,1)S(1)}, bf16[64,128]{1,0:T(8,128)(2,1)S(1)}, u32[]{:S(2)}, u32[]{:S(2)}) %collective-permute-start.4) | collective-permute-done | bytes 16416 | tf_op jit(solution)/shard_map/ppermute | solution.py:209
  17.0 0.0 collective-permute-done.3.refs_1_
  17.0 0.8 %shard_map.107 = (f32[16,4,128]{2,1,0:T(4,128)}, f32[8,4,128]{2,1,0:T(4,128)}) custom-call(bf16[64,128]{1,0:T(8,128)(2,1)S(1)} %get-tuple-element.29.refs_0_, bf16[64,128]{1,0:T(8,128)(2,1)S(1)} %collective-permute-done.3.refs_1_, bf16[64,128]{1,0:T(8,128)(2,1)S(1)} %collective-permute-done.4.refs_2_, bf16[64,128]{1,0:T(8,128)(2,1)S(1)} %collective-permute-done.5.refs_3_, ...), custom_call_target="tpu_custom_call" | custom-call | flops 1000000 | bytes 49152 | tf_op jit(solution)/shard_map/pallas_call | solution.py:284
Async XLA Ops:
  0.6 8.5 %copy-start.1 = (f32[16,4,128]{2,1,0:T(4,128)S(1)}, f32[16,4,128]{2,1,0:T(4,128)}, u32[]{:S(2)}) copy-start(f32[16,4,128]{2,1,0:T(4,128)} %measured_ref.1) | copy-start | bytes 98308
  0.6 8.5 %copy-start.2 = (bf16[4,24,24]{2,1,0:T(8,128)(2,1)S(1)}, bf16[4,24,24]{2,1,0:T(8,128)(2,1)}, u32[]{:S(2)}) copy-start(bf16[4,24,24]{2,1,0:T(8,128)(2,1)} %aw_ref.1) | copy-start | bytes 13828
  0.7 8.5 %copy-start.3 = (bf16[4,24,24]{2,1,0:T(8,128)(2,1)S(1)}, bf16[4,24,24]{2,1,0:T(8,128)(2,1)}, u32[]{:S(2)}) copy-start(bf16[4,24,24]{2,1,0:T(8,128)(2,1)} %cw_ref.1) | copy-start | bytes 13828
  2.1 9.5 %collective-permute-start = (bf16[240,128]{1,0:T(8,128)(2,1)S(1)}, bf16[240,128]{1,0:T(8,128)(2,1)S(1)}, u32[]{:S(2)}, u32[]{:S(2)}) collective-permute-start(bf16[240,128]{1,0:T(8,128)(2,1)S(1)} %get-tuple-element.19), channel_id=1, source_target_pairs={{0,4},{4,8},{8,12},{12,0},{1,5},{5,9},{9,13},{13,1},{2,6},{6,10},{... | collective-permute-start | bytes 184328 | tf_op jit(solution)/shard_map/ppermute | solution.py:199
  5.2 6.9 %collective-permute-start.1 = (bf16[240,128]{1,0:T(8,128)(2,1)S(1)}, bf16[240,128]{1,0:T(8,128)(2,1)S(1)}, u32[]{:S(2)}, u32[]{:S(2)}) collective-permute-start(bf16[240,128]{1,0:T(8,128)(2,1)S(1)} %get-tuple-element.20), channel_id=1, source_target_pairs={{0,8},{4,12},{8,0},{12,4},{1,9},{5,13},{9,1},{13,5},{2,10},{6,14},... | collective-permute-start | bytes 184328 | tf_op jit(solution)/shard_map/ppermute | solution.py:199
  7.8 4.6 %collective-permute-start.2 = (bf16[240,128]{1,0:T(8,128)(2,1)S(1)}, bf16[240,128]{1,0:T(8,128)(2,1)S(1)}, u32[]{:S(2)}, u32[]{:S(2)}) collective-permute-start(bf16[240,128]{1,0:T(8,128)(2,1)S(1)} %get-tuple-element.21), channel_id=1, source_target_pairs={{0,12},{4,0},{8,4},{12,8},{1,13},{5,1},{9,5},{13,9},{2,14},{6,2},{... | collective-permute-start | bytes 184328 | tf_op jit(solution)/shard_map/ppermute | solution.py:199
  9.1 0.7 %copy-start.7 = (s32[1,16]{1,0:T(1,128)S(1)}, s32[1,16]{1,0:T(1,128)}, u32[]{:S(2)}) copy-start(s32[1,16]{1,0:T(1,128)} %sparse_ref.1) | copy-start | bytes 196
  9.1 0.7 %copy-start.4 = (f32[24]{0:T(128)S(1)}, f32[24]{0:T(128)}, u32[]{:S(2)}) copy-start(f32[24]{0:T(128)} %param.11) | copy-start | bytes 292
  9.1 0.7 %copy-start.5 = (f32[24]{0:T(128)S(1)}, f32[24]{0:T(128)}, u32[]{:S(2)}) copy-start(f32[24]{0:T(128)} %param.13) | copy-start | bytes 292
  9.1 0.7 %copy-start.6 = (f32[24]{0:T(128)S(1)}, f32[24]{0:T(128)}, u32[]{:S(2)}) copy-start(f32[24]{0:T(128)} %param.14) | copy-start | bytes 292
  9.8 0.9 %copy-start = (f32[128,512]{1,0:T(8,128)S(1)}, f32[128,512]{1,0:T(8,128)}, u32[]{:S(2)}) copy-start(f32[128,512]{1,0:T(8,128)} %rw_ref.1) | copy-start | bytes 786436
  13.1 3.4 %collective-permute-start.5 = (bf16[64,128]{1,0:T(8,128)(2,1)S(1)}, bf16[64,128]{1,0:T(8,128)(2,1)S(1)}, u32[]{:S(2)}, u32[]{:S(2)}) collective-permute-start(bf16[64,128]{1,0:T(8,128)(2,1)S(1)} %get-tuple-element.29.refs_0_), channel_id=1, source_target_pairs={{0,3},{1,2},{2,1},{3,0},{4,7},{5,6},{6,5},{7,4},{8,11},{9,10},{10,... | collective-permute-start | bytes 49160 | tf_op jit(solution)/shard_map/ppermute | solution.py:209
  13.2 3.8 %collective-permute-start.4 = (bf16[64,128]{1,0:T(8,128)(2,1)S(1)}, bf16[64,128]{1,0:T(8,128)(2,1)S(1)}, u32[]{:S(2)}, u32[]{:S(2)}) collective-permute-start(bf16[64,128]{1,0:T(8,128)(2,1)S(1)} %get-tuple-element.29.refs_0_), channel_id=1, source_target_pairs={{0,2},{1,3},{2,0},{3,1},{4,6},{5,7},{6,4},{7,5},{8,10},{9,11},{10,... | collective-permute-start | bytes 49160 | tf_op jit(solution)/shard_map/ppermute | solution.py:209
  14.8 2.3 %collective-permute-start.3 = (bf16[64,128]{1,0:T(8,128)(2,1)S(1)}, bf16[64,128]{1,0:T(8,128)(2,1)S(1)}, u32[]{:S(2)}, u32[]{:S(2)}) collective-permute-start(bf16[64,128]{1,0:T(8,128)(2,1)S(1)} %get-tuple-element.29.refs_0_), channel_id=1, source_target_pairs={{0,1},{1,0},{2,3},{3,2},{4,5},{5,4},{6,7},{7,6},{8,9},{9,8},{10,11... | collective-permute-start | bytes 49160 | tf_op jit(solution)/shard_map/ppermute | solution.py:209

commit v7 on v6

--- a/solution.py
+++ b/solution.py
@@ -38,8 +38,26 @@
     return lax.broadcasted_iota(jnp.int32, shape, axis)
 
 
-def pack_kernel(wide, low_ref, *refs):
-    windows, (block_ref, rows_ref, sems) = refs[:wide], refs[wide:]
+def rounds(count):
+    if count == 4:
+        return [(2, 3, 1, 0), (3, 2, 0, 1), (1, 0, 3, 2)]
+    return [tuple((i + shift) % count for i in range(count)) for shift in range(1, count)]
+
+
+def entry(table, index):
+    value = jnp.int32(table[0])
+    for i in range(1, len(table)):
+        value = jnp.where(index == i, jnp.int32(table[i]), value)
+    return value
+
+
+def column_groups(channels, span):
+    most = max(1, 256 // (2 * channels) // 2 * 2)
+    return [(first, min(most, span - first)) for first in range(0, span, most)]
+
+
+def pack_kernel(routes, low_ref, *refs):
+    windows, (block_ref, rows_ref, sems) = refs[: len(routes) + 1], refs[len(routes) + 1 :]
     _, channels, width, rows = low_ref.shape
     parts = sems.shape[0]
     each = channels // parts
@@ -48,24 +66,25 @@
         piece = pl.ds(i * each, each)
         pieces.append(pltpu.make_async_copy(low_ref.at[0, piece], block_ref.at[piece], sems.at[i]))
         pieces[-1].start()
+    edge = jnp.zeros((8, rows), F32)
+    rows_ref[0:8, :] = edge
+    rows_ref[8 + channels * width : 16 + channels * width, :] = edge
     for i in range(parts):
         pieces[i].wait()
         values = block_ref[i * each : (i + 1) * each].astype(F32).reshape(each * width, rows)
-        rows_ref[i * each * width : (i + 1) * each * width, :] = values
-    own = width // wide
+        rows_ref[8 + i * each * width : 8 + (i + 1) * each * width, :] = values
+    own = width // (len(routes) + 1)
     me = lax.axis_index("wide")
-    for shift in range(wide):
-        first = lax.rem(me + shift, wide) * own - 1
-        columns = []
-        for i in range(own + 2):
-            column = jnp.clip(first + i, 0, width - 1)
-            columns.append(rows_ref[pl.ds(column, channels, stride=width), :])
-        windows[shift][...] = jnp.concatenate(columns, axis=0).astype(BF16)
+    for window, target in zip(windows, [me] + [entry(route, me) for route in routes]):
+        first = target * own + 7
+        columns = [rows_ref[pl.ds(first + i, channels, stride=width), :] for i in range(own + 2)]
+        window[...] = jnp.concatenate(columns, axis=0).astype(BF16)
 
 
 def prepare_kernel(
     wide,
     own_out,
+    groups,
     aw_ref,
     ab_ref,
     cw_ref,
@@ -74,15 +93,9 @@
     rw_ref,
     measured_ref,
     sparse_ref,
-    a1_ref,
-    a2_ref,
-    b1_ref,
-    b2_ref,
-    h_ref,
-    turned_ref,
-    select_ref,
-    target_ref,
+    *refs,
 ):
+    firsts, (a2_ref, b1_ref, b2_ref, h_ref, turned_ref, select_ref, target_ref) = refs[:-7], refs[-7:]
     channels = aw_ref.shape[1]
     span = 2 * own_out + 2
     size, outs = span * channels, own_out * channels
@@ -93,14 +106,23 @@
     pick_out = (out_channel == iota((outs, channels), 1)).astype(F32)
     pick_out16 = pick_out.astype(BF16)
 
-    def spread(left, weight):
+    def spread(left, weight, right):
         half = lax.dot_general(left, weight, (((1,), (1,)), ((), ())), preferred_element_type=F32)
-        return lax.dot_general(half.astype(BF16), pick16, (((1,), (1,)), ((), ())), preferred_element_type=F32)
-
-    same = split(iota((size, size), 0), channels)[0] == split(iota((size, size), 1), channels)[0]
-    for tap in range(4):
-        full = jnp.where(same, spread(pick16, aw_ref[tap]), 0.0).astype(BF16)
-        a1_ref[tap // 2, (tap % 2) * size : (tap % 2 + 1) * size, :] = full
+        return lax.dot_general(half.astype(BF16), right, (((1,), (1,)), ((), ())), preferred_element_type=F32)
+
+    for first_ref in firsts:
+        many = first_ref.shape[0] // 2
+        taken = many // channels
+        which, channel = split(iota((2 * many, channels), 0), channels)
+        is_channel = channel == iota((2 * many, channels), 1)
+        sides = [is_channel & (which >= side * taken) & (which < (side + 1) * taken) for side in range(2)]
+        sides = [side.astype(F32).astype(BF16) for side in sides]
+        row_column = split(iota((many, 2 * many), 0), channels)[0]
+        column_column = split(iota((many, 2 * many), 1), channels)[0]
+        same = (row_column == column_column) | (row_column + taken == column_column)
+        for e in range(2):
+            full = spread(pick16[:many], aw_ref[e], sides[0]) + spread(pick16[:many], aw_ref[e + 2], sides[1])
+            first_ref[e * many : (e + 1) * many, :] = jnp.where(same, full, 0.0).astype(BF16)
 
     in_column = split(iota((outs, size), 1), channels)[0]
     out_column = split(iota((outs, size), 0), own_out)[1]
@@ -110,11 +132,12 @@
     total = jnp.zeros((outs, size), F32)
     for tap in range(TAPS):
         here = (in_column == 2 * out_column + tap) & inside
-        total = jnp.where(here, spread(pick_out16, cw_ref[tap]), total)
+        total = jnp.where(here, spread(pick_out16, cw_ref[tap], pick16), total)
     a2_ref[...] = total.astype(BF16)
 
     def along(left, vector_ref, out_ref):
-        out_ref[...] = jnp.broadcast_to(jnp.sum(left * vector_ref[...].astype(F32), axis=1, keepdims=True), out_ref.shape)
+        summed = jnp.sum(left * vector_ref[...].astype(F32), axis=1, keepdims=True)
+        out_ref[...] = jnp.broadcast_to(summed, out_ref.shape)
 
     along(pick, ab_ref, b1_ref)
     along(pick_out, cb_ref, b2_ref)
@@ -133,28 +156,37 @@
         target_ref[k * own_out : (k + 1) * own_out, :] = measured_ref[k]
 
 
-def net_kernel(wide, own_out, *refs):
-    views, refs = [ref[...] for ref in refs[:wide]], refs[wide:]
-    a1_ref, a2_ref, b1_ref, b2_ref, h_ref, select_ref, target_ref, predicted_ref, residual_ref = refs
-    size, lanes = views[0].shape
+def net_kernel(routes, own_out, groups, *refs):
+    wide = len(routes) + 1
+    windows, firsts, refs = refs[:wide], refs[wide : wide + len(groups)], refs[wide + len(groups) :]
+    a2_ref, b1_ref, b2_ref, h_ref, select_ref, target_ref, predicted_ref, residual_ref, views_ref = refs
+    size, lanes = windows[0].shape
     outs = a2_ref.shape[0]
+    channels = outs // own_out
     me = lax.axis_index("wide")
-    group = 2 if wide % 2 == 0 else 1
+    sources = [me] + [entry(tuple(route.index(i) for i in range(wide)), me) for route in routes]
+    for window, source in zip(windows, sources):
+        views_ref[:, pl.ds(pl.multiple_of((source + 1) * lanes, lanes), lanes)] = window[...]
+    views_ref[:, :lanes] = views_ref[:, wide * lanes :]
+
+    many = 2 if wide % 2 == 0 else 1
     wider = lambda ref, times: jnp.concatenate([ref[...]] * times, axis=1)
-    b1 = wider(b1_ref, group)
-    b2, h = wider(b2_ref, 2 * group), wider(h_ref, 2 * group)
+    b1 = wider(b1_ref, many)
+    b2, h = wider(b2_ref, 2 * many), wider(h_ref, 2 * many)
     select = select_ref[...]
     picked = jnp.zeros(select.shape, F32)
-    for start in range(0, wide, group):
-        current = jnp.concatenate([views[start + i] for i in range(group)], axis=1)
-        previous = jnp.concatenate([views[(start + i + 1) % wide] for i in range(group)], axis=1)
-        upsampled = []
-        for e in range(2):
-            rows = pl.ds(e * size, size)
-            summed = jnp.dot(a1_ref[0, rows, :], current, preferred_element_type=F32)
-            summed += jnp.dot(a1_ref[1, rows, :], previous, preferred_element_type=F32)
-            upsampled.append(leaky_relu(summed + b1).astype(BF16))
-        both = jnp.concatenate(upsampled, axis=1)
+    for view in range(0, wide, many):
+        previous = slice(view * lanes, (view + many) * lanes)
+        current = slice((view + 1) * lanes, (view + 1 + many) * lanes)
+        pieces = ([], [])
+        for (first, taken), first_ref in zip(groups, firsts):
+            rows = slice(first * channels, (first + taken) * channels)
+            half = taken * channels
+            stacked = jnp.concatenate([views_ref[rows, current], views_ref[rows, previous]], axis=0)
+            summed = jnp.dot(first_ref[...], stacked, preferred_element_type=F32)
+            for e in range(2):
+                pieces[e].append(leaky_relu(summed[e * half : (e + 1) * half] + b1[rows]).astype(BF16))
+        both = jnp.concatenate([jnp.concatenate(piece, axis=0) for piece in pieces], axis=1)
         hidden = leaky_relu(jnp.dot(a2_ref[...], both, preferred_element_type=F32) + b2) * h
         value = jnp.sum(hidden.reshape(outs // 8, 8, hidden.shape[1]), axis=0)
         apart = own_out
@@ -162,13 +194,13 @@
             value += pltpu.roll(value, apart, 0)
             apart *= 2
         for e in range(2):
-            for i in range(group):
-                view = 2 * lax.rem(me - (start + i) + wide, wide) + e
-                at = (e * group + i) * lanes
+            for i in range(many):
+                out_view = 2 * (view + i) + e
+                at = (e * many + i) * lanes
                 tile = value[:, at : at + lanes]
-                predicted_ref[view] = tile[:own_out]
+                predicted_ref[out_view] = tile[:own_out]
                 repeated = jnp.concatenate([tile] * (select.shape[0] // 8), axis=0)
-                picked = jnp.where(select == view.astype(F32), repeated, picked)
+                picked = jnp.where(select == out_view, repeated, picked)
     residual_ref[...] = (picked - target_ref[...]).astype(BF16)
 
 
@@ -192,11 +224,6 @@
 def came_from(axis, distance):
     count = lax.axis_size(axis)
     return lax.rem(lax.axis_index(axis) - distance + count, count)
-
-
-def send(block, axis, distance):
-    count = lax.axis_size(axis)
-    return lax.ppermute(block, axis, [(i, (i + distance) % count) for i in range(count)])
 
 
 def send_both(block, narrow_distance, pair_distance):
@@ -241,23 +268,28 @@
         measured,
         sparse_views,
     )
+    routes = rounds(wide)
+    groups = column_groups(channels, span)
     windows = call(
-        functools.partial(pack_kernel, wide),
+        functools.partial(pack_kernel, routes),
         [shape((size, lanes), BF16)] * wide,
         [pl.BlockSpec(memory_space=pltpu.HBM)],
         [
             pltpu.VMEM((channels, width, lanes), BF16),
-            pltpu.VMEM((channels * width, lanes), F32),
+            pltpu.VMEM((16 + channels * width, lanes), F32),
             pltpu.SemaphoreType.DMA((4,)),
         ],
         vmem=53.6 if width <= 64 else 48,
     )(low_sino)
-    views = [windows[0]] + [send(windows[s], "wide", s) for s in range(1, wide)]
-
-    a1, a2, b1, b2, head, turned, select, target = call(
-        functools.partial(prepare_kernel, wide, own_out),
-        [
-            shape((2, 2 * size, size), BF16),
+    windows = [windows[0]] + [
+        lax.ppermute(window, "wide", list(enumerate(route))) for window, route in zip(windows[1:], routes)
+    ]
+
+    widths = sorted({taken for _, taken in groups})
+    *firsts, a2, b1, b2, head, turned, select, target = call(
+        functools.partial(prepare_kernel, wide, own_out, groups),
+        [shape((2 * taken * channels, 2 * taken * channels), BF16) for taken in widths]
+        + [
             shape((outs, size), BF16),
             shape((size, lanes), F32),
             shape((outs, lanes), F32),
@@ -269,13 +301,15 @@
         [VMEM] * 8,
         vmem=big,
     )(*small)
+    firsts = [firsts[widths.index(taken)] for _, taken in groups]
 
     predicted, residual = call(
-        functools.partial(net_kernel, wide, own_out),
+        functools.partial(net_kernel, routes, own_out, groups),
         [shape((2 * wide, own_out, lanes), F32), shape(flat, BF16)],
-        [VMEM] * (wide + 7),
+        [VMEM] * (wide + len(groups) + 6),
+        [pltpu.VMEM((size, (wide + 1) * lanes), BF16)],
         vmem=big,
-    )(*views, a1, a2, b1, b2, head, select, target)
+    )(*windows, *firsts, a2, b1, b2, head, select, target)
 
     shifts = [(0, t) for t in range(1, pair)] + [(s, 0) for s in range(1, narrow)]
     shifts += [(s, t) for s in range(1, narrow) for t in range(1, pair)]

time: 18 us -> 17.9 us (level)
  waiting for transfers between devices: 2.71 us -> 4.15 us
  starting transfers between devices: 8.93 us -> 7.59 us
  Pallas kernels: 3.8 us -> 3.56 us
    ppermute x3, waiting for transfers between devices: 0.75 us -> 2.19 us  [local(): lax.ppermute(window, 'wide', list(enumerate(route)))]
    ppermute x3, starting transfers between devices: 7.01 us -> 5.67 us  [local(): lax.ppermute(window, 'wide', list(enumerate(route)))]
    pallas_call x3, Pallas kernels: 3.01 us -> 2.77 us  [the longest x1 1.2 us: local(): call(functools.partial(pack_kernel, routes), [shape((size, lanes), BF16)]...]
  transfers between devices with their start and end apart: 6 -> 6, of which waited for: 4 -> 3; matrix products, arithmetic and copies ran while one was open for 0% -> 0% of each run, Pallas kernels for 5% -> 5%
where the time goes in v7:
time: 17.9 us; the launch traced here: 17.7 us
  starting transfers between devices  7.59 us (42%)
  waiting for transfers between devices  4.15 us (23%)
  Pallas kernels  3.56 us (20%)
  local copies, waits for them, and re-layouts  1.63 us (9%)
  between operations  0.73 us (4%)
    ppermute x3, starting transfers between devices, local(): lax.ppermute(window, 'wide', list(enumerate(route)))  5.67 us
    ppermute x3, waiting for transfers between devices, local(): lax.ppermute(window, 'wide', list(enumerate(route)))  2.19 us
    ppermute x3, waiting for transfers between devices, send_both(): return lax.ppermute(block, ('narrow', 'pair'), route)  1.96 us
    ppermute x3, starting transfers between devices, send_both(): return lax.ppermute(block, ('narrow', 'pair'), route)  1.92 us
    unnamed x16, local copies, waits for them, and re-layouts  1.63 us
    pallas_call x1, Pallas kernels, local(): call(functools.partial(pack_kernel, routes), [shape((size, lanes), BF16)]...  1.2 us
    pallas_call x1, Pallas kernels, local(): call(functools.partial(prepare_kernel, wide, own_out, groups), [shape((2...  0.87 us
    pallas_call x1, Pallas kernels, local(): call(functools.partial(adjoint_kernel, shifts, own_out), [shape((sparse_c...  0.79 us
  transfers between devices with their start and end apart: 6, of which 3 were waited for; matrix products, arithmetic and copies ran while one was open for 0% of the time, Pallas kernels for 5%

profile of v7, /device:TPU:0, one launch (start us, length us, event | category | flops | bytes accessed | tf_op | source)
XLA Modules:
  0.0 17.7 jit_solution(15382390745613961285)
XLA Ops:
  0.6 0.0 copy-start.1
  0.6 0.0 copy-start.2
  0.7 0.0 copy-start.3
  0.7 1.2 %shard_map.104 = (bf16[240,128]{1,0:T(8,128)(2,1)S(1)}, bf16[240,128]{1,0:T(8,128)(2,1)S(1)}, bf16[240,128]{1,0:T(8,128)(2,1)S(1)}, bf16[240,128]{1,0:T(8,128)(2,1)S(1)}) custom-call(bf16[1,24,32,128]{3,2,1,0:T(8,128)(2,1)} %low_ref.1), custom_call_target="tpu_custom_call" | custom-call | flops 1000000 | bytes 245760 | tf_op jit(solution)/shard_map/pallas_call | solution.py:273
  1.9 4.1 %collective-permute-start = (bf16[240,128]{1,0:T(8,128)(2,1)S(1)}, bf16[240,128]{1,0:T(8,128)(2,1)S(1)}, u32[]{:S(2)}, u32[]{:S(2)}) collective-permute-start(bf16[240,128]{1,0:T(8,128)(2,1)S(1)} %get-tuple-element.20), channel_id=1, source_target_pairs={{0,8},{4,12},{8,4},{12,0},{1,9},{5,13},{9,5},{13,1},{2,10},{6,14},... | collective-permute-start | bytes 184328 | tf_op jit(solution)/shard_map/ppermute | solution.py:285
  6.0 1.1 %collective-permute-start.1 = (bf16[240,128]{1,0:T(8,128)(2,1)S(1)}, bf16[240,128]{1,0:T(8,128)(2,1)S(1)}, u32[]{:S(2)}, u32[]{:S(2)}) collective-permute-start(bf16[240,128]{1,0:T(8,128)(2,1)S(1)} %get-tuple-element.21), channel_id=1, source_target_pairs={{0,12},{4,8},{8,0},{12,4},{1,13},{5,9},{9,1},{13,5},{2,14},{6,10},... | collective-permute-start | bytes 184328 | tf_op jit(solution)/shard_map/ppermute | solution.py:285
  7.0 0.5 %collective-permute-start.2 = (bf16[240,128]{1,0:T(8,128)(2,1)S(1)}, bf16[240,128]{1,0:T(8,128)(2,1)S(1)}, u32[]{:S(2)}, u32[]{:S(2)}) collective-permute-start(bf16[240,128]{1,0:T(8,128)(2,1)S(1)} %get-tuple-element.22), channel_id=1, source_target_pairs={{0,4},{4,0},{8,12},{12,8},{1,5},{5,1},{9,13},{13,9},{2,6},{6,2},{1... | collective-permute-start | bytes 184328 | tf_op jit(solution)/shard_map/ppermute | solution.py:285
  7.5 0.0 copy-start.7
  7.5 0.0 copy-start.4
  7.5 0.0 copy-start.5
  7.5 0.0 copy-start.6
  7.5 0.0 copy-done.1
  7.6 0.0 copy-done.2
  7.6 0.0 copy-done.3
  7.6 0.6 %copy-done.7 = s32[1,16]{1,0:T(1,128)S(1)} copy-done((s32[1,16]{1,0:T(1,128)S(1)}, s32[1,16]{1,0:T(1,128)}, u32[]{:S(2)}) %copy-start.7) | copy-done | bytes 88
  8.2 0.0 copy-done.4
  8.2 0.0 copy-done.5
  8.2 0.0 copy-done.6
  8.2 0.0 copy-start
  8.2 0.9 %copy-done = f32[128,512]{1,0:T(8,128)S(1)} copy-done((f32[128,512]{1,0:T(8,128)S(1)}, f32[128,512]{1,0:T(8,128)}, u32[]{:S(2)}) %copy-start) | copy-done | bytes 262168
  9.2 0.9 %shard_map.105 = (bf16[96,96]{1,0:T(8,128)(2,1)S(1)}, bf16[192,192]{1,0:T(8,128)(2,1)S(1)}, bf16[96,240]{1,0:T(8,128)(2,1)S(1)}, f32[240,128]{1,0:T(8,128)S(1)},...) custom-call(bf16[4,24,24]{2,1,0:T(8,128)(2,1)S(1)} %copy-done.2, ...), custom_call_target="tpu_custom_call" | custom-call | flops 1000000 | bytes 687104 | tf_op jit(solution)/shard_map/pallas_call | solution.py:289
  10.1 0.0 collective-permute-done.refs_1_
  10.1 2.2 %collective-permute-done.1.refs_2_ = bf16[240,128]{1,0:T(8,128)(2,1)S(1)} collective-permute-done((bf16[240,128]{1,0:T(8,128)(2,1)S(1)}, bf16[240,128]{1,0:T(8,128)(2,1)S(1)}, u32[]{:S(2)}, u32[]{:S(2)}) %collective-permute-start.1) | collective-permute-done | bytes 61472 | tf_op jit(solution)/shard_map/ppermute | solution.py:285
  12.3 0.0 collective-permute-done.2.refs_3_
  12.3 0.7 %shard_map.106 = (f32[8,4,128]{2,1,0:T(4,128)S(1)}, bf16[64,128]{1,0:T(8,128)(2,1)S(1)}) custom-call(bf16[240,128]{1,0:T(8,128)(2,1)S(1)} %get-tuple-element.19.refs_0_, bf16[240,128]{1,0:T(8,128)(2,1)S(1)} %collective-permute-done.refs_1_, bf16[240,128]{1,0:T(8,128)(2,1)S(1)} %collective-permute-done.1.refs_2_, ...), custom_call_target="tpu_custom_call" | custom-call | flops 1000000 | bytes 32768 | tf_op jit(solution)/shard_map/pallas_call | solution.py:306
  13.0 0.1 collective-permute-start.5
  13.1 1.6 %collective-permute-start.4 = (bf16[64,128]{1,0:T(8,128)(2,1)S(1)}, bf16[64,128]{1,0:T(8,128)(2,1)S(1)}, u32[]{:S(2)}, u32[]{:S(2)}) collective-permute-start(bf16[64,128]{1,0:T(8,128)(2,1)S(1)} %get-tuple-element.31.refs_0_), channel_id=1, source_target_pairs={{0,2},{1,3},{2,0},{3,1},{4,6},{5,7},{6,4},{7,5},{8,10},{9,11},{10,... | collective-permute-start | bytes 49160 | tf_op jit(solution)/shard_map/ppermute | solution.py:236
  14.6 0.3 %collective-permute-start.3 = (bf16[64,128]{1,0:T(8,128)(2,1)S(1)}, bf16[64,128]{1,0:T(8,128)(2,1)S(1)}, u32[]{:S(2)}, u32[]{:S(2)}) collective-permute-start(bf16[64,128]{1,0:T(8,128)(2,1)S(1)} %get-tuple-element.31.refs_0_), channel_id=1, source_target_pairs={{0,1},{1,0},{2,3},{3,2},{4,5},{5,4},{6,7},{7,6},{8,9},{9,8},{10,11... | collective-permute-start | bytes 49160 | tf_op jit(solution)/shard_map/ppermute | solution.py:236
  14.9 1.4 %collective-permute-done.5.refs_3_ = bf16[64,128]{1,0:T(8,128)(2,1)S(1)} collective-permute-done((bf16[64,128]{1,0:T(8,128)(2,1)S(1)}, bf16[64,128]{1,0:T(8,128)(2,1)S(1)}, u32[]{:S(2)}, u32[]{:S(2)}) %collective-permute-start.5) | collective-permute-done | bytes 16416 | tf_op jit(solution)/shard_map/ppermute | solution.py:236
  16.3 0.5 %collective-permute-done.4.refs_2_ = bf16[64,128]{1,0:T(8,128)(2,1)S(1)} collective-permute-done((bf16[64,128]{1,0:T(8,128)(2,1)S(1)}, bf16[64,128]{1,0:T(8,128)(2,1)S(1)}, u32[]{:S(2)}, u32[]{:S(2)}) %collective-permute-start.4) | collective-permute-done | bytes 16416 | tf_op jit(solution)/shard_map/ppermute | solution.py:236
  16.9 0.0 collective-permute-done.3.refs_1_
  16.9 0.8 %shard_map.107 = (f32[16,4,128]{2,1,0:T(4,128)}, f32[8,4,128]{2,1,0:T(4,128)}) custom-call(bf16[64,128]{1,0:T(8,128)(2,1)S(1)} %get-tuple-element.31.refs_0_, bf16[64,128]{1,0:T(8,128)(2,1)S(1)} %collective-permute-done.3.refs_1_, bf16[64,128]{1,0:T(8,128)(2,1)S(1)} %collective-permute-done.4.refs_2_, bf16[64,128]{1,0:T(8,128)(2,1)S(1)} %collective-permute-done.5.refs_3_, ...), custom_call_target="tpu_custom_call" | custom-call | flops 1000000 | bytes 49152 | tf_op jit(solution)/shard_map/pallas_call | solution.py:318
Async XLA Ops:
  0.6 6.9 %copy-start.1 = (f32[16,4,128]{2,1,0:T(4,128)S(1)}, f32[16,4,128]{2,1,0:T(4,128)}, u32[]{:S(2)}) copy-start(f32[16,4,128]{2,1,0:T(4,128)} %measured_ref.1) | copy-start | bytes 98308
  0.6 6.9 %copy-start.2 = (bf16[4,24,24]{2,1,0:T(8,128)(2,1)S(1)}, bf16[4,24,24]{2,1,0:T(8,128)(2,1)}, u32[]{:S(2)}) copy-start(bf16[4,24,24]{2,1,0:T(8,128)(2,1)} %aw_ref.1) | copy-start | bytes 13828
  0.7 6.9 %copy-start.3 = (bf16[4,24,24]{2,1,0:T(8,128)(2,1)S(1)}, bf16[4,24,24]{2,1,0:T(8,128)(2,1)}, u32[]{:S(2)}) copy-start(bf16[4,24,24]{2,1,0:T(8,128)(2,1)} %cw_ref.1) | copy-start | bytes 13828
  1.9 8.2 %collective-permute-start = (bf16[240,128]{1,0:T(8,128)(2,1)S(1)}, bf16[240,128]{1,0:T(8,128)(2,1)S(1)}, u32[]{:S(2)}, u32[]{:S(2)}) collective-permute-start(bf16[240,128]{1,0:T(8,128)(2,1)S(1)} %get-tuple-element.20), channel_id=1, source_target_pairs={{0,8},{4,12},{8,4},{12,0},{1,9},{5,13},{9,5},{13,1},{2,10},{6,14},... | collective-permute-start | bytes 184328 | tf_op jit(solution)/shard_map/ppermute | solution.py:285
  6.0 6.3 %collective-permute-start.1 = (bf16[240,128]{1,0:T(8,128)(2,1)S(1)}, bf16[240,128]{1,0:T(8,128)(2,1)S(1)}, u32[]{:S(2)}, u32[]{:S(2)}) collective-permute-start(bf16[240,128]{1,0:T(8,128)(2,1)S(1)} %get-tuple-element.21), channel_id=1, source_target_pairs={{0,12},{4,8},{8,0},{12,4},{1,13},{5,9},{9,1},{13,5},{2,14},{6,10},... | collective-permute-start | bytes 184328 | tf_op jit(solution)/shard_map/ppermute | solution.py:285
  7.0 5.2 %collective-permute-start.2 = (bf16[240,128]{1,0:T(8,128)(2,1)S(1)}, bf16[240,128]{1,0:T(8,128)(2,1)S(1)}, u32[]{:S(2)}, u32[]{:S(2)}) collective-permute-start(bf16[240,128]{1,0:T(8,128)(2,1)S(1)} %get-tuple-element.22), channel_id=1, source_target_pairs={{0,4},{4,0},{8,12},{12,8},{1,5},{5,1},{9,13},{13,9},{2,6},{6,2},{1... | collective-permute-start | bytes 184328 | tf_op jit(solution)/shard_map/ppermute | solution.py:285
  7.5 0.7 %copy-start.7 = (s32[1,16]{1,0:T(1,128)S(1)}, s32[1,16]{1,0:T(1,128)}, u32[]{:S(2)}) copy-start(s32[1,16]{1,0:T(1,128)} %sparse_ref.1) | copy-start | bytes 196
  7.5 0.7 %copy-start.4 = (f32[24]{0:T(128)S(1)}, f32[24]{0:T(128)}, u32[]{:S(2)}) copy-start(f32[24]{0:T(128)} %param.11) | copy-start | bytes 292
  7.5 0.7 %copy-start.5 = (f32[24]{0:T(128)S(1)}, f32[24]{0:T(128)}, u32[]{:S(2)}) copy-start(f32[24]{0:T(128)} %param.13) | copy-start | bytes 292
  7.5 0.7 %copy-start.6 = (f32[24]{0:T(128)S(1)}, f32[24]{0:T(128)}, u32[]{:S(2)}) copy-start(f32[24]{0:T(128)} %param.14) | copy-start | bytes 292
  8.2 0.9 %copy-start = (f32[128,512]{1,0:T(8,128)S(1)}, f32[128,512]{1,0:T(8,128)}, u32[]{:S(2)}) copy-start(f32[128,512]{1,0:T(8,128)} %rw_ref.1) | copy-start | bytes 786436
  13.0 3.4 %collective-permute-start.5 = (bf16[64,128]{1,0:T(8,128)(2,1)S(1)}, bf16[64,128]{1,0:T(8,128)(2,1)S(1)}, u32[]{:S(2)}, u32[]{:S(2)}) collective-permute-start(bf16[64,128]{1,0:T(8,128)(2,1)S(1)} %get-tuple-element.31.refs_0_), channel_id=1, source_target_pairs={{0,3},{1,2},{2,1},{3,0},{4,7},{5,6},{6,5},{7,4},{8,11},{9,10},{10,... | collective-permute-start | bytes 49160 | tf_op jit(solution)/shard_map/ppermute | solution.py:236
  13.1 3.8 %collective-permute-start.4 = (bf16[64,128]{1,0:T(8,128)(2,1)S(1)}, bf16[64,128]{1,0:T(8,128)(2,1)S(1)}, u32[]{:S(2)}, u32[]{:S(2)}) collective-permute-start(bf16[64,128]{1,0:T(8,128)(2,1)S(1)} %get-tuple-element.31.refs_0_), channel_id=1, source_target_pairs={{0,2},{1,3},{2,0},{3,1},{4,6},{5,7},{6,4},{7,5},{8,10},{9,11},{10,... | collective-permute-start | bytes 49160 | tf_op jit(solution)/shard_map/ppermute | solution.py:236
  14.6 2.3 %collective-permute-start.3 = (bf16[64,128]{1,0:T(8,128)(2,1)S(1)}, bf16[64,128]{1,0:T(8,128)(2,1)S(1)}, u32[]{:S(2)}, u32[]{:S(2)}) collective-permute-start(bf16[64,128]{1,0:T(8,128)(2,1)S(1)} %get-tuple-element.31.refs_0_), channel_id=1, source_target_pairs={{0,1},{1,0},{2,3},{3,2},{4,5},{5,4},{6,7},{7,6},{8,9},{9,8},{10,11... | collective-permute-start | bytes 49160 | tf_op jit(solution)/shard_map/ppermute | solution.py:236

commit v8 on v7

--- a/solution.py
+++ b/solution.py
@@ -39,8 +39,6 @@
 
 
 def rounds(count):
-    if count == 4:
-        return [(2, 3, 1, 0), (3, 2, 0, 1), (1, 0, 3, 2)]
     return [tuple((i + shift) % count for i in range(count)) for shift in range(1, count)]
 
 
@@ -204,10 +202,7 @@
     residual_ref[...] = (picked - target_ref[...]).astype(BF16)
 
 
-def adjoint_kernel(shifts, own_out, *refs):
-    residuals, refs = refs[: len(shifts)], refs[len(shifts) :]
-    turned_ref, predicted_ref, out_ref, copied_ref = refs
-    copied_ref[...] = predicted_ref[...]
+def adjoint_sum(residuals, shifts, turned_ref):
     lanes = residuals[0].shape[1]
     weights = []
     for narrow_shift, pair_shift in shifts:
@@ -216,7 +211,18 @@
         weights.append(turned_ref[pl.ds(pl.multiple_of(block * lanes, lanes), lanes), :])
     values = jnp.concatenate([ref[...] for ref in residuals], axis=1)
     both = jnp.dot(values, jnp.concatenate(weights, axis=0), preferred_element_type=F32)
-    total = both[:, :lanes] + both[:, lanes:]
+    return both[:, :lanes] + both[:, lanes:]
+
+
+def near_kernel(shifts, *refs):
+    residuals, (turned_ref, predicted_ref, partial_ref, copied_ref) = refs[: len(shifts)], refs[len(shifts) :]
+    copied_ref[...] = predicted_ref[...]
+    partial_ref[...] = adjoint_sum(residuals, shifts, turned_ref)
+
+
+def far_kernel(shifts, own_out, *refs):
+    residuals, (turned_ref, partial_ref, out_ref) = refs[: len(shifts)], refs[len(shifts) :]
+    total = partial_ref[...] + adjoint_sum(residuals, shifts, turned_ref)
     for k in range(out_ref.shape[0]):
         out_ref[k] = total[k * own_out : (k + 1) * own_out]
 
@@ -311,16 +317,22 @@
         vmem=big,
     )(*windows, *firsts, a2, b1, b2, head, select, target)
 
-    shifts = [(0, t) for t in range(1, pair)] + [(s, 0) for s in range(1, narrow)]
-    shifts += [(s, t) for s in range(1, narrow) for t in range(1, pair)]
-    blocks = [residual] + [send_both(residual, s, t) for s, t in shifts]
-    shifts.insert(0, (0, 0))
-    adjoint, predicted = call(
-        functools.partial(adjoint_kernel, shifts, own_out),
-        [shape((sparse_count, own_out, lanes), F32), shape(predicted.shape, F32)],
-        [VMEM] * (len(blocks) + 2),
+    near_shifts = [(s, t) for s in range(1, narrow) for t in range(1, pair)]
+    far_shifts = [(0, t) for t in range(1, pair)] + [(s, 0) for s in range(1, narrow)]
+    near = [residual] + [send_both(residual, s, t) for s, t in near_shifts]
+    far = [send_both(residual, s, t) for s, t in far_shifts]
+    partial, predicted = call(
+        functools.partial(near_kernel, [(0, 0)] + near_shifts),
+        [shape(flat, F32), shape(predicted.shape, F32)],
+        [VMEM] * (len(near) + 2),
         vmem=big,
-    )(*blocks, turned, predicted)
+    )(*near, turned, predicted)
+    adjoint = call(
+        functools.partial(far_kernel, far_shifts, own_out),
+        shape((sparse_count, own_out, lanes), F32),
+        [VMEM] * (len(far) + 2),
+        vmem=big,
+    )(*far, turned, partial)
     return (predicted, adjoint)
 
 

time: 17.9 us -> 17.8 us (level)
  waiting for transfers between devices: 4.15 us -> 2.13 us
  starting transfers between devices: 7.59 us -> 8.93 us
  Pallas kernels: 3.56 us -> 4.16 us
    ppermute x3, waiting for transfers between devices: 2.19 us -> 0.69 us  [local(): lax.ppermute(window, 'wide', list(enumerate(route)))]
    ppermute x3, starting transfers between devices: 5.67 us -> 7.01 us  [local(): lax.ppermute(window, 'wide', list(enumerate(route)))]
    pallas_call x1 -> x2, Pallas kernels: 0.79 us -> 1.39 us  [the longest x1 0.78 us: local(): call(functools.partial(far_kernel, far_shifts, own_out), shape((sparse_co...]
    ppermute x3, waiting for transfers between devices: 1.96 us -> 1.44 us  [send_both(): return lax.ppermute(block, ('narrow', 'pair'), route)]
  transfers between devices with their start and end apart: 6 -> 6, of which waited for: 3 -> 3; matrix products, arithmetic and copies ran while one was open for 0% -> 0% of each run, Pallas kernels for 5% -> 8%
where the time goes in v8:
time: 17.8 us; the launch traced here: 17.6 us
  starting transfers between devices  8.93 us (50%)
  Pallas kernels  4.16 us (23%)
  waiting for transfers between devices  2.13 us (12%)
  local copies, waits for them, and re-layouts  1.63 us (9%)
  between operations  0.73 us (4%)
    ppermute x3, starting transfers between devices, local(): lax.ppermute(window, 'wide', list(enumerate(route)))  7.01 us
    ppermute x3, starting transfers between devices, send_both(): return lax.ppermute(block, ('narrow', 'pair'), route)  1.92 us
    unnamed x16, local copies, waits for them, and re-layouts  1.63 us
    ppermute x3, waiting for transfers between devices, send_both(): return lax.ppermute(block, ('narrow', 'pair'), route)  1.44 us
    pallas_call x1, Pallas kernels, local(): call(functools.partial(pack_kernel, routes), [shape((size, lanes), BF16)]...  1.2 us
    pallas_call x1, Pallas kernels, local(): call(functools.partial(prepare_kernel, wide, own_out, groups), [shape((2...  0.87 us
    pallas_call x1, Pallas kernels, local(): call(functools.partial(far_kernel, far_shifts, own_out), shape((sparse_co...  0.78 us
    pallas_call x1, Pallas kernels, local(): call(functools.partial(net_kernel, routes, own_out, groups), [shape((2 *...  0.7 us
  transfers between devices with their start and end apart: 6, of which 3 were waited for; matrix products, arithmetic and copies ran while one was open for 0% of the time, Pallas kernels for 8%

profile of v8, /device:TPU:0, one launch (start us, length us, event | category | flops | bytes accessed | tf_op | source)
XLA Modules:
  0.0 17.6 jit_solution(13388363067779481103)
XLA Ops:
  0.6 0.0 copy-start.1
  0.6 0.0 copy-start.2
  0.7 0.0 copy-start.3
  0.7 1.2 %shard_map.104 = (bf16[240,128]{1,0:T(8,128)(2,1)S(1)}, bf16[240,128]{1,0:T(8,128)(2,1)S(1)}, bf16[240,128]{1,0:T(8,128)(2,1)S(1)}, bf16[240,128]{1,0:T(8,128)(2,1)S(1)}) custom-call(bf16[1,24,32,128]{3,2,1,0:T(8,128)(2,1)} %low_ref.1), custom_call_target="tpu_custom_call" | custom-call | flops 1000000 | bytes 245760 | tf_op jit(solution)/shard_map/pallas_call | solution.py:279
  1.9 3.1 %collective-permute-start = (bf16[240,128]{1,0:T(8,128)(2,1)S(1)}, bf16[240,128]{1,0:T(8,128)(2,1)S(1)}, u32[]{:S(2)}, u32[]{:S(2)}) collective-permute-start(bf16[240,128]{1,0:T(8,128)(2,1)S(1)} %get-tuple-element.20), channel_id=1, source_target_pairs={{0,4},{4,8},{8,12},{12,0},{1,5},{5,9},{9,13},{13,1},{2,6},{6,10},{... | collective-permute-start | bytes 184328 | tf_op jit(solution)/shard_map/ppermute | solution.py:291
  4.9 2.6 %collective-permute-start.1 = (bf16[240,128]{1,0:T(8,128)(2,1)S(1)}, bf16[240,128]{1,0:T(8,128)(2,1)S(1)}, u32[]{:S(2)}, u32[]{:S(2)}) collective-permute-start(bf16[240,128]{1,0:T(8,128)(2,1)S(1)} %get-tuple-element.21), channel_id=1, source_target_pairs={{0,8},{4,12},{8,0},{12,4},{1,9},{5,13},{9,1},{13,5},{2,10},{6,14},... | collective-permute-start | bytes 184328 | tf_op jit(solution)/shard_map/ppermute | solution.py:291
  7.5 1.3 %collective-permute-start.2 = (bf16[240,128]{1,0:T(8,128)(2,1)S(1)}, bf16[240,128]{1,0:T(8,128)(2,1)S(1)}, u32[]{:S(2)}, u32[]{:S(2)}) collective-permute-start(bf16[240,128]{1,0:T(8,128)(2,1)S(1)} %get-tuple-element.22), channel_id=1, source_target_pairs={{0,12},{4,0},{8,4},{12,8},{1,13},{5,1},{9,5},{13,9},{2,14},{6,2},{... | collective-permute-start | bytes 184328 | tf_op jit(solution)/shard_map/ppermute | solution.py:291
  8.9 0.0 copy-start.7
  8.9 0.0 copy-start.4
  8.9 0.0 copy-start.5
  8.9 0.0 copy-start.6
  8.9 0.0 copy-done.1
  8.9 0.0 copy-done.2
  8.9 0.0 copy-done.3
  8.9 0.6 %copy-done.7 = s32[1,16]{1,0:T(1,128)S(1)} copy-done((s32[1,16]{1,0:T(1,128)S(1)}, s32[1,16]{1,0:T(1,128)}, u32[]{:S(2)}) %copy-start.7) | copy-done | bytes 88
  9.5 0.0 copy-done.4
  9.6 0.0 copy-done.5
  9.6 0.0 copy-done.6
  9.6 0.9 %copy-done = f32[128,512]{1,0:T(8,128)S(1)} copy-done((f32[128,512]{1,0:T(8,128)S(1)}, f32[128,512]{1,0:T(8,128)}, u32[]{:S(2)}) %copy-start) | copy-done | bytes 262168
  10.5 0.9 %shard_map.105 = (bf16[96,96]{1,0:T(8,128)(2,1)S(1)}, bf16[192,192]{1,0:T(8,128)(2,1)S(1)}, bf16[96,240]{1,0:T(8,128)(2,1)S(1)}, f32[240,128]{1,0:T(8,128)S(1)},...) custom-call(bf16[4,24,24]{2,1,0:T(8,128)(2,1)S(1)} %copy-done.2, ...), custom_call_target="tpu_custom_call" | custom-call | flops 1000000 | bytes 687104 | tf_op jit(solution)/shard_map/pallas_call | solution.py:295
  11.4 0.0 collective-permute-done.refs_1_
  11.4 0.4 %collective-permute-done.1.refs_2_ = bf16[240,128]{1,0:T(8,128)(2,1)S(1)} collective-permute-done((bf16[240,128]{1,0:T(8,128)(2,1)S(1)}, bf16[240,128]{1,0:T(8,128)(2,1)S(1)}, u32[]{:S(2)}, u32[]{:S(2)}) %collective-permute-start.1) | collective-permute-done | bytes 61472 | tf_op jit(solution)/shard_map/ppermute | solution.py:291
  11.8 0.3 %collective-permute-done.2.refs_3_ = bf16[240,128]{1,0:T(8,128)(2,1)S(1)} collective-permute-done((bf16[240,128]{1,0:T(8,128)(2,1)S(1)}, bf16[240,128]{1,0:T(8,128)(2,1)S(1)}, u32[]{:S(2)}, u32[]{:S(2)}) %collective-permute-start.2) | collective-permute-done | bytes 61472 | tf_op jit(solution)/shard_map/ppermute | solution.py:291
  12.1 0.7 %shard_map.106 = (f32[8,4,128]{2,1,0:T(4,128)S(1)}, bf16[64,128]{1,0:T(8,128)(2,1)S(1)}) custom-call(bf16[240,128]{1,0:T(8,128)(2,1)S(1)} %get-tuple-element.19.refs_0_, bf16[240,128]{1,0:T(8,128)(2,1)S(1)} %collective-permute-done.refs_1_, bf16[240,128]{1,0:T(8,128)(2,1)S(1)} %collective-permute-done.1.refs_2_, ...), custom_call_target="tpu_custom_call" | custom-call | flops 1000000 | bytes 32768 | tf_op jit(solution)/shard_map/pallas_call | solution.py:312
  12.8 0.1 collective-permute-start.3
  12.9 1.6 %collective-permute-start.5 = (bf16[64,128]{1,0:T(8,128)(2,1)S(1)}, bf16[64,128]{1,0:T(8,128)(2,1)S(1)}, u32[]{:S(2)}, u32[]{:S(2)}) collective-permute-start(bf16[64,128]{1,0:T(8,128)(2,1)S(1)} %get-tuple-element.31.refs_0_), channel_id=1, source_target_pairs={{0,2},{1,3},{2,0},{3,1},{4,6},{5,7},{6,4},{7,5},{8,10},{9,11},{10,... | collective-permute-start | bytes 49160 | tf_op jit(solution)/shard_map/ppermute | solution.py:242
  14.5 0.3 %collective-permute-start.4 = (bf16[64,128]{1,0:T(8,128)(2,1)S(1)}, bf16[64,128]{1,0:T(8,128)(2,1)S(1)}, u32[]{:S(2)}, u32[]{:S(2)}) collective-permute-start(bf16[64,128]{1,0:T(8,128)(2,1)S(1)} %get-tuple-element.31.refs_0_), channel_id=1, source_target_pairs={{0,1},{1,0},{2,3},{3,2},{4,5},{5,4},{6,7},{7,6},{8,9},{9,8},{10,11... | collective-permute-start | bytes 49160 | tf_op jit(solution)/shard_map/ppermute | solution.py:242
  14.8 1.4 %collective-permute-done.3.refs_1_ = bf16[64,128]{1,0:T(8,128)(2,1)S(1)} collective-permute-done((bf16[64,128]{1,0:T(8,128)(2,1)S(1)}, bf16[64,128]{1,0:T(8,128)(2,1)S(1)}, u32[]{:S(2)}, u32[]{:S(2)}) %collective-permute-start.3) | collective-permute-done | bytes 16416 | tf_op jit(solution)/shard_map/ppermute | solution.py:242
  16.2 0.6 %shard_map.107 = (f32[64,128]{1,0:T(8,128)S(1)}, f32[8,4,128]{2,1,0:T(4,128)}) custom-call(bf16[64,128]{1,0:T(8,128)(2,1)S(1)} %get-tuple-element.31.refs_0_, bf16[64,128]{1,0:T(8,128)(2,1)S(1)} %collective-permute-done.3.refs_1_, bf16[512,256]{1,0:T(8,128)(2,1)S(1)} %get-tuple-element.32.refs_2_, f32[8,4,128]{2,1,0:T(4,128)S(1)} %get-tuple-element.33.refs_3_), custom_call_target="tpu_custom_call" | custom-call | flops 1000000 | bytes 49152 | tf_op jit(solution)/shard_map/pallas_call | solution.py:324
  16.8 0.0 collective-permute-done.5.refs_1_
  16.8 0.0 collective-permute-done.4.refs_0_
  16.8 0.8 %shard_map.108 = f32[16,4,128]{2,1,0:T(4,128)} custom-call(bf16[64,128]{1,0:T(8,128)(2,1)S(1)} %collective-permute-done.4.refs_0_, bf16[64,128]{1,0:T(8,128)(2,1)S(1)} %collective-permute-done.5.refs_1_, bf16[512,256]{1,0:T(8,128)(2,1)S(1)} %get-tuple-element.32.refs_2_, f32[64,128]{1,0:T(8,128)S(1)} %get-tuple-element.35.refs_3_), custom_call_target="tpu_custom_call" | custom-call | flops 1000000 | bytes 32768 | tf_op jit(solution)/shard_map/pallas_call | solution.py:330
  (1 shorter events, 0.0 us)
Async XLA Ops:
  0.6 8.3 %copy-start.1 = (f32[16,4,128]{2,1,0:T(4,128)S(1)}, f32[16,4,128]{2,1,0:T(4,128)}, u32[]{:S(2)}) copy-start(f32[16,4,128]{2,1,0:T(4,128)} %measured_ref.1) | copy-start | bytes 98308
  0.6 8.3 %copy-start.2 = (bf16[4,24,24]{2,1,0:T(8,128)(2,1)S(1)}, bf16[4,24,24]{2,1,0:T(8,128)(2,1)}, u32[]{:S(2)}) copy-start(bf16[4,24,24]{2,1,0:T(8,128)(2,1)} %aw_ref.1) | copy-start | bytes 13828
  0.7 8.3 %copy-start.3 = (bf16[4,24,24]{2,1,0:T(8,128)(2,1)S(1)}, bf16[4,24,24]{2,1,0:T(8,128)(2,1)}, u32[]{:S(2)}) copy-start(bf16[4,24,24]{2,1,0:T(8,128)(2,1)} %cw_ref.1) | copy-start | bytes 13828
  1.9 9.6 %collective-permute-start = (bf16[240,128]{1,0:T(8,128)(2,1)S(1)}, bf16[240,128]{1,0:T(8,128)(2,1)S(1)}, u32[]{:S(2)}, u32[]{:S(2)}) collective-permute-start(bf16[240,128]{1,0:T(8,128)(2,1)S(1)} %get-tuple-element.20), channel_id=1, source_target_pairs={{0,4},{4,8},{8,12},{12,0},{1,5},{5,9},{9,13},{13,1},{2,6},{6,10},{... | collective-permute-start | bytes 184328 | tf_op jit(solution)/shard_map/ppermute | solution.py:291
  4.9 6.9 %collective-permute-start.1 = (bf16[240,128]{1,0:T(8,128)(2,1)S(1)}, bf16[240,128]{1,0:T(8,128)(2,1)S(1)}, u32[]{:S(2)}, u32[]{:S(2)}) collective-permute-start(bf16[240,128]{1,0:T(8,128)(2,1)S(1)} %get-tuple-element.21), channel_id=1, source_target_pairs={{0,8},{4,12},{8,0},{12,4},{1,9},{5,13},{9,1},{13,5},{2,10},{6,14},... | collective-permute-start | bytes 184328 | tf_op jit(solution)/shard_map/ppermute | solution.py:291
  7.5 4.6 %collective-permute-start.2 = (bf16[240,128]{1,0:T(8,128)(2,1)S(1)}, bf16[240,128]{1,0:T(8,128)(2,1)S(1)}, u32[]{:S(2)}, u32[]{:S(2)}) collective-permute-start(bf16[240,128]{1,0:T(8,128)(2,1)S(1)} %get-tuple-element.22), channel_id=1, source_target_pairs={{0,12},{4,0},{8,4},{12,8},{1,13},{5,1},{9,5},{13,9},{2,14},{6,2},{... | collective-permute-start | bytes 184328 | tf_op jit(solution)/shard_map/ppermute | solution.py:291
  8.9 0.7 %copy-start.7 = (s32[1,16]{1,0:T(1,128)S(1)}, s32[1,16]{1,0:T(1,128)}, u32[]{:S(2)}) copy-start(s32[1,16]{1,0:T(1,128)} %sparse_ref.1) | copy-start | bytes 196
  8.9 0.7 %copy-start.4 = (f32[24]{0:T(128)S(1)}, f32[24]{0:T(128)}, u32[]{:S(2)}) copy-start(f32[24]{0:T(128)} %param.11) | copy-start | bytes 292
  8.9 0.7 %copy-start.5 = (f32[24]{0:T(128)S(1)}, f32[24]{0:T(128)}, u32[]{:S(2)}) copy-start(f32[24]{0:T(128)} %param.13) | copy-start | bytes 292
  8.9 0.7 %copy-start.6 = (f32[24]{0:T(128)S(1)}, f32[24]{0:T(128)}, u32[]{:S(2)}) copy-start(f32[24]{0:T(128)} %param.14) | copy-start | bytes 292
  9.6 0.9 %copy-start = (f32[128,512]{1,0:T(8,128)S(1)}, f32[128,512]{1,0:T(8,128)}, u32[]{:S(2)}) copy-start(f32[128,512]{1,0:T(8,128)} %rw_ref.1) | copy-start | bytes 786436
  12.8 3.4 %collective-permute-start.3 = (bf16[64,128]{1,0:T(8,128)(2,1)S(1)}, bf16[64,128]{1,0:T(8,128)(2,1)S(1)}, u32[]{:S(2)}, u32[]{:S(2)}) collective-permute-start(bf16[64,128]{1,0:T(8,128)(2,1)S(1)} %get-tuple-element.31.refs_0_), channel_id=1, source_target_pairs={{0,3},{1,2},{2,1},{3,0},{4,7},{5,6},{6,5},{7,4},{8,11},{9,10},{10,... | collective-permute-start | bytes 49160 | tf_op jit(solution)/shard_map/ppermute | solution.py:242
  12.9 3.9 %collective-permute-start.5 = (bf16[64,128]{1,0:T(8,128)(2,1)S(1)}, bf16[64,128]{1,0:T(8,128)(2,1)S(1)}, u32[]{:S(2)}, u32[]{:S(2)}) collective-permute-start(bf16[64,128]{1,0:T(8,128)(2,1)S(1)} %get-tuple-element.31.refs_0_), channel_id=1, source_target_pairs={{0,2},{1,3},{2,0},{3,1},{4,6},{5,7},{6,4},{7,5},{8,10},{9,11},{10,... | collective-permute-start | bytes 49160 | tf_op jit(solution)/shard_map/ppermute | solution.py:242
  14.5 2.3 %collective-permute-start.4 = (bf16[64,128]{1,0:T(8,128)(2,1)S(1)}, bf16[64,128]{1,0:T(8,128)(2,1)S(1)}, u32[]{:S(2)}, u32[]{:S(2)}) collective-permute-start(bf16[64,128]{1,0:T(8,128)(2,1)S(1)} %get-tuple-element.31.refs_0_), channel_id=1, source_target_pairs={{0,1},{1,0},{2,3},{3,2},{4,5},{5,4},{6,7},{7,6},{8,9},{9,8},{10,11... | collective-permute-start | bytes 49160 | tf_op jit(solution)/shard_map/ppermute | solution.py:242

commit v9 on v7

--- a/solution.py
+++ b/solution.py
@@ -38,13 +38,29 @@
     return lax.broadcasted_iota(jnp.int32, shape, axis)
 
 
-def rounds(count):
+def rounds(count, cores):
     if count == 4:
-        return [(2, 3, 1, 0), (3, 2, 0, 1), (1, 0, 3, 2)]
-    return [tuple((i + shift) % count for i in range(count)) for shift in range(1, count)]
-
-
-def entry(table, index):
+        schedules = [
+            [(1, 3, 0, 2), (3, 2, 1, 0), (2, 0, 3, 1)],
+            [(2, 3, 1, 0), (3, 2, 0, 1), (1, 0, 3, 2)],
+        ]
+    else:
+        schedules = [[tuple((i + shift) % count for i in range(count)) for shift in range(1, count)]]
+    return [
+        tuple(schedules[core % len(schedules)][r][i] for i in range(count) for core in range(cores))
+        for r in range(count - 1)
+    ]
+
+
+def sources(route, cores):
+    back = [0] * len(route)
+    for place, target in enumerate(route):
+        back[target * cores + place % cores] = place // cores
+    return tuple(back)
+
+
+def entry(table, axes):
+    index = lax.axis_index(axes)
     value = jnp.int32(table[0])
     for i in range(1, len(table)):
         value = jnp.where(index == i, jnp.int32(table[i]), value)
@@ -75,7 +91,7 @@
         rows_ref[8 + i * each * width : 8 + (i + 1) * each * width, :] = values
     own = width // (len(routes) + 1)
     me = lax.axis_index("wide")
-    for window, target in zip(windows, [me] + [entry(route, me) for route in routes]):
+    for window, target in zip(windows, [me] + [entry(route, ("wide", "pair")) for route in routes]):
         first = target * own + 7
         columns = [rows_ref[pl.ds(first + i, channels, stride=width), :] for i in range(own + 2)]
         window[...] = jnp.concatenate(columns, axis=0).astype(BF16)
@@ -164,8 +180,9 @@
     outs = a2_ref.shape[0]
     channels = outs // own_out
     me = lax.axis_index("wide")
-    sources = [me] + [entry(tuple(route.index(i) for i in range(wide)), me) for route in routes]
-    for window, source in zip(windows, sources):
+    cores = lax.axis_size("pair")
+    origins = [me] + [entry(sources(route, cores), ("wide", "pair")) for route in routes]
+    for window, source in zip(windows, origins):
         views_ref[:, pl.ds(pl.multiple_of((source + 1) * lanes, lanes), lanes)] = window[...]
     views_ref[:, :lanes] = views_ref[:, wide * lanes :]
 
@@ -268,7 +285,7 @@
         measured,
         sparse_views,
     )
-    routes = rounds(wide)
+    routes = rounds(wide, pair)
     groups = column_groups(channels, span)
     windows = call(
         functools.partial(pack_kernel, routes),
@@ -282,7 +299,8 @@
         vmem=53.6 if width <= 64 else 48,
     )(low_sino)
     windows = [windows[0]] + [
-        lax.ppermute(window, "wide", list(enumerate(route))) for window, route in zip(windows[1:], routes)
+        lax.ppermute(window, ("wide", "pair"), [(p, t * pair + p % pair) for p, t in enumerate(route)])
+        for window, route in zip(windows[1:], routes)
     ]
 
     widths = sorted({taken for _, taken in groups})

time: 17.9 us -> 17.6 us (0.983)
  waiting for transfers between devices: 4.15 us -> 2.4 us
  starting transfers between devices: 7.59 us -> 9.05 us
    ppermute x3, waiting for transfers between devices: 2.19 us -> 0.44 us  [local(): lax.ppermute(window, ('wide', 'pair'), [(p, t * pair + p % pair) for p, t...]
    ppermute x3, starting transfers between devices: 5.67 us -> 7.13 us  [local(): lax.ppermute(window, ('wide', 'pair'), [(p, t * pair + p % pair) for p, t...]
  transfers between devices with their start and end apart: 6 -> 6, of which waited for: 3 -> 4; matrix products, arithmetic and copies ran while one was open for 0% -> 0% of each run, Pallas kernels for 5% -> 5%
where the time goes in v9:
time: 17.6 us; the launch traced here: 17.4 us
  starting transfers between devices  9.05 us (51%)
  Pallas kernels  3.56 us (20%)
  waiting for transfers between devices  2.4 us (14%)
  local copies, waits for them, and re-layouts  1.63 us (9%)
  between operations  0.73 us (4%)
    ppermute x3, starting transfers between devices, local(): lax.ppermute(window, ('wide', 'pair'), [(p, t * pair + p % pair) for p, t...  7.13 us
    ppermute x3, waiting for transfers between devices, send_both(): return lax.ppermute(block, ('narrow', 'pair'), route)  1.96 us
    ppermute x3, starting transfers between devices, send_both(): return lax.ppermute(block, ('narrow', 'pair'), route)  1.92 us
    unnamed x16, local copies, waits for them, and re-layouts  1.63 us
    pallas_call x1, Pallas kernels, local(): call(functools.partial(pack_kernel, routes), [shape((size, lanes), BF16)]...  1.21 us
    pallas_call x1, Pallas kernels, local(): call(functools.partial(prepare_kernel, wide, own_out, groups), [shape((2...  0.87 us
    pallas_call x1, Pallas kernels, local(): call(functools.partial(adjoint_kernel, shifts, own_out), [shape((sparse_c...  0.79 us
    pallas_call x1, Pallas kernels, local(): call(functools.partial(net_kernel, routes, own_out, groups), [shape((2 *...  0.69 us
  transfers between devices with their start and end apart: 6, of which 4 were waited for; matrix products, arithmetic and copies ran while one was open for 0% of the time, Pallas kernels for 5%

profile of v9, /device:TPU:0, one launch (start us, length us, event | category | flops | bytes accessed | tf_op | source)
XLA Modules:
  0.0 17.4 jit_solution(8019167913537667214)
XLA Ops:
  0.6 0.0 copy-start.1
  0.6 0.0 copy-start.2
  0.7 0.0 copy-start.3
  0.7 1.2 %shard_map.104 = (bf16[240,128]{1,0:T(8,128)(2,1)S(1)}, bf16[240,128]{1,0:T(8,128)(2,1)S(1)}, bf16[240,128]{1,0:T(8,128)(2,1)S(1)}, bf16[240,128]{1,0:T(8,128)(2,1)S(1)}) custom-call(bf16[1,24,32,128]{3,2,1,0:T(8,128)(2,1)} %low_ref.1), custom_call_target="tpu_custom_call" | custom-call | flops 1000000 | bytes 245760 | tf_op jit(solution)/shard_map/pallas_call | solution.py:290
  1.9 3.1 %collective-permute-start = (bf16[240,128]{1,0:T(8,128)(2,1)S(1)}, bf16[240,128]{1,0:T(8,128)(2,1)S(1)}, u32[]{:S(2)}, u32[]{:S(2)}) collective-permute-start(bf16[240,128]{1,0:T(8,128)(2,1)S(1)} %get-tuple-element.20), channel_id=1, source_target_pairs={{0,4},{1,9},{4,12},{5,13},{8,0},{9,5},{12,8},{13,1},{2,6},{3,11},{... | collective-permute-start | bytes 184328 | tf_op jit(solution)/shard_map/ppermute | solution.py:302
  5.0 2.5 %collective-permute-start.1 = (bf16[240,128]{1,0:T(8,128)(2,1)S(1)}, bf16[240,128]{1,0:T(8,128)(2,1)S(1)}, u32[]{:S(2)}, u32[]{:S(2)}) collective-permute-start(bf16[240,128]{1,0:T(8,128)(2,1)S(1)} %get-tuple-element.21), channel_id=1, source_target_pairs={{0,12},{1,13},{4,8},{5,9},{8,4},{9,1},{12,0},{13,5},{2,14},{3,15},... | collective-permute-start | bytes 184328 | tf_op jit(solution)/shard_map/ppermute | solution.py:302
  7.4 1.6 %collective-permute-start.2 = (bf16[240,128]{1,0:T(8,128)(2,1)S(1)}, bf16[240,128]{1,0:T(8,128)(2,1)S(1)}, u32[]{:S(2)}, u32[]{:S(2)}) collective-permute-start(bf16[240,128]{1,0:T(8,128)(2,1)S(1)} %get-tuple-element.22), channel_id=1, source_target_pairs={{0,8},{1,5},{4,0},{5,1},{8,12},{9,13},{12,4},{13,9},{2,10},{3,7},{... | collective-permute-start | bytes 184328 | tf_op jit(solution)/shard_map/ppermute | solution.py:302
  9.0 0.0 copy-start.7
  9.0 0.0 copy-start.4
  9.0 0.0 copy-start.5
  9.0 0.0 copy-start.6
  9.0 0.0 copy-done.1
  9.0 0.0 copy-done.2
  9.0 0.0 copy-done.3
  9.0 0.6 %copy-done.7 = s32[1,16]{1,0:T(1,128)S(1)} copy-done((s32[1,16]{1,0:T(1,128)S(1)}, s32[1,16]{1,0:T(1,128)}, u32[]{:S(2)}) %copy-start.7) | copy-done | bytes 88
  9.7 0.0 copy-done.4
  9.7 0.0 copy-done.5
  9.7 0.0 copy-done.6
  9.7 0.0 copy-start
  9.7 0.9 %copy-done = f32[128,512]{1,0:T(8,128)S(1)} copy-done((f32[128,512]{1,0:T(8,128)S(1)}, f32[128,512]{1,0:T(8,128)}, u32[]{:S(2)}) %copy-start) | copy-done | bytes 262168
  10.7 0.9 %shard_map.105 = (bf16[96,96]{1,0:T(8,128)(2,1)S(1)}, bf16[192,192]{1,0:T(8,128)(2,1)S(1)}, bf16[96,240]{1,0:T(8,128)(2,1)S(1)}, f32[240,128]{1,0:T(8,128)S(1)},...) custom-call(bf16[4,24,24]{2,1,0:T(8,128)(2,1)S(1)} %copy-done.2, ...), custom_call_target="tpu_custom_call" | custom-call | flops 1000000 | bytes 687104 | tf_op jit(solution)/shard_map/pallas_call | solution.py:307
  11.5 0.0 collective-permute-done.refs_1_
  11.5 0.1 collective-permute-done.1.refs_2_
  11.6 0.4 %collective-permute-done.2.refs_3_ = bf16[240,128]{1,0:T(8,128)(2,1)S(1)} collective-permute-done((bf16[240,128]{1,0:T(8,128)(2,1)S(1)}, bf16[240,128]{1,0:T(8,128)(2,1)S(1)}, u32[]{:S(2)}, u32[]{:S(2)}) %collective-permute-start.2) | collective-permute-done | bytes 61472 | tf_op jit(solution)/shard_map/ppermute | solution.py:302
  12.0 0.7 %shard_map.106 = (f32[8,4,128]{2,1,0:T(4,128)S(1)}, bf16[64,128]{1,0:T(8,128)(2,1)S(1)}) custom-call(bf16[240,128]{1,0:T(8,128)(2,1)S(1)} %get-tuple-element.19.refs_0_, bf16[240,128]{1,0:T(8,128)(2,1)S(1)} %collective-permute-done.refs_1_, bf16[240,128]{1,0:T(8,128)(2,1)S(1)} %collective-permute-done.1.refs_2_, ...), custom_call_target="tpu_custom_call" | custom-call | flops 1000000 | bytes 32768 | tf_op jit(solution)/shard_map/pallas_call | solution.py:324
  12.7 0.1 collective-permute-start.5
  12.8 1.6 %collective-permute-start.4 = (bf16[64,128]{1,0:T(8,128)(2,1)S(1)}, bf16[64,128]{1,0:T(8,128)(2,1)S(1)}, u32[]{:S(2)}, u32[]{:S(2)}) collective-permute-start(bf16[64,128]{1,0:T(8,128)(2,1)S(1)} %get-tuple-element.31.refs_0_), channel_id=1, source_target_pairs={{0,2},{1,3},{2,0},{3,1},{4,6},{5,7},{6,4},{7,5},{8,10},{9,11},{10,... | collective-permute-start | bytes 49160 | tf_op jit(solution)/shard_map/ppermute | solution.py:253
  14.3 0.3 %collective-permute-start.3 = (bf16[64,128]{1,0:T(8,128)(2,1)S(1)}, bf16[64,128]{1,0:T(8,128)(2,1)S(1)}, u32[]{:S(2)}, u32[]{:S(2)}) collective-permute-start(bf16[64,128]{1,0:T(8,128)(2,1)S(1)} %get-tuple-element.31.refs_0_), channel_id=1, source_target_pairs={{0,1},{1,0},{2,3},{3,2},{4,5},{5,4},{6,7},{7,6},{8,9},{9,8},{10,11... | collective-permute-start | bytes 49160 | tf_op jit(solution)/shard_map/ppermute | solution.py:253
  14.6 1.4 %collective-permute-done.5.refs_3_ = bf16[64,128]{1,0:T(8,128)(2,1)S(1)} collective-permute-done((bf16[64,128]{1,0:T(8,128)(2,1)S(1)}, bf16[64,128]{1,0:T(8,128)(2,1)S(1)}, u32[]{:S(2)}, u32[]{:S(2)}) %collective-permute-start.5) | collective-permute-done | bytes 16416 | tf_op jit(solution)/shard_map/ppermute | solution.py:253
  16.0 0.5 %collective-permute-done.4.refs_2_ = bf16[64,128]{1,0:T(8,128)(2,1)S(1)} collective-permute-done((bf16[64,128]{1,0:T(8,128)(2,1)S(1)}, bf16[64,128]{1,0:T(8,128)(2,1)S(1)}, u32[]{:S(2)}, u32[]{:S(2)}) %collective-permute-start.4) | collective-permute-done | bytes 16416 | tf_op jit(solution)/shard_map/ppermute | solution.py:253
  16.6 0.0 collective-permute-done.3.refs_1_
  16.6 0.8 %shard_map.107 = (f32[16,4,128]{2,1,0:T(4,128)}, f32[8,4,128]{2,1,0:T(4,128)}) custom-call(bf16[64,128]{1,0:T(8,128)(2,1)S(1)} %get-tuple-element.31.refs_0_, bf16[64,128]{1,0:T(8,128)(2,1)S(1)} %collective-permute-done.3.refs_1_, bf16[64,128]{1,0:T(8,128)(2,1)S(1)} %collective-permute-done.4.refs_2_, bf16[64,128]{1,0:T(8,128)(2,1)S(1)} %collective-permute-done.5.refs_3_, ...), custom_call_target="tpu_custom_call" | custom-call | flops 1000000 | bytes 49152 | tf_op jit(solution)/shard_map/pallas_call | solution.py:336
Async XLA Ops:
  0.6 8.4 %copy-start.1 = (f32[16,4,128]{2,1,0:T(4,128)S(1)}, f32[16,4,128]{2,1,0:T(4,128)}, u32[]{:S(2)}) copy-start(f32[16,4,128]{2,1,0:T(4,128)} %measured_ref.1) | copy-start | bytes 98308
  0.6 8.4 %copy-start.2 = (bf16[4,24,24]{2,1,0:T(8,128)(2,1)S(1)}, bf16[4,24,24]{2,1,0:T(8,128)(2,1)}, u32[]{:S(2)}) copy-start(bf16[4,24,24]{2,1,0:T(8,128)(2,1)} %aw_ref.1) | copy-start | bytes 13828
  0.7 8.4 %copy-start.3 = (bf16[4,24,24]{2,1,0:T(8,128)(2,1)S(1)}, bf16[4,24,24]{2,1,0:T(8,128)(2,1)}, u32[]{:S(2)}) copy-start(bf16[4,24,24]{2,1,0:T(8,128)(2,1)} %cw_ref.1) | copy-start | bytes 13828
  1.9 9.7 %collective-permute-start = (bf16[240,128]{1,0:T(8,128)(2,1)S(1)}, bf16[240,128]{1,0:T(8,128)(2,1)S(1)}, u32[]{:S(2)}, u32[]{:S(2)}) collective-permute-start(bf16[240,128]{1,0:T(8,128)(2,1)S(1)} %get-tuple-element.20), channel_id=1, source_target_pairs={{0,4},{1,9},{4,12},{5,13},{8,0},{9,5},{12,8},{13,1},{2,6},{3,11},{... | collective-permute-start | bytes 184328 | tf_op jit(solution)/shard_map/ppermute | solution.py:302
  5.0 6.7 %collective-permute-start.1 = (bf16[240,128]{1,0:T(8,128)(2,1)S(1)}, bf16[240,128]{1,0:T(8,128)(2,1)S(1)}, u32[]{:S(2)}, u32[]{:S(2)}) collective-permute-start(bf16[240,128]{1,0:T(8,128)(2,1)S(1)} %get-tuple-element.21), channel_id=1, source_target_pairs={{0,12},{1,13},{4,8},{5,9},{8,4},{9,1},{12,0},{13,5},{2,14},{3,15},... | collective-permute-start | bytes 184328 | tf_op jit(solution)/shard_map/ppermute | solution.py:302
  7.4 4.6 %collective-permute-start.2 = (bf16[240,128]{1,0:T(8,128)(2,1)S(1)}, bf16[240,128]{1,0:T(8,128)(2,1)S(1)}, u32[]{:S(2)}, u32[]{:S(2)}) collective-permute-start(bf16[240,128]{1,0:T(8,128)(2,1)S(1)} %get-tuple-element.22), channel_id=1, source_target_pairs={{0,8},{1,5},{4,0},{5,1},{8,12},{9,13},{12,4},{13,9},{2,10},{3,7},{... | collective-permute-start | bytes 184328 | tf_op jit(solution)/shard_map/ppermute | solution.py:302
  9.0 0.7 %copy-start.7 = (s32[1,16]{1,0:T(1,128)S(1)}, s32[1,16]{1,0:T(1,128)}, u32[]{:S(2)}) copy-start(s32[1,16]{1,0:T(1,128)} %sparse_ref.1) | copy-start | bytes 196
  9.0 0.7 %copy-start.4 = (f32[24]{0:T(128)S(1)}, f32[24]{0:T(128)}, u32[]{:S(2)}) copy-start(f32[24]{0:T(128)} %param.11) | copy-start | bytes 292
  9.0 0.7 %copy-start.5 = (f32[24]{0:T(128)S(1)}, f32[24]{0:T(128)}, u32[]{:S(2)}) copy-start(f32[24]{0:T(128)} %param.13) | copy-start | bytes 292
  9.0 0.7 %copy-start.6 = (f32[24]{0:T(128)S(1)}, f32[24]{0:T(128)}, u32[]{:S(2)}) copy-start(f32[24]{0:T(128)} %param.14) | copy-start | bytes 292
  9.7 0.9 %copy-start = (f32[128,512]{1,0:T(8,128)S(1)}, f32[128,512]{1,0:T(8,128)}, u32[]{:S(2)}) copy-start(f32[128,512]{1,0:T(8,128)} %rw_ref.1) | copy-start | bytes 786436
  12.7 3.4 %collective-permute-start.5 = (bf16[64,128]{1,0:T(8,128)(2,1)S(1)}, bf16[64,128]{1,0:T(8,128)(2,1)S(1)}, u32[]{:S(2)}, u32[]{:S(2)}) collective-permute-start(bf16[64,128]{1,0:T(8,128)(2,1)S(1)} %get-tuple-element.31.refs_0_), channel_id=1, source_target_pairs={{0,3},{1,2},{2,1},{3,0},{4,7},{5,6},{6,5},{7,4},{8,11},{9,10},{10,... | collective-permute-start | bytes 49160 | tf_op jit(solution)/shard_map/ppermute | solution.py:253
  12.8 3.8 %collective-permute-start.4 = (bf16[64,128]{1,0:T(8,128)(2,1)S(1)}, bf16[64,128]{1,0:T(8,128)(2,1)S(1)}, u32[]{:S(2)}, u32[]{:S(2)}) collective-permute-start(bf16[64,128]{1,0:T(8,128)(2,1)S(1)} %get-tuple-element.31.refs_0_), channel_id=1, source_target_pairs={{0,2},{1,3},{2,0},{3,1},{4,6},{5,7},{6,4},{7,5},{8,10},{9,11},{10,... | collective-permute-start | bytes 49160 | tf_op jit(solution)/shard_map/ppermute | solution.py:253
  14.3 2.3 %collective-permute-start.3 = (bf16[64,128]{1,0:T(8,128)(2,1)S(1)}, bf16[64,128]{1,0:T(8,128)(2,1)S(1)}, u32[]{:S(2)}, u32[]{:S(2)}) collective-permute-start(bf16[64,128]{1,0:T(8,128)(2,1)S(1)} %get-tuple-element.31.refs_0_), channel_id=1, source_target_pairs={{0,1},{1,0},{2,3},{3,2},{4,5},{5,4},{6,7},{7,6},{8,9},{9,8},{10,11... | collective-permute-start | bytes 49160 | tf_op jit(solution)/shard_map/ppermute | solution.py:253

commit v10 on v9

--- a/solution.py
+++ b/solution.py
@@ -41,8 +41,8 @@
 def rounds(count, cores):
     if count == 4:
         schedules = [
+            [(1, 2, 3, 0), (2, 3, 0, 1), (3, 0, 1, 2)],
             [(1, 3, 0, 2), (3, 2, 1, 0), (2, 0, 3, 1)],
-            [(2, 3, 1, 0), (3, 2, 0, 1), (1, 0, 3, 2)],
         ]
     else:
         schedules = [[tuple((i + shift) % count for i in range(count)) for shift in range(1, count)]]
@@ -106,12 +106,11 @@
     cw_ref,
     cb_ref,
     hw_ref,
-    rw_ref,
     measured_ref,
     sparse_ref,
     *refs,
 ):
-    firsts, (a2_ref, b1_ref, b2_ref, h_ref, turned_ref, select_ref, target_ref) = refs[:-7], refs[-7:]
+    firsts, (a2_ref, b1_ref, b2_ref, h_ref, select_ref, target_ref) = refs[:-6], refs[-6:]
     channels = aw_ref.shape[1]
     span = 2 * own_out + 2
     size, outs = span * channels, own_out * channels
@@ -159,17 +158,19 @@
     along(pick_out, cb_ref, b2_ref)
     along(pick_out, hw_ref, h_ref)
 
-    turned = rw_ref[...].T
-    high = turned.astype(BF16)
-    turned_ref[:, : high.shape[1]] = high
-    turned_ref[:, high.shape[1] :] = (turned - high.astype(F32)).astype(BF16)
-
     sparse_count = measured_ref.shape[0]
     wanted = (select_ref.shape[0], sparse_count)
     pick_view = (split(iota(wanted, 0), own_out)[0] == iota(wanted, 1)).astype(F32)
     along(pick_view, sparse_ref, select_ref)
     for k in range(sparse_count):
         target_ref[k * own_out : (k + 1) * own_out, :] = measured_ref[k]
+
+
+def turn_kernel(rw_ref, _, turned_ref):
+    turned = rw_ref[...].T
+    high = turned.astype(BF16)
+    turned_ref[:, : high.shape[1]] = high
+    turned_ref[:, high.shape[1] :] = (turned - high.astype(F32)).astype(BF16)
 
 
 def net_kernel(routes, own_out, groups, *refs):
@@ -281,7 +282,6 @@
         column_weight,
         column_bias[None],
         head_weight[None],
-        row_weights,
         measured,
         sparse_views,
     )
@@ -304,7 +304,7 @@
     ]
 
     widths = sorted({taken for _, taken in groups})
-    *firsts, a2, b1, b2, head, turned, select, target = call(
+    *firsts, a2, b1, b2, head, select, target = call(
         functools.partial(prepare_kernel, wide, own_out, groups),
         [shape((2 * taken * channels, 2 * taken * channels), BF16) for taken in widths]
         + [
@@ -312,11 +312,10 @@
             shape((size, lanes), F32),
             shape((outs, lanes), F32),
             shape((outs, lanes), F32),
-            shape((rows, 2 * lanes), BF16),
             shape(flat, F32),
             shape(flat, F32),
         ],
-        [VMEM] * 8,
+        [VMEM] * 7,
         vmem=big,
     )(*small)
     firsts = [firsts[widths.index(taken)] for _, taken in groups]
@@ -329,6 +328,7 @@
         vmem=big,
     )(*windows, *firsts, a2, b1, b2, head, select, target)
 
+    turned = call(turn_kernel, shape((rows, 2 * lanes), BF16), [VMEM] * 2, vmem=big)(row_weights, residual)
     shifts = [(0, t) for t in range(1, pair)] + [(s, 0) for s in range(1, narrow)]
     shifts += [(s, t) for s in range(1, narrow) for t in range(1, pair)]
     blocks = [residual] + [send_both(residual, s, t) for s, t in shifts]

time: 17.6 us -> 18.2 us (1.034)
  waiting for transfers between devices: 2.4 us -> 3.81 us
  local copies, waits for them, and re-layouts: 1.63 us -> 0.68 us
    ppermute x3, waiting for transfers between devices: 0.44 us -> 2.01 us  [local(): lax.ppermute(window, ('wide', 'pair'), [(p, t * pair + p % pair) for p, t...]
    unnamed x16, local copies, waits for them, and re-layouts: 1.63 us -> 0.68 us
  transfers between devices with their start and end apart: 6 -> 6, of which waited for: 4 -> 3; matrix products, arithmetic and copies ran while one was open for 0% -> 0% of each run, Pallas kernels for 5% -> 6%
where the time goes in v10:
time: 18.2 us; the launch traced here: 17.9 us
  starting transfers between devices  8.95 us (49%)
  waiting for transfers between devices  3.81 us (21%)
  Pallas kernels  3.69 us (20%)
  between operations  0.74 us (4%)
  local copies, waits for them, and re-layouts  0.68 us (4%)
    ppermute x3, starting transfers between devices, local(): lax.ppermute(window, ('wide', 'pair'), [(p, t * pair + p % pair) for p, t...  7.01 us
    ppermute x3, waiting for transfers between devices, local(): lax.ppermute(window, ('wide', 'pair'), [(p, t * pair + p % pair) for p, t...  2.01 us
    ppermute x3, starting transfers between devices, send_both(): return lax.ppermute(block, ('narrow', 'pair'), route)  1.93 us
    ppermute x3, waiting for transfers between devices, send_both(): return lax.ppermute(block, ('narrow', 'pair'), route)  1.8 us
    pallas_call x1, Pallas kernels, local(): call(functools.partial(pack_kernel, routes), [shape((size, lanes), BF16)]...  1.21 us
    pallas_call x1, Pallas kernels, local(): call(functools.partial(prepare_kernel, wide, own_out, groups), [shape((2...  0.86 us
    pallas_call x1, Pallas kernels, local(): call(functools.partial(adjoint_kernel, shifts, own_out), [shape((sparse_c...  0.79 us
    pallas_call x1, Pallas kernels, local(): call(functools.partial(net_kernel, routes, own_out, groups), [shape((2 *...  0.69 us
  transfers between devices with their start and end apart: 6, of which 3 were waited for; matrix products, arithmetic and copies ran while one was open for 0% of the time, Pallas kernels for 6%

profile of v10, /device:TPU:0, one launch (start us, length us, event | category | flops | bytes accessed | tf_op | source)
XLA Modules:
  0.0 17.9 jit_solution(10709208087090589179)
XLA Ops:
  0.6 0.0 copy-start.1
  0.6 0.0 copy-start.2
  0.7 0.0 copy-start.3
  0.7 1.2 %shard_map.104 = (bf16[240,128]{1,0:T(8,128)(2,1)S(1)}, bf16[240,128]{1,0:T(8,128)(2,1)S(1)}, bf16[240,128]{1,0:T(8,128)(2,1)S(1)}, bf16[240,128]{1,0:T(8,128)(2,1)S(1)}) custom-call(bf16[1,24,32,128]{3,2,1,0:T(8,128)(2,1)} %low_ref.1), custom_call_target="tpu_custom_call" | custom-call | flops 1000000 | bytes 245760 | tf_op jit(solution)/shard_map/pallas_call | solution.py:290
  1.9 3.1 %collective-permute-start = (bf16[240,128]{1,0:T(8,128)(2,1)S(1)}, bf16[240,128]{1,0:T(8,128)(2,1)S(1)}, u32[]{:S(2)}, u32[]{:S(2)}) collective-permute-start(bf16[240,128]{1,0:T(8,128)(2,1)S(1)} %get-tuple-element.19), channel_id=1, source_target_pairs={{0,4},{1,5},{4,8},{5,13},{8,12},{9,1},{12,0},{13,9},{2,6},{3,7},{6... | collective-permute-start | bytes 184328 | tf_op jit(solution)/shard_map/ppermute | solution.py:302
  5.0 2.6 %collective-permute-start.1 = (bf16[240,128]{1,0:T(8,128)(2,1)S(1)}, bf16[240,128]{1,0:T(8,128)(2,1)S(1)}, u32[]{:S(2)}, u32[]{:S(2)}) collective-permute-start(bf16[240,128]{1,0:T(8,128)(2,1)S(1)} %get-tuple-element.20), channel_id=1, source_target_pairs={{0,8},{1,13},{4,12},{5,9},{8,0},{9,5},{12,4},{13,1},{2,10},{3,15},... | collective-permute-start | bytes 184328 | tf_op jit(solution)/shard_map/ppermute | solution.py:302
  7.5 1.3 %collective-permute-start.2 = (bf16[240,128]{1,0:T(8,128)(2,1)S(1)}, bf16[240,128]{1,0:T(8,128)(2,1)S(1)}, u32[]{:S(2)}, u32[]{:S(2)}) collective-permute-start(bf16[240,128]{1,0:T(8,128)(2,1)S(1)} %get-tuple-element.21), channel_id=1, source_target_pairs={{0,12},{1,9},{4,0},{5,1},{8,4},{9,13},{12,8},{13,5},{2,14},{3,11},... | collective-permute-start | bytes 184328 | tf_op jit(solution)/shard_map/ppermute | solution.py:302
  8.9 0.0 copy-start.7
  8.9 0.0 copy-start.4
  8.9 0.0 copy-start.5
  8.9 0.0 copy-start.6
  8.9 0.0 copy-done.1
  8.9 0.0 copy-done.2
  8.9 0.0 copy-done.3
  8.9 0.6 %copy-done.7 = s32[1,16]{1,0:T(1,128)S(1)} copy-done((s32[1,16]{1,0:T(1,128)S(1)}, s32[1,16]{1,0:T(1,128)}, u32[]{:S(2)}) %copy-start.7) | copy-done | bytes 88
  9.5 0.0 copy-done.4
  9.6 0.0 copy-done.5
  9.6 0.0 copy-done.6
  9.6 0.9 %shard_map.105 = (bf16[96,96]{1,0:T(8,128)(2,1)S(1)}, bf16[192,192]{1,0:T(8,128)(2,1)S(1)}, bf16[96,240]{1,0:T(8,128)(2,1)S(1)}, f32[240,128]{1,0:T(8,128)S(1)},...) custom-call(bf16[4,24,24]{2,1,0:T(8,128)(2,1)S(1)} %copy-done.2, ...), custom_call_target="tpu_custom_call" | custom-call | flops 1000000 | bytes 424960 | tf_op jit(solution)/shard_map/pallas_call | solution.py:307
  10.5 0.0 collective-permute-done.refs_1_
  10.5 2.0 %collective-permute-done.1.refs_2_ = bf16[240,128]{1,0:T(8,128)(2,1)S(1)} collective-permute-done((bf16[240,128]{1,0:T(8,128)(2,1)S(1)}, bf16[240,128]{1,0:T(8,128)(2,1)S(1)}, u32[]{:S(2)}, u32[]{:S(2)}) %collective-permute-start.1) | collective-permute-done | bytes 61472 | tf_op jit(solution)/shard_map/ppermute | solution.py:302
  12.5 0.0 collective-permute-done.2.refs_3_
  12.5 0.7 %shard_map.106 = (f32[8,4,128]{2,1,0:T(4,128)S(1)}, bf16[64,128]{1,0:T(8,128)(2,1)S(1)}) custom-call(bf16[240,128]{1,0:T(8,128)(2,1)S(1)} %get-tuple-element.18.refs_0_, bf16[240,128]{1,0:T(8,128)(2,1)S(1)} %collective-permute-done.refs_1_, bf16[240,128]{1,0:T(8,128)(2,1)S(1)} %collective-permute-done.1.refs_2_, ...), custom_call_target="tpu_custom_call" | custom-call | flops 1000000 | bytes 32768 | tf_op jit(solution)/shard_map/pallas_call | solution.py:323
  13.2 0.1 collective-permute-start.5
  13.3 1.8 %collective-permute-start.4 = (bf16[64,128]{1,0:T(8,128)(2,1)S(1)}, bf16[64,128]{1,0:T(8,128)(2,1)S(1)}, u32[]{:S(2)}, u32[]{:S(2)}) collective-permute-start(bf16[64,128]{1,0:T(8,128)(2,1)S(1)} %get-tuple-element.30._.refs_0_), channel_id=1, source_target_pairs={{0,2},{1,3},{2,0},{3,1},{4,6},{5,7},{6,4},{7,5},{8,10},{9,11},{10,... | collective-permute-start | bytes 49160 | tf_op jit(solution)/shard_map/ppermute | solution.py:254
  15.0 0.1 collective-permute-start.3
  15.1 0.0 copy-done
  15.1 0.1 shard_map.107.refs_4_
  15.3 1.1 %collective-permute-done.5.refs_3_ = bf16[64,128]{1,0:T(8,128)(2,1)S(1)} collective-permute-done((bf16[64,128]{1,0:T(8,128)(2,1)S(1)}, bf16[64,128]{1,0:T(8,128)(2,1)S(1)}, u32[]{:S(2)}, u32[]{:S(2)}) %collective-permute-start.5) | collective-permute-done | bytes 16416 | tf_op jit(solution)/shard_map/ppermute | solution.py:254
  16.4 0.7 %collective-permute-done.4.refs_2_ = bf16[64,128]{1,0:T(8,128)(2,1)S(1)} collective-permute-done((bf16[64,128]{1,0:T(8,128)(2,1)S(1)}, bf16[64,128]{1,0:T(8,128)(2,1)S(1)}, u32[]{:S(2)}, u32[]{:S(2)}) %collective-permute-start.4) | collective-permute-done | bytes 16416 | tf_op jit(solution)/shard_map/ppermute | solution.py:254
  17.1 0.0 collective-permute-done.3.refs_1_
  17.1 0.8 %shard_map.108 = (f32[16,4,128]{2,1,0:T(4,128)}, f32[8,4,128]{2,1,0:T(4,128)}) custom-call(bf16[64,128]{1,0:T(8,128)(2,1)S(1)} %get-tuple-element.30._.refs_0_, bf16[64,128]{1,0:T(8,128)(2,1)S(1)} %collective-permute-done.3.refs_1_, bf16[64,128]{1,0:T(8,128)(2,1)S(1)} %collective-permute-done.4.refs_2_, bf16[64,128]{1,0:T(8,128)(2,1)S(1)} %collective-permute-done.5.refs_3_, ...), custom_call_target="tpu_custom_call" | custom-call | flops 1000000 | bytes 49152 | tf_op jit(solution)/shard_map/pallas_call | solution.py:336
  (1 shorter events, 0.0 us)
Async XLA Ops:
  0.6 8.3 %copy-start.1 = (f32[16,4,128]{2,1,0:T(4,128)S(1)}, f32[16,4,128]{2,1,0:T(4,128)}, u32[]{:S(2)}) copy-start(f32[16,4,128]{2,1,0:T(4,128)} %measured_ref.1) | copy-start | bytes 98308
  0.6 8.3 %copy-start.2 = (bf16[4,24,24]{2,1,0:T(8,128)(2,1)S(1)}, bf16[4,24,24]{2,1,0:T(8,128)(2,1)}, u32[]{:S(2)}) copy-start(bf16[4,24,24]{2,1,0:T(8,128)(2,1)} %aw_ref.1) | copy-start | bytes 13828
  0.7 8.3 %copy-start.3 = (bf16[4,24,24]{2,1,0:T(8,128)(2,1)S(1)}, bf16[4,24,24]{2,1,0:T(8,128)(2,1)}, u32[]{:S(2)}) copy-start(bf16[4,24,24]{2,1,0:T(8,128)(2,1)} %cw_ref.1) | copy-start | bytes 13828
  1.9 8.6 %collective-permute-start = (bf16[240,128]{1,0:T(8,128)(2,1)S(1)}, bf16[240,128]{1,0:T(8,128)(2,1)S(1)}, u32[]{:S(2)}, u32[]{:S(2)}) collective-permute-start(bf16[240,128]{1,0:T(8,128)(2,1)S(1)} %get-tuple-element.19), channel_id=1, source_target_pairs={{0,4},{1,5},{4,8},{5,13},{8,12},{9,1},{12,0},{13,9},{2,6},{3,7},{6... | collective-permute-start | bytes 184328 | tf_op jit(solution)/shard_map/ppermute | solution.py:302
  5.0 7.5 %collective-permute-start.1 = (bf16[240,128]{1,0:T(8,128)(2,1)S(1)}, bf16[240,128]{1,0:T(8,128)(2,1)S(1)}, u32[]{:S(2)}, u32[]{:S(2)}) collective-permute-start(bf16[240,128]{1,0:T(8,128)(2,1)S(1)} %get-tuple-element.20), channel_id=1, source_target_pairs={{0,8},{1,13},{4,12},{5,9},{8,0},{9,5},{12,4},{13,1},{2,10},{3,15},... | collective-permute-start | bytes 184328 | tf_op jit(solution)/shard_map/ppermute | solution.py:302
  7.5 4.9 %collective-permute-start.2 = (bf16[240,128]{1,0:T(8,128)(2,1)S(1)}, bf16[240,128]{1,0:T(8,128)(2,1)S(1)}, u32[]{:S(2)}, u32[]{:S(2)}) collective-permute-start(bf16[240,128]{1,0:T(8,128)(2,1)S(1)} %get-tuple-element.21), channel_id=1, source_target_pairs={{0,12},{1,9},{4,0},{5,1},{8,4},{9,13},{12,8},{13,5},{2,14},{3,11},... | collective-permute-start | bytes 184328 | tf_op jit(solution)/shard_map/ppermute | solution.py:302
  8.9 0.7 %copy-start.7 = (s32[1,16]{1,0:T(1,128)S(1)}, s32[1,16]{1,0:T(1,128)}, u32[]{:S(2)}) copy-start(s32[1,16]{1,0:T(1,128)} %sparse_ref.1) | copy-start | bytes 196
  8.9 0.7 %copy-start.4 = (f32[24]{0:T(128)S(1)}, f32[24]{0:T(128)}, u32[]{:S(2)}) copy-start(f32[24]{0:T(128)} %param.11) | copy-start | bytes 292
  8.9 0.7 %copy-start.5 = (f32[24]{0:T(128)S(1)}, f32[24]{0:T(128)}, u32[]{:S(2)}) copy-start(f32[24]{0:T(128)} %param.13) | copy-start | bytes 292
  8.9 0.7 %copy-start.6 = (f32[24]{0:T(128)S(1)}, f32[24]{0:T(128)}, u32[]{:S(2)}) copy-start(f32[24]{0:T(128)} %param.14) | copy-start | bytes 292
  12.5 2.6 %copy-start = (f32[128,512]{1,0:T(8,128)S(1)}, f32[128,512]{1,0:T(8,128)}, u32[]{:S(2)}) copy-start(f32[128,512]{1,0:T(8,128)} %rw_ref.1) | copy-start | bytes 786436
  13.2 3.2 %collective-permute-start.5 = (bf16[64,128]{1,0:T(8,128)(2,1)S(1)}, bf16[64,128]{1,0:T(8,128)(2,1)S(1)}, u32[]{:S(2)}, u32[]{:S(2)}) collective-permute-start(bf16[64,128]{1,0:T(8,128)(2,1)S(1)} %get-tuple-element.30._.refs_0_), channel_id=1, source_target_pairs={{0,3},{1,2},{2,1},{3,0},{4,7},{5,6},{6,5},{7,4},{8,11},{9,10},{10,... | collective-permute-start | bytes 49160 | tf_op jit(solution)/shard_map/ppermute | solution.py:254
  13.3 3.8 %collective-permute-start.4 = (bf16[64,128]{1,0:T(8,128)(2,1)S(1)}, bf16[64,128]{1,0:T(8,128)(2,1)S(1)}, u32[]{:S(2)}, u32[]{:S(2)}) collective-permute-start(bf16[64,128]{1,0:T(8,128)(2,1)S(1)} %get-tuple-element.30._.refs_0_), channel_id=1, source_target_pairs={{0,2},{1,3},{2,0},{3,1},{4,6},{5,7},{6,4},{7,5},{8,10},{9,11},{10,... | collective-permute-start | bytes 49160 | tf_op jit(solution)/shard_map/ppermute | solution.py:254
  15.0 2.0 %collective-permute-start.3 = (bf16[64,128]{1,0:T(8,128)(2,1)S(1)}, bf16[64,128]{1,0:T(8,128)(2,1)S(1)}, u32[]{:S(2)}, u32[]{:S(2)}) collective-permute-start(bf16[64,128]{1,0:T(8,128)(2,1)S(1)} %get-tuple-element.30._.refs_0_), channel_id=1, source_target_pairs={{0,1},{1,0},{2,3},{3,2},{4,5},{5,4},{6,7},{7,6},{8,9},{9,8},{10,11... | collective-permute-start | bytes 49160 | tf_op jit(solution)/shard_map/ppermute | solution.py:254

commit v11 on v10

--- a/solution.py
+++ b/solution.py
@@ -41,8 +41,8 @@
 def rounds(count, cores):
     if count == 4:
         schedules = [
-            [(1, 2, 3, 0), (2, 3, 0, 1), (3, 0, 1, 2)],
             [(1, 3, 0, 2), (3, 2, 1, 0), (2, 0, 3, 1)],
+            [(2, 3, 1, 0), (3, 2, 0, 1), (1, 0, 3, 2)],
         ]
     else:
         schedules = [[tuple((i + shift) % count for i in range(count)) for shift in range(1, count)]]

time: 18.2 us -> 17.6 us (0.967)
  waiting for transfers between devices: 3.81 us -> 3.21 us
    ppermute x3, waiting for transfers between devices: 2.01 us -> 1.4 us  [local(): lax.ppermute(window, ('wide', 'pair'), [(p, t * pair + p % pair) for p, t...]
  transfers between devices with their start and end apart: 6 -> 6, of which waited for: 3 -> 4; matrix products, arithmetic and copies ran while one was open for 0% -> 0% of each run, Pallas kernels for 6% -> 6%
where the time goes in v11:
time: 17.6 us; the launch traced here: 17.4 us
  starting transfers between devices  9.05 us (51%)
  Pallas kernels  3.7 us (21%)
  waiting for transfers between devices  3.21 us (18%)
  between operations  0.74 us (4%)
  local copies, waits for them, and re-layouts  0.68 us (4%)
    ppermute x3, starting transfers between devices, local(): lax.ppermute(window, ('wide', 'pair'), [(p, t * pair + p % pair) for p, t...  7.13 us
    ppermute x3, starting transfers between devices, send_both(): return lax.ppermute(block, ('narrow', 'pair'), route)  1.92 us
    ppermute x3, waiting for transfers between devices, send_both(): return lax.ppermute(block, ('narrow', 'pair'), route)  1.81 us
    ppermute x3, waiting for transfers between devices, local(): lax.ppermute(window, ('wide', 'pair'), [(p, t * pair + p % pair) for p, t...  1.4 us
    pallas_call x1, Pallas kernels, local(): call(functools.partial(pack_kernel, routes), [shape((size, lanes), BF16)]...  1.21 us
    pallas_call x1, Pallas kernels, local(): call(functools.partial(prepare_kernel, wide, own_out, groups), [shape((2...  0.87 us
    pallas_call x1, Pallas kernels, local(): call(functools.partial(adjoint_kernel, shifts, own_out), [shape((sparse_c...  0.79 us
    pallas_call x1, Pallas kernels, local(): call(functools.partial(net_kernel, routes, own_out, groups), [shape((2 *...  0.7 us
  transfers between devices with their start and end apart: 6, of which 4 were waited for; matrix products, arithmetic and copies ran while one was open for 0% of the time, Pallas kernels for 6%

profile of v11, /device:TPU:0, one launch (start us, length us, event | category | flops | bytes accessed | tf_op | source)
XLA Modules:
  0.0 17.4 jit_solution(9954660146010085197)
XLA Ops:
  0.6 0.0 copy-start.1
  0.6 0.0 copy-start.2
  0.7 0.0 copy-start.3
  0.7 1.2 %shard_map.104 = (bf16[240,128]{1,0:T(8,128)(2,1)S(1)}, bf16[240,128]{1,0:T(8,128)(2,1)S(1)}, bf16[240,128]{1,0:T(8,128)(2,1)S(1)}, bf16[240,128]{1,0:T(8,128)(2,1)S(1)}) custom-call(bf16[1,24,32,128]{3,2,1,0:T(8,128)(2,1)} %low_ref.1), custom_call_target="tpu_custom_call" | custom-call | flops 1000000 | bytes 245760 | tf_op jit(solution)/shard_map/pallas_call | solution.py:290
  1.9 3.1 %collective-permute-start = (bf16[240,128]{1,0:T(8,128)(2,1)S(1)}, bf16[240,128]{1,0:T(8,128)(2,1)S(1)}, u32[]{:S(2)}, u32[]{:S(2)}) collective-permute-start(bf16[240,128]{1,0:T(8,128)(2,1)S(1)} %get-tuple-element.19), channel_id=1, source_target_pairs={{0,4},{1,9},{4,12},{5,13},{8,0},{9,5},{12,8},{13,1},{2,6},{3,11},{... | collective-permute-start | bytes 184328 | tf_op jit(solution)/shard_map/ppermute | solution.py:302
  5.0 2.5 %collective-permute-start.1 = (bf16[240,128]{1,0:T(8,128)(2,1)S(1)}, bf16[240,128]{1,0:T(8,128)(2,1)S(1)}, u32[]{:S(2)}, u32[]{:S(2)}) collective-permute-start(bf16[240,128]{1,0:T(8,128)(2,1)S(1)} %get-tuple-element.20), channel_id=1, source_target_pairs={{0,12},{1,13},{4,8},{5,9},{8,4},{9,1},{12,0},{13,5},{2,14},{3,15},... | collective-permute-start | bytes 184328 | tf_op jit(solution)/shard_map/ppermute | solution.py:302
  7.4 1.6 %collective-permute-start.2 = (bf16[240,128]{1,0:T(8,128)(2,1)S(1)}, bf16[240,128]{1,0:T(8,128)(2,1)S(1)}, u32[]{:S(2)}, u32[]{:S(2)}) collective-permute-start(bf16[240,128]{1,0:T(8,128)(2,1)S(1)} %get-tuple-element.21), channel_id=1, source_target_pairs={{0,8},{1,5},{4,0},{5,1},{8,12},{9,13},{12,4},{13,9},{2,10},{3,7},{... | collective-permute-start | bytes 184328 | tf_op jit(solution)/shard_map/ppermute | solution.py:302
  9.0 0.0 copy-start.7
  9.0 0.0 copy-start.5
  9.0 0.0 copy-start.6
  9.0 0.0 copy-done.1
  9.0 0.0 copy-done.2
  9.0 0.0 copy-done.3
  9.0 0.6 %copy-done.7 = s32[1,16]{1,0:T(1,128)S(1)} copy-done((s32[1,16]{1,0:T(1,128)S(1)}, s32[1,16]{1,0:T(1,128)}, u32[]{:S(2)}) %copy-start.7) | copy-done | bytes 88
  9.7 0.0 copy-done.4
  9.7 0.0 copy-done.5
  9.7 0.0 copy-done.6
  9.7 0.9 %shard_map.105 = (bf16[96,96]{1,0:T(8,128)(2,1)S(1)}, bf16[192,192]{1,0:T(8,128)(2,1)S(1)}, bf16[96,240]{1,0:T(8,128)(2,1)S(1)}, f32[240,128]{1,0:T(8,128)S(1)},...) custom-call(bf16[4,24,24]{2,1,0:T(8,128)(2,1)S(1)} %copy-done.2, ...), custom_call_target="tpu_custom_call" | custom-call | flops 1000000 | bytes 424960 | tf_op jit(solution)/shard_map/pallas_call | solution.py:307
  10.6 0.0 collective-permute-done.refs_1_
  10.6 1.0 %collective-permute-done.1.refs_2_ = bf16[240,128]{1,0:T(8,128)(2,1)S(1)} collective-permute-done((bf16[240,128]{1,0:T(8,128)(2,1)S(1)}, bf16[240,128]{1,0:T(8,128)(2,1)S(1)}, u32[]{:S(2)}, u32[]{:S(2)}) %collective-permute-start.1) | collective-permute-done | bytes 61472 | tf_op jit(solution)/shard_map/ppermute | solution.py:302
  11.6 0.4 %collective-permute-done.2.refs_3_ = bf16[240,128]{1,0:T(8,128)(2,1)S(1)} collective-permute-done((bf16[240,128]{1,0:T(8,128)(2,1)S(1)}, bf16[240,128]{1,0:T(8,128)(2,1)S(1)}, u32[]{:S(2)}, u32[]{:S(2)}) %collective-permute-start.2) | collective-permute-done | bytes 61472 | tf_op jit(solution)/shard_map/ppermute | solution.py:302
  12.0 0.0 copy-start
  12.0 0.7 %shard_map.106 = (f32[8,4,128]{2,1,0:T(4,128)S(1)}, bf16[64,128]{1,0:T(8,128)(2,1)S(1)}) custom-call(bf16[240,128]{1,0:T(8,128)(2,1)S(1)} %get-tuple-element.18.refs_0_, bf16[240,128]{1,0:T(8,128)(2,1)S(1)} %collective-permute-done.refs_1_, bf16[240,128]{1,0:T(8,128)(2,1)S(1)} %collective-permute-done.1.refs_2_, ...), custom_call_target="tpu_custom_call" | custom-call | flops 1000000 | bytes 32768 | tf_op jit(solution)/shard_map/pallas_call | solution.py:323
  12.7 0.1 collective-permute-start.5
  12.8 1.6 %collective-permute-start.4 = (bf16[64,128]{1,0:T(8,128)(2,1)S(1)}, bf16[64,128]{1,0:T(8,128)(2,1)S(1)}, u32[]{:S(2)}, u32[]{:S(2)}) collective-permute-start(bf16[64,128]{1,0:T(8,128)(2,1)S(1)} %get-tuple-element.30._.refs_0_), channel_id=1, source_target_pairs={{0,2},{1,3},{2,0},{3,1},{4,6},{5,7},{6,4},{7,5},{8,10},{9,11},{10,... | collective-permute-start | bytes 49160 | tf_op jit(solution)/shard_map/ppermute | solution.py:254
  14.3 0.3 %collective-permute-start.3 = (bf16[64,128]{1,0:T(8,128)(2,1)S(1)}, bf16[64,128]{1,0:T(8,128)(2,1)S(1)}, u32[]{:S(2)}, u32[]{:S(2)}) collective-permute-start(bf16[64,128]{1,0:T(8,128)(2,1)S(1)} %get-tuple-element.30._.refs_0_), channel_id=1, source_target_pairs={{0,1},{1,0},{2,3},{3,2},{4,5},{5,4},{6,7},{7,6},{8,9},{9,8},{10,11... | collective-permute-start | bytes 49160 | tf_op jit(solution)/shard_map/ppermute | solution.py:254
  14.6 0.0 copy-done
  14.6 0.1 shard_map.107.refs_4_
  14.8 1.3 %collective-permute-done.5.refs_3_ = bf16[64,128]{1,0:T(8,128)(2,1)S(1)} collective-permute-done((bf16[64,128]{1,0:T(8,128)(2,1)S(1)}, bf16[64,128]{1,0:T(8,128)(2,1)S(1)}, u32[]{:S(2)}, u32[]{:S(2)}) %collective-permute-start.5) | collective-permute-done | bytes 16416 | tf_op jit(solution)/shard_map/ppermute | solution.py:254
  16.0 0.5 %collective-permute-done.4.refs_2_ = bf16[64,128]{1,0:T(8,128)(2,1)S(1)} collective-permute-done((bf16[64,128]{1,0:T(8,128)(2,1)S(1)}, bf16[64,128]{1,0:T(8,128)(2,1)S(1)}, u32[]{:S(2)}, u32[]{:S(2)}) %collective-permute-start.4) | collective-permute-done | bytes 16416 | tf_op jit(solution)/shard_map/ppermute | solution.py:254
  16.6 0.0 collective-permute-done.3.refs_1_
  16.6 0.8 %shard_map.108 = (f32[16,4,128]{2,1,0:T(4,128)}, f32[8,4,128]{2,1,0:T(4,128)}) custom-call(bf16[64,128]{1,0:T(8,128)(2,1)S(1)} %get-tuple-element.30._.refs_0_, bf16[64,128]{1,0:T(8,128)(2,1)S(1)} %collective-permute-done.3.refs_1_, bf16[64,128]{1,0:T(8,128)(2,1)S(1)} %collective-permute-done.4.refs_2_, bf16[64,128]{1,0:T(8,128)(2,1)S(1)} %collective-permute-done.5.refs_3_, ...), custom_call_target="tpu_custom_call" | custom-call | flops 1000000 | bytes 49152 | tf_op jit(solution)/shard_map/pallas_call | solution.py:336
  (1 shorter events, 0.0 us)
Async XLA Ops:
  0.6 8.4 %copy-start.1 = (f32[16,4,128]{2,1,0:T(4,128)S(1)}, f32[16,4,128]{2,1,0:T(4,128)}, u32[]{:S(2)}) copy-start(f32[16,4,128]{2,1,0:T(4,128)} %measured_ref.1) | copy-start | bytes 98308
  0.6 8.4 %copy-start.2 = (bf16[4,24,24]{2,1,0:T(8,128)(2,1)S(1)}, bf16[4,24,24]{2,1,0:T(8,128)(2,1)}, u32[]{:S(2)}) copy-start(bf16[4,24,24]{2,1,0:T(8,128)(2,1)} %aw_ref.1) | copy-start | bytes 13828
  0.7 8.4 %copy-start.3 = (bf16[4,24,24]{2,1,0:T(8,128)(2,1)S(1)}, bf16[4,24,24]{2,1,0:T(8,128)(2,1)}, u32[]{:S(2)}) copy-start(bf16[4,24,24]{2,1,0:T(8,128)(2,1)} %cw_ref.1) | copy-start | bytes 13828
  1.9 8.7 %collective-permute-start = (bf16[240,128]{1,0:T(8,128)(2,1)S(1)}, bf16[240,128]{1,0:T(8,128)(2,1)S(1)}, u32[]{:S(2)}, u32[]{:S(2)}) collective-permute-start(bf16[240,128]{1,0:T(8,128)(2,1)S(1)} %get-tuple-element.19), channel_id=1, source_target_pairs={{0,4},{1,9},{4,12},{5,13},{8,0},{9,5},{12,8},{13,1},{2,6},{3,11},{... | collective-permute-start | bytes 184328 | tf_op jit(solution)/shard_map/ppermute | solution.py:302
  5.0 6.7 %collective-permute-start.1 = (bf16[240,128]{1,0:T(8,128)(2,1)S(1)}, bf16[240,128]{1,0:T(8,128)(2,1)S(1)}, u32[]{:S(2)}, u32[]{:S(2)}) collective-permute-start(bf16[240,128]{1,0:T(8,128)(2,1)S(1)} %get-tuple-element.20), channel_id=1, source_target_pairs={{0,12},{1,13},{4,8},{5,9},{8,4},{9,1},{12,0},{13,5},{2,14},{3,15},... | collective-permute-start | bytes 184328 | tf_op jit(solution)/shard_map/ppermute | solution.py:302
  7.4 4.6 %collective-permute-start.2 = (bf16[240,128]{1,0:T(8,128)(2,1)S(1)}, bf16[240,128]{1,0:T(8,128)(2,1)S(1)}, u32[]{:S(2)}, u32[]{:S(2)}) collective-permute-start(bf16[240,128]{1,0:T(8,128)(2,1)S(1)} %get-tuple-element.21), channel_id=1, source_target_pairs={{0,8},{1,5},{4,0},{5,1},{8,12},{9,13},{12,4},{13,9},{2,10},{3,7},{... | collective-permute-start | bytes 184328 | tf_op jit(solution)/shard_map/ppermute | solution.py:302
  9.0 0.7 %copy-start.7 = (s32[1,16]{1,0:T(1,128)S(1)}, s32[1,16]{1,0:T(1,128)}, u32[]{:S(2)}) copy-start(s32[1,16]{1,0:T(1,128)} %sparse_ref.1) | copy-start | bytes 196
  9.0 0.7 %copy-start.4 = (f32[24]{0:T(128)S(1)}, f32[24]{0:T(128)}, u32[]{:S(2)}) copy-start(f32[24]{0:T(128)} %param.11) | copy-start | bytes 292
  9.0 0.7 %copy-start.5 = (f32[24]{0:T(128)S(1)}, f32[24]{0:T(128)}, u32[]{:S(2)}) copy-start(f32[24]{0:T(128)} %param.13) | copy-start | bytes 292
  9.0 0.7 %copy-start.6 = (f32[24]{0:T(128)S(1)}, f32[24]{0:T(128)}, u32[]{:S(2)}) copy-start(f32[24]{0:T(128)} %param.14) | copy-start | bytes 292
  12.0 2.6 %copy-start = (f32[128,512]{1,0:T(8,128)S(1)}, f32[128,512]{1,0:T(8,128)}, u32[]{:S(2)}) copy-start(f32[128,512]{1,0:T(8,128)} %rw_ref.1) | copy-start | bytes 786436
  12.7 3.4 %collective-permute-start.5 = (bf16[64,128]{1,0:T(8,128)(2,1)S(1)}, bf16[64,128]{1,0:T(8,128)(2,1)S(1)}, u32[]{:S(2)}, u32[]{:S(2)}) collective-permute-start(bf16[64,128]{1,0:T(8,128)(2,1)S(1)} %get-tuple-element.30._.refs_0_), channel_id=1, source_target_pairs={{0,3},{1,2},{2,1},{3,0},{4,7},{5,6},{6,5},{7,4},{8,11},{9,10},{10,... | collective-permute-start | bytes 49160 | tf_op jit(solution)/shard_map/ppermute | solution.py:254
  12.8 3.8 %collective-permute-start.4 = (bf16[64,128]{1,0:T(8,128)(2,1)S(1)}, bf16[64,128]{1,0:T(8,128)(2,1)S(1)}, u32[]{:S(2)}, u32[]{:S(2)}) collective-permute-start(bf16[64,128]{1,0:T(8,128)(2,1)S(1)} %get-tuple-element.30._.refs_0_), channel_id=1, source_target_pairs={{0,2},{1,3},{2,0},{3,1},{4,6},{5,7},{6,4},{7,5},{8,10},{9,11},{10,... | collective-permute-start | bytes 49160 | tf_op jit(solution)/shard_map/ppermute | solution.py:254
  14.3 2.2 %collective-permute-start.3 = (bf16[64,128]{1,0:T(8,128)(2,1)S(1)}, bf16[64,128]{1,0:T(8,128)(2,1)S(1)}, u32[]{:S(2)}, u32[]{:S(2)}) collective-permute-start(bf16[64,128]{1,0:T(8,128)(2,1)S(1)} %get-tuple-element.30._.refs_0_), channel_id=1, source_target_pairs={{0,1},{1,0},{2,3},{3,2},{4,5},{5,4},{6,7},{7,6},{8,9},{9,8},{10,11... | collective-permute-start | bytes 49160 | tf_op jit(solution)/shard_map/ppermute | solution.py:254

commit v12 on v11

--- a/solution.py
+++ b/solution.py
@@ -75,26 +75,25 @@
 def pack_kernel(routes, low_ref, *refs):
     windows, (block_ref, rows_ref, sems) = refs[: len(routes) + 1], refs[len(routes) + 1 :]
     _, channels, width, rows = low_ref.shape
-    parts = sems.shape[0]
-    each = channels // parts
-    pieces = []
-    for i in range(parts):
-        piece = pl.ds(i * each, each)
-        pieces.append(pltpu.make_async_copy(low_ref.at[0, piece], block_ref.at[piece], sems.at[i]))
-        pieces[-1].start()
+    own = width // (len(routes) + 1)
+    span = own + 2
+    copies = []
+    for g in range(channels // 8):
+        group = pl.ds(8 * g, 8)
+        copies.append(pltpu.make_async_copy(low_ref.at[0, group], block_ref.at[group], sems.at[g]))
+        copies[-1].start()
+    me = lax.axis_index("wide")
+    firsts = [target * own + 7 for target in [me] + [entry(route, ("wide", "pair")) for route in routes]]
     edge = jnp.zeros((8, rows), F32)
-    rows_ref[0:8, :] = edge
-    rows_ref[8 + channels * width : 16 + channels * width, :] = edge
-    for i in range(parts):
-        pieces[i].wait()
-        values = block_ref[i * each : (i + 1) * each].astype(F32).reshape(each * width, rows)
-        rows_ref[8 + i * each * width : 8 + (i + 1) * each * width, :] = values
-    own = width // (len(routes) + 1)
-    me = lax.axis_index("wide")
-    for window, target in zip(windows, [me] + [entry(route, ("wide", "pair")) for route in routes]):
-        first = target * own + 7
-        columns = [rows_ref[pl.ds(first + i, channels, stride=width), :] for i in range(own + 2)]
-        window[...] = jnp.concatenate(columns, axis=0).astype(BF16)
+    for g, copy in enumerate(copies):
+        rows_ref[g, 0:8, :] = edge
+        rows_ref[g, 8 + 8 * width : 16 + 8 * width, :] = edge
+        copy.wait()
+        values = block_ref[8 * g : 8 * g + 8].astype(F32).reshape(8 * width, rows)
+        rows_ref[g, 8 : 8 + 8 * width, :] = values
+        for window, first in zip(windows, firsts):
+            columns = [rows_ref[g, pl.ds(first + i, 8, stride=width), :] for i in range(span)]
+            window[8 * g * span : 8 * (g + 1) * span, :] = jnp.concatenate(columns, axis=0).astype(BF16)
 
 
 def prepare_kernel(
@@ -128,13 +127,17 @@
     for first_ref in firsts:
         many = first_ref.shape[0] // 2
         taken = many // channels
-        which, channel = split(iota((2 * many, channels), 0), channels)
+
+        def place(shape, axis):
+            side, within = split(iota(shape, axis), many)
+            group, within = split(within, 8 * taken)
+            column, channel = split(within, 8)
+            return side, column, 8 * group + channel
+
+        side, _, channel = place((2 * many, channels), 0)
         is_channel = channel == iota((2 * many, channels), 1)
-        sides = [is_channel & (which >= side * taken) & (which < (side + 1) * taken) for side in range(2)]
-        sides = [side.astype(F32).astype(BF16) for side in sides]
-        row_column = split(iota((many, 2 * many), 0), channels)[0]
-        column_column = split(iota((many, 2 * many), 1), channels)[0]
-        same = (row_column == column_column) | (row_column + taken == column_column)
+        sides = [(is_channel & (side == i)).astype(F32).astype(BF16) for i in range(2)]
+        same = split(iota((many, 2 * many), 0), channels)[0] == place((many, 2 * many), 1)[1]
         for e in range(2):
             full = spread(pick16[:many], aw_ref[e], sides[0]) + spread(pick16[:many], aw_ref[e + 2], sides[1])
             first_ref[e * many : (e + 1) * many, :] = jnp.where(same, full, 0.0).astype(BF16)
@@ -180,6 +183,7 @@
     size, lanes = windows[0].shape
     outs = a2_ref.shape[0]
     channels = outs // own_out
+    span = size // channels
     me = lax.axis_index("wide")
     cores = lax.axis_size("pair")
     origins = [me] + [entry(sources(route, cores), ("wide", "pair")) for route in routes]
@@ -200,7 +204,12 @@
         for (first, taken), first_ref in zip(groups, firsts):
             rows = slice(first * channels, (first + taken) * channels)
             half = taken * channels
-            stacked = jnp.concatenate([views_ref[rows, current], views_ref[rows, previous]], axis=0)
+            parts = [
+                views_ref[8 * (g * span + first) : 8 * (g * span + first + taken), lane]
+                for lane in (current, previous)
+                for g in range(channels // 8)
+            ]
+            stacked = jnp.concatenate(parts, axis=0)
             summed = jnp.dot(first_ref[...], stacked, preferred_element_type=F32)
             for e in range(2):
                 pieces[e].append(leaky_relu(summed[e * half : (e + 1) * half] + b1[rows]).astype(BF16))
@@ -293,8 +302,8 @@
         [pl.BlockSpec(memory_space=pltpu.HBM)],
         [
             pltpu.VMEM((channels, width, lanes), BF16),
-            pltpu.VMEM((16 + channels * width, lanes), F32),
-            pltpu.SemaphoreType.DMA((4,)),
+            pltpu.VMEM((channels // 8, 16 + 8 * width, lanes), F32),
+            pltpu.SemaphoreType.DMA((channels // 8,)),
         ],
         vmem=53.6 if width <= 64 else 48,
     )(low_sino)

time: 17.6 us -> 17.5 us (level)
  no operation moved by 1% of the time
where the time goes in v12:
time: 17.5 us; the launch traced here: 17.4 us
  starting transfers between devices  9.05 us (52%)
  Pallas kernels  3.71 us (21%)
  waiting for transfers between devices  3.19 us (18%)
  between operations  0.74 us (4%)
  local copies, waits for them, and re-layouts  0.68 us (4%)
    ppermute x3, starting transfers between devices, local(): lax.ppermute(window, ('wide', 'pair'), [(p, t * pair + p % pair) for p, t...  7.13 us
    ppermute x3, starting transfers between devices, send_both(): return lax.ppermute(block, ('narrow', 'pair'), route)  1.92 us
    ppermute x3, waiting for transfers between devices, send_both(): return lax.ppermute(block, ('narrow', 'pair'), route)  1.81 us
    ppermute x3, waiting for transfers between devices, local(): lax.ppermute(window, ('wide', 'pair'), [(p, t * pair + p % pair) for p, t...  1.37 us
    pallas_call x1, Pallas kernels, local(): call(functools.partial(pack_kernel, routes), [shape((size, lanes), BF16)]...  1.2 us
    pallas_call x1, Pallas kernels, local(): call(functools.partial(prepare_kernel, wide, own_out, groups), [shape((2...  0.89 us
    pallas_call x1, Pallas kernels, local(): call(functools.partial(adjoint_kernel, shifts, own_out), [shape((sparse_c...  0.79 us
    pallas_call x1, Pallas kernels, local(): call(functools.partial(net_kernel, routes, own_out, groups), [shape((2 *...  0.69 us
  transfers between devices with their start and end apart: 6, of which 4 were waited for; matrix products, arithmetic and copies ran while one was open for 0% of the time, Pallas kernels for 6%

profile of v12, /device:TPU:0, one launch (start us, length us, event | category | flops | bytes accessed | tf_op | source)
XLA Modules:
  0.0 17.4 jit_solution(403407558252194544)
XLA Ops:
  0.6 0.0 copy-start.1
  0.6 0.0 copy-start.2
  0.7 0.0 copy-start.3
  0.7 1.2 %shard_map.104 = (bf16[240,128]{1,0:T(8,128)(2,1)S(1)}, bf16[240,128]{1,0:T(8,128)(2,1)S(1)}, bf16[240,128]{1,0:T(8,128)(2,1)S(1)}, bf16[240,128]{1,0:T(8,128)(2,1)S(1)}) custom-call(bf16[1,24,32,128]{3,2,1,0:T(8,128)(2,1)} %low_ref.1), custom_call_target="tpu_custom_call" | custom-call | flops 1000000 | bytes 245760 | tf_op jit(solution)/shard_map/pallas_call | solution.py:299
  1.9 3.1 %collective-permute-start = (bf16[240,128]{1,0:T(8,128)(2,1)S(1)}, bf16[240,128]{1,0:T(8,128)(2,1)S(1)}, u32[]{:S(2)}, u32[]{:S(2)}) collective-permute-start(bf16[240,128]{1,0:T(8,128)(2,1)S(1)} %get-tuple-element.19), channel_id=1, source_target_pairs={{0,4},{1,9},{4,12},{5,13},{8,0},{9,5},{12,8},{13,1},{2,6},{3,11},{... | collective-permute-start | bytes 184328 | tf_op jit(solution)/shard_map/ppermute | solution.py:311
  4.9 2.5 %collective-permute-start.1 = (bf16[240,128]{1,0:T(8,128)(2,1)S(1)}, bf16[240,128]{1,0:T(8,128)(2,1)S(1)}, u32[]{:S(2)}, u32[]{:S(2)}) collective-permute-start(bf16[240,128]{1,0:T(8,128)(2,1)S(1)} %get-tuple-element.20), channel_id=1, source_target_pairs={{0,12},{1,13},{4,8},{5,9},{8,4},{9,1},{12,0},{13,5},{2,14},{3,15},... | collective-permute-start | bytes 184328 | tf_op jit(solution)/shard_map/ppermute | solution.py:311
  7.4 1.6 %collective-permute-start.2 = (bf16[240,128]{1,0:T(8,128)(2,1)S(1)}, bf16[240,128]{1,0:T(8,128)(2,1)S(1)}, u32[]{:S(2)}, u32[]{:S(2)}) collective-permute-start(bf16[240,128]{1,0:T(8,128)(2,1)S(1)} %get-tuple-element.21), channel_id=1, source_target_pairs={{0,8},{1,5},{4,0},{5,1},{8,12},{9,13},{12,4},{13,9},{2,10},{3,7},{... | collective-permute-start | bytes 184328 | tf_op jit(solution)/shard_map/ppermute | solution.py:311
  9.0 0.0 copy-start.7
  9.0 0.0 copy-start.4
  9.0 0.0 copy-start.5
  9.0 0.0 copy-done.1
  9.0 0.0 copy-done.2
  9.0 0.0 copy-done.3
  9.0 0.6 %copy-done.7 = s32[1,16]{1,0:T(1,128)S(1)} copy-done((s32[1,16]{1,0:T(1,128)S(1)}, s32[1,16]{1,0:T(1,128)}, u32[]{:S(2)}) %copy-start.7) | copy-done | bytes 88
  9.7 0.0 copy-done.4
  9.7 0.0 copy-done.5
  9.7 0.0 copy-done.6
  9.7 0.9 %shard_map.105 = (bf16[96,96]{1,0:T(8,128)(2,1)S(1)}, bf16[192,192]{1,0:T(8,128)(2,1)S(1)}, bf16[96,240]{1,0:T(8,128)(2,1)S(1)}, f32[240,128]{1,0:T(8,128)S(1)},...) custom-call(bf16[4,24,24]{2,1,0:T(8,128)(2,1)S(1)} %copy-done.2, ...), custom_call_target="tpu_custom_call" | custom-call | flops 1000000 | bytes 424960 | tf_op jit(solution)/shard_map/pallas_call | solution.py:316
  10.6 0.0 collective-permute-done.refs_1_
  10.6 1.0 %collective-permute-done.1.refs_2_ = bf16[240,128]{1,0:T(8,128)(2,1)S(1)} collective-permute-done((bf16[240,128]{1,0:T(8,128)(2,1)S(1)}, bf16[240,128]{1,0:T(8,128)(2,1)S(1)}, u32[]{:S(2)}, u32[]{:S(2)}) %collective-permute-start.1) | collective-permute-done | bytes 61472 | tf_op jit(solution)/shard_map/ppermute | solution.py:311
  11.6 0.4 %collective-permute-done.2.refs_3_ = bf16[240,128]{1,0:T(8,128)(2,1)S(1)} collective-permute-done((bf16[240,128]{1,0:T(8,128)(2,1)S(1)}, bf16[240,128]{1,0:T(8,128)(2,1)S(1)}, u32[]{:S(2)}, u32[]{:S(2)}) %collective-permute-start.2) | collective-permute-done | bytes 61472 | tf_op jit(solution)/shard_map/ppermute | solution.py:311
  12.0 0.0 copy-start
  12.0 0.7 %shard_map.106 = (f32[8,4,128]{2,1,0:T(4,128)S(1)}, bf16[64,128]{1,0:T(8,128)(2,1)S(1)}) custom-call(bf16[240,128]{1,0:T(8,128)(2,1)S(1)} %get-tuple-element.18.refs_0_, bf16[240,128]{1,0:T(8,128)(2,1)S(1)} %collective-permute-done.refs_1_, bf16[240,128]{1,0:T(8,128)(2,1)S(1)} %collective-permute-done.1.refs_2_, ...), custom_call_target="tpu_custom_call" | custom-call | flops 1000000 | bytes 32768 | tf_op jit(solution)/shard_map/pallas_call | solution.py:332
  12.7 0.1 collective-permute-start.5
  12.8 1.6 %collective-permute-start.4 = (bf16[64,128]{1,0:T(8,128)(2,1)S(1)}, bf16[64,128]{1,0:T(8,128)(2,1)S(1)}, u32[]{:S(2)}, u32[]{:S(2)}) collective-permute-start(bf16[64,128]{1,0:T(8,128)(2,1)S(1)} %get-tuple-element.30._.refs_0_), channel_id=1, source_target_pairs={{0,2},{1,3},{2,0},{3,1},{4,6},{5,7},{6,4},{7,5},{8,10},{9,11},{10,... | collective-permute-start | bytes 49160 | tf_op jit(solution)/shard_map/ppermute | solution.py:263
  14.3 0.3 %collective-permute-start.3 = (bf16[64,128]{1,0:T(8,128)(2,1)S(1)}, bf16[64,128]{1,0:T(8,128)(2,1)S(1)}, u32[]{:S(2)}, u32[]{:S(2)}) collective-permute-start(bf16[64,128]{1,0:T(8,128)(2,1)S(1)} %get-tuple-element.30._.refs_0_), channel_id=1, source_target_pairs={{0,1},{1,0},{2,3},{3,2},{4,5},{5,4},{6,7},{7,6},{8,9},{9,8},{10,11... | collective-permute-start | bytes 49160 | tf_op jit(solution)/shard_map/ppermute | solution.py:263
  14.6 0.0 copy-done
  14.6 0.1 shard_map.107.refs_4_
  14.8 1.3 %collective-permute-done.5.refs_3_ = bf16[64,128]{1,0:T(8,128)(2,1)S(1)} collective-permute-done((bf16[64,128]{1,0:T(8,128)(2,1)S(1)}, bf16[64,128]{1,0:T(8,128)(2,1)S(1)}, u32[]{:S(2)}, u32[]{:S(2)}) %collective-permute-start.5) | collective-permute-done | bytes 16416 | tf_op jit(solution)/shard_map/ppermute | solution.py:263
  16.0 0.5 %collective-permute-done.4.refs_2_ = bf16[64,128]{1,0:T(8,128)(2,1)S(1)} collective-permute-done((bf16[64,128]{1,0:T(8,128)(2,1)S(1)}, bf16[64,128]{1,0:T(8,128)(2,1)S(1)}, u32[]{:S(2)}, u32[]{:S(2)}) %collective-permute-start.4) | collective-permute-done | bytes 16416 | tf_op jit(solution)/shard_map/ppermute | solution.py:263
  16.6 0.0 collective-permute-done.3.refs_1_
  16.6 0.8 %shard_map.108 = (f32[16,4,128]{2,1,0:T(4,128)}, f32[8,4,128]{2,1,0:T(4,128)}) custom-call(bf16[64,128]{1,0:T(8,128)(2,1)S(1)} %get-tuple-element.30._.refs_0_, bf16[64,128]{1,0:T(8,128)(2,1)S(1)} %collective-permute-done.3.refs_1_, bf16[64,128]{1,0:T(8,128)(2,1)S(1)} %collective-permute-done.4.refs_2_, bf16[64,128]{1,0:T(8,128)(2,1)S(1)} %collective-permute-done.5.refs_3_, ...), custom_call_target="tpu_custom_call" | custom-call | flops 1000000 | bytes 49152 | tf_op jit(solution)/shard_map/pallas_call | solution.py:345
  (1 shorter events, 0.0 us)
Async XLA Ops:
  0.6 8.4 %copy-start.1 = (f32[16,4,128]{2,1,0:T(4,128)S(1)}, f32[16,4,128]{2,1,0:T(4,128)}, u32[]{:S(2)}) copy-start(f32[16,4,128]{2,1,0:T(4,128)} %measured_ref.1) | copy-start | bytes 98308
  0.6 8.4 %copy-start.2 = (bf16[4,24,24]{2,1,0:T(8,128)(2,1)S(1)}, bf16[4,24,24]{2,1,0:T(8,128)(2,1)}, u32[]{:S(2)}) copy-start(bf16[4,24,24]{2,1,0:T(8,128)(2,1)} %aw_ref.1) | copy-start | bytes 13828
  0.7 8.4 %copy-start.3 = (bf16[4,24,24]{2,1,0:T(8,128)(2,1)S(1)}, bf16[4,24,24]{2,1,0:T(8,128)(2,1)}, u32[]{:S(2)}) copy-start(bf16[4,24,24]{2,1,0:T(8,128)(2,1)} %cw_ref.1) | copy-start | bytes 13828
  1.9 8.7 %collective-permute-start = (bf16[240,128]{1,0:T(8,128)(2,1)S(1)}, bf16[240,128]{1,0:T(8,128)(2,1)S(1)}, u32[]{:S(2)}, u32[]{:S(2)}) collective-permute-start(bf16[240,128]{1,0:T(8,128)(2,1)S(1)} %get-tuple-element.19), channel_id=1, source_target_pairs={{0,4},{1,9},{4,12},{5,13},{8,0},{9,5},{12,8},{13,1},{2,6},{3,11},{... | collective-permute-start | bytes 184328 | tf_op jit(solution)/shard_map/ppermute | solution.py:311
  4.9 6.7 %collective-permute-start.1 = (bf16[240,128]{1,0:T(8,128)(2,1)S(1)}, bf16[240,128]{1,0:T(8,128)(2,1)S(1)}, u32[]{:S(2)}, u32[]{:S(2)}) collective-permute-start(bf16[240,128]{1,0:T(8,128)(2,1)S(1)} %get-tuple-element.20), channel_id=1, source_target_pairs={{0,12},{1,13},{4,8},{5,9},{8,4},{9,1},{12,0},{13,5},{2,14},{3,15},... | collective-permute-start | bytes 184328 | tf_op jit(solution)/shard_map/ppermute | solution.py:311
  7.4 4.6 %collective-permute-start.2 = (bf16[240,128]{1,0:T(8,128)(2,1)S(1)}, bf16[240,128]{1,0:T(8,128)(2,1)S(1)}, u32[]{:S(2)}, u32[]{:S(2)}) collective-permute-start(bf16[240,128]{1,0:T(8,128)(2,1)S(1)} %get-tuple-element.21), channel_id=1, source_target_pairs={{0,8},{1,5},{4,0},{5,1},{8,12},{9,13},{12,4},{13,9},{2,10},{3,7},{... | collective-permute-start | bytes 184328 | tf_op jit(solution)/shard_map/ppermute | solution.py:311
  9.0 0.7 %copy-start.7 = (s32[1,16]{1,0:T(1,128)S(1)}, s32[1,16]{1,0:T(1,128)}, u32[]{:S(2)}) copy-start(s32[1,16]{1,0:T(1,128)} %sparse_ref.1) | copy-start | bytes 196
  9.0 0.7 %copy-start.4 = (f32[24]{0:T(128)S(1)}, f32[24]{0:T(128)}, u32[]{:S(2)}) copy-start(f32[24]{0:T(128)} %param.11) | copy-start | bytes 292
  9.0 0.7 %copy-start.5 = (f32[24]{0:T(128)S(1)}, f32[24]{0:T(128)}, u32[]{:S(2)}) copy-start(f32[24]{0:T(128)} %param.13) | copy-start | bytes 292
  9.0 0.7 %copy-start.6 = (f32[24]{0:T(128)S(1)}, f32[24]{0:T(128)}, u32[]{:S(2)}) copy-start(f32[24]{0:T(128)} %param.14) | copy-start | bytes 292
  12.0 2.6 %copy-start = (f32[128,512]{1,0:T(8,128)S(1)}, f32[128,512]{1,0:T(8,128)}, u32[]{:S(2)}) copy-start(f32[128,512]{1,0:T(8,128)} %rw_ref.1) | copy-start | bytes 786436
  12.7 3.4 %collective-permute-start.5 = (bf16[64,128]{1,0:T(8,128)(2,1)S(1)}, bf16[64,128]{1,0:T(8,128)(2,1)S(1)}, u32[]{:S(2)}, u32[]{:S(2)}) collective-permute-start(bf16[64,128]{1,0:T(8,128)(2,1)S(1)} %get-tuple-element.30._.refs_0_), channel_id=1, source_target_pairs={{0,3},{1,2},{2,1},{3,0},{4,7},{5,6},{6,5},{7,4},{8,11},{9,10},{10,... | collective-permute-start | bytes 49160 | tf_op jit(solution)/shard_map/ppermute | solution.py:263
  12.8 3.8 %collective-permute-start.4 = (bf16[64,128]{1,0:T(8,128)(2,1)S(1)}, bf16[64,128]{1,0:T(8,128)(2,1)S(1)}, u32[]{:S(2)}, u32[]{:S(2)}) collective-permute-start(bf16[64,128]{1,0:T(8,128)(2,1)S(1)} %get-tuple-element.30._.refs_0_), channel_id=1, source_target_pairs={{0,2},{1,3},{2,0},{3,1},{4,6},{5,7},{6,4},{7,5},{8,10},{9,11},{10,... | collective-permute-start | bytes 49160 | tf_op jit(solution)/shard_map/ppermute | solution.py:263
  14.3 2.2 %collective-permute-start.3 = (bf16[64,128]{1,0:T(8,128)(2,1)S(1)}, bf16[64,128]{1,0:T(8,128)(2,1)S(1)}, u32[]{:S(2)}, u32[]{:S(2)}) collective-permute-start(bf16[64,128]{1,0:T(8,128)(2,1)S(1)} %get-tuple-element.30._.refs_0_), channel_id=1, source_target_pairs={{0,1},{1,0},{2,3},{3,2},{4,5},{5,4},{6,7},{7,6},{8,9},{9,8},{10,11... | collective-permute-start | bytes 49160 | tf_op jit(solution)/shard_map/ppermute | solution.py:263

commit v13 on v11

--- a/solution.py
+++ b/solution.py
@@ -173,59 +173,98 @@
     turned_ref[:, high.shape[1] :] = (turned - high.astype(F32)).astype(BF16)
 
 
-def net_kernel(routes, own_out, groups, *refs):
-    wide = len(routes) + 1
-    windows, firsts, refs = refs[:wide], refs[wide : wide + len(groups)], refs[wide + len(groups) :]
-    a2_ref, b1_ref, b2_ref, h_ref, select_ref, target_ref, predicted_ref, residual_ref, views_ref = refs
-    size, lanes = windows[0].shape
+def origin(route):
+    return entry(sources(route, lax.axis_size("pair")), ("wide", "pair"))
+
+
+def first_and_second_layer(current, previous, groups, firsts, a2_ref, b1, b2, h, own_out):
     outs = a2_ref.shape[0]
     channels = outs // own_out
+    pieces = ([], [])
+    for (first, taken), first_ref in zip(groups, firsts):
+        rows = slice(first * channels, (first + taken) * channels)
+        half = taken * channels
+        stacked = jnp.concatenate([current[rows], previous[rows]], axis=0)
+        summed = jnp.dot(first_ref[...], stacked, preferred_element_type=F32)
+        for e in range(2):
+            pieces[e].append(leaky_relu(summed[e * half : (e + 1) * half] + b1[rows]).astype(BF16))
+    both = jnp.concatenate([jnp.concatenate(piece, axis=0) for piece in pieces], axis=1)
+    hidden = leaky_relu(jnp.dot(a2_ref[...], both, preferred_element_type=F32) + b2) * h
+    value = jnp.sum(hidden.reshape(outs // 8, 8, hidden.shape[1]), axis=0)
+    apart = own_out
+    while apart < 8:
+        value += pltpu.roll(value, apart, 0)
+        apart *= 2
+    return value
+
+
+def wider(ref, times):
+    return jnp.concatenate([ref[...]] * times, axis=1)
+
+
+def choose(select, view, tile, picked):
+    repeated = jnp.concatenate([tile] * (select.shape[0] // 8), axis=0)
+    return jnp.where(select == view.astype(F32), repeated, picked)
+
+
+def early_kernel(routes, own_out, groups, *refs):
+    wide = len(routes) + 1
+    windows, firsts, refs = refs[: wide - 1], refs[wide - 1 : wide - 1 + len(groups)], refs[wide - 1 + len(groups) :]
+    a2_ref, b1_ref, b2_ref, h_ref, select_ref, tiles_ref, picked_ref, next_ref, before_ref, views_ref = refs
+    lanes = windows[0].shape[1]
     me = lax.axis_index("wide")
-    cores = lax.axis_size("pair")
-    origins = [me] + [entry(sources(route, cores), ("wide", "pair")) for route in routes]
-    for window, source in zip(windows, origins):
-        views_ref[:, pl.ds(pl.multiple_of((source + 1) * lanes, lanes), lanes)] = window[...]
-    views_ref[:, :lanes] = views_ref[:, wide * lanes :]
-
+    missing = origin(routes[-1])
+    for window, source in zip(windows, [me] + [origin(route) for route in routes[:-1]]):
+        slot = lax.rem(source - missing + wide, wide) - 1
+        views_ref[:, pl.ds(pl.multiple_of(slot * lanes, lanes), lanes)] = window[...]
+    next_ref[...] = views_ref[:, :lanes]
+    before_ref[...] = views_ref[:, (wide - 2) * lanes :]
     many = 2 if wide % 2 == 0 else 1
-    wider = lambda ref, times: jnp.concatenate([ref[...]] * times, axis=1)
-    b1 = wider(b1_ref, many)
-    b2, h = wider(b2_ref, 2 * many), wider(h_ref, 2 * many)
+    b1, b2, h = wider(b1_ref, many), wider(b2_ref, 2 * many), wider(h_ref, 2 * many)
     select = select_ref[...]
     picked = jnp.zeros(select.shape, F32)
-    for view in range(0, wide, many):
-        previous = slice(view * lanes, (view + many) * lanes)
-        current = slice((view + 1) * lanes, (view + 1 + many) * lanes)
-        pieces = ([], [])
-        for (first, taken), first_ref in zip(groups, firsts):
-            rows = slice(first * channels, (first + taken) * channels)
-            half = taken * channels
-            stacked = jnp.concatenate([views_ref[rows, current], views_ref[rows, previous]], axis=0)
-            summed = jnp.dot(first_ref[...], stacked, preferred_element_type=F32)
-            for e in range(2):
-                pieces[e].append(leaky_relu(summed[e * half : (e + 1) * half] + b1[rows]).astype(BF16))
-        both = jnp.concatenate([jnp.concatenate(piece, axis=0) for piece in pieces], axis=1)
-        hidden = leaky_relu(jnp.dot(a2_ref[...], both, preferred_element_type=F32) + b2) * h
-        value = jnp.sum(hidden.reshape(outs // 8, 8, hidden.shape[1]), axis=0)
-        apart = own_out
-        while apart < 8:
-            value += pltpu.roll(value, apart, 0)
-            apart *= 2
+    for pair in range(0, wide - 2, many):
+        previous = views_ref[:, pair * lanes : (pair + many) * lanes]
+        current = views_ref[:, (pair + 1) * lanes : (pair + 1 + many) * lanes]
+        value = first_and_second_layer(current, previous, groups, firsts, a2_ref, b1, b2, h, own_out)
         for e in range(2):
             for i in range(many):
-                out_view = 2 * (view + i) + e
-                at = (e * many + i) * lanes
-                tile = value[:, at : at + lanes]
-                predicted_ref[out_view] = tile[:own_out]
-                repeated = jnp.concatenate([tile] * (select.shape[0] // 8), axis=0)
-                picked = jnp.where(select == out_view, repeated, picked)
+                tile = value[:, (e * many + i) * lanes : (e * many + i + 1) * lanes]
+                tiles_ref[2 * (pair + i) + e] = tile
+                view = 2 * lax.rem(missing + 2 + pair + i, wide) + e
+                picked = choose(select, view, tile, picked)
+    picked_ref[...] = picked
+
+
+def late_kernel(routes, own_out, groups, *refs):
+    wide = len(routes) + 1
+    window_ref, next_ref, before_ref, *firsts = refs[: 3 + len(groups)]
+    a2_ref, b1_ref, b2_ref, h_ref, select_ref, target_ref, picked_ref, tiles_ref, residual_ref = refs[3 + len(groups) :]
+    lanes = window_ref.shape[1]
+    missing = origin(routes[-1])
+    current = jnp.concatenate([window_ref[...], next_ref[...]], axis=1)
+    previous = jnp.concatenate([before_ref[...], window_ref[...]], axis=1)
+    b1, b2, h = wider(b1_ref, 2), wider(b2_ref, 4), wider(h_ref, 4)
+    value = first_and_second_layer(current, previous, groups, firsts, a2_ref, b1, b2, h, own_out)
+    select, picked = select_ref[...], picked_ref[...]
+    for e in range(2):
+        for i in range(2):
+            tile = value[:, (2 * e + i) * lanes : (2 * e + i + 1) * lanes]
+            tiles_ref[2 * i + e] = tile
+            picked = choose(select, 2 * lax.rem(missing + i, wide) + e, tile, picked)
     residual_ref[...] = (picked - target_ref[...]).astype(BF16)
 
 
-def adjoint_kernel(shifts, own_out, *refs):
+def adjoint_kernel(routes, shifts, own_out, *refs):
     residuals, refs = refs[: len(shifts)], refs[len(shifts) :]
-    turned_ref, predicted_ref, out_ref, copied_ref = refs
-    copied_ref[...] = predicted_ref[...]
+    turned_ref, early_ref, late_ref, out_ref, predicted_ref = refs
+    wide = len(routes) + 1
+    missing = origin(routes[-1])
+    for pair in range(wide):
+        view = lax.rem(missing + pair, wide)
+        for e in range(2):
+            tile = late_ref[2 * pair + e] if pair < 2 else early_ref[2 * (pair - 2) + e]
+            predicted_ref[2 * view + e] = tile[:own_out]
     lanes = residuals[0].shape[1]
     weights = []
     for narrow_shift, pair_shift in shifts:
@@ -320,13 +359,20 @@
     )(*small)
     firsts = [firsts[widths.index(taken)] for _, taken in groups]
 
-    predicted, residual = call(
-        functools.partial(net_kernel, routes, own_out, groups),
-        [shape((2 * wide, own_out, lanes), F32), shape(flat, BF16)],
-        [VMEM] * (wide + len(groups) + 6),
-        [pltpu.VMEM((size, (wide + 1) * lanes), BF16)],
+    window = shape((size, lanes), BF16)
+    early_tiles, picked, following, before = call(
+        functools.partial(early_kernel, routes, own_out, groups),
+        [shape((2 * wide - 4, 8, lanes), F32), shape(flat, F32), window, window],
+        [VMEM] * (wide + len(groups) + 4),
+        [pltpu.VMEM((size, (wide - 1) * lanes), BF16)],
         vmem=big,
-    )(*windows, *firsts, a2, b1, b2, head, select, target)
+    )(*windows[:-1], *firsts, a2, b1, b2, head, select)
+    late_tiles, residual = call(
+        functools.partial(late_kernel, routes, own_out, groups),
+        [shape((4, 8, lanes), F32), shape(flat, BF16)],
+        [VMEM] * (len(groups) + 10),
+        vmem=big,
+    )(windows[-1], following, before, *firsts, a2, b1, b2, head, select, target, picked)
 
     turned = call(turn_kernel, shape((rows, 2 * lanes), BF16), [VMEM] * 2, vmem=big)(row_weights, residual)
     shifts = [(0, t) for t in range(1, pair)] + [(s, 0) for s in range(1, narrow)]
@@ -334,11 +380,11 @@
     blocks = [residual] + [send_both(residual, s, t) for s, t in shifts]
     shifts.insert(0, (0, 0))
     adjoint, predicted = call(
-        functools.partial(adjoint_kernel, shifts, own_out),
-        [shape((sparse_count, own_out, lanes), F32), shape(predicted.shape, F32)],
-        [VMEM] * (len(blocks) + 2),
+        functools.partial(adjoint_kernel, routes, shifts, own_out),
+        [shape((sparse_count, own_out, lanes), F32), shape((2 * wide, own_out, lanes), F32)],
+        [VMEM] * (len(blocks) + 3),
         vmem=big,
-    )(*blocks, turned, predicted)
+    )(*blocks, turned, early_tiles, late_tiles)
     return (predicted, adjoint)
 
 

time: 17.6 us -> 17.4 us (0.989)
  waiting for transfers between devices: 3.21 us -> 2.85 us
    ppermute x3, waiting for transfers between devices: 1.4 us -> 1.04 us  [local(): lax.ppermute(window, ('wide', 'pair'), [(p, t * pair + p % pair) for p, t...]
    pallas_call x2 -> x3, Pallas kernels: 1.49 us -> 1.65 us  [the longest x1 0.8 us: local(): call(functools.partial(adjoint_kernel, routes, shifts, own_out), [shape((...]
  transfers between devices with their start and end apart: 6 -> 6, of which waited for: 4 -> 3; matrix products, arithmetic and copies ran while one was open for 0% -> 0% of each run, Pallas kernels for 6% -> 8%
where the time goes in v13:
time: 17.4 us; the launch traced here: 17.2 us
  starting transfers between devices  9.05 us (52%)
  Pallas kernels  3.85 us (22%)
  waiting for transfers between devices  2.85 us (16%)
  between operations  0.76 us (4%)
  local copies, waits for them, and re-layouts  0.69 us (4%)
    ppermute x3, starting transfers between devices, local(): lax.ppermute(window, ('wide', 'pair'), [(p, t * pair + p % pair) for p, t...  7.13 us
    ppermute x3, starting transfers between devices, send_both(): return lax.ppermute(block, ('narrow', 'pair'), route)  1.92 us
    ppermute x3, waiting for transfers between devices, send_both(): return lax.ppermute(block, ('narrow', 'pair'), route)  1.81 us
    pallas_call x1, Pallas kernels, local(): call(functools.partial(pack_kernel, routes), [shape((size, lanes), BF16)]...  1.21 us
    ppermute x3, waiting for transfers between devices, local(): lax.ppermute(window, ('wide', 'pair'), [(p, t * pair + p % pair) for p, t...  1.04 us
    pallas_call x1, Pallas kernels, local(): call(functools.partial(prepare_kernel, wide, own_out, groups), [shape((2...  0.87 us
    pallas_call x1, Pallas kernels, local(): call(functools.partial(adjoint_kernel, routes, shifts, own_out), [shape((...  0.8 us
    unnamed x16, local copies, waits for them, and re-layouts  0.69 us
  transfers between devices with their start and end apart: 6, of which 3 were waited for; matrix products, arithmetic and copies ran while one was open for 0% of the time, Pallas kernels for 8%

profile of v13, /device:TPU:0, one launch (start us, length us, event | category | flops | bytes accessed | tf_op | source)
XLA Modules:
  0.0 17.2 jit_solution(17438716708668525277)
XLA Ops:
  0.6 0.0 copy-start.1
  0.6 0.0 copy-start.2
  0.7 0.0 copy-start.3
  0.7 1.2 %shard_map.104 = (bf16[240,128]{1,0:T(8,128)(2,1)S(1)}, bf16[240,128]{1,0:T(8,128)(2,1)S(1)}, bf16[240,128]{1,0:T(8,128)(2,1)S(1)}, bf16[240,128]{1,0:T(8,128)(2,1)S(1)}) custom-call(bf16[1,24,32,128]{3,2,1,0:T(8,128)(2,1)} %low_ref.1), custom_call_target="tpu_custom_call" | custom-call | flops 1000000 | bytes 245760 | tf_op jit(solution)/shard_map/pallas_call | solution.py:329
  1.9 3.1 %collective-permute-start.1 = (bf16[240,128]{1,0:T(8,128)(2,1)S(1)}, bf16[240,128]{1,0:T(8,128)(2,1)S(1)}, u32[]{:S(2)}, u32[]{:S(2)}) collective-permute-start(bf16[240,128]{1,0:T(8,128)(2,1)S(1)} %get-tuple-element.24), channel_id=1, source_target_pairs={{0,4},{1,9},{4,12},{5,13},{8,0},{9,5},{12,8},{13,1},{2,6},{3,11},{... | collective-permute-start | bytes 184328 | tf_op jit(solution)/shard_map/ppermute | solution.py:341
  5.0 2.5 %collective-permute-start.2 = (bf16[240,128]{1,0:T(8,128)(2,1)S(1)}, bf16[240,128]{1,0:T(8,128)(2,1)S(1)}, u32[]{:S(2)}, u32[]{:S(2)}) collective-permute-start(bf16[240,128]{1,0:T(8,128)(2,1)S(1)} %get-tuple-element.25), channel_id=1, source_target_pairs={{0,12},{1,13},{4,8},{5,9},{8,4},{9,1},{12,0},{13,5},{2,14},{3,15},... | collective-permute-start | bytes 184328 | tf_op jit(solution)/shard_map/ppermute | solution.py:341
  7.4 1.6 %collective-permute-start = (bf16[240,128]{1,0:T(8,128)(2,1)S(1)}, bf16[240,128]{1,0:T(8,128)(2,1)S(1)}, u32[]{:S(2)}, u32[]{:S(2)}) collective-permute-start(bf16[240,128]{1,0:T(8,128)(2,1)S(1)} %get-tuple-element.22), channel_id=1, source_target_pairs={{0,8},{1,5},{4,0},{5,1},{8,12},{9,13},{12,4},{13,9},{2,10},{3,7},{... | collective-permute-start | bytes 184328 | tf_op jit(solution)/shard_map/ppermute | solution.py:341
  9.0 0.0 copy-start.7
  9.0 0.0 copy-start.4
  9.0 0.0 copy-done.1
  9.0 0.0 copy-done.2
  9.0 0.0 copy-done.3
  9.0 0.6 %copy-done.7 = s32[1,16]{1,0:T(1,128)S(1)} copy-done((s32[1,16]{1,0:T(1,128)S(1)}, s32[1,16]{1,0:T(1,128)}, u32[]{:S(2)}) %copy-start.7) | copy-done | bytes 88
  9.7 0.0 copy-done.4
  9.7 0.0 copy-done.5
  9.7 0.0 copy-done.6
  9.7 0.9 %shard_map.105 = (bf16[96,96]{1,0:T(8,128)(2,1)S(1)}, bf16[192,192]{1,0:T(8,128)(2,1)S(1)}, bf16[96,240]{1,0:T(8,128)(2,1)S(1)}, f32[240,128]{1,0:T(8,128)S(1)},...) custom-call(bf16[4,24,24]{2,1,0:T(8,128)(2,1)S(1)} %copy-done.2, ...), custom_call_target="tpu_custom_call" | custom-call | flops 1000000 | bytes 424960 | tf_op jit(solution)/shard_map/pallas_call | solution.py:346
  10.6 0.0 collective-permute-done.1.refs_1_
  10.6 1.0 %collective-permute-done.2.refs_2_ = bf16[240,128]{1,0:T(8,128)(2,1)S(1)} collective-permute-done((bf16[240,128]{1,0:T(8,128)(2,1)S(1)}, bf16[240,128]{1,0:T(8,128)(2,1)S(1)}, u32[]{:S(2)}, u32[]{:S(2)}) %collective-permute-start.2) | collective-permute-done | bytes 61472 | tf_op jit(solution)/shard_map/ppermute | solution.py:341
  11.6 0.5 %shard_map.106 = (f32[4,8,128]{2,1,0:T(8,128)S(1)}, f32[64,128]{1,0:T(8,128)S(1)}, bf16[240,128]{1,0:T(8,128)(2,1)S(1)}, bf16[240,128]{1,0:T(8,128)(2,1)S(1)}) custom-call(bf16[240,128]{1,0:T(8,128)(2,1)S(1)} %get-tuple-element.23.refs_0_, bf16[240,128]{1,0:T(8,128)(2,1)S(1)} %collective-permute-done.1.refs_1_, ...), custom_call_target="tpu_custom_call" | custom-call | flops 1000000 | bytes 172032 | tf_op jit(solution)/shard_map/pallas_call | solution.py:363
  12.1 0.0 collective-permute-done.refs_0_
  12.1 0.0 copy-start
  12.1 0.4 %shard_map.107 = (f32[4,8,128]{2,1,0:T(8,128)S(1)}, bf16[64,128]{1,0:T(8,128)(2,1)S(1)}) custom-call(bf16[240,128]{1,0:T(8,128)(2,1)S(1)} %collective-permute-done.refs_0_, bf16[240,128]{1,0:T(8,128)(2,1)S(1)} %get-tuple-element.33.refs_1_, bf16[240,128]{1,0:T(8,128)(2,1)S(1)} %get-tuple-element.34.refs_2_, ...), custom_call_target="tpu_custom_call" | custom-call | flops 1000000 | bytes 32768 | tf_op jit(solution)/shard_map/pallas_call | solution.py:370
  12.5 0.1 collective-permute-start.5
  12.6 1.6 %collective-permute-start.4 = (bf16[64,128]{1,0:T(8,128)(2,1)S(1)}, bf16[64,128]{1,0:T(8,128)(2,1)S(1)}, u32[]{:S(2)}, u32[]{:S(2)}) collective-permute-start(bf16[64,128]{1,0:T(8,128)(2,1)S(1)} %get-tuple-element.37._.refs_0_), channel_id=1, source_target_pairs={{0,2},{1,3},{2,0},{3,1},{4,6},{5,7},{6,4},{7,5},{8,10},{9,11},{10,... | collective-permute-start | bytes 49160 | tf_op jit(solution)/shard_map/ppermute | solution.py:293
  14.2 0.3 %collective-permute-start.3 = (bf16[64,128]{1,0:T(8,128)(2,1)S(1)}, bf16[64,128]{1,0:T(8,128)(2,1)S(1)}, u32[]{:S(2)}, u32[]{:S(2)}) collective-permute-start(bf16[64,128]{1,0:T(8,128)(2,1)S(1)} %get-tuple-element.37._.refs_0_), channel_id=1, source_target_pairs={{0,1},{1,0},{2,3},{3,2},{4,5},{5,4},{6,7},{7,6},{8,9},{9,8},{10,11... | collective-permute-start | bytes 49160 | tf_op jit(solution)/shard_map/ppermute | solution.py:293
  14.4 0.0 copy-done
  14.4 0.1 shard_map.108.refs_4_
  14.6 1.3 %collective-permute-done.5.refs_3_ = bf16[64,128]{1,0:T(8,128)(2,1)S(1)} collective-permute-done((bf16[64,128]{1,0:T(8,128)(2,1)S(1)}, bf16[64,128]{1,0:T(8,128)(2,1)S(1)}, u32[]{:S(2)}, u32[]{:S(2)}) %collective-permute-start.5) | collective-permute-done | bytes 16416 | tf_op jit(solution)/shard_map/ppermute | solution.py:293
  15.9 0.5 %collective-permute-done.4.refs_2_ = bf16[64,128]{1,0:T(8,128)(2,1)S(1)} collective-permute-done((bf16[64,128]{1,0:T(8,128)(2,1)S(1)}, bf16[64,128]{1,0:T(8,128)(2,1)S(1)}, u32[]{:S(2)}, u32[]{:S(2)}) %collective-permute-start.4) | collective-permute-done | bytes 16416 | tf_op jit(solution)/shard_map/ppermute | solution.py:293
  16.4 0.0 collective-permute-done.3.refs_1_
  16.4 0.8 %shard_map.109 = (f32[16,4,128]{2,1,0:T(4,128)}, f32[8,4,128]{2,1,0:T(4,128)}) custom-call(bf16[64,128]{1,0:T(8,128)(2,1)S(1)} %get-tuple-element.37._.refs_0_, bf16[64,128]{1,0:T(8,128)(2,1)S(1)} %collective-permute-done.3.refs_1_, bf16[64,128]{1,0:T(8,128)(2,1)S(1)} %collective-permute-done.4.refs_2_, bf16[64,128]{1,0:T(8,128)(2,1)S(1)} %collective-permute-done.5.refs_3_, ...), custom_call_target="tpu_custom_call" | custom-call | flops 1000000 | bytes 49152 | tf_op jit(solution)/shard_map/pallas_call | solution.py:382
  (2 shorter events, 0.0 us)
Async XLA Ops:
  0.6 8.4 %copy-start.1 = (f32[16,4,128]{2,1,0:T(4,128)S(1)}, f32[16,4,128]{2,1,0:T(4,128)}, u32[]{:S(2)}) copy-start(f32[16,4,128]{2,1,0:T(4,128)} %measured_ref.1) | copy-start | bytes 98308
  0.6 8.4 %copy-start.2 = (bf16[4,24,24]{2,1,0:T(8,128)(2,1)S(1)}, bf16[4,24,24]{2,1,0:T(8,128)(2,1)}, u32[]{:S(2)}) copy-start(bf16[4,24,24]{2,1,0:T(8,128)(2,1)} %aw_ref.1) | copy-start | bytes 13828
  0.7 8.4 %copy-start.3 = (bf16[4,24,24]{2,1,0:T(8,128)(2,1)S(1)}, bf16[4,24,24]{2,1,0:T(8,128)(2,1)}, u32[]{:S(2)}) copy-start(bf16[4,24,24]{2,1,0:T(8,128)(2,1)} %cw_ref.1) | copy-start | bytes 13828
  1.9 8.7 %collective-permute-start.1 = (bf16[240,128]{1,0:T(8,128)(2,1)S(1)}, bf16[240,128]{1,0:T(8,128)(2,1)S(1)}, u32[]{:S(2)}, u32[]{:S(2)}) collective-permute-start(bf16[240,128]{1,0:T(8,128)(2,1)S(1)} %get-tuple-element.24), channel_id=1, source_target_pairs={{0,4},{1,9},{4,12},{5,13},{8,0},{9,5},{12,8},{13,1},{2,6},{3,11},{... | collective-permute-start | bytes 184328 | tf_op jit(solution)/shard_map/ppermute | solution.py:341
  5.0 6.7 %collective-permute-start.2 = (bf16[240,128]{1,0:T(8,128)(2,1)S(1)}, bf16[240,128]{1,0:T(8,128)(2,1)S(1)}, u32[]{:S(2)}, u32[]{:S(2)}) collective-permute-start(bf16[240,128]{1,0:T(8,128)(2,1)S(1)} %get-tuple-element.25), channel_id=1, source_target_pairs={{0,12},{1,13},{4,8},{5,9},{8,4},{9,1},{12,0},{13,5},{2,14},{3,15},... | collective-permute-start | bytes 184328 | tf_op jit(solution)/shard_map/ppermute | solution.py:341
  7.4 4.7 %collective-permute-start = (bf16[240,128]{1,0:T(8,128)(2,1)S(1)}, bf16[240,128]{1,0:T(8,128)(2,1)S(1)}, u32[]{:S(2)}, u32[]{:S(2)}) collective-permute-start(bf16[240,128]{1,0:T(8,128)(2,1)S(1)} %get-tuple-element.22), channel_id=1, source_target_pairs={{0,8},{1,5},{4,0},{5,1},{8,12},{9,13},{12,4},{13,9},{2,10},{3,7},{... | collective-permute-start | bytes 184328 | tf_op jit(solution)/shard_map/ppermute | solution.py:341
  9.0 0.7 %copy-start.7 = (s32[1,16]{1,0:T(1,128)S(1)}, s32[1,16]{1,0:T(1,128)}, u32[]{:S(2)}) copy-start(s32[1,16]{1,0:T(1,128)} %sparse_ref.1) | copy-start | bytes 196
  9.0 0.7 %copy-start.4 = (f32[24]{0:T(128)S(1)}, f32[24]{0:T(128)}, u32[]{:S(2)}) copy-start(f32[24]{0:T(128)} %param.11) | copy-start | bytes 292
  9.0 0.7 %copy-start.5 = (f32[24]{0:T(128)S(1)}, f32[24]{0:T(128)}, u32[]{:S(2)}) copy-start(f32[24]{0:T(128)} %param.13) | copy-start | bytes 292
  9.0 0.7 %copy-start.6 = (f32[24]{0:T(128)S(1)}, f32[24]{0:T(128)}, u32[]{:S(2)}) copy-start(f32[24]{0:T(128)} %param.14) | copy-start | bytes 292
  12.1 2.4 %copy-start = (f32[128,512]{1,0:T(8,128)S(1)}, f32[128,512]{1,0:T(8,128)}, u32[]{:S(2)}) copy-start(f32[128,512]{1,0:T(8,128)} %rw_ref.1) | copy-start | bytes 786436
  12.5 3.4 %collective-permute-start.5 = (bf16[64,128]{1,0:T(8,128)(2,1)S(1)}, bf16[64,128]{1,0:T(8,128)(2,1)S(1)}, u32[]{:S(2)}, u32[]{:S(2)}) collective-permute-start(bf16[64,128]{1,0:T(8,128)(2,1)S(1)} %get-tuple-element.37._.refs_0_), channel_id=1, source_target_pairs={{0,3},{1,2},{2,1},{3,0},{4,7},{5,6},{6,5},{7,4},{8,11},{9,10},{10,... | collective-permute-start | bytes 49160 | tf_op jit(solution)/shard_map/ppermute | solution.py:293
  12.6 3.8 %collective-permute-start.4 = (bf16[64,128]{1,0:T(8,128)(2,1)S(1)}, bf16[64,128]{1,0:T(8,128)(2,1)S(1)}, u32[]{:S(2)}, u32[]{:S(2)}) collective-permute-start(bf16[64,128]{1,0:T(8,128)(2,1)S(1)} %get-tuple-element.37._.refs_0_), channel_id=1, source_target_pairs={{0,2},{1,3},{2,0},{3,1},{4,6},{5,7},{6,4},{7,5},{8,10},{9,11},{10,... | collective-permute-start | bytes 49160 | tf_op jit(solution)/shard_map/ppermute | solution.py:293
  14.2 2.3 %collective-permute-start.3 = (bf16[64,128]{1,0:T(8,128)(2,1)S(1)}, bf16[64,128]{1,0:T(8,128)(2,1)S(1)}, u32[]{:S(2)}, u32[]{:S(2)}) collective-permute-start(bf16[64,128]{1,0:T(8,128)(2,1)S(1)} %get-tuple-element.37._.refs_0_), channel_id=1, source_target_pairs={{0,1},{1,0},{2,3},{3,2},{4,5},{5,4},{6,7},{7,6},{8,9},{9,8},{10,11... | collective-permute-start | bytes 49160 | tf_op jit(solution)/shard_map/ppermute | solution.py:293

commit v14 on v13

--- a/solution.py
+++ b/solution.py
@@ -41,8 +41,8 @@
 def rounds(count, cores):
     if count == 4:
         schedules = [
+            [(3, 2, 1, 0), (1, 0, 3, 2), (2, 3, 0, 1)],
             [(1, 3, 0, 2), (3, 2, 1, 0), (2, 0, 3, 1)],
-            [(2, 3, 1, 0), (3, 2, 0, 1), (1, 0, 3, 2)],
         ]
     else:
         schedules = [[tuple((i + shift) % count for i in range(count)) for shift in range(1, count)]]

time: 17.4 us -> 17.4 us (level)
  waiting for transfers between devices: 2.85 us -> 4.27 us
  starting transfers between devices: 9.05 us -> 7.66 us
    ppermute x3, waiting for transfers between devices: 1.04 us -> 2.45 us  [local(): lax.ppermute(window, ('wide', 'pair'), [(p, t * pair + p % pair) for p, t...]
    ppermute x3, starting transfers between devices: 7.13 us -> 5.74 us  [local(): lax.ppermute(window, ('wide', 'pair'), [(p, t * pair + p % pair) for p, t...]
  transfers between devices with their start and end apart: 6 -> 6, of which waited for: 3 -> 5; matrix products, arithmetic and copies ran while one was open for 0% -> 0% of each run, Pallas kernels for 8% -> 8%
where the time goes in v14:
time: 17.4 us; the launch traced here: 17.2 us
  starting transfers between devices  7.66 us (44%)
  waiting for transfers between devices  4.27 us (25%)
  Pallas kernels  3.84 us (22%)
  between operations  0.74 us (4%)
  local copies, waits for them, and re-layouts  0.68 us (4%)
    ppermute x3, starting transfers between devices, local(): lax.ppermute(window, ('wide', 'pair'), [(p, t * pair + p % pair) for p, t...  5.74 us
    ppermute x3, waiting for transfers between devices, local(): lax.ppermute(window, ('wide', 'pair'), [(p, t * pair + p % pair) for p, t...  2.45 us
    ppermute x3, starting transfers between devices, send_both(): return lax.ppermute(block, ('narrow', 'pair'), route)  1.92 us
    ppermute x3, waiting for transfers between devices, send_both(): return lax.ppermute(block, ('narrow', 'pair'), route)  1.81 us
    pallas_call x1, Pallas kernels, local(): call(functools.partial(pack_kernel, routes), [shape((size, lanes), BF16)]...  1.21 us
    pallas_call x1, Pallas kernels, local(): call(functools.partial(prepare_kernel, wide, own_out, groups), [shape((2...  0.86 us
    pallas_call x1, Pallas kernels, local(): call(functools.partial(adjoint_kernel, routes, shifts, own_out), [shape((...  0.8 us
    unnamed x16, local copies, waits for them, and re-layouts  0.68 us
  transfers between devices with their start and end apart: 6, of which 5 were waited for; matrix products, arithmetic and copies ran while one was open for 0% of the time, Pallas kernels for 8%

profile of v14, /device:TPU:0, one launch (start us, length us, event | category | flops | bytes accessed | tf_op | source)
XLA Modules:
  0.0 17.2 jit_solution(8524733899014510307)
XLA Ops:
  0.6 0.0 copy-start.1
  0.6 0.0 copy-start.2
  0.7 0.0 copy-start.3
  0.7 1.2 %shard_map.104 = (bf16[240,128]{1,0:T(8,128)(2,1)S(1)}, bf16[240,128]{1,0:T(8,128)(2,1)S(1)}, bf16[240,128]{1,0:T(8,128)(2,1)S(1)}, bf16[240,128]{1,0:T(8,128)(2,1)S(1)}) custom-call(bf16[1,24,32,128]{3,2,1,0:T(8,128)(2,1)} %low_ref.1), custom_call_target="tpu_custom_call" | custom-call | flops 1000000 | bytes 245760 | tf_op jit(solution)/shard_map/pallas_call | solution.py:329
  1.9 5.1 %collective-permute-start.1 = (bf16[240,128]{1,0:T(8,128)(2,1)S(1)}, bf16[240,128]{1,0:T(8,128)(2,1)S(1)}, u32[]{:S(2)}, u32[]{:S(2)}) collective-permute-start(bf16[240,128]{1,0:T(8,128)(2,1)S(1)} %get-tuple-element.24), channel_id=1, source_target_pairs={{0,12},{1,5},{4,8},{5,13},{8,4},{9,1},{12,0},{13,9},{2,14},{3,7},{... | collective-permute-start | bytes 184328 | tf_op jit(solution)/shard_map/ppermute | solution.py:341
  7.0 0.0 collective-permute-start.2
  7.0 0.6 %collective-permute-start = (bf16[240,128]{1,0:T(8,128)(2,1)S(1)}, bf16[240,128]{1,0:T(8,128)(2,1)S(1)}, u32[]{:S(2)}, u32[]{:S(2)}) collective-permute-start(bf16[240,128]{1,0:T(8,128)(2,1)S(1)} %get-tuple-element.22), channel_id=1, source_target_pairs={{0,8},{1,9},{4,12},{5,1},{8,0},{9,13},{12,4},{13,5},{2,10},{3,11},... | collective-permute-start | bytes 184328 | tf_op jit(solution)/shard_map/ppermute | solution.py:341
  7.6 0.0 copy-start.7
  7.6 0.0 copy-start.4
  7.6 0.0 copy-start.5
  7.6 0.0 copy-done.1
  7.6 0.0 copy-done.2
  7.6 0.0 copy-done.3
  7.7 0.6 %copy-done.7 = s32[1,16]{1,0:T(1,128)S(1)} copy-done((s32[1,16]{1,0:T(1,128)S(1)}, s32[1,16]{1,0:T(1,128)}, u32[]{:S(2)}) %copy-start.7) | copy-done | bytes 88
  8.3 0.0 copy-done.4
  8.3 0.0 copy-done.5
  8.3 0.0 copy-done.6
  8.3 0.9 %shard_map.105 = (bf16[96,96]{1,0:T(8,128)(2,1)S(1)}, bf16[192,192]{1,0:T(8,128)(2,1)S(1)}, bf16[96,240]{1,0:T(8,128)(2,1)S(1)}, f32[240,128]{1,0:T(8,128)S(1)},...) custom-call(bf16[4,24,24]{2,1,0:T(8,128)(2,1)S(1)} %copy-done.2, ...), custom_call_target="tpu_custom_call" | custom-call | flops 1000000 | bytes 424960 | tf_op jit(solution)/shard_map/pallas_call | solution.py:346
  9.2 0.5 %collective-permute-done.1.refs_1_ = bf16[240,128]{1,0:T(8,128)(2,1)S(1)} collective-permute-done((bf16[240,128]{1,0:T(8,128)(2,1)S(1)}, bf16[240,128]{1,0:T(8,128)(2,1)S(1)}, u32[]{:S(2)}, u32[]{:S(2)}) %collective-permute-start.1) | collective-permute-done | bytes 61472 | tf_op jit(solution)/shard_map/ppermute | solution.py:341
  9.7 1.6 %collective-permute-done.2.refs_2_ = bf16[240,128]{1,0:T(8,128)(2,1)S(1)} collective-permute-done((bf16[240,128]{1,0:T(8,128)(2,1)S(1)}, bf16[240,128]{1,0:T(8,128)(2,1)S(1)}, u32[]{:S(2)}, u32[]{:S(2)}) %collective-permute-start.2) | collective-permute-done | bytes 61472 | tf_op jit(solution)/shard_map/ppermute | solution.py:341
  11.2 0.5 %shard_map.106 = (f32[4,8,128]{2,1,0:T(8,128)S(1)}, f32[64,128]{1,0:T(8,128)S(1)}, bf16[240,128]{1,0:T(8,128)(2,1)S(1)}, bf16[240,128]{1,0:T(8,128)(2,1)S(1)}) custom-call(bf16[240,128]{1,0:T(8,128)(2,1)S(1)} %get-tuple-element.23.refs_0_, bf16[240,128]{1,0:T(8,128)(2,1)S(1)} %collective-permute-done.1.refs_1_, ...), custom_call_target="tpu_custom_call" | custom-call | flops 1000000 | bytes 172032 | tf_op jit(solution)/shard_map/pallas_call | solution.py:363
  11.7 0.4 %collective-permute-done.refs_0_ = bf16[240,128]{1,0:T(8,128)(2,1)S(1)} collective-permute-done((bf16[240,128]{1,0:T(8,128)(2,1)S(1)}, bf16[240,128]{1,0:T(8,128)(2,1)S(1)}, u32[]{:S(2)}, u32[]{:S(2)}) %collective-permute-start) | collective-permute-done | bytes 61472 | tf_op jit(solution)/shard_map/ppermute | solution.py:341
  12.1 0.4 %shard_map.107 = (f32[4,8,128]{2,1,0:T(8,128)S(1)}, bf16[64,128]{1,0:T(8,128)(2,1)S(1)}) custom-call(bf16[240,128]{1,0:T(8,128)(2,1)S(1)} %collective-permute-done.refs_0_, bf16[240,128]{1,0:T(8,128)(2,1)S(1)} %get-tuple-element.33.refs_1_, bf16[240,128]{1,0:T(8,128)(2,1)S(1)} %get-tuple-element.34.refs_2_, ...), custom_call_target="tpu_custom_call" | custom-call | flops 1000000 | bytes 32768 | tf_op jit(solution)/shard_map/pallas_call | solution.py:370
  12.5 0.1 collective-permute-start.5
  12.6 1.6 %collective-permute-start.4 = (bf16[64,128]{1,0:T(8,128)(2,1)S(1)}, bf16[64,128]{1,0:T(8,128)(2,1)S(1)}, u32[]{:S(2)}, u32[]{:S(2)}) collective-permute-start(bf16[64,128]{1,0:T(8,128)(2,1)S(1)} %get-tuple-element.37._.refs_0_), channel_id=1, source_target_pairs={{0,2},{1,3},{2,0},{3,1},{4,6},{5,7},{6,4},{7,5},{8,10},{9,11},{10,... | collective-permute-start | bytes 49160 | tf_op jit(solution)/shard_map/ppermute | solution.py:293
  14.1 0.3 %collective-permute-start.3 = (bf16[64,128]{1,0:T(8,128)(2,1)S(1)}, bf16[64,128]{1,0:T(8,128)(2,1)S(1)}, u32[]{:S(2)}, u32[]{:S(2)}) collective-permute-start(bf16[64,128]{1,0:T(8,128)(2,1)S(1)} %get-tuple-element.37._.refs_0_), channel_id=1, source_target_pairs={{0,1},{1,0},{2,3},{3,2},{4,5},{5,4},{6,7},{7,6},{8,9},{9,8},{10,11... | collective-permute-start | bytes 49160 | tf_op jit(solution)/shard_map/ppermute | solution.py:293
  14.4 0.0 copy-done
  14.4 0.1 shard_map.108.refs_4_
  14.6 1.3 %collective-permute-done.5.refs_3_ = bf16[64,128]{1,0:T(8,128)(2,1)S(1)} collective-permute-done((bf16[64,128]{1,0:T(8,128)(2,1)S(1)}, bf16[64,128]{1,0:T(8,128)(2,1)S(1)}, u32[]{:S(2)}, u32[]{:S(2)}) %collective-permute-start.5) | collective-permute-done | bytes 16416 | tf_op jit(solution)/shard_map/ppermute | solution.py:293
  15.9 0.5 %collective-permute-done.4.refs_2_ = bf16[64,128]{1,0:T(8,128)(2,1)S(1)} collective-permute-done((bf16[64,128]{1,0:T(8,128)(2,1)S(1)}, bf16[64,128]{1,0:T(8,128)(2,1)S(1)}, u32[]{:S(2)}, u32[]{:S(2)}) %collective-permute-start.4) | collective-permute-done | bytes 16416 | tf_op jit(solution)/shard_map/ppermute | solution.py:293
  16.4 0.0 collective-permute-done.3.refs_1_
  16.4 0.8 %shard_map.109 = (f32[16,4,128]{2,1,0:T(4,128)}, f32[8,4,128]{2,1,0:T(4,128)}) custom-call(bf16[64,128]{1,0:T(8,128)(2,1)S(1)} %get-tuple-element.37._.refs_0_, bf16[64,128]{1,0:T(8,128)(2,1)S(1)} %collective-permute-done.3.refs_1_, bf16[64,128]{1,0:T(8,128)(2,1)S(1)} %collective-permute-done.4.refs_2_, bf16[64,128]{1,0:T(8,128)(2,1)S(1)} %collective-permute-done.5.refs_3_, ...), custom_call_target="tpu_custom_call" | custom-call | flops 1000000 | bytes 49152 | tf_op jit(solution)/shard_map/pallas_call | solution.py:382
  (2 shorter events, 0.0 us)
Async XLA Ops:
  0.6 7.0 %copy-start.1 = (f32[16,4,128]{2,1,0:T(4,128)S(1)}, f32[16,4,128]{2,1,0:T(4,128)}, u32[]{:S(2)}) copy-start(f32[16,4,128]{2,1,0:T(4,128)} %measured_ref.1) | copy-start | bytes 98308
  0.6 7.0 %copy-start.2 = (bf16[4,24,24]{2,1,0:T(8,128)(2,1)S(1)}, bf16[4,24,24]{2,1,0:T(8,128)(2,1)}, u32[]{:S(2)}) copy-start(bf16[4,24,24]{2,1,0:T(8,128)(2,1)} %aw_ref.1) | copy-start | bytes 13828
  0.7 7.0 %copy-start.3 = (bf16[4,24,24]{2,1,0:T(8,128)(2,1)S(1)}, bf16[4,24,24]{2,1,0:T(8,128)(2,1)}, u32[]{:S(2)}) copy-start(bf16[4,24,24]{2,1,0:T(8,128)(2,1)} %cw_ref.1) | copy-start | bytes 13828
  1.9 7.8 %collective-permute-start.1 = (bf16[240,128]{1,0:T(8,128)(2,1)S(1)}, bf16[240,128]{1,0:T(8,128)(2,1)S(1)}, u32[]{:S(2)}, u32[]{:S(2)}) collective-permute-start(bf16[240,128]{1,0:T(8,128)(2,1)S(1)} %get-tuple-element.24), channel_id=1, source_target_pairs={{0,12},{1,5},{4,8},{5,13},{8,4},{9,1},{12,0},{13,9},{2,14},{3,7},{... | collective-permute-start | bytes 184328 | tf_op jit(solution)/shard_map/ppermute | solution.py:341
  7.0 4.3 %collective-permute-start.2 = (bf16[240,128]{1,0:T(8,128)(2,1)S(1)}, bf16[240,128]{1,0:T(8,128)(2,1)S(1)}, u32[]{:S(2)}, u32[]{:S(2)}) collective-permute-start(bf16[240,128]{1,0:T(8,128)(2,1)S(1)} %get-tuple-element.25), channel_id=1, source_target_pairs={{0,4},{1,13},{4,0},{5,9},{8,12},{9,5},{12,8},{13,1},{2,6},{3,15},{... | collective-permute-start | bytes 184328 | tf_op jit(solution)/shard_map/ppermute | solution.py:341
  7.0 5.1 %collective-permute-start = (bf16[240,128]{1,0:T(8,128)(2,1)S(1)}, bf16[240,128]{1,0:T(8,128)(2,1)S(1)}, u32[]{:S(2)}, u32[]{:S(2)}) collective-permute-start(bf16[240,128]{1,0:T(8,128)(2,1)S(1)} %get-tuple-element.22), channel_id=1, source_target_pairs={{0,8},{1,9},{4,12},{5,1},{8,0},{9,13},{12,4},{13,5},{2,10},{3,11},... | collective-permute-start | bytes 184328 | tf_op jit(solution)/shard_map/ppermute | solution.py:341
  7.6 0.7 %copy-start.7 = (s32[1,16]{1,0:T(1,128)S(1)}, s32[1,16]{1,0:T(1,128)}, u32[]{:S(2)}) copy-start(s32[1,16]{1,0:T(1,128)} %sparse_ref.1) | copy-start | bytes 196
  7.6 0.7 %copy-start.4 = (f32[24]{0:T(128)S(1)}, f32[24]{0:T(128)}, u32[]{:S(2)}) copy-start(f32[24]{0:T(128)} %param.11) | copy-start | bytes 292
  7.6 0.7 %copy-start.5 = (f32[24]{0:T(128)S(1)}, f32[24]{0:T(128)}, u32[]{:S(2)}) copy-start(f32[24]{0:T(128)} %param.13) | copy-start | bytes 292
  7.6 0.7 %copy-start.6 = (f32[24]{0:T(128)S(1)}, f32[24]{0:T(128)}, u32[]{:S(2)}) copy-start(f32[24]{0:T(128)} %param.14) | copy-start | bytes 292
  12.1 2.3 %copy-start = (f32[128,512]{1,0:T(8,128)S(1)}, f32[128,512]{1,0:T(8,128)}, u32[]{:S(2)}) copy-start(f32[128,512]{1,0:T(8,128)} %rw_ref.1) | copy-start | bytes 786436
  12.5 3.4 %collective-permute-start.5 = (bf16[64,128]{1,0:T(8,128)(2,1)S(1)}, bf16[64,128]{1,0:T(8,128)(2,1)S(1)}, u32[]{:S(2)}, u32[]{:S(2)}) collective-permute-start(bf16[64,128]{1,0:T(8,128)(2,1)S(1)} %get-tuple-element.37._.refs_0_), channel_id=1, source_target_pairs={{0,3},{1,2},{2,1},{3,0},{4,7},{5,6},{6,5},{7,4},{8,11},{9,10},{10,... | collective-permute-start | bytes 49160 | tf_op jit(solution)/shard_map/ppermute | solution.py:293
  12.6 3.8 %collective-permute-start.4 = (bf16[64,128]{1,0:T(8,128)(2,1)S(1)}, bf16[64,128]{1,0:T(8,128)(2,1)S(1)}, u32[]{:S(2)}, u32[]{:S(2)}) collective-permute-start(bf16[64,128]{1,0:T(8,128)(2,1)S(1)} %get-tuple-element.37._.refs_0_), channel_id=1, source_target_pairs={{0,2},{1,3},{2,0},{3,1},{4,6},{5,7},{6,4},{7,5},{8,10},{9,11},{10,... | collective-permute-start | bytes 49160 | tf_op jit(solution)/shard_map/ppermute | solution.py:293
  14.1 2.2 %collective-permute-start.3 = (bf16[64,128]{1,0:T(8,128)(2,1)S(1)}, bf16[64,128]{1,0:T(8,128)(2,1)S(1)}, u32[]{:S(2)}, u32[]{:S(2)}) collective-permute-start(bf16[64,128]{1,0:T(8,128)(2,1)S(1)} %get-tuple-element.37._.refs_0_), channel_id=1, source_target_pairs={{0,1},{1,0},{2,3},{3,2},{4,5},{5,4},{6,7},{7,6},{8,9},{9,8},{10,11... | collective-permute-start | bytes 49160 | tf_op jit(solution)/shard_map/ppermute | solution.py:293

commit v15 on v13

--- a/solution.py
+++ b/solution.py
@@ -180,14 +180,23 @@
 def first_and_second_layer(current, previous, groups, firsts, a2_ref, b1, b2, h, own_out):
     outs = a2_ref.shape[0]
     channels = outs // own_out
+    lanes = current.shape[1]
+    summed = {}
+    for width in sorted({taken for _, taken in groups}, reverse=True):
+        alike = [i for i, (_, taken) in enumerate(groups) if taken == width]
+        stacks = []
+        for i in alike:
+            rows = slice(groups[i][0] * channels, (groups[i][0] + width) * channels)
+            stacks.append(jnp.concatenate([current[rows], previous[rows]], axis=0))
+        wide_sum = jnp.dot(firsts[alike[0]][...], jnp.concatenate(stacks, axis=1), preferred_element_type=F32)
+        for place, i in enumerate(alike):
+            summed[i] = wide_sum[:, place * lanes : (place + 1) * lanes]
     pieces = ([], [])
-    for (first, taken), first_ref in zip(groups, firsts):
-        rows = slice(first * channels, (first + taken) * channels)
+    for i, (first, taken) in enumerate(groups):
         half = taken * channels
-        stacked = jnp.concatenate([current[rows], previous[rows]], axis=0)
-        summed = jnp.dot(first_ref[...], stacked, preferred_element_type=F32)
         for e in range(2):
-            pieces[e].append(leaky_relu(summed[e * half : (e + 1) * half] + b1[rows]).astype(BF16))
+            bias = b1[first * channels : (first + taken) * channels]
+            pieces[e].append(leaky_relu(summed[i][e * half : (e + 1) * half] + bias).astype(BF16))
     both = jnp.concatenate([jnp.concatenate(piece, axis=0) for piece in pieces], axis=1)
     hidden = leaky_relu(jnp.dot(a2_ref[...], both, preferred_element_type=F32) + b2) * h
     value = jnp.sum(hidden.reshape(outs // 8, 8, hidden.shape[1]), axis=0)

time: 17.4 us -> 17.4 us (level)
  no operation moved by 1% of the time
where the time goes in v15:
time: 17.4 us; the launch traced here: 17.2 us
  starting transfers between devices  9.05 us (52%)
  Pallas kernels  3.85 us (22%)
  waiting for transfers between devices  2.85 us (16%)
  between operations  0.76 us (4%)
  local copies, waits for them, and re-layouts  0.69 us (4%)
    ppermute x3, starting transfers between devices, local(): lax.ppermute(window, ('wide', 'pair'), [(p, t * pair + p % pair) for p, t...  7.13 us
    ppermute x3, starting transfers between devices, send_both(): return lax.ppermute(block, ('narrow', 'pair'), route)  1.92 us
    ppermute x3, waiting for transfers between devices, send_both(): return lax.ppermute(block, ('narrow', 'pair'), route)  1.81 us
    pallas_call x1, Pallas kernels, local(): call(functools.partial(pack_kernel, routes), [shape((size, lanes), BF16)]...  1.21 us
    ppermute x3, waiting for transfers between devices, local(): lax.ppermute(window, ('wide', 'pair'), [(p, t * pair + p % pair) for p, t...  1.04 us
    pallas_call x1, Pallas kernels, local(): call(functools.partial(prepare_kernel, wide, own_out, groups), [shape((2...  0.87 us
    pallas_call x1, Pallas kernels, local(): call(functools.partial(adjoint_kernel, routes, shifts, own_out), [shape((...  0.79 us
    unnamed x16, local copies, waits for them, and re-layouts  0.69 us
  transfers between devices with their start and end apart: 6, of which 3 were waited for; matrix products, arithmetic and copies ran while one was open for 0% of the time, Pallas kernels for 8%

profile of v15, /device:TPU:0, one launch (start us, length us, event | category | flops | bytes accessed | tf_op | source)
XLA Modules:
  0.0 17.2 jit_solution(2180991278620771453)
XLA Ops:
  0.6 0.0 copy-start.1
  0.6 0.0 copy-start.2
  0.7 0.0 copy-start.3
  0.7 1.2 %shard_map.104 = (bf16[240,128]{1,0:T(8,128)(2,1)S(1)}, bf16[240,128]{1,0:T(8,128)(2,1)S(1)}, bf16[240,128]{1,0:T(8,128)(2,1)S(1)}, bf16[240,128]{1,0:T(8,128)(2,1)S(1)}) custom-call(bf16[1,24,32,128]{3,2,1,0:T(8,128)(2,1)} %low_ref.1), custom_call_target="tpu_custom_call" | custom-call | flops 1000000 | bytes 245760 | tf_op jit(solution)/shard_map/pallas_call | solution.py:338
  1.9 3.1 %collective-permute-start.1 = (bf16[240,128]{1,0:T(8,128)(2,1)S(1)}, bf16[240,128]{1,0:T(8,128)(2,1)S(1)}, u32[]{:S(2)}, u32[]{:S(2)}) collective-permute-start(bf16[240,128]{1,0:T(8,128)(2,1)S(1)} %get-tuple-element.24), channel_id=1, source_target_pairs={{0,4},{1,9},{4,12},{5,13},{8,0},{9,5},{12,8},{13,1},{2,6},{3,11},{... | collective-permute-start | bytes 184328 | tf_op jit(solution)/shard_map/ppermute | solution.py:350
  5.0 2.5 %collective-permute-start.2 = (bf16[240,128]{1,0:T(8,128)(2,1)S(1)}, bf16[240,128]{1,0:T(8,128)(2,1)S(1)}, u32[]{:S(2)}, u32[]{:S(2)}) collective-permute-start(bf16[240,128]{1,0:T(8,128)(2,1)S(1)} %get-tuple-element.25), channel_id=1, source_target_pairs={{0,12},{1,13},{4,8},{5,9},{8,4},{9,1},{12,0},{13,5},{2,14},{3,15},... | collective-permute-start | bytes 184328 | tf_op jit(solution)/shard_map/ppermute | solution.py:350
  7.4 1.6 %collective-permute-start = (bf16[240,128]{1,0:T(8,128)(2,1)S(1)}, bf16[240,128]{1,0:T(8,128)(2,1)S(1)}, u32[]{:S(2)}, u32[]{:S(2)}) collective-permute-start(bf16[240,128]{1,0:T(8,128)(2,1)S(1)} %get-tuple-element.22), channel_id=1, source_target_pairs={{0,8},{1,5},{4,0},{5,1},{8,12},{9,13},{12,4},{13,9},{2,10},{3,7},{... | collective-permute-start | bytes 184328 | tf_op jit(solution)/shard_map/ppermute | solution.py:350
  9.0 0.0 copy-start.7
  9.0 0.0 copy-start.4
  9.0 0.0 copy-done.1
  9.0 0.0 copy-done.2
  9.0 0.0 copy-done.3
  9.0 0.6 %copy-done.7 = s32[1,16]{1,0:T(1,128)S(1)} copy-done((s32[1,16]{1,0:T(1,128)S(1)}, s32[1,16]{1,0:T(1,128)}, u32[]{:S(2)}) %copy-start.7) | copy-done | bytes 88
  9.7 0.0 copy-done.4
  9.7 0.0 copy-done.5
  9.7 0.0 copy-done.6
  9.7 0.9 %shard_map.105 = (bf16[96,96]{1,0:T(8,128)(2,1)S(1)}, bf16[192,192]{1,0:T(8,128)(2,1)S(1)}, bf16[96,240]{1,0:T(8,128)(2,1)S(1)}, f32[240,128]{1,0:T(8,128)S(1)},...) custom-call(bf16[4,24,24]{2,1,0:T(8,128)(2,1)S(1)} %copy-done.2, ...), custom_call_target="tpu_custom_call" | custom-call | flops 1000000 | bytes 424960 | tf_op jit(solution)/shard_map/pallas_call | solution.py:355
  10.6 0.0 collective-permute-done.1.refs_1_
  10.6 1.0 %collective-permute-done.2.refs_2_ = bf16[240,128]{1,0:T(8,128)(2,1)S(1)} collective-permute-done((bf16[240,128]{1,0:T(8,128)(2,1)S(1)}, bf16[240,128]{1,0:T(8,128)(2,1)S(1)}, u32[]{:S(2)}, u32[]{:S(2)}) %collective-permute-start.2) | collective-permute-done | bytes 61472 | tf_op jit(solution)/shard_map/ppermute | solution.py:350
  11.6 0.5 %shard_map.106 = (f32[4,8,128]{2,1,0:T(8,128)S(1)}, f32[64,128]{1,0:T(8,128)S(1)}, bf16[240,128]{1,0:T(8,128)(2,1)S(1)}, bf16[240,128]{1,0:T(8,128)(2,1)S(1)}) custom-call(bf16[240,128]{1,0:T(8,128)(2,1)S(1)} %get-tuple-element.23.refs_0_, bf16[240,128]{1,0:T(8,128)(2,1)S(1)} %collective-permute-done.1.refs_1_, ...), custom_call_target="tpu_custom_call" | custom-call | flops 1000000 | bytes 172032 | tf_op jit(solution)/shard_map/pallas_call | solution.py:372
  12.1 0.0 collective-permute-done.refs_0_
  12.1 0.0 copy-start
  12.1 0.4 %shard_map.107 = (f32[4,8,128]{2,1,0:T(8,128)S(1)}, bf16[64,128]{1,0:T(8,128)(2,1)S(1)}) custom-call(bf16[240,128]{1,0:T(8,128)(2,1)S(1)} %collective-permute-done.refs_0_, bf16[240,128]{1,0:T(8,128)(2,1)S(1)} %get-tuple-element.33.refs_1_, bf16[240,128]{1,0:T(8,128)(2,1)S(1)} %get-tuple-element.34.refs_2_, ...), custom_call_target="tpu_custom_call" | custom-call | flops 1000000 | bytes 32768 | tf_op jit(solution)/shard_map/pallas_call | solution.py:379
  12.5 0.1 collective-permute-start.5
  12.6 1.6 %collective-permute-start.4 = (bf16[64,128]{1,0:T(8,128)(2,1)S(1)}, bf16[64,128]{1,0:T(8,128)(2,1)S(1)}, u32[]{:S(2)}, u32[]{:S(2)}) collective-permute-start(bf16[64,128]{1,0:T(8,128)(2,1)S(1)} %get-tuple-element.37._.refs_0_), channel_id=1, source_target_pairs={{0,2},{1,3},{2,0},{3,1},{4,6},{5,7},{6,4},{7,5},{8,10},{9,11},{10,... | collective-permute-start | bytes 49160 | tf_op jit(solution)/shard_map/ppermute | solution.py:302
  14.2 0.3 %collective-permute-start.3 = (bf16[64,128]{1,0:T(8,128)(2,1)S(1)}, bf16[64,128]{1,0:T(8,128)(2,1)S(1)}, u32[]{:S(2)}, u32[]{:S(2)}) collective-permute-start(bf16[64,128]{1,0:T(8,128)(2,1)S(1)} %get-tuple-element.37._.refs_0_), channel_id=1, source_target_pairs={{0,1},{1,0},{2,3},{3,2},{4,5},{5,4},{6,7},{7,6},{8,9},{9,8},{10,11... | collective-permute-start | bytes 49160 | tf_op jit(solution)/shard_map/ppermute | solution.py:302
  14.4 0.0 copy-done
  14.4 0.1 shard_map.108.refs_4_
  14.6 1.3 %collective-permute-done.5.refs_3_ = bf16[64,128]{1,0:T(8,128)(2,1)S(1)} collective-permute-done((bf16[64,128]{1,0:T(8,128)(2,1)S(1)}, bf16[64,128]{1,0:T(8,128)(2,1)S(1)}, u32[]{:S(2)}, u32[]{:S(2)}) %collective-permute-start.5) | collective-permute-done | bytes 16416 | tf_op jit(solution)/shard_map/ppermute | solution.py:302
  15.9 0.5 %collective-permute-done.4.refs_2_ = bf16[64,128]{1,0:T(8,128)(2,1)S(1)} collective-permute-done((bf16[64,128]{1,0:T(8,128)(2,1)S(1)}, bf16[64,128]{1,0:T(8,128)(2,1)S(1)}, u32[]{:S(2)}, u32[]{:S(2)}) %collective-permute-start.4) | collective-permute-done | bytes 16416 | tf_op jit(solution)/shard_map/ppermute | solution.py:302
  16.4 0.0 collective-permute-done.3.refs_1_
  16.4 0.8 %shard_map.109 = (f32[16,4,128]{2,1,0:T(4,128)}, f32[8,4,128]{2,1,0:T(4,128)}) custom-call(bf16[64,128]{1,0:T(8,128)(2,1)S(1)} %get-tuple-element.37._.refs_0_, bf16[64,128]{1,0:T(8,128)(2,1)S(1)} %collective-permute-done.3.refs_1_, bf16[64,128]{1,0:T(8,128)(2,1)S(1)} %collective-permute-done.4.refs_2_, bf16[64,128]{1,0:T(8,128)(2,1)S(1)} %collective-permute-done.5.refs_3_, ...), custom_call_target="tpu_custom_call" | custom-call | flops 1000000 | bytes 49152 | tf_op jit(solution)/shard_map/pallas_call | solution.py:391
  (2 shorter events, 0.0 us)
Async XLA Ops:
  0.6 8.4 %copy-start.1 = (f32[16,4,128]{2,1,0:T(4,128)S(1)}, f32[16,4,128]{2,1,0:T(4,128)}, u32[]{:S(2)}) copy-start(f32[16,4,128]{2,1,0:T(4,128)} %measured_ref.1) | copy-start | bytes 98308
  0.6 8.4 %copy-start.2 = (bf16[4,24,24]{2,1,0:T(8,128)(2,1)S(1)}, bf16[4,24,24]{2,1,0:T(8,128)(2,1)}, u32[]{:S(2)}) copy-start(bf16[4,24,24]{2,1,0:T(8,128)(2,1)} %aw_ref.1) | copy-start | bytes 13828
  0.7 8.4 %copy-start.3 = (bf16[4,24,24]{2,1,0:T(8,128)(2,1)S(1)}, bf16[4,24,24]{2,1,0:T(8,128)(2,1)}, u32[]{:S(2)}) copy-start(bf16[4,24,24]{2,1,0:T(8,128)(2,1)} %cw_ref.1) | copy-start | bytes 13828
  1.9 8.7 %collective-permute-start.1 = (bf16[240,128]{1,0:T(8,128)(2,1)S(1)}, bf16[240,128]{1,0:T(8,128)(2,1)S(1)}, u32[]{:S(2)}, u32[]{:S(2)}) collective-permute-start(bf16[240,128]{1,0:T(8,128)(2,1)S(1)} %get-tuple-element.24), channel_id=1, source_target_pairs={{0,4},{1,9},{4,12},{5,13},{8,0},{9,5},{12,8},{13,1},{2,6},{3,11},{... | collective-permute-start | bytes 184328 | tf_op jit(solution)/shard_map/ppermute | solution.py:350
  5.0 6.7 %collective-permute-start.2 = (bf16[240,128]{1,0:T(8,128)(2,1)S(1)}, bf16[240,128]{1,0:T(8,128)(2,1)S(1)}, u32[]{:S(2)}, u32[]{:S(2)}) collective-permute-start(bf16[240,128]{1,0:T(8,128)(2,1)S(1)} %get-tuple-element.25), channel_id=1, source_target_pairs={{0,12},{1,13},{4,8},{5,9},{8,4},{9,1},{12,0},{13,5},{2,14},{3,15},... | collective-permute-start | bytes 184328 | tf_op jit(solution)/shard_map/ppermute | solution.py:350
  7.4 4.7 %collective-permute-start = (bf16[240,128]{1,0:T(8,128)(2,1)S(1)}, bf16[240,128]{1,0:T(8,128)(2,1)S(1)}, u32[]{:S(2)}, u32[]{:S(2)}) collective-permute-start(bf16[240,128]{1,0:T(8,128)(2,1)S(1)} %get-tuple-element.22), channel_id=1, source_target_pairs={{0,8},{1,5},{4,0},{5,1},{8,12},{9,13},{12,4},{13,9},{2,10},{3,7},{... | collective-permute-start | bytes 184328 | tf_op jit(solution)/shard_map/ppermute | solution.py:350
  9.0 0.7 %copy-start.7 = (s32[1,16]{1,0:T(1,128)S(1)}, s32[1,16]{1,0:T(1,128)}, u32[]{:S(2)}) copy-start(s32[1,16]{1,0:T(1,128)} %sparse_ref.1) | copy-start | bytes 196
  9.0 0.7 %copy-start.4 = (f32[24]{0:T(128)S(1)}, f32[24]{0:T(128)}, u32[]{:S(2)}) copy-start(f32[24]{0:T(128)} %param.11) | copy-start | bytes 292
  9.0 0.7 %copy-start.5 = (f32[24]{0:T(128)S(1)}, f32[24]{0:T(128)}, u32[]{:S(2)}) copy-start(f32[24]{0:T(128)} %param.13) | copy-start | bytes 292
  9.0 0.7 %copy-start.6 = (f32[24]{0:T(128)S(1)}, f32[24]{0:T(128)}, u32[]{:S(2)}) copy-start(f32[24]{0:T(128)} %param.14) | copy-start | bytes 292
  12.1 2.4 %copy-start = (f32[128,512]{1,0:T(8,128)S(1)}, f32[128,512]{1,0:T(8,128)}, u32[]{:S(2)}) copy-start(f32[128,512]{1,0:T(8,128)} %rw_ref.1) | copy-start | bytes 786436
  12.5 3.4 %collective-permute-start.5 = (bf16[64,128]{1,0:T(8,128)(2,1)S(1)}, bf16[64,128]{1,0:T(8,128)(2,1)S(1)}, u32[]{:S(2)}, u32[]{:S(2)}) collective-permute-start(bf16[64,128]{1,0:T(8,128)(2,1)S(1)} %get-tuple-element.37._.refs_0_), channel_id=1, source_target_pairs={{0,3},{1,2},{2,1},{3,0},{4,7},{5,6},{6,5},{7,4},{8,11},{9,10},{10,... | collective-permute-start | bytes 49160 | tf_op jit(solution)/shard_map/ppermute | solution.py:302
  12.6 3.8 %collective-permute-start.4 = (bf16[64,128]{1,0:T(8,128)(2,1)S(1)}, bf16[64,128]{1,0:T(8,128)(2,1)S(1)}, u32[]{:S(2)}, u32[]{:S(2)}) collective-permute-start(bf16[64,128]{1,0:T(8,128)(2,1)S(1)} %get-tuple-element.37._.refs_0_), channel_id=1, source_target_pairs={{0,2},{1,3},{2,0},{3,1},{4,6},{5,7},{6,4},{7,5},{8,10},{9,11},{10,... | collective-permute-start | bytes 49160 | tf_op jit(solution)/shard_map/ppermute | solution.py:302
  14.2 2.3 %collective-permute-start.3 = (bf16[64,128]{1,0:T(8,128)(2,1)S(1)}, bf16[64,128]{1,0:T(8,128)(2,1)S(1)}, u32[]{:S(2)}, u32[]{:S(2)}) collective-permute-start(bf16[64,128]{1,0:T(8,128)(2,1)S(1)} %get-tuple-element.37._.refs_0_), channel_id=1, source_target_pairs={{0,1},{1,0},{2,3},{3,2},{4,5},{5,4},{6,7},{7,6},{8,9},{9,8},{10,11... | collective-permute-start | bytes 49160 | tf_op jit(solution)/shard_map/ppermute | solution.py:302

commit v16 on v13

--- a/solution.py
+++ b/solution.py
@@ -332,7 +332,7 @@
         [pl.BlockSpec(memory_space=pltpu.HBM)],
         [
             pltpu.VMEM((channels, width, lanes), BF16),
-            pltpu.VMEM((16 + channels * width, lanes), F32),
+            pltpu.VMEM((16 + (channels + 1) * width, lanes), F32),
             pltpu.SemaphoreType.DMA((4,)),
         ],
         vmem=53.6 if width <= 64 else 48,

time: 17.4 us -> 17.4 us (level)
  no operation moved by 1% of the time
where the time goes in v16:
time: 17.4 us; the launch traced here: 17.2 us
  starting transfers between devices  9.05 us (52%)
  Pallas kernels  3.85 us (22%)
  waiting for transfers between devices  2.85 us (16%)
  between operations  0.76 us (4%)
  local copies, waits for them, and re-layouts  0.69 us (4%)
    ppermute x3, starting transfers between devices, local(): lax.ppermute(window, ('wide', 'pair'), [(p, t * pair + p % pair) for p, t...  7.13 us
    ppermute x3, starting transfers between devices, send_both(): return lax.ppermute(block, ('narrow', 'pair'), route)  1.92 us
    ppermute x3, waiting for transfers between devices, send_both(): return lax.ppermute(block, ('narrow', 'pair'), route)  1.81 us
    pallas_call x1, Pallas kernels, local(): call(functools.partial(pack_kernel, routes), [shape((size, lanes), BF16)]...  1.21 us
    ppermute x3, waiting for transfers between devices, local(): lax.ppermute(window, ('wide', 'pair'), [(p, t * pair + p % pair) for p, t...  1.04 us
    pallas_call x1, Pallas kernels, local(): call(functools.partial(prepare_kernel, wide, own_out, groups), [shape((2...  0.87 us
    pallas_call x1, Pallas kernels, local(): call(functools.partial(adjoint_kernel, routes, shifts, own_out), [shape((...  0.8 us
    unnamed x16, local copies, waits for them, and re-layouts  0.69 us
  transfers between devices with their start and end apart: 6, of which 3 were waited for; matrix products, arithmetic and copies ran while one was open for 0% of the time, Pallas kernels for 8%

profile of v16, /device:TPU:0, one launch (start us, length us, event | category | flops | bytes accessed | tf_op | source)
XLA Modules:
  0.0 17.2 jit_solution(17438716708668525277)
XLA Ops:
  0.6 0.0 copy-start.1
  0.6 0.0 copy-start.2
  0.7 0.0 copy-start.3
  0.7 1.2 %shard_map.104 = (bf16[240,128]{1,0:T(8,128)(2,1)S(1)}, bf16[240,128]{1,0:T(8,128)(2,1)S(1)}, bf16[240,128]{1,0:T(8,128)(2,1)S(1)}, bf16[240,128]{1,0:T(8,128)(2,1)S(1)}) custom-call(bf16[1,24,32,128]{3,2,1,0:T(8,128)(2,1)} %low_ref.1), custom_call_target="tpu_custom_call" | custom-call | flops 1000000 | bytes 245760 | tf_op jit(solution)/shard_map/pallas_call | solution.py:329
  1.9 3.1 %collective-permute-start.1 = (bf16[240,128]{1,0:T(8,128)(2,1)S(1)}, bf16[240,128]{1,0:T(8,128)(2,1)S(1)}, u32[]{:S(2)}, u32[]{:S(2)}) collective-permute-start(bf16[240,128]{1,0:T(8,128)(2,1)S(1)} %get-tuple-element.24), channel_id=1, source_target_pairs={{0,4},{1,9},{4,12},{5,13},{8,0},{9,5},{12,8},{13,1},{2,6},{3,11},{... | collective-permute-start | bytes 184328 | tf_op jit(solution)/shard_map/ppermute | solution.py:341
  5.0 2.5 %collective-permute-start.2 = (bf16[240,128]{1,0:T(8,128)(2,1)S(1)}, bf16[240,128]{1,0:T(8,128)(2,1)S(1)}, u32[]{:S(2)}, u32[]{:S(2)}) collective-permute-start(bf16[240,128]{1,0:T(8,128)(2,1)S(1)} %get-tuple-element.25), channel_id=1, source_target_pairs={{0,12},{1,13},{4,8},{5,9},{8,4},{9,1},{12,0},{13,5},{2,14},{3,15},... | collective-permute-start | bytes 184328 | tf_op jit(solution)/shard_map/ppermute | solution.py:341
  7.4 1.6 %collective-permute-start = (bf16[240,128]{1,0:T(8,128)(2,1)S(1)}, bf16[240,128]{1,0:T(8,128)(2,1)S(1)}, u32[]{:S(2)}, u32[]{:S(2)}) collective-permute-start(bf16[240,128]{1,0:T(8,128)(2,1)S(1)} %get-tuple-element.22), channel_id=1, source_target_pairs={{0,8},{1,5},{4,0},{5,1},{8,12},{9,13},{12,4},{13,9},{2,10},{3,7},{... | collective-permute-start | bytes 184328 | tf_op jit(solution)/shard_map/ppermute | solution.py:341
  9.0 0.0 copy-start.7
  9.0 0.0 copy-start.4
  9.0 0.0 copy-done.1
  9.0 0.0 copy-done.2
  9.0 0.0 copy-done.3
  9.0 0.6 %copy-done.7 = s32[1,16]{1,0:T(1,128)S(1)} copy-done((s32[1,16]{1,0:T(1,128)S(1)}, s32[1,16]{1,0:T(1,128)}, u32[]{:S(2)}) %copy-start.7) | copy-done | bytes 88
  9.7 0.0 copy-done.4
  9.7 0.0 copy-done.5
  9.7 0.0 copy-done.6
  9.7 0.9 %shard_map.105 = (bf16[96,96]{1,0:T(8,128)(2,1)S(1)}, bf16[192,192]{1,0:T(8,128)(2,1)S(1)}, bf16[96,240]{1,0:T(8,128)(2,1)S(1)}, f32[240,128]{1,0:T(8,128)S(1)},...) custom-call(bf16[4,24,24]{2,1,0:T(8,128)(2,1)S(1)} %copy-done.2, ...), custom_call_target="tpu_custom_call" | custom-call | flops 1000000 | bytes 424960 | tf_op jit(solution)/shard_map/pallas_call | solution.py:346
  10.6 0.0 collective-permute-done.1.refs_1_
  10.6 1.0 %collective-permute-done.2.refs_2_ = bf16[240,128]{1,0:T(8,128)(2,1)S(1)} collective-permute-done((bf16[240,128]{1,0:T(8,128)(2,1)S(1)}, bf16[240,128]{1,0:T(8,128)(2,1)S(1)}, u32[]{:S(2)}, u32[]{:S(2)}) %collective-permute-start.2) | collective-permute-done | bytes 61472 | tf_op jit(solution)/shard_map/ppermute | solution.py:341
  11.6 0.5 %shard_map.106 = (f32[4,8,128]{2,1,0:T(8,128)S(1)}, f32[64,128]{1,0:T(8,128)S(1)}, bf16[240,128]{1,0:T(8,128)(2,1)S(1)}, bf16[240,128]{1,0:T(8,128)(2,1)S(1)}) custom-call(bf16[240,128]{1,0:T(8,128)(2,1)S(1)} %get-tuple-element.23.refs_0_, bf16[240,128]{1,0:T(8,128)(2,1)S(1)} %collective-permute-done.1.refs_1_, ...), custom_call_target="tpu_custom_call" | custom-call | flops 1000000 | bytes 172032 | tf_op jit(solution)/shard_map/pallas_call | solution.py:363
  12.1 0.0 collective-permute-done.refs_0_
  12.1 0.0 copy-start
  12.1 0.4 %shard_map.107 = (f32[4,8,128]{2,1,0:T(8,128)S(1)}, bf16[64,128]{1,0:T(8,128)(2,1)S(1)}) custom-call(bf16[240,128]{1,0:T(8,128)(2,1)S(1)} %collective-permute-done.refs_0_, bf16[240,128]{1,0:T(8,128)(2,1)S(1)} %get-tuple-element.33.refs_1_, bf16[240,128]{1,0:T(8,128)(2,1)S(1)} %get-tuple-element.34.refs_2_, ...), custom_call_target="tpu_custom_call" | custom-call | flops 1000000 | bytes 32768 | tf_op jit(solution)/shard_map/pallas_call | solution.py:370
  12.5 0.1 collective-permute-start.5
  12.6 1.6 %collective-permute-start.4 = (bf16[64,128]{1,0:T(8,128)(2,1)S(1)}, bf16[64,128]{1,0:T(8,128)(2,1)S(1)}, u32[]{:S(2)}, u32[]{:S(2)}) collective-permute-start(bf16[64,128]{1,0:T(8,128)(2,1)S(1)} %get-tuple-element.37._.refs_0_), channel_id=1, source_target_pairs={{0,2},{1,3},{2,0},{3,1},{4,6},{5,7},{6,4},{7,5},{8,10},{9,11},{10,... | collective-permute-start | bytes 49160 | tf_op jit(solution)/shard_map/ppermute | solution.py:293
  14.2 0.3 %collective-permute-start.3 = (bf16[64,128]{1,0:T(8,128)(2,1)S(1)}, bf16[64,128]{1,0:T(8,128)(2,1)S(1)}, u32[]{:S(2)}, u32[]{:S(2)}) collective-permute-start(bf16[64,128]{1,0:T(8,128)(2,1)S(1)} %get-tuple-element.37._.refs_0_), channel_id=1, source_target_pairs={{0,1},{1,0},{2,3},{3,2},{4,5},{5,4},{6,7},{7,6},{8,9},{9,8},{10,11... | collective-permute-start | bytes 49160 | tf_op jit(solution)/shard_map/ppermute | solution.py:293
  14.4 0.0 copy-done
  14.4 0.1 shard_map.108.refs_4_
  14.6 1.3 %collective-permute-done.5.refs_3_ = bf16[64,128]{1,0:T(8,128)(2,1)S(1)} collective-permute-done((bf16[64,128]{1,0:T(8,128)(2,1)S(1)}, bf16[64,128]{1,0:T(8,128)(2,1)S(1)}, u32[]{:S(2)}, u32[]{:S(2)}) %collective-permute-start.5) | collective-permute-done | bytes 16416 | tf_op jit(solution)/shard_map/ppermute | solution.py:293
  15.9 0.5 %collective-permute-done.4.refs_2_ = bf16[64,128]{1,0:T(8,128)(2,1)S(1)} collective-permute-done((bf16[64,128]{1,0:T(8,128)(2,1)S(1)}, bf16[64,128]{1,0:T(8,128)(2,1)S(1)}, u32[]{:S(2)}, u32[]{:S(2)}) %collective-permute-start.4) | collective-permute-done | bytes 16416 | tf_op jit(solution)/shard_map/ppermute | solution.py:293
  16.4 0.0 collective-permute-done.3.refs_1_
  16.4 0.8 %shard_map.109 = (f32[16,4,128]{2,1,0:T(4,128)}, f32[8,4,128]{2,1,0:T(4,128)}) custom-call(bf16[64,128]{1,0:T(8,128)(2,1)S(1)} %get-tuple-element.37._.refs_0_, bf16[64,128]{1,0:T(8,128)(2,1)S(1)} %collective-permute-done.3.refs_1_, bf16[64,128]{1,0:T(8,128)(2,1)S(1)} %collective-permute-done.4.refs_2_, bf16[64,128]{1,0:T(8,128)(2,1)S(1)} %collective-permute-done.5.refs_3_, ...), custom_call_target="tpu_custom_call" | custom-call | flops 1000000 | bytes 49152 | tf_op jit(solution)/shard_map/pallas_call | solution.py:382
  (2 shorter events, 0.0 us)
Async XLA Ops:
  0.6 8.4 %copy-start.1 = (f32[16,4,128]{2,1,0:T(4,128)S(1)}, f32[16,4,128]{2,1,0:T(4,128)}, u32[]{:S(2)}) copy-start(f32[16,4,128]{2,1,0:T(4,128)} %measured_ref.1) | copy-start | bytes 98308
  0.6 8.4 %copy-start.2 = (bf16[4,24,24]{2,1,0:T(8,128)(2,1)S(1)}, bf16[4,24,24]{2,1,0:T(8,128)(2,1)}, u32[]{:S(2)}) copy-start(bf16[4,24,24]{2,1,0:T(8,128)(2,1)} %aw_ref.1) | copy-start | bytes 13828
  0.7 8.4 %copy-start.3 = (bf16[4,24,24]{2,1,0:T(8,128)(2,1)S(1)}, bf16[4,24,24]{2,1,0:T(8,128)(2,1)}, u32[]{:S(2)}) copy-start(bf16[4,24,24]{2,1,0:T(8,128)(2,1)} %cw_ref.1) | copy-start | bytes 13828
  1.9 8.7 %collective-permute-start.1 = (bf16[240,128]{1,0:T(8,128)(2,1)S(1)}, bf16[240,128]{1,0:T(8,128)(2,1)S(1)}, u32[]{:S(2)}, u32[]{:S(2)}) collective-permute-start(bf16[240,128]{1,0:T(8,128)(2,1)S(1)} %get-tuple-element.24), channel_id=1, source_target_pairs={{0,4},{1,9},{4,12},{5,13},{8,0},{9,5},{12,8},{13,1},{2,6},{3,11},{... | collective-permute-start | bytes 184328 | tf_op jit(solution)/shard_map/ppermute | solution.py:341
  5.0 6.7 %collective-permute-start.2 = (bf16[240,128]{1,0:T(8,128)(2,1)S(1)}, bf16[240,128]{1,0:T(8,128)(2,1)S(1)}, u32[]{:S(2)}, u32[]{:S(2)}) collective-permute-start(bf16[240,128]{1,0:T(8,128)(2,1)S(1)} %get-tuple-element.25), channel_id=1, source_target_pairs={{0,12},{1,13},{4,8},{5,9},{8,4},{9,1},{12,0},{13,5},{2,14},{3,15},... | collective-permute-start | bytes 184328 | tf_op jit(solution)/shard_map/ppermute | solution.py:341
  7.4 4.7 %collective-permute-start = (bf16[240,128]{1,0:T(8,128)(2,1)S(1)}, bf16[240,128]{1,0:T(8,128)(2,1)S(1)}, u32[]{:S(2)}, u32[]{:S(2)}) collective-permute-start(bf16[240,128]{1,0:T(8,128)(2,1)S(1)} %get-tuple-element.22), channel_id=1, source_target_pairs={{0,8},{1,5},{4,0},{5,1},{8,12},{9,13},{12,4},{13,9},{2,10},{3,7},{... | collective-permute-start | bytes 184328 | tf_op jit(solution)/shard_map/ppermute | solution.py:341
  9.0 0.7 %copy-start.7 = (s32[1,16]{1,0:T(1,128)S(1)}, s32[1,16]{1,0:T(1,128)}, u32[]{:S(2)}) copy-start(s32[1,16]{1,0:T(1,128)} %sparse_ref.1) | copy-start | bytes 196
  9.0 0.7 %copy-start.4 = (f32[24]{0:T(128)S(1)}, f32[24]{0:T(128)}, u32[]{:S(2)}) copy-start(f32[24]{0:T(128)} %param.11) | copy-start | bytes 292
  9.0 0.7 %copy-start.5 = (f32[24]{0:T(128)S(1)}, f32[24]{0:T(128)}, u32[]{:S(2)}) copy-start(f32[24]{0:T(128)} %param.13) | copy-start | bytes 292
  9.0 0.7 %copy-start.6 = (f32[24]{0:T(128)S(1)}, f32[24]{0:T(128)}, u32[]{:S(2)}) copy-start(f32[24]{0:T(128)} %param.14) | copy-start | bytes 292
  12.1 2.4 %copy-start = (f32[128,512]{1,0:T(8,128)S(1)}, f32[128,512]{1,0:T(8,128)}, u32[]{:S(2)}) copy-start(f32[128,512]{1,0:T(8,128)} %rw_ref.1) | copy-start | bytes 786436
  12.5 3.4 %collective-permute-start.5 = (bf16[64,128]{1,0:T(8,128)(2,1)S(1)}, bf16[64,128]{1,0:T(8,128)(2,1)S(1)}, u32[]{:S(2)}, u32[]{:S(2)}) collective-permute-start(bf16[64,128]{1,0:T(8,128)(2,1)S(1)} %get-tuple-element.37._.refs_0_), channel_id=1, source_target_pairs={{0,3},{1,2},{2,1},{3,0},{4,7},{5,6},{6,5},{7,4},{8,11},{9,10},{10,... | collective-permute-start | bytes 49160 | tf_op jit(solution)/shard_map/ppermute | solution.py:293
  12.6 3.8 %collective-permute-start.4 = (bf16[64,128]{1,0:T(8,128)(2,1)S(1)}, bf16[64,128]{1,0:T(8,128)(2,1)S(1)}, u32[]{:S(2)}, u32[]{:S(2)}) collective-permute-start(bf16[64,128]{1,0:T(8,128)(2,1)S(1)} %get-tuple-element.37._.refs_0_), channel_id=1, source_target_pairs={{0,2},{1,3},{2,0},{3,1},{4,6},{5,7},{6,4},{7,5},{8,10},{9,11},{10,... | collective-permute-start | bytes 49160 | tf_op jit(solution)/shard_map/ppermute | solution.py:293
  14.2 2.3 %collective-permute-start.3 = (bf16[64,128]{1,0:T(8,128)(2,1)S(1)}, bf16[64,128]{1,0:T(8,128)(2,1)S(1)}, u32[]{:S(2)}, u32[]{:S(2)}) collective-permute-start(bf16[64,128]{1,0:T(8,128)(2,1)S(1)} %get-tuple-element.37._.refs_0_), channel_id=1, source_target_pairs={{0,1},{1,0},{2,3},{3,2},{4,5},{5,4},{6,7},{7,6},{8,9},{9,8},{10,11... | collective-permute-start | bytes 49160 | tf_op jit(solution)/shard_map/ppermute | solution.py:293

commit v17 on v16

--- a/solution.py
+++ b/solution.py
@@ -255,8 +255,15 @@
     residual_ref[...] = (picked - target_ref[...]).astype(BF16)
 
 
-def adjoint_kernel(routes, shifts, own_out, *refs):
-    residuals, refs = refs[: len(shifts)], refs[len(shifts) :]
+def adjoint_kernel(routes, shifts, straight, own_out, *refs):
+    many, across = len(shifts), len(straight)
+    cores = lax.axis_size("pair")
+    evens, odds = refs[cores : cores + across], refs[many + across : many + 2 * across]
+    near, diagonal, refs = refs[:cores], refs[cores + across : many + across], refs[many + 2 * across :]
+    residuals = [ref[...] for ref in near + diagonal]
+    is_odd = lax.rem(lax.axis_index("pair"), 2) == 1
+    residuals += [jnp.where(is_odd, odd[...], even[...]) for even, odd in zip(evens, odds)]
+    shifts = shifts + straight
     turned_ref, early_ref, late_ref, out_ref, predicted_ref = refs
     wide = len(routes) + 1
     missing = origin(routes[-1])
@@ -271,7 +278,7 @@
         narrow, pair = came_from("narrow", narrow_shift), came_from("pair", pair_shift)
         block = narrow * lax.axis_size("pair") + pair
         weights.append(turned_ref[pl.ds(pl.multiple_of(block * lanes, lanes), lanes), :])
-    values = jnp.concatenate([ref[...] for ref in residuals], axis=1)
+    values = jnp.concatenate(residuals, axis=1)
     both = jnp.dot(values, jnp.concatenate(weights, axis=0), preferred_element_type=F32)
     total = both[:, :lanes] + both[:, lanes:]
     for k in range(out_ref.shape[0]):
@@ -283,12 +290,14 @@
     return lax.rem(lax.axis_index(axis) - distance + count, count)
 
 
-def send_both(block, narrow_distance, pair_distance):
+def send_both(block, narrow_distance, pair_distance, parity=None):
     narrow, pair = lax.axis_size("narrow"), lax.axis_size("pair")
     route = []
     for i in range(narrow):
         for j in range(pair):
             target = (i + narrow_distance) % narrow * pair + (j + pair_distance) % pair
+            if parity is not None and j % 2 != parity:
+                target = i * pair + j
             route.append((i * pair + j, target))
     return lax.ppermute(block, ("narrow", "pair"), route)
 
@@ -375,12 +384,17 @@
     )(windows[-1], following, before, *firsts, a2, b1, b2, head, select, target, picked)
 
     turned = call(turn_kernel, shape((rows, 2 * lanes), BF16), [VMEM] * 2, vmem=big)(row_weights, residual)
-    shifts = [(0, t) for t in range(1, pair)] + [(s, 0) for s in range(1, narrow)]
-    shifts += [(s, t) for s in range(1, narrow) for t in range(1, pair)]
-    blocks = [residual] + [send_both(residual, s, t) for s, t in shifts]
+    across = range(1, narrow)
+    shifts = [(0, t) for t in range(1, pair)] + [(s, t) for s in across for t in range(1, pair)]
+    straight = [(s, 0) for s in across]
+    near = [send_both(residual, 0, t) for t in range(1, pair)]
+    even = [send_both(residual, s, 0, 0) for s in across]
+    diagonal = [send_both(residual, s, t) for s in across for t in range(1, pair)]
+    odd = [send_both(residual, s, 0, 1) for s in across]
+    blocks = [residual] + near + even + diagonal + odd
     shifts.insert(0, (0, 0))
     adjoint, predicted = call(
-        functools.partial(adjoint_kernel, routes, shifts, own_out),
+        functools.partial(adjoint_kernel, routes, shifts, straight, own_out),
         [shape((sparse_count, own_out, lanes), F32), shape((2 * wide, own_out, lanes), F32)],
         [VMEM] * (len(blocks) + 3),
         vmem=big,

time: 17.4 us -> 20.8 us (1.20)
  starting transfers between devices: 9.05 us -> 12.3 us
    ppermute x3 -> x4, starting transfers between devices: 1.92 us -> 5.13 us  [send_both(): return lax.ppermute(block, ('narrow', 'pair'), route)]
    ppermute x3 -> x4, waiting for transfers between devices: 1.81 us -> 1.98 us  [send_both(): return lax.ppermute(block, ('narrow', 'pair'), route)]
  transfers between devices with their start and end apart: 6 -> 7, of which waited for: 3 -> 2; matrix products, arithmetic and copies ran while one was open for 0% -> 0% of each run, Pallas kernels for 8% -> 7%
where the time goes in v17:
time: 20.8 us; the launch traced here: 20.6 us
  starting transfers between devices  12.3 us (59%)
  Pallas kernels  3.86 us (19%)
  waiting for transfers between devices  3.02 us (15%)
  between operations  0.8 us (4%)
  local copies, waits for them, and re-layouts  0.69 us (3%)
    ppermute x3, starting transfers between devices, local(): lax.ppermute(window, ('wide', 'pair'), [(p, t * pair + p % pair) for p, t...  7.13 us
    ppermute x4, starting transfers between devices, send_both(): return lax.ppermute(block, ('narrow', 'pair'), route)  5.13 us
    ppermute x4, waiting for transfers between devices, send_both(): return lax.ppermute(block, ('narrow', 'pair'), route)  1.98 us
    pallas_call x1, Pallas kernels, local(): call(functools.partial(pack_kernel, routes), [shape((size, lanes), BF16)]...  1.21 us
    ppermute x3, waiting for transfers between devices, local(): lax.ppermute(window, ('wide', 'pair'), [(p, t * pair + p % pair) for p, t...  1.04 us
    pallas_call x1, Pallas kernels, local(): call(functools.partial(prepare_kernel, wide, own_out, groups), [shape((2...  0.87 us
    pallas_call x1, Pallas kernels, local(): call(functools.partial(adjoint_kernel, routes, shifts, straight, own_out)...  0.8 us
    unnamed x16, local copies, waits for them, and re-layouts  0.69 us
  transfers between devices with their start and end apart: 7, of which 2 were waited for; matrix products, arithmetic and copies ran while one was open for 0% of the time, Pallas kernels for 7%

profile of v17, /device:TPU:0, one launch (start us, length us, event | category | flops | bytes accessed | tf_op | source)
XLA Modules:
  0.0 20.6 jit_solution(421363251093657073)
XLA Ops:
  0.6 0.0 copy-start.1
  0.6 0.0 copy-start.2
  0.7 0.0 copy-start.3
  0.7 1.2 %shard_map.104 = (bf16[240,128]{1,0:T(8,128)(2,1)S(1)}, bf16[240,128]{1,0:T(8,128)(2,1)S(1)}, bf16[240,128]{1,0:T(8,128)(2,1)S(1)}, bf16[240,128]{1,0:T(8,128)(2,1)S(1)}) custom-call(bf16[1,24,32,128]{3,2,1,0:T(8,128)(2,1)} %low_ref.1), custom_call_target="tpu_custom_call" | custom-call | flops 1000000 | bytes 245760 | tf_op jit(solution)/shard_map/pallas_call | solution.py:338
  1.9 3.1 %collective-permute-start.1 = (bf16[240,128]{1,0:T(8,128)(2,1)S(1)}, bf16[240,128]{1,0:T(8,128)(2,1)S(1)}, u32[]{:S(2)}, u32[]{:S(2)}) collective-permute-start(bf16[240,128]{1,0:T(8,128)(2,1)S(1)} %get-tuple-element.24), channel_id=1, source_target_pairs={{0,4},{1,9},{4,12},{5,13},{8,0},{9,5},{12,8},{13,1},{2,6},{3,11},{... | collective-permute-start | bytes 184328 | tf_op jit(solution)/shard_map/ppermute | solution.py:350
  5.0 2.5 %collective-permute-start.2 = (bf16[240,128]{1,0:T(8,128)(2,1)S(1)}, bf16[240,128]{1,0:T(8,128)(2,1)S(1)}, u32[]{:S(2)}, u32[]{:S(2)}) collective-permute-start(bf16[240,128]{1,0:T(8,128)(2,1)S(1)} %get-tuple-element.25), channel_id=1, source_target_pairs={{0,12},{1,13},{4,8},{5,9},{8,4},{9,1},{12,0},{13,5},{2,14},{3,15},... | collective-permute-start | bytes 184328 | tf_op jit(solution)/shard_map/ppermute | solution.py:350
  7.4 1.6 %collective-permute-start = (bf16[240,128]{1,0:T(8,128)(2,1)S(1)}, bf16[240,128]{1,0:T(8,128)(2,1)S(1)}, u32[]{:S(2)}, u32[]{:S(2)}) collective-permute-start(bf16[240,128]{1,0:T(8,128)(2,1)S(1)} %get-tuple-element.22), channel_id=1, source_target_pairs={{0,8},{1,5},{4,0},{5,1},{8,12},{9,13},{12,4},{13,9},{2,10},{3,7},{... | collective-permute-start | bytes 184328 | tf_op jit(solution)/shard_map/ppermute | solution.py:350
  9.0 0.0 copy-done.1
  9.0 0.0 copy-done.2
  9.0 0.0 copy-done.3
  9.0 0.6 %copy-done.7 = s32[1,16]{1,0:T(1,128)S(1)} copy-done((s32[1,16]{1,0:T(1,128)S(1)}, s32[1,16]{1,0:T(1,128)}, u32[]{:S(2)}) %copy-start.7) | copy-done | bytes 88
  9.7 0.0 copy-done.4
  9.7 0.0 copy-done.5
  9.7 0.0 copy-done.6
  9.7 0.9 %shard_map.105 = (bf16[96,96]{1,0:T(8,128)(2,1)S(1)}, bf16[192,192]{1,0:T(8,128)(2,1)S(1)}, bf16[96,240]{1,0:T(8,128)(2,1)S(1)}, f32[240,128]{1,0:T(8,128)S(1)},...) custom-call(bf16[4,24,24]{2,1,0:T(8,128)(2,1)S(1)} %copy-done.2, ...), custom_call_target="tpu_custom_call" | custom-call | flops 1000000 | bytes 424960 | tf_op jit(solution)/shard_map/pallas_call | solution.py:355
  10.6 0.0 collective-permute-done.1.refs_1_
  10.6 1.0 %collective-permute-done.2.refs_2_ = bf16[240,128]{1,0:T(8,128)(2,1)S(1)} collective-permute-done((bf16[240,128]{1,0:T(8,128)(2,1)S(1)}, bf16[240,128]{1,0:T(8,128)(2,1)S(1)}, u32[]{:S(2)}, u32[]{:S(2)}) %collective-permute-start.2) | collective-permute-done | bytes 61472 | tf_op jit(solution)/shard_map/ppermute | solution.py:350
  11.6 0.5 %shard_map.106 = (f32[4,8,128]{2,1,0:T(8,128)S(1)}, f32[64,128]{1,0:T(8,128)S(1)}, bf16[240,128]{1,0:T(8,128)(2,1)S(1)}, bf16[240,128]{1,0:T(8,128)(2,1)S(1)}) custom-call(bf16[240,128]{1,0:T(8,128)(2,1)S(1)} %get-tuple-element.23.refs_0_, bf16[240,128]{1,0:T(8,128)(2,1)S(1)} %collective-permute-done.1.refs_1_, ...), custom_call_target="tpu_custom_call" | custom-call | flops 1000000 | bytes 172032 | tf_op jit(solution)/shard_map/pallas_call | solution.py:372
  12.1 0.0 collective-permute-done.refs_0_
  12.1 0.0 copy-start
  12.1 0.4 %shard_map.107 = (f32[4,8,128]{2,1,0:T(8,128)S(1)}, bf16[64,128]{1,0:T(8,128)(2,1)S(1)}) custom-call(bf16[240,128]{1,0:T(8,128)(2,1)S(1)} %collective-permute-done.refs_0_, bf16[240,128]{1,0:T(8,128)(2,1)S(1)} %get-tuple-element.33.refs_1_, bf16[240,128]{1,0:T(8,128)(2,1)S(1)} %get-tuple-element.34.refs_2_, ...), custom_call_target="tpu_custom_call" | custom-call | flops 1000000 | bytes 32768 | tf_op jit(solution)/shard_map/pallas_call | solution.py:379
  12.5 0.7 %collective-permute-start.6 = (bf16[64,128]{1,0:T(8,128)(2,1)S(1)}, bf16[64,128]{1,0:T(8,128)(2,1)S(1)}, u32[]{:S(2)}, u32[]{:S(2)}) collective-permute-start(bf16[64,128]{1,0:T(8,128)(2,1)S(1)} %get-tuple-element.37._.refs_0_), channel_id=1, source_target_pairs={{0,0},{1,3},{2,2},{3,1},{4,4},{5,7},{6,6},{7,5},{8,8},{9,11},{10,1... | collective-permute-start | bytes 49160 | tf_op jit(solution)/shard_map/ppermute | solution.py:302
  13.2 1.0 %collective-permute-start.5 = (bf16[64,128]{1,0:T(8,128)(2,1)S(1)}, bf16[64,128]{1,0:T(8,128)(2,1)S(1)}, u32[]{:S(2)}, u32[]{:S(2)}) collective-permute-start(bf16[64,128]{1,0:T(8,128)(2,1)S(1)} %get-tuple-element.37._.refs_0_), channel_id=1, source_target_pairs={{0,3},{1,2},{2,1},{3,0},{4,7},{5,6},{6,5},{7,4},{8,11},{9,10},{10,... | collective-permute-start | bytes 49160 | tf_op jit(solution)/shard_map/ppermute | solution.py:302
  14.2 3.4 %collective-permute-start.4 = (bf16[64,128]{1,0:T(8,128)(2,1)S(1)}, bf16[64,128]{1,0:T(8,128)(2,1)S(1)}, u32[]{:S(2)}, u32[]{:S(2)}) collective-permute-start(bf16[64,128]{1,0:T(8,128)(2,1)S(1)} %get-tuple-element.37._.refs_0_), channel_id=1, source_target_pairs={{0,2},{1,1},{2,0},{3,3},{4,6},{5,5},{6,4},{7,7},{8,10},{9,9},{10,8... | collective-permute-start | bytes 49160 | tf_op jit(solution)/shard_map/ppermute | solution.py:302
  17.6 0.1 collective-permute-start.3
  17.7 0.0 copy-done
  17.7 0.1 shard_map.108.refs_5_
  17.8 0.0 collective-permute-done.6.refs_4_
  17.8 0.0 collective-permute-done.5.refs_3_
  17.8 2.0 %collective-permute-done.4.refs_2_ = bf16[64,128]{1,0:T(8,128)(2,1)S(1)} collective-permute-done((bf16[64,128]{1,0:T(8,128)(2,1)S(1)}, bf16[64,128]{1,0:T(8,128)(2,1)S(1)}, u32[]{:S(2)}, u32[]{:S(2)}) %collective-permute-start.4) | collective-permute-done | bytes 16416 | tf_op jit(solution)/shard_map/ppermute | solution.py:302
  19.8 0.0 collective-permute-done.3.refs_1_
  19.8 0.8 %shard_map.109 = (f32[16,4,128]{2,1,0:T(4,128)}, f32[8,4,128]{2,1,0:T(4,128)}) custom-call(bf16[64,128]{1,0:T(8,128)(2,1)S(1)} %get-tuple-element.37._.refs_0_, bf16[64,128]{1,0:T(8,128)(2,1)S(1)} %collective-permute-done.3.refs_1_, bf16[64,128]{1,0:T(8,128)(2,1)S(1)} %collective-permute-done.4.refs_2_, bf16[64,128]{1,0:T(8,128)(2,1)S(1)} %collective-permute-done.5.refs_3_, ...), custom_call_target="tpu_custom_call" | custom-call | flops 1000000 | bytes 49152 | tf_op jit(solution)/shard_map/pallas_call | solution.py:396
  (4 shorter events, 0.0 us)
Async XLA Ops:
  0.6 8.4 %copy-start.1 = (f32[16,4,128]{2,1,0:T(4,128)S(1)}, f32[16,4,128]{2,1,0:T(4,128)}, u32[]{:S(2)}) copy-start(f32[16,4,128]{2,1,0:T(4,128)} %measured_ref.1) | copy-start | bytes 98308
  0.6 8.4 %copy-start.2 = (bf16[4,24,24]{2,1,0:T(8,128)(2,1)S(1)}, bf16[4,24,24]{2,1,0:T(8,128)(2,1)}, u32[]{:S(2)}) copy-start(bf16[4,24,24]{2,1,0:T(8,128)(2,1)} %aw_ref.1) | copy-start | bytes 13828
  0.7 8.4 %copy-start.3 = (bf16[4,24,24]{2,1,0:T(8,128)(2,1)S(1)}, bf16[4,24,24]{2,1,0:T(8,128)(2,1)}, u32[]{:S(2)}) copy-start(bf16[4,24,24]{2,1,0:T(8,128)(2,1)} %cw_ref.1) | copy-start | bytes 13828
  1.9 8.7 %collective-permute-start.1 = (bf16[240,128]{1,0:T(8,128)(2,1)S(1)}, bf16[240,128]{1,0:T(8,128)(2,1)S(1)}, u32[]{:S(2)}, u32[]{:S(2)}) collective-permute-start(bf16[240,128]{1,0:T(8,128)(2,1)S(1)} %get-tuple-element.24), channel_id=1, source_target_pairs={{0,4},{1,9},{4,12},{5,13},{8,0},{9,5},{12,8},{13,1},{2,6},{3,11},{... | collective-permute-start | bytes 184328 | tf_op jit(solution)/shard_map/ppermute | solution.py:350
  5.0 6.7 %collective-permute-start.2 = (bf16[240,128]{1,0:T(8,128)(2,1)S(1)}, bf16[240,128]{1,0:T(8,128)(2,1)S(1)}, u32[]{:S(2)}, u32[]{:S(2)}) collective-permute-start(bf16[240,128]{1,0:T(8,128)(2,1)S(1)} %get-tuple-element.25), channel_id=1, source_target_pairs={{0,12},{1,13},{4,8},{5,9},{8,4},{9,1},{12,0},{13,5},{2,14},{3,15},... | collective-permute-start | bytes 184328 | tf_op jit(solution)/shard_map/ppermute | solution.py:350
  7.4 4.7 %collective-permute-start = (bf16[240,128]{1,0:T(8,128)(2,1)S(1)}, bf16[240,128]{1,0:T(8,128)(2,1)S(1)}, u32[]{:S(2)}, u32[]{:S(2)}) collective-permute-start(bf16[240,128]{1,0:T(8,128)(2,1)S(1)} %get-tuple-element.22), channel_id=1, source_target_pairs={{0,8},{1,5},{4,0},{5,1},{8,12},{9,13},{12,4},{13,9},{2,10},{3,7},{... | collective-permute-start | bytes 184328 | tf_op jit(solution)/shard_map/ppermute | solution.py:350
  9.0 0.7 %copy-start.7 = (s32[1,16]{1,0:T(1,128)S(1)}, s32[1,16]{1,0:T(1,128)}, u32[]{:S(2)}) copy-start(s32[1,16]{1,0:T(1,128)} %sparse_ref.1) | copy-start | bytes 196
  9.0 0.7 %copy-start.4 = (f32[24]{0:T(128)S(1)}, f32[24]{0:T(128)}, u32[]{:S(2)}) copy-start(f32[24]{0:T(128)} %param.11) | copy-start | bytes 292
  9.0 0.7 %copy-start.5 = (f32[24]{0:T(128)S(1)}, f32[24]{0:T(128)}, u32[]{:S(2)}) copy-start(f32[24]{0:T(128)} %param.13) | copy-start | bytes 292
  9.0 0.7 %copy-start.6 = (f32[24]{0:T(128)S(1)}, f32[24]{0:T(128)}, u32[]{:S(2)}) copy-start(f32[24]{0:T(128)} %param.14) | copy-start | bytes 292
  12.1 5.6 %copy-start = (f32[128,512]{1,0:T(8,128)S(1)}, f32[128,512]{1,0:T(8,128)}, u32[]{:S(2)}) copy-start(f32[128,512]{1,0:T(8,128)} %rw_ref.1) | copy-start | bytes 786436
  12.5 5.3 %collective-permute-start.6 = (bf16[64,128]{1,0:T(8,128)(2,1)S(1)}, bf16[64,128]{1,0:T(8,128)(2,1)S(1)}, u32[]{:S(2)}, u32[]{:S(2)}) collective-permute-start(bf16[64,128]{1,0:T(8,128)(2,1)S(1)} %get-tuple-element.37._.refs_0_), channel_id=1, source_target_pairs={{0,0},{1,3},{2,2},{3,1},{4,4},{5,7},{6,6},{7,5},{8,8},{9,11},{10,1... | collective-permute-start | bytes 49160 | tf_op jit(solution)/shard_map/ppermute | solution.py:302
  13.2 4.6 %collective-permute-start.5 = (bf16[64,128]{1,0:T(8,128)(2,1)S(1)}, bf16[64,128]{1,0:T(8,128)(2,1)S(1)}, u32[]{:S(2)}, u32[]{:S(2)}) collective-permute-start(bf16[64,128]{1,0:T(8,128)(2,1)S(1)} %get-tuple-element.37._.refs_0_), channel_id=1, source_target_pairs={{0,3},{1,2},{2,1},{3,0},{4,7},{5,6},{6,5},{7,4},{8,11},{9,10},{10,... | collective-permute-start | bytes 49160 | tf_op jit(solution)/shard_map/ppermute | solution.py:302
  14.2 5.6 %collective-permute-start.4 = (bf16[64,128]{1,0:T(8,128)(2,1)S(1)}, bf16[64,128]{1,0:T(8,128)(2,1)S(1)}, u32[]{:S(2)}, u32[]{:S(2)}) collective-permute-start(bf16[64,128]{1,0:T(8,128)(2,1)S(1)} %get-tuple-element.37._.refs_0_), channel_id=1, source_target_pairs={{0,2},{1,1},{2,0},{3,3},{4,6},{5,5},{6,4},{7,7},{8,10},{9,9},{10,8... | collective-permute-start | bytes 49160 | tf_op jit(solution)/shard_map/ppermute | solution.py:302
  17.6 2.2 %collective-permute-start.3 = (bf16[64,128]{1,0:T(8,128)(2,1)S(1)}, bf16[64,128]{1,0:T(8,128)(2,1)S(1)}, u32[]{:S(2)}, u32[]{:S(2)}) collective-permute-start(bf16[64,128]{1,0:T(8,128)(2,1)S(1)} %get-tuple-element.37._.refs_0_), channel_id=1, source_target_pairs={{0,1},{1,0},{2,3},{3,2},{4,5},{5,4},{6,7},{7,6},{8,9},{9,8},{10,11... | collective-permute-start | bytes 49160 | tf_op jit(solution)/shard_map/ppermute | solution.py:302

commit v18 on v16

--- a/solution.py
+++ b/solution.py
@@ -72,8 +72,20 @@
     return [(first, min(most, span - first)) for first in range(0, span, most)]
 
 
+def pack_window(window_ref, rows_ref, channels, width, span, target):
+    first = target * (span - 2) + 7
+    columns = [rows_ref[pl.ds(first + i, channels, stride=width), :] for i in range(span)]
+    window_ref[...] = jnp.concatenate(columns, axis=0).astype(BF16)
+
+
+def clear_edges(rows_ref, count):
+    edge = jnp.zeros((8, rows_ref.shape[1]), F32)
+    rows_ref[0:8, :] = edge
+    rows_ref[8 + count : 16 + count, :] = edge
+
+
 def pack_kernel(routes, low_ref, *refs):
-    windows, (block_ref, rows_ref, sems) = refs[: len(routes) + 1], refs[len(routes) + 1 :]
+    windows, (block_ref, rows_ref, sems) = refs[: len(routes)], refs[len(routes) :]
     _, channels, width, rows = low_ref.shape
     parts = sems.shape[0]
     each = channels // parts
@@ -82,19 +94,14 @@
         piece = pl.ds(i * each, each)
         pieces.append(pltpu.make_async_copy(low_ref.at[0, piece], block_ref.at[piece], sems.at[i]))
         pieces[-1].start()
-    edge = jnp.zeros((8, rows), F32)
-    rows_ref[0:8, :] = edge
-    rows_ref[8 + channels * width : 16 + channels * width, :] = edge
+    clear_edges(rows_ref, channels * width)
+    targets = [entry(route, ("wide", "pair")) for route in routes]
     for i in range(parts):
         pieces[i].wait()
         values = block_ref[i * each : (i + 1) * each].astype(F32).reshape(each * width, rows)
         rows_ref[8 + i * each * width : 8 + (i + 1) * each * width, :] = values
-    own = width // (len(routes) + 1)
-    me = lax.axis_index("wide")
-    for window, target in zip(windows, [me] + [entry(route, ("wide", "pair")) for route in routes]):
-        first = target * own + 7
-        columns = [rows_ref[pl.ds(first + i, channels, stride=width), :] for i in range(own + 2)]
-        window[...] = jnp.concatenate(columns, axis=0).astype(BF16)
+    for window, target in zip(windows, targets):
+        pack_window(window, rows_ref, channels, width, width // (len(routes) + 1) + 2, target)
 
 
 def prepare_kernel(
@@ -108,11 +115,16 @@
     hw_ref,
     measured_ref,
     sparse_ref,
+    block_ref,
     *refs,
 ):
-    firsts, (a2_ref, b1_ref, b2_ref, h_ref, select_ref, target_ref) = refs[:-6], refs[-6:]
-    channels = aw_ref.shape[1]
+    firsts, refs = refs[:-8], refs[-8:]
+    a2_ref, b1_ref, b2_ref, h_ref, select_ref, target_ref, own_ref, rows_ref = refs
+    channels, width, lanes = block_ref.shape
     span = 2 * own_out + 2
+    clear_edges(rows_ref, channels * width)
+    rows_ref[8 : 8 + channels * width, :] = block_ref[...].astype(F32).reshape(channels * width, lanes)
+    pack_window(own_ref, rows_ref, channels, width, span, lax.axis_index("wide"))
     size, outs = span * channels, own_out * channels
     rows, columns = split(iota((size, channels), 0), channels)
     pick = (columns == iota((size, channels), 1)).astype(F32)
@@ -166,7 +178,14 @@
         target_ref[k * own_out : (k + 1) * own_out, :] = measured_ref[k]
 
 
-def turn_kernel(rw_ref, _, turned_ref):
+def turn_kernel(routes, rw_ref, early_ref, late_ref, turned_ref, predicted_ref):
+    wide = len(routes) + 1
+    missing = origin(routes[-1])
+    for pair in range(wide):
+        view = lax.rem(missing + pair, wide)
+        for e in range(2):
+            tile = late_ref[2 * pair + e] if pair < 2 else early_ref[2 * (pair - 2) + e]
+            predicted_ref[2 * view + e] = tile[: predicted_ref.shape[1]]
     turned = rw_ref[...].T
     high = turned.astype(BF16)
     turned_ref[:, : high.shape[1]] = high
@@ -255,16 +274,9 @@
     residual_ref[...] = (picked - target_ref[...]).astype(BF16)
 
 
-def adjoint_kernel(routes, shifts, own_out, *refs):
+def adjoint_kernel(shifts, own_out, *refs):
     residuals, refs = refs[: len(shifts)], refs[len(shifts) :]
-    turned_ref, early_ref, late_ref, out_ref, predicted_ref = refs
-    wide = len(routes) + 1
-    missing = origin(routes[-1])
-    for pair in range(wide):
-        view = lax.rem(missing + pair, wide)
-        for e in range(2):
-            tile = late_ref[2 * pair + e] if pair < 2 else early_ref[2 * (pair - 2) + e]
-            predicted_ref[2 * view + e] = tile[:own_out]
+    turned_ref, out_ref = refs
     lanes = residuals[0].shape[1]
     weights = []
     for narrow_shift, pair_shift in shifts:
@@ -326,24 +338,21 @@
     )
     routes = rounds(wide, pair)
     groups = column_groups(channels, span)
-    windows = call(
+    rows_scratch = pltpu.VMEM((16 + (channels + 1) * width, lanes), F32)
+    *windows, block = call(
         functools.partial(pack_kernel, routes),
-        [shape((size, lanes), BF16)] * wide,
+        [shape((size, lanes), BF16)] * (wide - 1) + [shape(low_sino.shape[1:], BF16)],
         [pl.BlockSpec(memory_space=pltpu.HBM)],
-        [
-            pltpu.VMEM((channels, width, lanes), BF16),
-            pltpu.VMEM((16 + (channels + 1) * width, lanes), F32),
-            pltpu.SemaphoreType.DMA((4,)),
-        ],
-        vmem=53.6 if width <= 64 else 48,
+        [rows_scratch, pltpu.SemaphoreType.DMA((4,))],
+        vmem=53.5 if width <= 64 else 48,
     )(low_sino)
-    windows = [windows[0]] + [
+    windows = [
         lax.ppermute(window, ("wide", "pair"), [(p, t * pair + p % pair) for p, t in enumerate(route)])
-        for window, route in zip(windows[1:], routes)
+        for window, route in zip(windows, routes)
     ]
 
     widths = sorted({taken for _, taken in groups})
-    *firsts, a2, b1, b2, head, select, target = call(
+    *firsts, a2, b1, b2, head, select, target, own = call(
         functools.partial(prepare_kernel, wide, own_out, groups),
         [shape((2 * taken * channels, 2 * taken * channels), BF16) for taken in widths]
         + [
@@ -353,10 +362,13 @@
             shape((outs, lanes), F32),
             shape(flat, F32),
             shape(flat, F32),
+            shape((size, lanes), BF16),
         ],
-        [VMEM] * 7,
+        [VMEM] * 8,
+        [rows_scratch],
         vmem=big,
-    )(*small)
+    )(*small, block)
+    windows.insert(0, own)
     firsts = [firsts[widths.index(taken)] for _, taken in groups]
 
     window = shape((size, lanes), BF16)
@@ -374,17 +386,22 @@
         vmem=big,
     )(windows[-1], following, before, *firsts, a2, b1, b2, head, select, target, picked)
 
-    turned = call(turn_kernel, shape((rows, 2 * lanes), BF16), [VMEM] * 2, vmem=big)(row_weights, residual)
+    turned, predicted = call(
+        functools.partial(turn_kernel, routes),
+        [shape((rows, 2 * lanes), BF16), shape((2 * wide, own_out, lanes), F32)],
+        [VMEM] * 3,
+        vmem=big,
+    )(row_weights, early_tiles, late_tiles)
     shifts = [(0, t) for t in range(1, pair)] + [(s, 0) for s in range(1, narrow)]
     shifts += [(s, t) for s in range(1, narrow) for t in range(1, pair)]
     blocks = [residual] + [send_both(residual, s, t) for s, t in shifts]
     shifts.insert(0, (0, 0))
-    adjoint, predicted = call(
-        functools.partial(adjoint_kernel, routes, shifts, own_out),
-        [shape((sparse_count, own_out, lanes), F32), shape((2 * wide, own_out, lanes), F32)],
-        [VMEM] * (len(blocks) + 3),
+    adjoint = call(
+        functools.partial(adjoint_kernel, shifts, own_out),
+        shape((sparse_count, own_out, lanes), F32),
+        [VMEM] * (len(blocks) + 1),
         vmem=big,
-    )(*blocks, turned, early_tiles, late_tiles)
+    )(*blocks, turned)
     return (predicted, adjoint)
 
 

time: 17.4 us -> 17.3 us (level)
  waiting for transfers between devices: 2.85 us -> 2.33 us
  Pallas kernels: 3.85 us -> 4.31 us
    ppermute x3, waiting for transfers between devices: 1.81 us -> 1.31 us  [send_both(): return lax.ppermute(block, ('narrow', 'pair'), route)]
    pallas_call x2, Pallas kernels: 0.93 us -> 1.43 us  [the longest x1 0.79 us: local(): call(functools.partial(adjoint_kernel, shifts, own_out), shape((sparse_co...]
  transfers between devices with their start and end apart: 6 -> 6, of which waited for: 3 -> 3; matrix products, arithmetic and copies ran while one was open for 0% -> 0% of each run, Pallas kernels for 8% -> 12%
where the time goes in v18:
time: 17.3 us; the launch traced here: 17.1 us
  starting transfers between devices  9.05 us (52%)
  Pallas kernels  4.31 us (25%)
  waiting for transfers between devices  2.33 us (13%)
  between operations  0.75 us (4%)
  local copies, waits for them, and re-layouts  0.69 us (4%)
    ppermute x3, starting transfers between devices, local(): lax.ppermute(window, ('wide', 'pair'), [(p, t * pair + p % pair) for p, t...  7.13 us
    ppermute x3, starting transfers between devices, send_both(): return lax.ppermute(block, ('narrow', 'pair'), route)  1.92 us
    ppermute x3, waiting for transfers between devices, send_both(): return lax.ppermute(block, ('narrow', 'pair'), route)  1.31 us
    pallas_call x1, Pallas kernels, local(): call(functools.partial(pack_kernel, routes), [shape((size, lanes), BF16)]...  1.14 us
    ppermute x3, waiting for transfers between devices, local(): lax.ppermute(window, ('wide', 'pair'), [(p, t * pair + p % pair) for p, t...  1.02 us
    pallas_call x1, Pallas kernels, local(): call(functools.partial(prepare_kernel, wide, own_out, groups), [shape((2...  0.89 us
    pallas_call x1, Pallas kernels, local(): call(functools.partial(adjoint_kernel, shifts, own_out), shape((sparse_co...  0.79 us
    unnamed x16, local copies, waits for them, and re-layouts  0.69 us
  transfers between devices with their start and end apart: 6, of which 3 were waited for; matrix products, arithmetic and copies ran while one was open for 0% of the time, Pallas kernels for 12%

profile of v18, /device:TPU:0, one launch (start us, length us, event | category | flops | bytes accessed | tf_op | source)
XLA Modules:
  0.0 17.1 jit_solution(9902498369218989491)
XLA Ops:
  0.6 0.0 copy-start.1
  0.6 0.0 copy-start.2
  0.7 0.0 copy-start.3
  0.7 1.1 %shard_map.104 = (bf16[240,128]{1,0:T(8,128)(2,1)S(1)}, bf16[240,128]{1,0:T(8,128)(2,1)S(1)}, bf16[240,128]{1,0:T(8,128)(2,1)S(1)}, bf16[24,32,128]{2,1,0:T(8,128)(2,1)S(1)}) custom-call(bf16[1,24,32,128]{3,2,1,0:T(8,128)(2,1)} %low_ref.1), custom_call_target="tpu_custom_call" | custom-call | flops 1000000 | bytes 380928 | tf_op jit(solution)/shard_map/pallas_call | solution.py:342
  1.8 3.1 %collective-permute-start = (bf16[240,128]{1,0:T(8,128)(2,1)S(1)}, bf16[240,128]{1,0:T(8,128)(2,1)S(1)}, u32[]{:S(2)}, u32[]{:S(2)}) collective-permute-start(bf16[240,128]{1,0:T(8,128)(2,1)S(1)} %get-tuple-element.25), channel_id=1, source_target_pairs={{0,4},{1,9},{4,12},{5,13},{8,0},{9,5},{12,8},{13,1},{2,6},{3,11},{... | collective-permute-start | bytes 184328 | tf_op jit(solution)/shard_map/ppermute | solution.py:350
  4.9 2.5 %collective-permute-start.1 = (bf16[240,128]{1,0:T(8,128)(2,1)S(1)}, bf16[240,128]{1,0:T(8,128)(2,1)S(1)}, u32[]{:S(2)}, u32[]{:S(2)}) collective-permute-start(bf16[240,128]{1,0:T(8,128)(2,1)S(1)} %get-tuple-element.26), channel_id=1, source_target_pairs={{0,12},{1,13},{4,8},{5,9},{8,4},{9,1},{12,0},{13,5},{2,14},{3,15},... | collective-permute-start | bytes 184328 | tf_op jit(solution)/shard_map/ppermute | solution.py:350
  7.4 1.6 %collective-permute-start.2 = (bf16[240,128]{1,0:T(8,128)(2,1)S(1)}, bf16[240,128]{1,0:T(8,128)(2,1)S(1)}, u32[]{:S(2)}, u32[]{:S(2)}) collective-permute-start(bf16[240,128]{1,0:T(8,128)(2,1)S(1)} %get-tuple-element.35), channel_id=1, source_target_pairs={{0,8},{1,5},{4,0},{5,1},{8,12},{9,13},{12,4},{13,9},{2,10},{3,7},{... | collective-permute-start | bytes 184328 | tf_op jit(solution)/shard_map/ppermute | solution.py:350
  8.9 0.0 copy-start.7
  8.9 0.0 copy-start.4
  8.9 0.0 copy-done.1
  9.0 0.0 copy-done.2
  9.0 0.0 copy-done.3
  9.0 0.6 %copy-done.7 = s32[1,16]{1,0:T(1,128)S(1)} copy-done((s32[1,16]{1,0:T(1,128)S(1)}, s32[1,16]{1,0:T(1,128)}, u32[]{:S(2)}) %copy-start.7) | copy-done | bytes 88
  9.6 0.0 copy-done.4
  9.6 0.0 copy-done.5
  9.6 0.0 copy-done.6
  9.6 0.9 %shard_map.105 = (bf16[96,96]{1,0:T(8,128)(2,1)S(1)}, bf16[192,192]{1,0:T(8,128)(2,1)S(1)}, bf16[96,240]{1,0:T(8,128)(2,1)S(1)}, f32[240,128]{1,0:T(8,128)S(1)},...) custom-call(bf16[4,24,24]{2,1,0:T(8,128)(2,1)S(1)} %copy-done.2, ...), custom_call_target="tpu_custom_call" | custom-call | flops 1000000 | bytes 486400 | tf_op jit(solution)/shard_map/pallas_call | solution.py:355
  10.5 0.0 collective-permute-done.refs_1_
  10.5 1.0 %collective-permute-done.1.refs_2_ = bf16[240,128]{1,0:T(8,128)(2,1)S(1)} collective-permute-done((bf16[240,128]{1,0:T(8,128)(2,1)S(1)}, bf16[240,128]{1,0:T(8,128)(2,1)S(1)}, u32[]{:S(2)}, u32[]{:S(2)}) %collective-permute-start.1) | collective-permute-done | bytes 61472 | tf_op jit(solution)/shard_map/ppermute | solution.py:350
  11.6 0.5 %shard_map.106 = (f32[4,8,128]{2,1,0:T(8,128)S(1)}, f32[64,128]{1,0:T(8,128)S(1)}, bf16[240,128]{1,0:T(8,128)(2,1)S(1)}, bf16[240,128]{1,0:T(8,128)(2,1)S(1)}) custom-call(bf16[240,128]{1,0:T(8,128)(2,1)S(1)} %get-tuple-element.24.refs_0_, bf16[240,128]{1,0:T(8,128)(2,1)S(1)} %collective-permute-done.refs_1_, ...), custom_call_target="tpu_custom_call" | custom-call | flops 1000000 | bytes 172032 | tf_op jit(solution)/shard_map/pallas_call | solution.py:375
  12.0 0.0 collective-permute-done.2.refs_0_
  12.0 0.0 copy-start
  12.0 0.4 %shard_map.107 = (f32[4,8,128]{2,1,0:T(8,128)S(1)}, bf16[64,128]{1,0:T(8,128)(2,1)S(1)}) custom-call(bf16[240,128]{1,0:T(8,128)(2,1)S(1)} %collective-permute-done.2.refs_0_, bf16[240,128]{1,0:T(8,128)(2,1)S(1)} %get-tuple-element.36.refs_1_, bf16[240,128]{1,0:T(8,128)(2,1)S(1)} %get-tuple-element.37.refs_2_, ...), custom_call_target="tpu_custom_call" | custom-call | flops 1000000 | bytes 32768 | tf_op jit(solution)/shard_map/pallas_call | solution.py:382
  12.4 0.1 collective-permute-start.5
  12.5 1.6 %collective-permute-start.4 = (bf16[64,128]{1,0:T(8,128)(2,1)S(1)}, bf16[64,128]{1,0:T(8,128)(2,1)S(1)}, u32[]{:S(2)}, u32[]{:S(2)}) collective-permute-start(bf16[64,128]{1,0:T(8,128)(2,1)S(1)} %get-tuple-element.42.refs_0_), channel_id=1, source_target_pairs={{0,2},{1,3},{2,0},{3,1},{4,6},{5,7},{6,4},{7,5},{8,10},{9,11},{10,... | collective-permute-start | bytes 49160 | tf_op jit(solution)/shard_map/ppermute | solution.py:305
  14.1 0.3 %collective-permute-start.3 = (bf16[64,128]{1,0:T(8,128)(2,1)S(1)}, bf16[64,128]{1,0:T(8,128)(2,1)S(1)}, u32[]{:S(2)}, u32[]{:S(2)}) collective-permute-start(bf16[64,128]{1,0:T(8,128)(2,1)S(1)} %get-tuple-element.42.refs_0_), channel_id=1, source_target_pairs={{0,1},{1,0},{2,3},{3,2},{4,5},{5,4},{6,7},{7,6},{8,9},{9,8},{10,11... | collective-permute-start | bytes 49160 | tf_op jit(solution)/shard_map/ppermute | solution.py:305
  14.4 0.0 copy-done
  14.4 0.6 %shard_map.108 = (bf16[512,256]{1,0:T(8,128)(2,1)S(1)}, f32[8,4,128]{2,1,0:T(4,128)}) custom-call(f32[128,512]{1,0:T(8,128)S(1)} %copy-done, f32[4,8,128]{2,1,0:T(8,128)S(1)} %get-tuple-element.34.early_ref, f32[4,8,128]{2,1,0:T(8,128)S(1)} %get-tuple-element.40.late_ref), custom_call_target="tpu_custom_call" | custom-call | flops 1000000 | bytes 278528 | tf_op jit(solution)/shard_map/pallas_call | solution.py:389
  15.0 0.8 %collective-permute-done.5.refs_3_ = bf16[64,128]{1,0:T(8,128)(2,1)S(1)} collective-permute-done((bf16[64,128]{1,0:T(8,128)(2,1)S(1)}, bf16[64,128]{1,0:T(8,128)(2,1)S(1)}, u32[]{:S(2)}, u32[]{:S(2)}) %collective-permute-start.5) | collective-permute-done | bytes 16416 | tf_op jit(solution)/shard_map/ppermute | solution.py:305
  15.8 0.5 %collective-permute-done.4.refs_2_ = bf16[64,128]{1,0:T(8,128)(2,1)S(1)} collective-permute-done((bf16[64,128]{1,0:T(8,128)(2,1)S(1)}, bf16[64,128]{1,0:T(8,128)(2,1)S(1)}, u32[]{:S(2)}, u32[]{:S(2)}) %collective-permute-start.4) | collective-permute-done | bytes 16416 | tf_op jit(solution)/shard_map/ppermute | solution.py:305
  16.3 0.0 collective-permute-done.3.refs_1_
  16.3 0.8 %shard_map.109 = f32[16,4,128]{2,1,0:T(4,128)} custom-call(bf16[64,128]{1,0:T(8,128)(2,1)S(1)} %get-tuple-element.42.refs_0_, bf16[64,128]{1,0:T(8,128)(2,1)S(1)} %collective-permute-done.3.refs_1_, bf16[64,128]{1,0:T(8,128)(2,1)S(1)} %collective-permute-done.4.refs_2_, bf16[64,128]{1,0:T(8,128)(2,1)S(1)} %collective-permute-done.5.refs_3_, ...), custom_call_target="tpu_custom_call" | custom-call | flops 1000000 | bytes 32768 | tf_op jit(solution)/shard_map/pallas_call | solution.py:399
  (2 shorter events, 0.0 us)
Async XLA Ops:
  0.6 8.3 %copy-start.1 = (f32[16,4,128]{2,1,0:T(4,128)S(1)}, f32[16,4,128]{2,1,0:T(4,128)}, u32[]{:S(2)}) copy-start(f32[16,4,128]{2,1,0:T(4,128)} %measured_ref.1) | copy-start | bytes 98308
  0.6 8.3 %copy-start.2 = (bf16[4,24,24]{2,1,0:T(8,128)(2,1)S(1)}, bf16[4,24,24]{2,1,0:T(8,128)(2,1)}, u32[]{:S(2)}) copy-start(bf16[4,24,24]{2,1,0:T(8,128)(2,1)} %aw_ref.1) | copy-start | bytes 13828
  0.7 8.3 %copy-start.3 = (bf16[4,24,24]{2,1,0:T(8,128)(2,1)S(1)}, bf16[4,24,24]{2,1,0:T(8,128)(2,1)}, u32[]{:S(2)}) copy-start(bf16[4,24,24]{2,1,0:T(8,128)(2,1)} %cw_ref.1) | copy-start | bytes 13828
  1.8 8.7 %collective-permute-start = (bf16[240,128]{1,0:T(8,128)(2,1)S(1)}, bf16[240,128]{1,0:T(8,128)(2,1)S(1)}, u32[]{:S(2)}, u32[]{:S(2)}) collective-permute-start(bf16[240,128]{1,0:T(8,128)(2,1)S(1)} %get-tuple-element.25), channel_id=1, source_target_pairs={{0,4},{1,9},{4,12},{5,13},{8,0},{9,5},{12,8},{13,1},{2,6},{3,11},{... | collective-permute-start | bytes 184328 | tf_op jit(solution)/shard_map/ppermute | solution.py:350
  4.9 6.7 %collective-permute-start.1 = (bf16[240,128]{1,0:T(8,128)(2,1)S(1)}, bf16[240,128]{1,0:T(8,128)(2,1)S(1)}, u32[]{:S(2)}, u32[]{:S(2)}) collective-permute-start(bf16[240,128]{1,0:T(8,128)(2,1)S(1)} %get-tuple-element.26), channel_id=1, source_target_pairs={{0,12},{1,13},{4,8},{5,9},{8,4},{9,1},{12,0},{13,5},{2,14},{3,15},... | collective-permute-start | bytes 184328 | tf_op jit(solution)/shard_map/ppermute | solution.py:350
  7.4 4.7 %collective-permute-start.2 = (bf16[240,128]{1,0:T(8,128)(2,1)S(1)}, bf16[240,128]{1,0:T(8,128)(2,1)S(1)}, u32[]{:S(2)}, u32[]{:S(2)}) collective-permute-start(bf16[240,128]{1,0:T(8,128)(2,1)S(1)} %get-tuple-element.35), channel_id=1, source_target_pairs={{0,8},{1,5},{4,0},{5,1},{8,12},{9,13},{12,4},{13,9},{2,10},{3,7},{... | collective-permute-start | bytes 184328 | tf_op jit(solution)/shard_map/ppermute | solution.py:350
  8.9 0.7 %copy-start.7 = (s32[1,16]{1,0:T(1,128)S(1)}, s32[1,16]{1,0:T(1,128)}, u32[]{:S(2)}) copy-start(s32[1,16]{1,0:T(1,128)} %sparse_ref.1) | copy-start | bytes 196
  8.9 0.7 %copy-start.4 = (f32[24]{0:T(128)S(1)}, f32[24]{0:T(128)}, u32[]{:S(2)}) copy-start(f32[24]{0:T(128)} %param.11) | copy-start | bytes 292
  8.9 0.7 %copy-start.5 = (f32[24]{0:T(128)S(1)}, f32[24]{0:T(128)}, u32[]{:S(2)}) copy-start(f32[24]{0:T(128)} %param.13) | copy-start | bytes 292
  8.9 0.7 %copy-start.6 = (f32[24]{0:T(128)S(1)}, f32[24]{0:T(128)}, u32[]{:S(2)}) copy-start(f32[24]{0:T(128)} %param.14) | copy-start | bytes 292
  12.0 2.4 %copy-start = (f32[128,512]{1,0:T(8,128)S(1)}, f32[128,512]{1,0:T(8,128)}, u32[]{:S(2)}) copy-start(f32[128,512]{1,0:T(8,128)} %rw_ref.1) | copy-start | bytes 786436
  12.4 3.4 %collective-permute-start.5 = (bf16[64,128]{1,0:T(8,128)(2,1)S(1)}, bf16[64,128]{1,0:T(8,128)(2,1)S(1)}, u32[]{:S(2)}, u32[]{:S(2)}) collective-permute-start(bf16[64,128]{1,0:T(8,128)(2,1)S(1)} %get-tuple-element.42.refs_0_), channel_id=1, source_target_pairs={{0,3},{1,2},{2,1},{3,0},{4,7},{5,6},{6,5},{7,4},{8,11},{9,10},{10,... | collective-permute-start | bytes 49160 | tf_op jit(solution)/shard_map/ppermute | solution.py:305
  12.5 3.8 %collective-permute-start.4 = (bf16[64,128]{1,0:T(8,128)(2,1)S(1)}, bf16[64,128]{1,0:T(8,128)(2,1)S(1)}, u32[]{:S(2)}, u32[]{:S(2)}) collective-permute-start(bf16[64,128]{1,0:T(8,128)(2,1)S(1)} %get-tuple-element.42.refs_0_), channel_id=1, source_target_pairs={{0,2},{1,3},{2,0},{3,1},{4,6},{5,7},{6,4},{7,5},{8,10},{9,11},{10,... | collective-permute-start | bytes 49160 | tf_op jit(solution)/shard_map/ppermute | solution.py:305
  14.1 2.3 %collective-permute-start.3 = (bf16[64,128]{1,0:T(8,128)(2,1)S(1)}, bf16[64,128]{1,0:T(8,128)(2,1)S(1)}, u32[]{:S(2)}, u32[]{:S(2)}) collective-permute-start(bf16[64,128]{1,0:T(8,128)(2,1)S(1)} %get-tuple-element.42.refs_0_), channel_id=1, source_target_pairs={{0,1},{1,0},{2,3},{3,2},{4,5},{5,4},{6,7},{7,6},{8,9},{9,8},{10,11... | collective-permute-start | bytes 49160 | tf_op jit(solution)/shard_map/ppermute | solution.py:305

commit v19 on v18

--- a/solution.py
+++ b/solution.py
@@ -233,18 +233,29 @@
     lanes = windows[0].shape[1]
     me = lax.axis_index("wide")
     missing = origin(routes[-1])
-    for window, source in zip(windows, [me] + [origin(route) for route in routes[:-1]]):
-        slot = lax.rem(source - missing + wide, wide) - 1
-        views_ref[:, pl.ds(pl.multiple_of(slot * lanes, lanes), lanes)] = window[...]
-    next_ref[...] = views_ref[:, :lanes]
-    before_ref[...] = views_ref[:, (wide - 2) * lanes :]
+    slots = [lax.rem(source - missing + wide, wide) - 1 for source in [me] + [origin(route) for route in routes[:-1]]]
+    if wide <= 4:
+        values = [window[...] for window in windows]
+        ordered = []
+        for place in range(wide - 1):
+            chosen = values[0]
+            for value, slot in zip(values[1:], slots[1:]):
+                chosen = jnp.where(slot == place, value, chosen)
+            ordered.append(chosen)
+        views = jnp.concatenate(ordered, axis=1)
+    else:
+        for window, slot in zip(windows, slots):
+            views_ref[:, pl.ds(pl.multiple_of(slot * lanes, lanes), lanes)] = window[...]
+        views = views_ref
+    next_ref[...] = views[:, :lanes]
+    before_ref[...] = views[:, (wide - 2) * lanes :]
     many = 2 if wide % 2 == 0 else 1
     b1, b2, h = wider(b1_ref, many), wider(b2_ref, 2 * many), wider(h_ref, 2 * many)
     select = select_ref[...]
     picked = jnp.zeros(select.shape, F32)
     for pair in range(0, wide - 2, many):
-        previous = views_ref[:, pair * lanes : (pair + many) * lanes]
-        current = views_ref[:, (pair + 1) * lanes : (pair + 1 + many) * lanes]
+        previous = views[:, pair * lanes : (pair + many) * lanes]
+        current = views[:, (pair + 1) * lanes : (pair + 1 + many) * lanes]
         value = first_and_second_layer(current, previous, groups, firsts, a2_ref, b1, b2, h, own_out)
         for e in range(2):
             for i in range(many):

time: 17.3 us -> 17.3 us (level)
  transfers between devices with their start and end apart: 6 -> 6, of which waited for: 3 -> 3; matrix products, arithmetic and copies ran while one was open for 0% -> 0% of each run, Pallas kernels for 12% -> 11%
where the time goes in v19:
time: 17.3 us; the launch traced here: 17.1 us
  starting transfers between devices  9.05 us (52%)
  Pallas kernels  4.26 us (25%)
  waiting for transfers between devices  2.33 us (13%)
  between operations  0.75 us (4%)
  local copies, waits for them, and re-layouts  0.69 us (4%)
    ppermute x3, starting transfers between devices, local(): lax.ppermute(window, ('wide', 'pair'), [(p, t * pair + p % pair) for p, t...  7.13 us
    ppermute x3, starting transfers between devices, send_both(): return lax.ppermute(block, ('narrow', 'pair'), route)  1.92 us
    ppermute x3, waiting for transfers between devices, send_both(): return lax.ppermute(block, ('narrow', 'pair'), route)  1.31 us
    pallas_call x1, Pallas kernels, local(): call(functools.partial(pack_kernel, routes), [shape((size, lanes), BF16)]...  1.14 us
    ppermute x3, waiting for transfers between devices, local(): lax.ppermute(window, ('wide', 'pair'), [(p, t * pair + p % pair) for p, t...  1.02 us
    pallas_call x1, Pallas kernels, local(): call(functools.partial(prepare_kernel, wide, own_out, groups), [shape((2...  0.89 us
    pallas_call x1, Pallas kernels, local(): call(functools.partial(adjoint_kernel, shifts, own_out), shape((sparse_co...  0.79 us
    unnamed x16, local copies, waits for them, and re-layouts  0.69 us
  transfers between devices with their start and end apart: 6, of which 3 were waited for; matrix products, arithmetic and copies ran while one was open for 0% of the time, Pallas kernels for 11%

profile of v19, /device:TPU:0, one launch (start us, length us, event | category | flops | bytes accessed | tf_op | source)
XLA Modules:
  0.0 17.1 jit_solution(9818603984539953517)
XLA Ops:
  0.6 0.0 copy-start.1
  0.6 0.0 copy-start.2
  0.7 0.0 copy-start.3
  0.7 1.1 %shard_map.104 = (bf16[240,128]{1,0:T(8,128)(2,1)S(1)}, bf16[240,128]{1,0:T(8,128)(2,1)S(1)}, bf16[240,128]{1,0:T(8,128)(2,1)S(1)}, bf16[24,32,128]{2,1,0:T(8,128)(2,1)S(1)}) custom-call(bf16[1,24,32,128]{3,2,1,0:T(8,128)(2,1)} %low_ref.1), custom_call_target="tpu_custom_call" | custom-call | flops 1000000 | bytes 380928 | tf_op jit(solution)/shard_map/pallas_call | solution.py:353
  1.8 3.1 %collective-permute-start = (bf16[240,128]{1,0:T(8,128)(2,1)S(1)}, bf16[240,128]{1,0:T(8,128)(2,1)S(1)}, u32[]{:S(2)}, u32[]{:S(2)}) collective-permute-start(bf16[240,128]{1,0:T(8,128)(2,1)S(1)} %get-tuple-element.25), channel_id=1, source_target_pairs={{0,4},{1,9},{4,12},{5,13},{8,0},{9,5},{12,8},{13,1},{2,6},{3,11},{... | collective-permute-start | bytes 184328 | tf_op jit(solution)/shard_map/ppermute | solution.py:361
  4.9 2.5 %collective-permute-start.1 = (bf16[240,128]{1,0:T(8,128)(2,1)S(1)}, bf16[240,128]{1,0:T(8,128)(2,1)S(1)}, u32[]{:S(2)}, u32[]{:S(2)}) collective-permute-start(bf16[240,128]{1,0:T(8,128)(2,1)S(1)} %get-tuple-element.26), channel_id=1, source_target_pairs={{0,12},{1,13},{4,8},{5,9},{8,4},{9,1},{12,0},{13,5},{2,14},{3,15},... | collective-permute-start | bytes 184328 | tf_op jit(solution)/shard_map/ppermute | solution.py:361
  7.4 1.6 %collective-permute-start.2 = (bf16[240,128]{1,0:T(8,128)(2,1)S(1)}, bf16[240,128]{1,0:T(8,128)(2,1)S(1)}, u32[]{:S(2)}, u32[]{:S(2)}) collective-permute-start(bf16[240,128]{1,0:T(8,128)(2,1)S(1)} %get-tuple-element.35), channel_id=1, source_target_pairs={{0,8},{1,5},{4,0},{5,1},{8,12},{9,13},{12,4},{13,9},{2,10},{3,7},{... | collective-permute-start | bytes 184328 | tf_op jit(solution)/shard_map/ppermute | solution.py:361
  8.9 0.0 copy-start.7
  8.9 0.0 copy-start.4
  8.9 0.0 copy-done.1
  9.0 0.0 copy-done.2
  9.0 0.0 copy-done.3
  9.0 0.6 %copy-done.7 = s32[1,16]{1,0:T(1,128)S(1)} copy-done((s32[1,16]{1,0:T(1,128)S(1)}, s32[1,16]{1,0:T(1,128)}, u32[]{:S(2)}) %copy-start.7) | copy-done | bytes 88
  9.6 0.0 copy-done.4
  9.6 0.0 copy-done.5
  9.6 0.0 copy-done.6
  9.6 0.9 %shard_map.105 = (bf16[96,96]{1,0:T(8,128)(2,1)S(1)}, bf16[192,192]{1,0:T(8,128)(2,1)S(1)}, bf16[96,240]{1,0:T(8,128)(2,1)S(1)}, f32[240,128]{1,0:T(8,128)S(1)},...) custom-call(bf16[4,24,24]{2,1,0:T(8,128)(2,1)S(1)} %copy-done.2, ...), custom_call_target="tpu_custom_call" | custom-call | flops 1000000 | bytes 486400 | tf_op jit(solution)/shard_map/pallas_call | solution.py:366
  10.5 0.0 collective-permute-done.refs_1_
  10.5 1.0 %collective-permute-done.1.refs_2_ = bf16[240,128]{1,0:T(8,128)(2,1)S(1)} collective-permute-done((bf16[240,128]{1,0:T(8,128)(2,1)S(1)}, bf16[240,128]{1,0:T(8,128)(2,1)S(1)}, u32[]{:S(2)}, u32[]{:S(2)}) %collective-permute-start.1) | collective-permute-done | bytes 61472 | tf_op jit(solution)/shard_map/ppermute | solution.py:361
  11.6 0.4 %shard_map.106 = (f32[4,8,128]{2,1,0:T(8,128)S(1)}, f32[64,128]{1,0:T(8,128)S(1)}, bf16[240,128]{1,0:T(8,128)(2,1)S(1)}, bf16[240,128]{1,0:T(8,128)(2,1)S(1)}) custom-call(bf16[240,128]{1,0:T(8,128)(2,1)S(1)} %get-tuple-element.24.refs_0_, bf16[240,128]{1,0:T(8,128)(2,1)S(1)} %collective-permute-done.refs_1_, ...), custom_call_target="tpu_custom_call" | custom-call | flops 1000000 | bytes 172032 | tf_op jit(solution)/shard_map/pallas_call | solution.py:386
  12.0 0.0 collective-permute-done.2.refs_0_
  12.0 0.0 copy-start
  12.0 0.4 %shard_map.107 = (f32[4,8,128]{2,1,0:T(8,128)S(1)}, bf16[64,128]{1,0:T(8,128)(2,1)S(1)}) custom-call(bf16[240,128]{1,0:T(8,128)(2,1)S(1)} %collective-permute-done.2.refs_0_, bf16[240,128]{1,0:T(8,128)(2,1)S(1)} %get-tuple-element.36.refs_1_, bf16[240,128]{1,0:T(8,128)(2,1)S(1)} %get-tuple-element.37.refs_2_, ...), custom_call_target="tpu_custom_call" | custom-call | flops 1000000 | bytes 32768 | tf_op jit(solution)/shard_map/pallas_call | solution.py:393
  12.4 0.1 collective-permute-start.5
  12.5 1.6 %collective-permute-start.4 = (bf16[64,128]{1,0:T(8,128)(2,1)S(1)}, bf16[64,128]{1,0:T(8,128)(2,1)S(1)}, u32[]{:S(2)}, u32[]{:S(2)}) collective-permute-start(bf16[64,128]{1,0:T(8,128)(2,1)S(1)} %get-tuple-element.42.refs_0_), channel_id=1, source_target_pairs={{0,2},{1,3},{2,0},{3,1},{4,6},{5,7},{6,4},{7,5},{8,10},{9,11},{10,... | collective-permute-start | bytes 49160 | tf_op jit(solution)/shard_map/ppermute | solution.py:316
  14.0 0.3 %collective-permute-start.3 = (bf16[64,128]{1,0:T(8,128)(2,1)S(1)}, bf16[64,128]{1,0:T(8,128)(2,1)S(1)}, u32[]{:S(2)}, u32[]{:S(2)}) collective-permute-start(bf16[64,128]{1,0:T(8,128)(2,1)S(1)} %get-tuple-element.42.refs_0_), channel_id=1, source_target_pairs={{0,1},{1,0},{2,3},{3,2},{4,5},{5,4},{6,7},{7,6},{8,9},{9,8},{10,11... | collective-permute-start | bytes 49160 | tf_op jit(solution)/shard_map/ppermute | solution.py:316
  14.3 0.0 copy-done
  14.3 0.6 %shard_map.108 = (bf16[512,256]{1,0:T(8,128)(2,1)S(1)}, f32[8,4,128]{2,1,0:T(4,128)}) custom-call(f32[128,512]{1,0:T(8,128)S(1)} %copy-done, f32[4,8,128]{2,1,0:T(8,128)S(1)} %get-tuple-element.34.early_ref, f32[4,8,128]{2,1,0:T(8,128)S(1)} %get-tuple-element.40.late_ref), custom_call_target="tpu_custom_call" | custom-call | flops 1000000 | bytes 278528 | tf_op jit(solution)/shard_map/pallas_call | solution.py:400
  15.0 0.8 %collective-permute-done.5.refs_3_ = bf16[64,128]{1,0:T(8,128)(2,1)S(1)} collective-permute-done((bf16[64,128]{1,0:T(8,128)(2,1)S(1)}, bf16[64,128]{1,0:T(8,128)(2,1)S(1)}, u32[]{:S(2)}, u32[]{:S(2)}) %collective-permute-start.5) | collective-permute-done | bytes 16416 | tf_op jit(solution)/shard_map/ppermute | solution.py:316
  15.7 0.5 %collective-permute-done.4.refs_2_ = bf16[64,128]{1,0:T(8,128)(2,1)S(1)} collective-permute-done((bf16[64,128]{1,0:T(8,128)(2,1)S(1)}, bf16[64,128]{1,0:T(8,128)(2,1)S(1)}, u32[]{:S(2)}, u32[]{:S(2)}) %collective-permute-start.4) | collective-permute-done | bytes 16416 | tf_op jit(solution)/shard_map/ppermute | solution.py:316
  16.3 0.0 collective-permute-done.3.refs_1_
  16.3 0.8 %shard_map.109 = f32[16,4,128]{2,1,0:T(4,128)} custom-call(bf16[64,128]{1,0:T(8,128)(2,1)S(1)} %get-tuple-element.42.refs_0_, bf16[64,128]{1,0:T(8,128)(2,1)S(1)} %collective-permute-done.3.refs_1_, bf16[64,128]{1,0:T(8,128)(2,1)S(1)} %collective-permute-done.4.refs_2_, bf16[64,128]{1,0:T(8,128)(2,1)S(1)} %collective-permute-done.5.refs_3_, ...), custom_call_target="tpu_custom_call" | custom-call | flops 1000000 | bytes 32768 | tf_op jit(solution)/shard_map/pallas_call | solution.py:410
  (2 shorter events, 0.0 us)
Async XLA Ops:
  0.6 8.3 %copy-start.1 = (f32[16,4,128]{2,1,0:T(4,128)S(1)}, f32[16,4,128]{2,1,0:T(4,128)}, u32[]{:S(2)}) copy-start(f32[16,4,128]{2,1,0:T(4,128)} %measured_ref.1) | copy-start | bytes 98308
  0.6 8.3 %copy-start.2 = (bf16[4,24,24]{2,1,0:T(8,128)(2,1)S(1)}, bf16[4,24,24]{2,1,0:T(8,128)(2,1)}, u32[]{:S(2)}) copy-start(bf16[4,24,24]{2,1,0:T(8,128)(2,1)} %aw_ref.1) | copy-start | bytes 13828
  0.7 8.3 %copy-start.3 = (bf16[4,24,24]{2,1,0:T(8,128)(2,1)S(1)}, bf16[4,24,24]{2,1,0:T(8,128)(2,1)}, u32[]{:S(2)}) copy-start(bf16[4,24,24]{2,1,0:T(8,128)(2,1)} %cw_ref.1) | copy-start | bytes 13828
  1.8 8.7 %collective-permute-start = (bf16[240,128]{1,0:T(8,128)(2,1)S(1)}, bf16[240,128]{1,0:T(8,128)(2,1)S(1)}, u32[]{:S(2)}, u32[]{:S(2)}) collective-permute-start(bf16[240,128]{1,0:T(8,128)(2,1)S(1)} %get-tuple-element.25), channel_id=1, source_target_pairs={{0,4},{1,9},{4,12},{5,13},{8,0},{9,5},{12,8},{13,1},{2,6},{3,11},{... | collective-permute-start | bytes 184328 | tf_op jit(solution)/shard_map/ppermute | solution.py:361
  4.9 6.7 %collective-permute-start.1 = (bf16[240,128]{1,0:T(8,128)(2,1)S(1)}, bf16[240,128]{1,0:T(8,128)(2,1)S(1)}, u32[]{:S(2)}, u32[]{:S(2)}) collective-permute-start(bf16[240,128]{1,0:T(8,128)(2,1)S(1)} %get-tuple-element.26), channel_id=1, source_target_pairs={{0,12},{1,13},{4,8},{5,9},{8,4},{9,1},{12,0},{13,5},{2,14},{3,15},... | collective-permute-start | bytes 184328 | tf_op jit(solution)/shard_map/ppermute | solution.py:361
  7.4 4.6 %collective-permute-start.2 = (bf16[240,128]{1,0:T(8,128)(2,1)S(1)}, bf16[240,128]{1,0:T(8,128)(2,1)S(1)}, u32[]{:S(2)}, u32[]{:S(2)}) collective-permute-start(bf16[240,128]{1,0:T(8,128)(2,1)S(1)} %get-tuple-element.35), channel_id=1, source_target_pairs={{0,8},{1,5},{4,0},{5,1},{8,12},{9,13},{12,4},{13,9},{2,10},{3,7},{... | collective-permute-start | bytes 184328 | tf_op jit(solution)/shard_map/ppermute | solution.py:361
  8.9 0.7 %copy-start.7 = (s32[1,16]{1,0:T(1,128)S(1)}, s32[1,16]{1,0:T(1,128)}, u32[]{:S(2)}) copy-start(s32[1,16]{1,0:T(1,128)} %sparse_ref.1) | copy-start | bytes 196
  8.9 0.7 %copy-start.4 = (f32[24]{0:T(128)S(1)}, f32[24]{0:T(128)}, u32[]{:S(2)}) copy-start(f32[24]{0:T(128)} %param.11) | copy-start | bytes 292
  8.9 0.7 %copy-start.5 = (f32[24]{0:T(128)S(1)}, f32[24]{0:T(128)}, u32[]{:S(2)}) copy-start(f32[24]{0:T(128)} %param.13) | copy-start | bytes 292
  8.9 0.7 %copy-start.6 = (f32[24]{0:T(128)S(1)}, f32[24]{0:T(128)}, u32[]{:S(2)}) copy-start(f32[24]{0:T(128)} %param.14) | copy-start | bytes 292
  12.0 2.4 %copy-start = (f32[128,512]{1,0:T(8,128)S(1)}, f32[128,512]{1,0:T(8,128)}, u32[]{:S(2)}) copy-start(f32[128,512]{1,0:T(8,128)} %rw_ref.1) | copy-start | bytes 786436
  12.4 3.4 %collective-permute-start.5 = (bf16[64,128]{1,0:T(8,128)(2,1)S(1)}, bf16[64,128]{1,0:T(8,128)(2,1)S(1)}, u32[]{:S(2)}, u32[]{:S(2)}) collective-permute-start(bf16[64,128]{1,0:T(8,128)(2,1)S(1)} %get-tuple-element.42.refs_0_), channel_id=1, source_target_pairs={{0,3},{1,2},{2,1},{3,0},{4,7},{5,6},{6,5},{7,4},{8,11},{9,10},{10,... | collective-permute-start | bytes 49160 | tf_op jit(solution)/shard_map/ppermute | solution.py:316
  12.5 3.8 %collective-permute-start.4 = (bf16[64,128]{1,0:T(8,128)(2,1)S(1)}, bf16[64,128]{1,0:T(8,128)(2,1)S(1)}, u32[]{:S(2)}, u32[]{:S(2)}) collective-permute-start(bf16[64,128]{1,0:T(8,128)(2,1)S(1)} %get-tuple-element.42.refs_0_), channel_id=1, source_target_pairs={{0,2},{1,3},{2,0},{3,1},{4,6},{5,7},{6,4},{7,5},{8,10},{9,11},{10,... | collective-permute-start | bytes 49160 | tf_op jit(solution)/shard_map/ppermute | solution.py:316
  14.0 2.2 %collective-permute-start.3 = (bf16[64,128]{1,0:T(8,128)(2,1)S(1)}, bf16[64,128]{1,0:T(8,128)(2,1)S(1)}, u32[]{:S(2)}, u32[]{:S(2)}) collective-permute-start(bf16[64,128]{1,0:T(8,128)(2,1)S(1)} %get-tuple-element.42.refs_0_), channel_id=1, source_target_pairs={{0,1},{1,0},{2,3},{3,2},{4,5},{5,4},{6,7},{7,6},{8,9},{9,8},{10,11... | collective-permute-start | bytes 49160 | tf_op jit(solution)/shard_map/ppermute | solution.py:316

commit v20 on v19

--- a/solution.py
+++ b/solution.py
@@ -354,7 +354,7 @@
         functools.partial(pack_kernel, routes),
         [shape((size, lanes), BF16)] * (wide - 1) + [shape(low_sino.shape[1:], BF16)],
         [pl.BlockSpec(memory_space=pltpu.HBM)],
-        [rows_scratch, pltpu.SemaphoreType.DMA((4,))],
+        [rows_scratch, pltpu.SemaphoreType.DMA((8,))],
         vmem=53.5 if width <= 64 else 48,
     )(low_sino)
     windows = [

time: 17.3 us -> 17.3 us (level)
  no operation moved by 1% of the time
where the time goes in v20:
time: 17.3 us; the launch traced here: 17.1 us
  starting transfers between devices  9.05 us (52%)
  Pallas kernels  4.27 us (25%)
  waiting for transfers between devices  2.34 us (14%)
  between operations  0.75 us (4%)
  local copies, waits for them, and re-layouts  0.69 us (4%)
    ppermute x3, starting transfers between devices, local(): lax.ppermute(window, ('wide', 'pair'), [(p, t * pair + p % pair) for p, t...  7.13 us
    ppermute x3, starting transfers between devices, send_both(): return lax.ppermute(block, ('narrow', 'pair'), route)  1.92 us
    ppermute x3, waiting for transfers between devices, send_both(): return lax.ppermute(block, ('narrow', 'pair'), route)  1.31 us
    pallas_call x1, Pallas kernels, local(): call(functools.partial(pack_kernel, routes), [shape((size, lanes), BF16)]...  1.16 us
    ppermute x3, waiting for transfers between devices, local(): lax.ppermute(window, ('wide', 'pair'), [(p, t * pair + p % pair) for p, t...  1.03 us
    pallas_call x1, Pallas kernels, local(): call(functools.partial(prepare_kernel, wide, own_out, groups), [shape((2...  0.88 us
    pallas_call x1, Pallas kernels, local(): call(functools.partial(adjoint_kernel, shifts, own_out), shape((sparse_co...  0.79 us
    unnamed x16, local copies, waits for them, and re-layouts  0.69 us
  transfers between devices with their start and end apart: 6, of which 3 were waited for; matrix products, arithmetic and copies ran while one was open for 0% of the time, Pallas kernels for 11%

profile of v20, /device:TPU:0, one launch (start us, length us, event | category | flops | bytes accessed | tf_op | source)
XLA Modules:
  0.0 17.1 jit_solution(5825069610672643498)
XLA Ops:
  0.6 0.0 copy-start.1
  0.6 0.0 copy-start.2
  0.7 0.0 copy-start.3
  0.7 1.2 %shard_map.104 = (bf16[240,128]{1,0:T(8,128)(2,1)S(1)}, bf16[240,128]{1,0:T(8,128)(2,1)S(1)}, bf16[240,128]{1,0:T(8,128)(2,1)S(1)}, bf16[24,32,128]{2,1,0:T(8,128)(2,1)S(1)}) custom-call(bf16[1,24,32,128]{3,2,1,0:T(8,128)(2,1)} %low_ref.1), custom_call_target="tpu_custom_call" | custom-call | flops 1000000 | bytes 380928 | tf_op jit(solution)/shard_map/pallas_call | solution.py:353
  1.8 3.1 %collective-permute-start = (bf16[240,128]{1,0:T(8,128)(2,1)S(1)}, bf16[240,128]{1,0:T(8,128)(2,1)S(1)}, u32[]{:S(2)}, u32[]{:S(2)}) collective-permute-start(bf16[240,128]{1,0:T(8,128)(2,1)S(1)} %get-tuple-element.25), channel_id=1, source_target_pairs={{0,4},{1,9},{4,12},{5,13},{8,0},{9,5},{12,8},{13,1},{2,6},{3,11},{... | collective-permute-start | bytes 184328 | tf_op jit(solution)/shard_map/ppermute | solution.py:361
  4.9 2.5 %collective-permute-start.1 = (bf16[240,128]{1,0:T(8,128)(2,1)S(1)}, bf16[240,128]{1,0:T(8,128)(2,1)S(1)}, u32[]{:S(2)}, u32[]{:S(2)}) collective-permute-start(bf16[240,128]{1,0:T(8,128)(2,1)S(1)} %get-tuple-element.26), channel_id=1, source_target_pairs={{0,12},{1,13},{4,8},{5,9},{8,4},{9,1},{12,0},{13,5},{2,14},{3,15},... | collective-permute-start | bytes 184328 | tf_op jit(solution)/shard_map/ppermute | solution.py:361
  7.4 1.6 %collective-permute-start.2 = (bf16[240,128]{1,0:T(8,128)(2,1)S(1)}, bf16[240,128]{1,0:T(8,128)(2,1)S(1)}, u32[]{:S(2)}, u32[]{:S(2)}) collective-permute-start(bf16[240,128]{1,0:T(8,128)(2,1)S(1)} %get-tuple-element.35), channel_id=1, source_target_pairs={{0,8},{1,5},{4,0},{5,1},{8,12},{9,13},{12,4},{13,9},{2,10},{3,7},{... | collective-permute-start | bytes 184328 | tf_op jit(solution)/shard_map/ppermute | solution.py:361
  9.0 0.0 copy-start.7
  9.0 0.0 copy-start.4
  9.0 0.0 copy-done.1
  9.0 0.0 copy-done.2
  9.0 0.0 copy-done.3
  9.0 0.6 %copy-done.7 = s32[1,16]{1,0:T(1,128)S(1)} copy-done((s32[1,16]{1,0:T(1,128)S(1)}, s32[1,16]{1,0:T(1,128)}, u32[]{:S(2)}) %copy-start.7) | copy-done | bytes 88
  9.6 0.0 copy-done.4
  9.6 0.0 copy-done.5
  9.6 0.0 copy-done.6
  9.7 0.9 %shard_map.105 = (bf16[96,96]{1,0:T(8,128)(2,1)S(1)}, bf16[192,192]{1,0:T(8,128)(2,1)S(1)}, bf16[96,240]{1,0:T(8,128)(2,1)S(1)}, f32[240,128]{1,0:T(8,128)S(1)},...) custom-call(bf16[4,24,24]{2,1,0:T(8,128)(2,1)S(1)} %copy-done.2, ...), custom_call_target="tpu_custom_call" | custom-call | flops 1000000 | bytes 486400 | tf_op jit(solution)/shard_map/pallas_call | solution.py:366
  10.5 0.0 collective-permute-done.refs_1_
  10.6 1.0 %collective-permute-done.1.refs_2_ = bf16[240,128]{1,0:T(8,128)(2,1)S(1)} collective-permute-done((bf16[240,128]{1,0:T(8,128)(2,1)S(1)}, bf16[240,128]{1,0:T(8,128)(2,1)S(1)}, u32[]{:S(2)}, u32[]{:S(2)}) %collective-permute-start.1) | collective-permute-done | bytes 61472 | tf_op jit(solution)/shard_map/ppermute | solution.py:361
  11.6 0.4 %shard_map.106 = (f32[4,8,128]{2,1,0:T(8,128)S(1)}, f32[64,128]{1,0:T(8,128)S(1)}, bf16[240,128]{1,0:T(8,128)(2,1)S(1)}, bf16[240,128]{1,0:T(8,128)(2,1)S(1)}) custom-call(bf16[240,128]{1,0:T(8,128)(2,1)S(1)} %get-tuple-element.24.refs_0_, bf16[240,128]{1,0:T(8,128)(2,1)S(1)} %collective-permute-done.refs_1_, ...), custom_call_target="tpu_custom_call" | custom-call | flops 1000000 | bytes 172032 | tf_op jit(solution)/shard_map/pallas_call | solution.py:386
  12.0 0.0 collective-permute-done.2.refs_0_
  12.0 0.0 copy-start
  12.0 0.4 %shard_map.107 = (f32[4,8,128]{2,1,0:T(8,128)S(1)}, bf16[64,128]{1,0:T(8,128)(2,1)S(1)}) custom-call(bf16[240,128]{1,0:T(8,128)(2,1)S(1)} %collective-permute-done.2.refs_0_, bf16[240,128]{1,0:T(8,128)(2,1)S(1)} %get-tuple-element.36.refs_1_, bf16[240,128]{1,0:T(8,128)(2,1)S(1)} %get-tuple-element.37.refs_2_, ...), custom_call_target="tpu_custom_call" | custom-call | flops 1000000 | bytes 32768 | tf_op jit(solution)/shard_map/pallas_call | solution.py:393
  12.4 0.1 collective-permute-start.5
  12.5 1.6 %collective-permute-start.4 = (bf16[64,128]{1,0:T(8,128)(2,1)S(1)}, bf16[64,128]{1,0:T(8,128)(2,1)S(1)}, u32[]{:S(2)}, u32[]{:S(2)}) collective-permute-start(bf16[64,128]{1,0:T(8,128)(2,1)S(1)} %get-tuple-element.42.refs_0_), channel_id=1, source_target_pairs={{0,2},{1,3},{2,0},{3,1},{4,6},{5,7},{6,4},{7,5},{8,10},{9,11},{10,... | collective-permute-start | bytes 49160 | tf_op jit(solution)/shard_map/ppermute | solution.py:316
  14.1 0.3 %collective-permute-start.3 = (bf16[64,128]{1,0:T(8,128)(2,1)S(1)}, bf16[64,128]{1,0:T(8,128)(2,1)S(1)}, u32[]{:S(2)}, u32[]{:S(2)}) collective-permute-start(bf16[64,128]{1,0:T(8,128)(2,1)S(1)} %get-tuple-element.42.refs_0_), channel_id=1, source_target_pairs={{0,1},{1,0},{2,3},{3,2},{4,5},{5,4},{6,7},{7,6},{8,9},{9,8},{10,11... | collective-permute-start | bytes 49160 | tf_op jit(solution)/shard_map/ppermute | solution.py:316
  14.3 0.0 copy-done
  14.3 0.6 %shard_map.108 = (bf16[512,256]{1,0:T(8,128)(2,1)S(1)}, f32[8,4,128]{2,1,0:T(4,128)}) custom-call(f32[128,512]{1,0:T(8,128)S(1)} %copy-done, f32[4,8,128]{2,1,0:T(8,128)S(1)} %get-tuple-element.34.early_ref, f32[4,8,128]{2,1,0:T(8,128)S(1)} %get-tuple-element.40.late_ref), custom_call_target="tpu_custom_call" | custom-call | flops 1000000 | bytes 278528 | tf_op jit(solution)/shard_map/pallas_call | solution.py:400
  15.0 0.8 %collective-permute-done.5.refs_3_ = bf16[64,128]{1,0:T(8,128)(2,1)S(1)} collective-permute-done((bf16[64,128]{1,0:T(8,128)(2,1)S(1)}, bf16[64,128]{1,0:T(8,128)(2,1)S(1)}, u32[]{:S(2)}, u32[]{:S(2)}) %collective-permute-start.5) | collective-permute-done | bytes 16416 | tf_op jit(solution)/shard_map/ppermute | solution.py:316
  15.8 0.5 %collective-permute-done.4.refs_2_ = bf16[64,128]{1,0:T(8,128)(2,1)S(1)} collective-permute-done((bf16[64,128]{1,0:T(8,128)(2,1)S(1)}, bf16[64,128]{1,0:T(8,128)(2,1)S(1)}, u32[]{:S(2)}, u32[]{:S(2)}) %collective-permute-start.4) | collective-permute-done | bytes 16416 | tf_op jit(solution)/shard_map/ppermute | solution.py:316
  16.3 0.0 collective-permute-done.3.refs_1_
  16.3 0.8 %shard_map.109 = f32[16,4,128]{2,1,0:T(4,128)} custom-call(bf16[64,128]{1,0:T(8,128)(2,1)S(1)} %get-tuple-element.42.refs_0_, bf16[64,128]{1,0:T(8,128)(2,1)S(1)} %collective-permute-done.3.refs_1_, bf16[64,128]{1,0:T(8,128)(2,1)S(1)} %collective-permute-done.4.refs_2_, bf16[64,128]{1,0:T(8,128)(2,1)S(1)} %collective-permute-done.5.refs_3_, ...), custom_call_target="tpu_custom_call" | custom-call | flops 1000000 | bytes 32768 | tf_op jit(solution)/shard_map/pallas_call | solution.py:410
  (2 shorter events, 0.0 us)
Async XLA Ops:
  0.6 8.3 %copy-start.1 = (f32[16,4,128]{2,1,0:T(4,128)S(1)}, f32[16,4,128]{2,1,0:T(4,128)}, u32[]{:S(2)}) copy-start(f32[16,4,128]{2,1,0:T(4,128)} %measured_ref.1) | copy-start | bytes 98308
  0.6 8.3 %copy-start.2 = (bf16[4,24,24]{2,1,0:T(8,128)(2,1)S(1)}, bf16[4,24,24]{2,1,0:T(8,128)(2,1)}, u32[]{:S(2)}) copy-start(bf16[4,24,24]{2,1,0:T(8,128)(2,1)} %aw_ref.1) | copy-start | bytes 13828
  0.7 8.3 %copy-start.3 = (bf16[4,24,24]{2,1,0:T(8,128)(2,1)S(1)}, bf16[4,24,24]{2,1,0:T(8,128)(2,1)}, u32[]{:S(2)}) copy-start(bf16[4,24,24]{2,1,0:T(8,128)(2,1)} %cw_ref.1) | copy-start | bytes 13828
  1.8 8.7 %collective-permute-start = (bf16[240,128]{1,0:T(8,128)(2,1)S(1)}, bf16[240,128]{1,0:T(8,128)(2,1)S(1)}, u32[]{:S(2)}, u32[]{:S(2)}) collective-permute-start(bf16[240,128]{1,0:T(8,128)(2,1)S(1)} %get-tuple-element.25), channel_id=1, source_target_pairs={{0,4},{1,9},{4,12},{5,13},{8,0},{9,5},{12,8},{13,1},{2,6},{3,11},{... | collective-permute-start | bytes 184328 | tf_op jit(solution)/shard_map/ppermute | solution.py:361
  4.9 6.7 %collective-permute-start.1 = (bf16[240,128]{1,0:T(8,128)(2,1)S(1)}, bf16[240,128]{1,0:T(8,128)(2,1)S(1)}, u32[]{:S(2)}, u32[]{:S(2)}) collective-permute-start(bf16[240,128]{1,0:T(8,128)(2,1)S(1)} %get-tuple-element.26), channel_id=1, source_target_pairs={{0,12},{1,13},{4,8},{5,9},{8,4},{9,1},{12,0},{13,5},{2,14},{3,15},... | collective-permute-start | bytes 184328 | tf_op jit(solution)/shard_map/ppermute | solution.py:361
  7.4 4.6 %collective-permute-start.2 = (bf16[240,128]{1,0:T(8,128)(2,1)S(1)}, bf16[240,128]{1,0:T(8,128)(2,1)S(1)}, u32[]{:S(2)}, u32[]{:S(2)}) collective-permute-start(bf16[240,128]{1,0:T(8,128)(2,1)S(1)} %get-tuple-element.35), channel_id=1, source_target_pairs={{0,8},{1,5},{4,0},{5,1},{8,12},{9,13},{12,4},{13,9},{2,10},{3,7},{... | collective-permute-start | bytes 184328 | tf_op jit(solution)/shard_map/ppermute | solution.py:361
  9.0 0.7 %copy-start.7 = (s32[1,16]{1,0:T(1,128)S(1)}, s32[1,16]{1,0:T(1,128)}, u32[]{:S(2)}) copy-start(s32[1,16]{1,0:T(1,128)} %sparse_ref.1) | copy-start | bytes 196
  9.0 0.7 %copy-start.4 = (f32[24]{0:T(128)S(1)}, f32[24]{0:T(128)}, u32[]{:S(2)}) copy-start(f32[24]{0:T(128)} %param.11) | copy-start | bytes 292
  9.0 0.7 %copy-start.5 = (f32[24]{0:T(128)S(1)}, f32[24]{0:T(128)}, u32[]{:S(2)}) copy-start(f32[24]{0:T(128)} %param.13) | copy-start | bytes 292
  9.0 0.7 %copy-start.6 = (f32[24]{0:T(128)S(1)}, f32[24]{0:T(128)}, u32[]{:S(2)}) copy-start(f32[24]{0:T(128)} %param.14) | copy-start | bytes 292
  12.0 2.4 %copy-start = (f32[128,512]{1,0:T(8,128)S(1)}, f32[128,512]{1,0:T(8,128)}, u32[]{:S(2)}) copy-start(f32[128,512]{1,0:T(8,128)} %rw_ref.1) | copy-start | bytes 786436
  12.4 3.4 %collective-permute-start.5 = (bf16[64,128]{1,0:T(8,128)(2,1)S(1)}, bf16[64,128]{1,0:T(8,128)(2,1)S(1)}, u32[]{:S(2)}, u32[]{:S(2)}) collective-permute-start(bf16[64,128]{1,0:T(8,128)(2,1)S(1)} %get-tuple-element.42.refs_0_), channel_id=1, source_target_pairs={{0,3},{1,2},{2,1},{3,0},{4,7},{5,6},{6,5},{7,4},{8,11},{9,10},{10,... | collective-permute-start | bytes 49160 | tf_op jit(solution)/shard_map/ppermute | solution.py:316
  12.5 3.8 %collective-permute-start.4 = (bf16[64,128]{1,0:T(8,128)(2,1)S(1)}, bf16[64,128]{1,0:T(8,128)(2,1)S(1)}, u32[]{:S(2)}, u32[]{:S(2)}) collective-permute-start(bf16[64,128]{1,0:T(8,128)(2,1)S(1)} %get-tuple-element.42.refs_0_), channel_id=1, source_target_pairs={{0,2},{1,3},{2,0},{3,1},{4,6},{5,7},{6,4},{7,5},{8,10},{9,11},{10,... | collective-permute-start | bytes 49160 | tf_op jit(solution)/shard_map/ppermute | solution.py:316
  14.1 2.3 %collective-permute-start.3 = (bf16[64,128]{1,0:T(8,128)(2,1)S(1)}, bf16[64,128]{1,0:T(8,128)(2,1)S(1)}, u32[]{:S(2)}, u32[]{:S(2)}) collective-permute-start(bf16[64,128]{1,0:T(8,128)(2,1)S(1)} %get-tuple-element.42.refs_0_), channel_id=1, source_target_pairs={{0,1},{1,0},{2,3},{3,2},{4,5},{5,4},{6,7},{7,6},{8,9},{9,8},{10,11... | collective-permute-start | bytes 49160 | tf_op jit(solution)/shard_map/ppermute | solution.py:316

commit v21 on v20

--- a/solution.py
+++ b/solution.py
@@ -354,7 +354,7 @@
         functools.partial(pack_kernel, routes),
         [shape((size, lanes), BF16)] * (wide - 1) + [shape(low_sino.shape[1:], BF16)],
         [pl.BlockSpec(memory_space=pltpu.HBM)],
-        [rows_scratch, pltpu.SemaphoreType.DMA((8,))],
+        [rows_scratch, pltpu.SemaphoreType.DMA((2,))],
         vmem=53.5 if width <= 64 else 48,
     )(low_sino)
     windows = [

time: 17.3 us -> 17.3 us (level)
  no operation moved by 1% of the time
where the time goes in v21:
time: 17.3 us; the launch traced here: 17.1 us
  starting transfers between devices  9.05 us (52%)
  Pallas kernels  4.32 us (25%)
  waiting for transfers between devices  2.33 us (13%)
  between operations  0.75 us (4%)
  local copies, waits for them, and re-layouts  0.69 us (4%)
    ppermute x3, starting transfers between devices, local(): lax.ppermute(window, ('wide', 'pair'), [(p, t * pair + p % pair) for p, t...  7.13 us
    ppermute x3, starting transfers between devices, send_both(): return lax.ppermute(block, ('narrow', 'pair'), route)  1.92 us
    ppermute x3, waiting for transfers between devices, send_both(): return lax.ppermute(block, ('narrow', 'pair'), route)  1.31 us
    pallas_call x1, Pallas kernels, local(): call(functools.partial(pack_kernel, routes), [shape((size, lanes), BF16)]...  1.2 us
    ppermute x3, waiting for transfers between devices, local(): lax.ppermute(window, ('wide', 'pair'), [(p, t * pair + p % pair) for p, t...  1.02 us
    pallas_call x1, Pallas kernels, local(): call(functools.partial(prepare_kernel, wide, own_out, groups), [shape((2...  0.88 us
    pallas_call x1, Pallas kernels, local(): call(functools.partial(adjoint_kernel, shifts, own_out), shape((sparse_co...  0.79 us
    unnamed x16, local copies, waits for them, and re-layouts  0.69 us
  transfers between devices with their start and end apart: 6, of which 3 were waited for; matrix products, arithmetic and copies ran while one was open for 0% of the time, Pallas kernels for 11%

profile of v21, /device:TPU:0, one launch (start us, length us, event | category | flops | bytes accessed | tf_op | source)
XLA Modules:
  0.0 17.1 jit_solution(17740882455306427416)
XLA Ops:
  0.6 0.0 copy-start.1
  0.6 0.0 copy-start.2
  0.7 0.0 copy-start.3
  0.7 1.2 %shard_map.104 = (bf16[240,128]{1,0:T(8,128)(2,1)S(1)}, bf16[240,128]{1,0:T(8,128)(2,1)S(1)}, bf16[240,128]{1,0:T(8,128)(2,1)S(1)}, bf16[24,32,128]{2,1,0:T(8,128)(2,1)S(1)}) custom-call(bf16[1,24,32,128]{3,2,1,0:T(8,128)(2,1)} %low_ref.1), custom_call_target="tpu_custom_call" | custom-call | flops 1000000 | bytes 380928 | tf_op jit(solution)/shard_map/pallas_call | solution.py:353
  1.9 3.1 %collective-permute-start = (bf16[240,128]{1,0:T(8,128)(2,1)S(1)}, bf16[240,128]{1,0:T(8,128)(2,1)S(1)}, u32[]{:S(2)}, u32[]{:S(2)}) collective-permute-start(bf16[240,128]{1,0:T(8,128)(2,1)S(1)} %get-tuple-element.25), channel_id=1, source_target_pairs={{0,4},{1,9},{4,12},{5,13},{8,0},{9,5},{12,8},{13,1},{2,6},{3,11},{... | collective-permute-start | bytes 184328 | tf_op jit(solution)/shard_map/ppermute | solution.py:361
  4.9 2.5 %collective-permute-start.1 = (bf16[240,128]{1,0:T(8,128)(2,1)S(1)}, bf16[240,128]{1,0:T(8,128)(2,1)S(1)}, u32[]{:S(2)}, u32[]{:S(2)}) collective-permute-start(bf16[240,128]{1,0:T(8,128)(2,1)S(1)} %get-tuple-element.26), channel_id=1, source_target_pairs={{0,12},{1,13},{4,8},{5,9},{8,4},{9,1},{12,0},{13,5},{2,14},{3,15},... | collective-permute-start | bytes 184328 | tf_op jit(solution)/shard_map/ppermute | solution.py:361
  7.4 1.6 %collective-permute-start.2 = (bf16[240,128]{1,0:T(8,128)(2,1)S(1)}, bf16[240,128]{1,0:T(8,128)(2,1)S(1)}, u32[]{:S(2)}, u32[]{:S(2)}) collective-permute-start(bf16[240,128]{1,0:T(8,128)(2,1)S(1)} %get-tuple-element.35), channel_id=1, source_target_pairs={{0,8},{1,5},{4,0},{5,1},{8,12},{9,13},{12,4},{13,9},{2,10},{3,7},{... | collective-permute-start | bytes 184328 | tf_op jit(solution)/shard_map/ppermute | solution.py:361
  9.0 0.0 copy-start.7
  9.0 0.0 copy-start.4
  9.0 0.0 copy-done.1
  9.0 0.0 copy-done.2
  9.0 0.0 copy-done.3
  9.0 0.6 %copy-done.7 = s32[1,16]{1,0:T(1,128)S(1)} copy-done((s32[1,16]{1,0:T(1,128)S(1)}, s32[1,16]{1,0:T(1,128)}, u32[]{:S(2)}) %copy-start.7) | copy-done | bytes 88
  9.6 0.0 copy-done.4
  9.7 0.0 copy-done.5
  9.7 0.0 copy-done.6
  9.7 0.9 %shard_map.105 = (bf16[96,96]{1,0:T(8,128)(2,1)S(1)}, bf16[192,192]{1,0:T(8,128)(2,1)S(1)}, bf16[96,240]{1,0:T(8,128)(2,1)S(1)}, f32[240,128]{1,0:T(8,128)S(1)},...) custom-call(bf16[4,24,24]{2,1,0:T(8,128)(2,1)S(1)} %copy-done.2, ...), custom_call_target="tpu_custom_call" | custom-call | flops 1000000 | bytes 486400 | tf_op jit(solution)/shard_map/pallas_call | solution.py:366
  10.6 0.0 collective-permute-done.refs_1_
  10.6 1.0 %collective-permute-done.1.refs_2_ = bf16[240,128]{1,0:T(8,128)(2,1)S(1)} collective-permute-done((bf16[240,128]{1,0:T(8,128)(2,1)S(1)}, bf16[240,128]{1,0:T(8,128)(2,1)S(1)}, u32[]{:S(2)}, u32[]{:S(2)}) %collective-permute-start.1) | collective-permute-done | bytes 61472 | tf_op jit(solution)/shard_map/ppermute | solution.py:361
  11.6 0.4 %shard_map.106 = (f32[4,8,128]{2,1,0:T(8,128)S(1)}, f32[64,128]{1,0:T(8,128)S(1)}, bf16[240,128]{1,0:T(8,128)(2,1)S(1)}, bf16[240,128]{1,0:T(8,128)(2,1)S(1)}) custom-call(bf16[240,128]{1,0:T(8,128)(2,1)S(1)} %get-tuple-element.24.refs_0_, bf16[240,128]{1,0:T(8,128)(2,1)S(1)} %collective-permute-done.refs_1_, ...), custom_call_target="tpu_custom_call" | custom-call | flops 1000000 | bytes 172032 | tf_op jit(solution)/shard_map/pallas_call | solution.py:386
  12.0 0.0 collective-permute-done.2.refs_0_
  12.0 0.0 copy-start
  12.0 0.4 %shard_map.107 = (f32[4,8,128]{2,1,0:T(8,128)S(1)}, bf16[64,128]{1,0:T(8,128)(2,1)S(1)}) custom-call(bf16[240,128]{1,0:T(8,128)(2,1)S(1)} %collective-permute-done.2.refs_0_, bf16[240,128]{1,0:T(8,128)(2,1)S(1)} %get-tuple-element.36.refs_1_, bf16[240,128]{1,0:T(8,128)(2,1)S(1)} %get-tuple-element.37.refs_2_, ...), custom_call_target="tpu_custom_call" | custom-call | flops 1000000 | bytes 32768 | tf_op jit(solution)/shard_map/pallas_call | solution.py:393
  12.5 0.1 collective-permute-start.5
  12.5 1.6 %collective-permute-start.4 = (bf16[64,128]{1,0:T(8,128)(2,1)S(1)}, bf16[64,128]{1,0:T(8,128)(2,1)S(1)}, u32[]{:S(2)}, u32[]{:S(2)}) collective-permute-start(bf16[64,128]{1,0:T(8,128)(2,1)S(1)} %get-tuple-element.42.refs_0_), channel_id=1, source_target_pairs={{0,2},{1,3},{2,0},{3,1},{4,6},{5,7},{6,4},{7,5},{8,10},{9,11},{10,... | collective-permute-start | bytes 49160 | tf_op jit(solution)/shard_map/ppermute | solution.py:316
  14.1 0.3 %collective-permute-start.3 = (bf16[64,128]{1,0:T(8,128)(2,1)S(1)}, bf16[64,128]{1,0:T(8,128)(2,1)S(1)}, u32[]{:S(2)}, u32[]{:S(2)}) collective-permute-start(bf16[64,128]{1,0:T(8,128)(2,1)S(1)} %get-tuple-element.42.refs_0_), channel_id=1, source_target_pairs={{0,1},{1,0},{2,3},{3,2},{4,5},{5,4},{6,7},{7,6},{8,9},{9,8},{10,11... | collective-permute-start | bytes 49160 | tf_op jit(solution)/shard_map/ppermute | solution.py:316
  14.4 0.0 copy-done
  14.4 0.6 %shard_map.108 = (bf16[512,256]{1,0:T(8,128)(2,1)S(1)}, f32[8,4,128]{2,1,0:T(4,128)}) custom-call(f32[128,512]{1,0:T(8,128)S(1)} %copy-done, f32[4,8,128]{2,1,0:T(8,128)S(1)} %get-tuple-element.34.early_ref, f32[4,8,128]{2,1,0:T(8,128)S(1)} %get-tuple-element.40.late_ref), custom_call_target="tpu_custom_call" | custom-call | flops 1000000 | bytes 278528 | tf_op jit(solution)/shard_map/pallas_call | solution.py:400
  15.0 0.8 %collective-permute-done.5.refs_3_ = bf16[64,128]{1,0:T(8,128)(2,1)S(1)} collective-permute-done((bf16[64,128]{1,0:T(8,128)(2,1)S(1)}, bf16[64,128]{1,0:T(8,128)(2,1)S(1)}, u32[]{:S(2)}, u32[]{:S(2)}) %collective-permute-start.5) | collective-permute-done | bytes 16416 | tf_op jit(solution)/shard_map/ppermute | solution.py:316
  15.8 0.5 %collective-permute-done.4.refs_2_ = bf16[64,128]{1,0:T(8,128)(2,1)S(1)} collective-permute-done((bf16[64,128]{1,0:T(8,128)(2,1)S(1)}, bf16[64,128]{1,0:T(8,128)(2,1)S(1)}, u32[]{:S(2)}, u32[]{:S(2)}) %collective-permute-start.4) | collective-permute-done | bytes 16416 | tf_op jit(solution)/shard_map/ppermute | solution.py:316
  16.3 0.0 collective-permute-done.3.refs_1_
  16.3 0.8 %shard_map.109 = f32[16,4,128]{2,1,0:T(4,128)} custom-call(bf16[64,128]{1,0:T(8,128)(2,1)S(1)} %get-tuple-element.42.refs_0_, bf16[64,128]{1,0:T(8,128)(2,1)S(1)} %collective-permute-done.3.refs_1_, bf16[64,128]{1,0:T(8,128)(2,1)S(1)} %collective-permute-done.4.refs_2_, bf16[64,128]{1,0:T(8,128)(2,1)S(1)} %collective-permute-done.5.refs_3_, ...), custom_call_target="tpu_custom_call" | custom-call | flops 1000000 | bytes 32768 | tf_op jit(solution)/shard_map/pallas_call | solution.py:410
  (2 shorter events, 0.0 us)
Async XLA Ops:
  0.6 8.4 %copy-start.1 = (f32[16,4,128]{2,1,0:T(4,128)S(1)}, f32[16,4,128]{2,1,0:T(4,128)}, u32[]{:S(2)}) copy-start(f32[16,4,128]{2,1,0:T(4,128)} %measured_ref.1) | copy-start | bytes 98308
  0.6 8.4 %copy-start.2 = (bf16[4,24,24]{2,1,0:T(8,128)(2,1)S(1)}, bf16[4,24,24]{2,1,0:T(8,128)(2,1)}, u32[]{:S(2)}) copy-start(bf16[4,24,24]{2,1,0:T(8,128)(2,1)} %aw_ref.1) | copy-start | bytes 13828
  0.7 8.4 %copy-start.3 = (bf16[4,24,24]{2,1,0:T(8,128)(2,1)S(1)}, bf16[4,24,24]{2,1,0:T(8,128)(2,1)}, u32[]{:S(2)}) copy-start(bf16[4,24,24]{2,1,0:T(8,128)(2,1)} %cw_ref.1) | copy-start | bytes 13828
  1.9 8.7 %collective-permute-start = (bf16[240,128]{1,0:T(8,128)(2,1)S(1)}, bf16[240,128]{1,0:T(8,128)(2,1)S(1)}, u32[]{:S(2)}, u32[]{:S(2)}) collective-permute-start(bf16[240,128]{1,0:T(8,128)(2,1)S(1)} %get-tuple-element.25), channel_id=1, source_target_pairs={{0,4},{1,9},{4,12},{5,13},{8,0},{9,5},{12,8},{13,1},{2,6},{3,11},{... | collective-permute-start | bytes 184328 | tf_op jit(solution)/shard_map/ppermute | solution.py:361
  4.9 6.7 %collective-permute-start.1 = (bf16[240,128]{1,0:T(8,128)(2,1)S(1)}, bf16[240,128]{1,0:T(8,128)(2,1)S(1)}, u32[]{:S(2)}, u32[]{:S(2)}) collective-permute-start(bf16[240,128]{1,0:T(8,128)(2,1)S(1)} %get-tuple-element.26), channel_id=1, source_target_pairs={{0,12},{1,13},{4,8},{5,9},{8,4},{9,1},{12,0},{13,5},{2,14},{3,15},... | collective-permute-start | bytes 184328 | tf_op jit(solution)/shard_map/ppermute | solution.py:361
  7.4 4.6 %collective-permute-start.2 = (bf16[240,128]{1,0:T(8,128)(2,1)S(1)}, bf16[240,128]{1,0:T(8,128)(2,1)S(1)}, u32[]{:S(2)}, u32[]{:S(2)}) collective-permute-start(bf16[240,128]{1,0:T(8,128)(2,1)S(1)} %get-tuple-element.35), channel_id=1, source_target_pairs={{0,8},{1,5},{4,0},{5,1},{8,12},{9,13},{12,4},{13,9},{2,10},{3,7},{... | collective-permute-start | bytes 184328 | tf_op jit(solution)/shard_map/ppermute | solution.py:361
  9.0 0.7 %copy-start.7 = (s32[1,16]{1,0:T(1,128)S(1)}, s32[1,16]{1,0:T(1,128)}, u32[]{:S(2)}) copy-start(s32[1,16]{1,0:T(1,128)} %sparse_ref.1) | copy-start | bytes 196
  9.0 0.7 %copy-start.4 = (f32[24]{0:T(128)S(1)}, f32[24]{0:T(128)}, u32[]{:S(2)}) copy-start(f32[24]{0:T(128)} %param.11) | copy-start | bytes 292
  9.0 0.7 %copy-start.5 = (f32[24]{0:T(128)S(1)}, f32[24]{0:T(128)}, u32[]{:S(2)}) copy-start(f32[24]{0:T(128)} %param.13) | copy-start | bytes 292
  9.0 0.7 %copy-start.6 = (f32[24]{0:T(128)S(1)}, f32[24]{0:T(128)}, u32[]{:S(2)}) copy-start(f32[24]{0:T(128)} %param.14) | copy-start | bytes 292
  12.0 2.4 %copy-start = (f32[128,512]{1,0:T(8,128)S(1)}, f32[128,512]{1,0:T(8,128)}, u32[]{:S(2)}) copy-start(f32[128,512]{1,0:T(8,128)} %rw_ref.1) | copy-start | bytes 786436
  12.5 3.4 %collective-permute-start.5 = (bf16[64,128]{1,0:T(8,128)(2,1)S(1)}, bf16[64,128]{1,0:T(8,128)(2,1)S(1)}, u32[]{:S(2)}, u32[]{:S(2)}) collective-permute-start(bf16[64,128]{1,0:T(8,128)(2,1)S(1)} %get-tuple-element.42.refs_0_), channel_id=1, source_target_pairs={{0,3},{1,2},{2,1},{3,0},{4,7},{5,6},{6,5},{7,4},{8,11},{9,10},{10,... | collective-permute-start | bytes 49160 | tf_op jit(solution)/shard_map/ppermute | solution.py:316
  12.5 3.8 %collective-permute-start.4 = (bf16[64,128]{1,0:T(8,128)(2,1)S(1)}, bf16[64,128]{1,0:T(8,128)(2,1)S(1)}, u32[]{:S(2)}, u32[]{:S(2)}) collective-permute-start(bf16[64,128]{1,0:T(8,128)(2,1)S(1)} %get-tuple-element.42.refs_0_), channel_id=1, source_target_pairs={{0,2},{1,3},{2,0},{3,1},{4,6},{5,7},{6,4},{7,5},{8,10},{9,11},{10,... | collective-permute-start | bytes 49160 | tf_op jit(solution)/shard_map/ppermute | solution.py:316
  14.1 2.2 %collective-permute-start.3 = (bf16[64,128]{1,0:T(8,128)(2,1)S(1)}, bf16[64,128]{1,0:T(8,128)(2,1)S(1)}, u32[]{:S(2)}, u32[]{:S(2)}) collective-permute-start(bf16[64,128]{1,0:T(8,128)(2,1)S(1)} %get-tuple-element.42.refs_0_), channel_id=1, source_target_pairs={{0,1},{1,0},{2,3},{3,2},{4,5},{5,4},{6,7},{7,6},{8,9},{9,8},{10,11... | collective-permute-start | bytes 49160 | tf_op jit(solution)/shard_map/ppermute | solution.py:316
